TPU v7x, 128 devices: a whole 4x4x4 slice. The times are simulated.
128 devices in a mesh: band: 8 (over z, core), mesh: 16 (over x, y).
Axes of the slice: x: 4, y: 4, z: 4, core: 2. Of those that a mesh axis runs over, the one named last changes fastest.
Arguments:
- grid: bfloat16 [65536, 512], P(('band', 'mesh')), may hold values from -6 to 6
- mesh_latent: bfloat16 [32768, 512], P(('band', 'mesh')), may hold values from -6 to 6
- edge_latent: bfloat16 [262144, 512], P(('band', 'mesh')), may hold values from -6 to 6
- edge_grid_block: int32 [2048], P(('band', 'mesh')), may hold values from 0 to 63
- edge_mesh_block: int32 [2048], P(('band', 'mesh')), may hold values from 0 to 15
- sender_offset: int32 [2048, 128], P(('band', 'mesh')), may hold values from 0 to 127
- receiver_offset: int32 [2048, 128], P(('band', 'mesh')), may hold values from 0 to 127
- live_groups: int32 [128], P(('band', 'mesh')), may hold values from 1 to 4, as said below
- w_grid: bfloat16 [512, 512], replicated, may hold values from -0.25 to 0.25
- w_mesh: bfloat16 [512, 512], replicated, may hold values from -0.25 to 0.25
- w_edge: bfloat16 [512, 512], replicated, may hold values from -0.25 to 0.25
- bias: float32 [512], replicated, may hold values from -3 to 3
- w_out: bfloat16 [512, 512], replicated, may hold values from -0.25 to 0.25
- w_node: bfloat16 [512, 512], replicated, may hold values from -0.25 to 0.25
- cotangent: bfloat16 [32768, 512], P(('band', 'mesh')), may hold values from -6 to 6
Outputs:
- mesh_out: bfloat16 [32768, 512], P(('band', 'mesh'))
- grid_grad: float32 [65536, 512], P(('band', 'mesh'))
Inputs may be any that keep to these rules, and one draw needn't show every extreme that they name: `live_groups`: each device has at least one live group, and some device has all 4 live.
All inputs are finite; a program needn't handle non-finite values.
Results may differ from a plain program's by a relative error of at most 0.0055.
Values may be sent and summed in bfloat16 or wider, within the bound.
No kernel may reach another device: no remote copies, remote signals or barrier semaphores. Data moves between devices by JAX's collectives and lax.ppermute only.
A program may use at most 128 MiB of HBM per device.

v0:
```python
import jax
import jax.numpy as jnp
from jax import lax
from jax.sharding import PartitionSpec as P

GROUP = 4


def silu_slope(value):
    sig = jax.nn.sigmoid(value)
    return sig * (1.0 + value * (1.0 - sig))


def per_device(
    grid,
    mesh_latent,
    edge_latent,
    edge_grid_block,
    edge_mesh_block,
    sender_offset,
    receiver_offset,
    live_groups,
    w_grid,
    w_mesh,
    w_edge,
    bias,
    w_out,
    w_node,
    cotangent,
):
    width = grid.shape[1]
    rows_group = GROUP * 128
    band_terms = lax.all_gather(grid, "mesh", axis=0, tiled=True)
    mesh_rows = lax.all_gather(mesh_latent, "band", axis=0, tiled=True)
    count = live_groups[0]

    def group_terms(group):
        start = group * GROUP
        grid_blocks = lax.dynamic_slice_in_dim(edge_grid_block, start, GROUP)
        mesh_blocks = lax.dynamic_slice_in_dim(edge_mesh_block, start, GROUP)
        send_off = lax.dynamic_slice_in_dim(sender_offset, start, GROUP)
        recv_off = lax.dynamic_slice_in_dim(receiver_offset, start, GROUP)
        senders = (grid_blocks[:, None] * 128 + send_off).reshape(-1)
        receivers = (mesh_blocks[:, None] * 128 + recv_off).reshape(-1)
        edges = lax.dynamic_slice_in_dim(edge_latent, start * 128, rows_group)
        pre = jnp.dot(band_terms[senders], w_grid, preferred_element_type=jnp.float32)
        pre = pre + jnp.dot(mesh_rows[receivers], w_mesh, preferred_element_type=jnp.float32)
        pre = pre + jnp.dot(edges, w_edge, preferred_element_type=jnp.float32) + bias
        return (senders, receivers, pre)

    def forward(group, total):
        senders, receivers, pre = group_terms(group)
        hidden = jax.nn.silu(pre).astype(jnp.bfloat16)
        message = jnp.dot(hidden, w_out, preferred_element_type=jnp.float32)
        return total.at[receivers].add(message)

    partial_sums = lax.fori_loop(
        0, count, forward, jnp.zeros((mesh_rows.shape[0], width), jnp.float32)
    )
    aggregate = lax.psum_scatter(partial_sums, "band", scatter_dimension=0, tiled=True)
    activation = jax.nn.silu(aggregate).astype(jnp.bfloat16)
    mesh_out = (
        mesh_latent.astype(jnp.float32)
        + jnp.dot(activation, w_node, preferred_element_type=jnp.float32)
    ).astype(jnp.bfloat16)
    d_aggregate = (
        jnp.dot(cotangent, w_node.T, preferred_element_type=jnp.float32) * silu_slope(aggregate)
    ).astype(jnp.bfloat16)
    d_rows = lax.all_gather(d_aggregate, "band", axis=0, tiled=True)

    def backward(group, total):
        senders, receivers, pre = group_terms(group)
        d_hidden = jnp.dot(d_rows[receivers], w_out.T, preferred_element_type=jnp.float32)
        d_pre = (d_hidden * silu_slope(pre)).astype(jnp.bfloat16)
        return total.at[senders].add(jnp.dot(d_pre, w_grid.T, preferred_element_type=jnp.float32))

    grid_partial = lax.fori_loop(
        0, count, backward, jnp.zeros((band_terms.shape[0], width), jnp.float32)
    )
    grid_grad = lax.psum_scatter(grid_partial, "mesh", scatter_dimension=0, tiled=True)
    return (mesh_out, grid_grad)


def solution(mesh):
    placed = (
        P(("band", "mesh"), None),
        P(("band", "mesh"), None),
        P(("band", "mesh"), None),
        P(("band", "mesh")),
        P(("band", "mesh")),
        P(("band", "mesh"), None),
        P(("band", "mesh"), None),
        P(("band", "mesh")),
        P(),
        P(),
        P(),
        P(),
        P(),
        P(),
        P(("band", "mesh"), None),
    )
    return jax.shard_map(
        per_device,
        mesh=mesh,
        in_specs=placed,
        out_specs=(P(("band", "mesh"), None), P(("band", "mesh"), None)),
        check_vma=False,
    )
```

profile of v0, /device:TPU:1, one launch (start us, length us, event | category | flops | bytes accessed | tf_op | source)
XLA Modules:
  0.0 568.3 jit_solution(8674553522165151385)
XLA Ops:
  7.2 0.0 copy-start
  7.2 0.0 all-gather.6.cloned.1.call-start
  7.3 0.7 all-gather.6.cloned.1.call-update
  8.0 0.0 all-gather.4.cloned.1.call-start
  8.0 0.7 all-gather.4.cloned.1.call-update
  8.7 0.0 reduce-scatter.3.cloned.1.call-start
  8.8 30.1 %all-gather.6.cloned.1.call-done = bf16[2048,512]{1,0:T(8,128)(2,1)} async-done(((bf16[256,512]{1,0:T(8,128)(2,1)}), bf16[2048,512]{1,0:T(8,128)(2,1)}) %all-gather.6.cloned.1.call-update) | async-done | bytes 2097168 | tf_op jit(solution)/shard_map/all_gather | solution.py:34
  38.8 72.7 %all-gather.4.cloned.1.call-done = bf16[8192,512]{1,0:T(8,128)(2,1)} async-done(((bf16[512,512]{1,0:T(8,128)(2,1)}), bf16[8192,512]{1,0:T(8,128)(2,1)}) %all-gather.4.cloned.1.call-update) | async-done | bytes 8388624 | tf_op jit(solution)/shard_map/all_gather | solution.py:33
  111.6 2.5 broadcast_in_dim.4
  114.1 52.6 %while.24 = (s32[]{:T(128)}, f32[2048,512]{1,0:T(8,128)}, s32[]{:T(128)}, s32[16]{0:T(128)S(1)}, s32[16,128]{1,0:T(8,128)S(1)}, /*index=5*/s32[16]{0:T(128)S(1)}...) while((s32[]{:T(128)}, f32[2048,512]{1,0:T(8,128)}, ...), condition=%wide.region_2.3_spmd, body=%wide.region_0.2_spmd.sunk | while | flops 1076107264 | bytes 14193041 | solution.py:57
  114.8 0.1 dynamic-slice_multiply_fusion.8
  114.8 0.1 dynamic-slice_multiply_fusion.9
  114.9 0.1 dynamic-slice_add_fusion.6
  115.0 2.0 gather_fusion.1
  117.0 7.1 %gather_fusion = bf16[512,512]{1,0:T(8,128)(2,1)} fusion(bf16[8192,512]{1,0:T(8,128)(2,1)} %get-tuple-element.705, s32[1024]{0:T(1024)S(1)} %pad_clamp_fusion.8), kind=kCustom, calls=%fused_computation.clone.1 | custom fusion | bytes 1050624 | tf_op jit(solution)/shard_map/while/body/gather | solution.py:46
  124.1 1.6 fusion.75
  125.8 2.5 convolution_add_fusion.7
  128.2 3.5 fusion.76
  131.7 8.3 %scatter_fusion = f32[2048,512]{1,0:T(8,128)} fusion(f32[2048,512]{1,0:T(8,128)} %get-tuple-element.678, s32[512]{0:T(512)S(1)} %bitcast.73, f32[512,512]{1,0:T(8,128)} %fusion.76), kind=kCustom, calls=%fused_computation.5.clone.1 | custom fusion | flops 262144 | bytes 3147776 | tf_op jit(solution)/shard_map/while/body/scatter-add | solution.py:55
  140.7 0.1 dynamic-slice_multiply_fusion.8
  140.8 0.1 dynamic-slice_multiply_fusion.9
  140.9 0.1 dynamic-slice_add_fusion.6
  141.0 2.0 gather_fusion.1
  143.0 7.1 %gather_fusion = bf16[512,512]{1,0:T(8,128)(2,1)} fusion(bf16[8192,512]{1,0:T(8,128)(2,1)} %get-tuple-element.705, s32[1024]{0:T(1024)S(1)} %pad_clamp_fusion.8), kind=kCustom, calls=%fused_computation.clone.1 | custom fusion | bytes 1050624 | tf_op jit(solution)/shard_map/while/body/gather | solution.py:46
  150.1 1.6 fusion.75
  151.7 2.5 convolution_add_fusion.7
  154.2 3.5 fusion.76
  157.7 8.3 %scatter_fusion = f32[2048,512]{1,0:T(8,128)} fusion(f32[2048,512]{1,0:T(8,128)} %get-tuple-element.678, s32[512]{0:T(512)S(1)} %bitcast.73, f32[512,512]{1,0:T(8,128)} %fusion.76), kind=kCustom, calls=%fused_computation.5.clone.1 | custom fusion | flops 262144 | bytes 3147776 | tf_op jit(solution)/shard_map/while/body/scatter-add | solution.py:55
  166.7 0.0 reduce-scatter.3.cloned.1.call-update
  166.8 0.0 all-gather.8.cloned.1.call-start
  166.8 86.9 %reduce-scatter.3.cloned.1.call-done = f32[256,512]{1,0:T(8,128)} async-done(((f32[2048,512]{1,0:T(8,128)}), f32[256,512]{1,0:T(8,128)}) %reduce-scatter.3.cloned.1.call-update) | async-done | bytes 524304 | tf_op jit(solution)/shard_map/reduce_scatter | solution.py:60
  253.7 2.1 fusion.25
  255.8 0.0 all-gather.8.cloned.1.call-update
  255.8 0.0 reduce-scatter.5.cloned.1.call-start
  255.9 27.6 %all-gather.8.cloned.1.call-done = bf16[2048,512]{1,0:T(8,128)(2,1)} async-done(((bf16[256,512]{1,0:T(8,128)(2,1)}), bf16[2048,512]{1,0:T(8,128)(2,1)}) %all-gather.8.cloned.1.call-update) | async-done | bytes 2097168 | tf_op jit(solution)/shard_map/all_gather | solution.py:69
  283.5 7.9 %broadcast_in_dim.5 = f32[8192,512]{1,0:T(8,128)} broadcast(f32[]{:T(128)} %constant.104.clone.1), dimensions={} | broadcast | bytes 16777220 | tf_op jit(solution)/shard_map/broadcast_in_dim | solution.py:78
  291.4 80.8 %while.25 = (s32[]{:T(128)}, f32[8192,512]{1,0:T(8,128)}, s32[]{:T(128)}, s32[16]{0:T(128)S(1)}, s32[16,128]{1,0:T(8,128)S(1)}, /*index=5*/s32[16]{0:T(128)S(1)}...) while((s32[]{:T(128)}, f32[8192,512]{1,0:T(8,128)}, ...), condition=%wide.region_6.7_spmd, body=%wide.region_4.6_spmd.sunk | while | flops 1345591296 | bytes 20486580 | solution.py:77
  292.2 0.1 dynamic-slice_multiply_fusion.10
  292.3 0.1 dynamic-slice_multiply_fusion.11
  292.4 0.1 dynamic-slice_add_fusion.7
  292.5 6.4 %gather_fusion.3 = bf16[512,512]{1,0:T(8,128)(2,1)S(1)} fusion(bf16[8192,512]{1,0:T(8,128)(2,1)} %get-tuple-element.772, s32[1024]{0:T(1024)S(1)} %pad_clamp_fusion.11), kind=kCustom, calls=%fused_computation.3.clone.1 | custom fusion | bytes 1050624 | tf_op jit(solution)/shard_map/while/body/gather | solution.py:46
  299.0 2.5 fusion.86
  301.4 2.0 gather_fusion.4
  303.4 1.8 convolution_add_fusion.8
  305.2 2.7 fusion.87
  307.9 4.5 gather_fusion.2
  312.4 3.4 fusion.88
  315.8 15.7 %scatter_fusion.1 = f32[8192,512]{1,0:T(8,128)} fusion(f32[8192,512]{1,0:T(8,128)} %get-tuple-element.742, s32[512]{0:T(512)S(1)} %bitcast.71, f32[512,512]{1,0:T(8,128)} %fusion.88), kind=kCustom, calls=%fused_computation.6.clone.1 | custom fusion | flops 262144 | bytes 3147776 | tf_op jit(solution)/shard_map/while/body/scatter-add | solution.py:75
  332.2 0.1 dynamic-slice_multiply_fusion.10
  332.3 0.1 dynamic-slice_multiply_fusion.11
  332.4 0.1 dynamic-slice_add_fusion.7
  332.5 6.4 %gather_fusion.3 = bf16[512,512]{1,0:T(8,128)(2,1)S(1)} fusion(bf16[8192,512]{1,0:T(8,128)(2,1)} %get-tuple-element.772, s32[1024]{0:T(1024)S(1)} %pad_clamp_fusion.11), kind=kCustom, calls=%fused_computation.3.clone.1 | custom fusion | bytes 1050624 | tf_op jit(solution)/shard_map/while/body/gather | solution.py:46
  339.0 2.5 fusion.86
  341.4 2.0 gather_fusion.4
  343.4 1.8 convolution_add_fusion.8
  345.2 2.7 fusion.87
  347.9 4.5 gather_fusion.2
  352.4 3.4 fusion.88
  355.9 15.7 %scatter_fusion.1 = f32[8192,512]{1,0:T(8,128)} fusion(f32[8192,512]{1,0:T(8,128)} %get-tuple-element.742, s32[512]{0:T(512)S(1)} %bitcast.71, f32[512,512]{1,0:T(8,128)} %fusion.88), kind=kCustom, calls=%fused_computation.6.clone.1 | custom fusion | flops 262144 | bytes 3147776 | tf_op jit(solution)/shard_map/while/body/scatter-add | solution.py:75
  372.2 0.0 reduce-scatter.5.cloned.1.call-update
  372.3 0.9 copy-done.3
  373.2 0.2 copy-done.7
  373.3 1.0 fusion.24
  374.4 187.4 %reduce-scatter.5.cloned.1.call-done = f32[512,512]{1,0:T(8,128)} async-done(((f32[8192,512]{1,0:T(8,128)}), f32[512,512]{1,0:T(8,128)}) %reduce-scatter.5.cloned.1.call-update) | async-done | bytes 1048592 | tf_op jit(solution)/shard_map/reduce_scatter | solution.py:80
  (37 shorter events, 0.2 us)
Async XLA Ops:
  7.2 246.5 %copy-start = (bf16[512,512]{1,0:T(8,128)(2,1)S(1)}, bf16[512,512]{1,0:T(8,128)(2,1)}, u32[]{:S(2)}) copy-start(bf16[512,512]{1,0:T(8,128)(2,1)} %param.32) | copy-start | bytes 1572868
  7.2 106.9 %copy-start.4 = (f32[512]{0:T(512)S(1)}, f32[512]{0:T(512)}, u32[]{:S(2)}) copy-start(f32[512]{0:T(512)} %param.30) | copy-start | bytes 6148
  7.2 106.9 %copy-start.5 = (s32[16,128]{1,0:T(8,128)S(1)}, s32[16,128]{1,0:T(8,128)}, u32[]{:S(2)}) copy-start(s32[16,128]{1,0:T(8,128)} %param.25) | copy-start | bytes 24580
  7.2 106.9 %copy-start.6 = (s32[16,128]{1,0:T(8,128)S(1)}, s32[16,128]{1,0:T(8,128)}, u32[]{:S(2)}) copy-start(s32[16,128]{1,0:T(8,128)} %param.24) | copy-start | bytes 24580
  7.2 106.9 %copy-start.9 = (s32[16]{0:T(128)S(1)}, s32[16]{0:T(128)}, u32[]{:S(2)}) copy-start(s32[16]{0:T(128)} %param.23) | copy-start | bytes 196
  7.2 106.9 %copy-start.10 = (s32[16]{0:T(128)S(1)}, s32[16]{0:T(128)}, u32[]{:S(2)}) copy-start(s32[16]{0:T(128)} %param.22) | copy-start | bytes 196
  7.2 31.6 %all-gather.6.cloned.1.call-start = ((), (), s32[]{:S(2)}) async-start(), calls=%async_computation.3 | async-start | bytes 2359296 | tf_op jit(solution)/shard_map/all_gather | solution.py:34
  8.0 103.6 %all-gather.4.cloned.1.call-start = ((), (), s32[]{:S(2)}) async-start(), calls=%async_computation.2 | async-start | bytes 8912896 | tf_op jit(solution)/shard_map/all_gather | solution.py:33
  8.7 244.9 %reduce-scatter.3.cloned.1.call-start = ((), (), s32[]{:S(2)}) async-start(), calls=%async_computation.4 | async-start | bytes 4718592 | tf_op jit(solution)/shard_map/reduce_scatter | solution.py:60
  38.8 75.3 %copy-start.1 = (bf16[2048,512]{1,0:T(8,128)(2,1)S(1)}, bf16[2048,512]{1,0:T(8,128)(2,1)}, u32[]{:S(2)}) copy-start(bf16[2048,512]{1,0:T(8,128)(2,1)} %all-gather.6.cloned.1.call-done) | copy-start | bytes 6291460
  166.7 86.9 %copy-start.8 = (bf16[256,512]{1,0:T(8,128)(2,1)S(1)}, bf16[256,512]{1,0:T(8,128)(2,1)}, u32[]{:S(2)}) copy-start(bf16[256,512]{1,0:T(8,128)(2,1)} %param.33) | copy-start | bytes 786436
  166.8 116.7 %all-gather.8.cloned.1.call-start = ((), (), s32[]{:S(2)}) async-start(), calls=%async_computation.5 | async-start | bytes 2359296 | tf_op jit(solution)/shard_map/all_gather | solution.py:69
  255.8 305.9 %reduce-scatter.5.cloned.1.call-start = ((), (), s32[]{:S(2)}) async-start(), calls=%async_computation.6 | async-start | bytes 17825792 | tf_op jit(solution)/shard_map/reduce_scatter | solution.py:80
  305.2 7.2 %copy-start.2 = (bf16[512,512]{1,0:T(8,128)(2,1)S(1)}, bf16[512,512]{1,0:T(8,128)(2,1)}, u32[]{:S(2)}) copy-start(bf16[512,512]{1,0:T(8,128)(2,1)} %get-tuple-element.773) | copy-start | bytes 1572868 | tf_op jit(solution)/shard_map/while
  345.2 7.2 %copy-start.2 = (bf16[512,512]{1,0:T(8,128)(2,1)S(1)}, bf16[512,512]{1,0:T(8,128)(2,1)}, u32[]{:S(2)}) copy-start(bf16[512,512]{1,0:T(8,128)(2,1)} %get-tuple-element.773) | copy-start | bytes 1572868 | tf_op jit(solution)/shard_map/while
  372.2 1.0 copy-start.3
  372.2 1.1 copy-start.7
Sparse Core Ops, SparseCore 0:
  9.8 28.9 all-gather.5
  41.0 70.5 all-gather.3
  166.9 86.7 reduce-scatter.2
  255.9 27.5 all-gather.7
  372.4 189.3 reduce-scatter.4
where the time goes:
time: 571 us; the launch traced here: 568 us
  waiting for transfers between devices  406 us (71%)
  local copies, waits for them, and re-layouts  55.5 us (10%)
  other arithmetic  49.1 us (9%)
  matrix products  39.1 us (7%)
  between operations  13.9 us (2%)
    reduce_scatter x1, waiting for transfers between devices, per_device(): lax.psum_scatter(grid_partial, 'mesh', scatter_dimension=0, tiled=True)  187 us
    reduce_scatter x1, waiting for transfers between devices, per_device(): lax.psum_scatter(partial_sums, 'band', scatter_dimension=0, tiled=True)  86.9 us
    all_gather x1, waiting for transfers between devices, per_device(): band_terms = lax.all_gather(grid, 'mesh', axis=0, tiled=True)  72.7 us
    scatter-add x2, other arithmetic, backward(): total.at[senders]  31.4 us
    all_gather x1, waiting for transfers between devices, per_device(): mesh_rows = lax.all_gather(mesh_latent, 'band', axis=0, tiled=True)  30.1 us
    all_gather x1, waiting for transfers between devices, per_device(): d_rows = lax.all_gather(d_aggregate, 'band', axis=0, tiled=True)  27.6 us
    gather x4, local copies, waits for them, and re-layouts, group_terms(): band_terms[senders]  27.1 us
    scatter-add x2, other arithmetic, forward(): return total.at[receivers].add(message)  16.7 us
  transfers between devices with their start and end apart: 5, of which 5 were waited for; matrix products, arithmetic and copies ran while one was open for 0% of the time, Pallas kernels for 0%

commit v1 on v0

v1 whole, which is shorter than its diff:
```python
import functools

import jax
import jax.numpy as jnp
from jax import lax
from jax.experimental import pallas as pl
from jax.experimental.pallas import tpu as pltpu
from jax.sharding import Mesh
from jax.sharding import PartitionSpec as P

F32 = jnp.float32
BF16 = jnp.bfloat16
RING = 4
BLOCK = 128
SLOTS = 16
GROUP = 4
WIDTH = 512
CHUNKS = 2
COLS = WIDTH // CHUNKS
HALF = 256
GATHERED = RING * HALF
VMEM = pl.BlockSpec(memory_space=pltpu.VMEM)
SMEM = pl.BlockSpec(memory_space=pltpu.SMEM)
ANY = pl.BlockSpec(memory_space=pl.ANY)
LIMIT = 48 * 1024 * 1024


def shape(rows, cols, dtype):
    return jax.ShapeDtypeStruct((rows, cols), dtype)


def params():
    return pltpu.CompilerParams(vmem_limit_bytes=LIMIT)


CHIP_AXES = ("core", "x", "y")


def along(first, step):
    pairs = []
    for core in range(2):
        for x in range(RING):
            for y in range(RING):
                if (core == 0) == first:
                    to = ((x + step) % RING, y)
                else:
                    to = (x, (y + step) % RING)
                pairs.append((core * 16 + x * RING + y, core * 16 + to[0] * RING + to[1]))
    return pairs


def shift(value, first, step):
    return lax.ppermute(value, CHIP_AXES, along(first, step))


def shift_z(value, step):
    return lax.ppermute(value, "z", [(i, (i + step) % RING) for i in range(RING)])


def swap(value):
    return lax.ppermute(value, "core", [(0, 1), (1, 0)])


def dot(a, b):
    return jnp.dot(a, b, preferred_element_type=F32)


def dot_t(a, b):
    return lax.dot_general(a, b, (((1,), (1,)), ((), ())), preferred_element_type=F32)


def t_dot(a, b):
    return lax.dot_general(a, b, (((0,), (0,)), ((), ())), preferred_element_type=F32)


def split_dot(a, b, product):
    high = a.astype(BF16)
    low = (a - high.astype(F32)).astype(BF16)
    return product(high, b) + product(low, b)


def sigmoid(value):
    return 1.0 / (1.0 + jnp.exp(-value))


def one_hot(offsets, slot):
    rows = lax.broadcasted_iota(jnp.int32, (BLOCK, BLOCK), 0)
    return (rows == offsets[pl.ds(slot, 1), :]).astype(BF16)


def grid_place(block, where):
    core, x, y = where[1], where[2], where[3]
    owner = block // 4
    kind = (block % 4) // 2
    dx = lax.rem(x - owner // 4 + RING, RING)
    dy = lax.rem(y - owner % 4 + RING, RING)
    mine = kind == core
    near = jnp.where(kind == 0, dx, dy)
    far = jnp.where(kind == 0, dy, dx)
    return mine, near, far, (block % 2) * BLOCK


def mesh_place(block, where):
    owner = block // 2
    dz = lax.rem(owner // 2 - where[0] + RING, RING)
    return owner % 2 == where[1], dz, (block % 2) * BLOCK


def first_product_kernel(where, grid, w_grid, *outs):
    core = where[1]
    keep = grid[pl.ds(pl.multiple_of(core * HALF, HALF), HALF), :]
    give = grid[pl.ds(pl.multiple_of((1 - core) * HALF, HALF), HALF), :]
    for chunk in range(CHUNKS):
        cols = pl.ds(chunk * COLS, COLS)
        outs[2 * chunk][...] = dot(keep, w_grid[:, cols]).astype(BF16)
        outs[2 * chunk + 1][...] = dot(give, w_grid[:, cols]).astype(BF16)


def edge_kernel(where, live, mesh_block, recv, edge, w_mesh, w_edge, bias, *rest):
    pieces, outs, rows = rest[:8], rest[8 : 8 + CHUNKS], rest[-1]
    group = pl.program_id(0)

    @pl.when(group < live[0])
    def _():
        for i in range(GROUP):
            slot = group * GROUP + i
            mine, dz, row = mesh_place(mesh_block[slot], where)
            hot = one_hot(recv, slot)
            for piece in range(8):

                @pl.when(jnp.logical_and(mine == (piece < 4), dz == piece % 4))
                def _():
                    rows[pl.ds(i * BLOCK, BLOCK), :] = t_dot(hot, pieces[piece][pl.ds(pl.multiple_of(row, BLOCK), BLOCK), :]).astype(BF16)

        total = dot(rows[...], w_mesh[...]) + dot(edge[...], w_edge[...]) + bias[...]
        for chunk in range(CHUNKS):
            outs[chunk][...] = total[:, chunk * COLS : (chunk + 1) * COLS]


def forward_kernel(where, live, grid_block, mesh_block, send, recv, rest_in, *rest):
    pieces, (slope, near, far) = rest[:8], rest[8:11]
    total, blocks, sems = rest[11:]
    group = pl.program_id(0)

    def copies(slot, act):
        mine, first, second, row = grid_place(grid_block[slot], where)
        start = first * HALF + row
        for piece in range(8):

            @pl.when(jnp.logical_and(mine == (piece < 4), second == piece % 4))
            def _():
                act(pltpu.make_async_copy(pieces[piece].at[pl.ds(pl.multiple_of(start, BLOCK), BLOCK), :], blocks.at[slot], sems.at[slot]))

    @pl.when(group == 0)
    def _():
        @pl.loop(0, live[0] * GROUP)
        def _(slot):
            copies(slot, lambda copy: copy.start())

        total[...] = jnp.zeros_like(total)

    @pl.when(group < live[0])
    def _():
        hidden = []
        for i in range(GROUP):
            slot = group * GROUP + i
            pltpu.make_async_copy(pieces[0].at[pl.ds(0, BLOCK), :], blocks.at[slot], sems.at[slot]).wait()
            lines = pl.ds(i * BLOCK, BLOCK)
            pre = rest_in[lines, :] + t_dot(one_hot(send, slot), blocks[slot])
            sig = sigmoid(pre)
            slope[lines, :] = sig * (1.0 + pre * (1.0 - sig))
            hidden.append((pre * sig).astype(BF16))
        for i in range(GROUP):
            slot = group * GROUP + i
            mine, dz, row = mesh_place(mesh_block[slot], where)
            start = jnp.where(mine, 0, RING * HALF) + dz * HALF + row
            lines = pl.ds(pl.multiple_of(start, BLOCK), BLOCK)
            total[lines, :] += dot(one_hot(recv, slot), hidden[i])

    @pl.when(group == SLOTS // GROUP - 1)
    def _():
        near[...] = total[: RING * HALF, :]
        far[...] = total[RING * HALF :, :].astype(BF16)


def pair_sum_kernel(near, other, own, *outs):
    own[...] = near[:HALF, :] + other[:HALF, :].astype(F32)
    for step in range(1, RING):
        lines = pl.ds(step * HALF, HALF)
        outs[step - 1][...] = (near[lines, :] + other[lines, :].astype(F32)).astype(BF16)


def node_kernel(cot, w_out, *rest):
    sums, (aggregate, *grads) = rest[: 4 * CHUNKS], rest[4 * CHUNKS :]
    total = jnp.zeros((HALF, WIDTH), F32)
    for chunk in range(CHUNKS):
        own, a, b, c = sums[4 * chunk : 4 * chunk + 4]
        part = own[...] + (a[...].astype(F32) + b[...].astype(F32) + c[...].astype(F32))
        total += split_dot(part, w_out[pl.ds(chunk * COLS, COLS), :], dot)
    aggregate[...] = total
    sig = sigmoid(total)
    grad = (cot[...] * (sig * (1.0 + total * (1.0 - sig)))).astype(BF16)
    for chunk in range(CHUNKS):
        grads[chunk][...] = dot_t(grad, w_out[pl.ds(chunk * COLS, COLS), :]).astype(BF16)


def backward_kernel(where, live, grid_block, mesh_block, first_of, send, recv, slope, *rest):
    pieces, outs, (total, blocks) = rest[:8], rest[8:16], rest[16:]
    group = pl.program_id(0)

    @pl.when(group == 0)
    def _():
        for out in outs:
            out[...] = jnp.zeros_like(out)

    @pl.when(group < live[0])
    def _():
        for i in range(GROUP):
            slot = group * GROUP + i
            mine, dz, row = mesh_place(mesh_block[slot], where)
            for piece in range(8):

                @pl.when(jnp.logical_and(mine == (piece < 4), dz == piece % 4))
                def _():
                    blocks[i] = pieces[piece][pl.ds(pl.multiple_of(row, BLOCK), BLOCK), :]

        parts = []
        for i in range(GROUP):
            slot = group * GROUP + i
            grad = t_dot(one_hot(recv, slot), blocks[i]) * slope[pl.ds(i * BLOCK, BLOCK), :]
            parts.append(dot(one_hot(send, slot), grad.astype(BF16)))
        for i in range(GROUP):
            slot = group * GROUP + i
            first = first_of[slot]

            @pl.when(first == slot)
            def _():
                total[slot] = parts[i]

            @pl.when(first != slot)
            def _():
                total[first] += parts[i]

    @pl.when(group == SLOTS // GROUP - 1)
    def _():
        @pl.loop(0, live[0] * GROUP)
        def _(slot):
            @pl.when(first_of[slot] == slot)
            def _():
                mine, near, far, row = grid_place(grid_block[slot], where)
                near = lax.rem(RING - near, RING)
                far = lax.rem(RING - far, RING)
                lines = pl.ds(pl.multiple_of(near * HALF + row, BLOCK), BLOCK)
                for piece in range(8):

                    @pl.when(jnp.logical_and(mine == (piece < 4), far == piece % 4))
                    def _():
                        outs[piece][lines, :] = total[slot].astype(BF16)


def add(a, b):
    return (a[...].astype(F32) + b[...].astype(F32)).astype(BF16)


def merge_kernel(up, other_up, into_up, down, other_down, into_down, out_up, out_down):
    out_up[:GATHERED, :] = add(up, into_up)
    out_up[GATHERED:, :] = other_up[...]
    out_down[:GATHERED, :] = down[...]
    out_down[GATHERED:, :] = add(other_down, into_down)


def column_sum_kernel(own, other, up, down, here, *outs):
    for half, term in enumerate((own, other)):
        for step in range(RING):
            lines = pl.ds(step * HALF, HALF)
            both = pl.ds(half * GATHERED + step * HALF, HALF)
            value = term[lines, :].astype(F32) + (up[both, :].astype(F32) + down[both, :].astype(F32))
            place = pl.ds(half * HALF, HALF)
            if step == 0:
                here[place, :] = value
            else:
                outs[step - 1][place, :] = value.astype(BF16)


def row_sum_kernel(here, up, down, across, own, other):
    value = here[...] + (up[...].astype(F32) + down[...].astype(F32) + across[...].astype(F32))
    own[...] = value[:HALF, :]
    other[...] = value[HALF:, :]


def grid_grad_kernel(where, w_grid, *rest):
    out = rest[-1]
    core = where[1]
    for which in range(2):
        value = jnp.zeros((HALF, WIDTH), F32)
        for chunk in range(CHUNKS):
            value += split_dot(rest[2 * chunk + which][...], w_grid[:, chunk * COLS : (chunk + 1) * COLS], dot_t)
        place = core if which == 0 else 1 - core
        out[pl.ds(pl.multiple_of(place * HALF, HALF), HALF), :] = value


def per_device(
    grid,
    mesh_latent,
    edge_latent,
    edge_grid_block,
    edge_mesh_block,
    sender_offset,
    receiver_offset,
    live_groups,
    w_grid,
    w_mesh,
    w_edge,
    bias,
    w_out,
    w_node,
    cotangent,
):
    where = jnp.stack([lax.axis_index(a) for a in ("z", "core", "x", "y")]).astype(jnp.int32)
    edges = SLOTS * BLOCK
    groups = SLOTS // GROUP
    per_group = GROUP * BLOCK
    offsets = pl.BlockSpec((SLOTS, BLOCK), lambda i: (0, 0))
    whole = pl.BlockSpec((HALF, COLS), lambda i: (0, 0))

    products = pl.pallas_call(
        first_product_kernel,
        in_specs=[SMEM, VMEM, VMEM],
        out_specs=[VMEM] * (2 * CHUNKS),
        out_shape=[shape(HALF, COLS, BF16)] * (2 * CHUNKS),
        compiler_params=params(),
        name="first_product",
    )(where, grid, w_grid)

    def gather_grid(chunk):
        keep, give = products[2 * chunk], products[2 * chunk + 1]
        mine = jnp.concatenate([keep, swap(give)], axis=0)
        up, down, across = shift(mine, True, 1), shift(mine, True, -1), shift(mine, True, 2)
        ring = (mine, up, across, down)
        both = jnp.concatenate([p[:HALF] for p in ring] + [p[HALF:] for p in ring], axis=0)
        far_up, far_down = shift(both, False, 1), shift(both, False, -1)
        own_across = shift(far_up[:GATHERED], False, 1)
        other_across = shift(far_down[GATHERED:], False, -1)
        own = [both, far_up, own_across, far_down]
        other = [swap(both[GATHERED:]), swap(far_up[GATHERED:]), swap(other_across), swap(far_down[GATHERED:])]
        return own + other

    mesh_ring = [mesh_latent, shift_z(mesh_latent, -1), shift_z(mesh_latent, 2), shift_z(mesh_latent, 1)]
    mesh_pieces = mesh_ring + [swap(p) for p in mesh_ring]
    edge_terms = pl.pallas_call(
        edge_kernel,
        grid=(groups,),
        in_specs=[
            SMEM,
            SMEM,
            SMEM,
            offsets,
            pl.BlockSpec((per_group, WIDTH), lambda i: (i, 0)),
            pl.BlockSpec((WIDTH, WIDTH), lambda i: (0, 0)),
            pl.BlockSpec((WIDTH, WIDTH), lambda i: (0, 0)),
            pl.BlockSpec((1, WIDTH), lambda i: (0, 0)),
        ]
        + [pl.BlockSpec((HALF, WIDTH), lambda i: (0, 0))] * 8,
        out_specs=[pl.BlockSpec((per_group, COLS), lambda i: (i, 0))] * CHUNKS,
        out_shape=[shape(edges, COLS, F32)] * CHUNKS,
        scratch_shapes=[pltpu.VMEM((per_group, WIDTH), BF16)],
        compiler_params=params(),
        name="edge_terms",
    )(where, live_groups, edge_mesh_block, receiver_offset, edge_latent, w_mesh, w_edge, bias.reshape(1, WIDTH), *mesh_pieces)

    cot = dot_t(cotangent, w_node)

    def forward(chunk, pieces):
        return pl.pallas_call(
            forward_kernel,
            grid=(groups,),
            in_specs=[SMEM] * 4 + [offsets, offsets, pl.BlockSpec((per_group, COLS), lambda i: (i, 0))] + [ANY] * 8,
            out_specs=[
                pl.BlockSpec((per_group, COLS), lambda i: (i, 0)),
                pl.BlockSpec((RING * HALF, COLS), lambda i: (0, 0)),
                pl.BlockSpec((RING * HALF, COLS), lambda i: (0, 0)),
            ],
            out_shape=[shape(edges, COLS, F32), shape(RING * HALF, COLS, F32), shape(RING * HALF, COLS, BF16)],
            scratch_shapes=[
                pltpu.VMEM((2 * RING * HALF, COLS), F32),
                pltpu.VMEM((SLOTS, BLOCK, COLS), BF16),
                pltpu.SemaphoreType.DMA((SLOTS,)),
            ],
            compiler_params=params(),
            name=f"forward_{chunk}",
        )(where, live_groups, edge_grid_block, edge_mesh_block, sender_offset, receiver_offset, edge_terms[chunk], *pieces)

    def band_sum(chunk, near, far):
        own, a, b, c = pl.pallas_call(
            pair_sum_kernel,
            in_specs=[VMEM] * 2,
            out_specs=[VMEM] * 4,
            out_shape=[shape(HALF, COLS, F32)] + [shape(HALF, COLS, BF16)] * 3,
            compiler_params=params(),
            name=f"pair_sum_{chunk}",
        )(near, swap(far))
        return [own, shift_z(a, 1), shift_z(c, -1), shift_z(b, 2)]

    sums, slopes = [], []
    for chunk in range(CHUNKS):
        slope, near, far = forward(chunk, gather_grid(chunk))
        slopes.append(slope)
        sums += band_sum(chunk, near, far)

    aggregate, *grads = pl.pallas_call(
        node_kernel,
        in_specs=[VMEM] * (2 + 4 * CHUNKS),
        out_specs=[VMEM] * (1 + CHUNKS),
        out_shape=[shape(HALF, WIDTH, F32)] + [shape(HALF, COLS, BF16)] * CHUNKS,
        compiler_params=params(),
        name="node",
    )(cot, w_out, *sums)

    slots = jnp.arange(SLOTS)
    same = edge_grid_block[:, None] == edge_grid_block[None, :]
    first_of = jnp.min(jnp.where(same, slots[None, :], SLOTS), axis=1).astype(jnp.int32)

    def backward(chunk):
        ring = [grads[chunk], shift_z(grads[chunk], -1), shift_z(grads[chunk], 2), shift_z(grads[chunk], 1)]
        pieces = ring + [swap(p) for p in ring]
        return pl.pallas_call(
            backward_kernel,
            grid=(groups,),
            in_specs=[SMEM] * 5 + [offsets, offsets, pl.BlockSpec((per_group, COLS), lambda i: (i, 0))] + [whole] * 8,
            out_specs=[pl.BlockSpec((GATHERED, COLS), lambda i: (0, 0))] * 8,
            out_shape=[shape(GATHERED, COLS, BF16)] * 8,
            scratch_shapes=[pltpu.VMEM((SLOTS, BLOCK, COLS), F32), pltpu.VMEM((GROUP, BLOCK, COLS), BF16)],
            compiler_params=params(),
            name=f"backward_{chunk}",
        )(where, live_groups, edge_grid_block, edge_mesh_block, first_of, sender_offset, receiver_offset, slopes[chunk], *pieces)

    def scatter_grid(chunk, partial):
        own, other = partial[:4], [swap(p) for p in partial[4:]]
        into_up, into_down = shift(own[2], False, 1), shift(other[2], False, -1)
        up, down = pl.pallas_call(
            merge_kernel,
            in_specs=[VMEM] * 6,
            out_specs=[VMEM] * 2,
            out_shape=[shape(2 * GATHERED, COLS, BF16)] * 2,
            compiler_params=params(),
            name=f"merge_{chunk}",
        )(own[1], other[1], into_up, own[3], other[3], into_down)
        here, a, b, c = pl.pallas_call(
            column_sum_kernel,
            in_specs=[VMEM] * 4,
            out_specs=[VMEM] * 4,
            out_shape=[shape(2 * HALF, COLS, F32)] + [shape(2 * HALF, COLS, BF16)] * 3,
            compiler_params=params(),
            name=f"column_sum_{chunk}",
        )(own[0], other[0], shift(up, False, 1), shift(down, False, -1))
        mine, give = pl.pallas_call(
            row_sum_kernel,
            in_specs=[VMEM] * 4,
            out_specs=[VMEM] * 2,
            out_shape=[shape(HALF, COLS, F32)] * 2,
            compiler_params=params(),
            name=f"row_sum_{chunk}",
        )(here, shift(a, True, 1), shift(c, True, -1), shift(b, True, 2))
        return [mine, swap(give)]

    parts = []
    for chunk in range(CHUNKS):
        parts += scatter_grid(chunk, backward(chunk))

    grid_grad = pl.pallas_call(
        grid_grad_kernel,
        in_specs=[SMEM, VMEM] + [VMEM] * (2 * CHUNKS),
        out_specs=VMEM,
        out_shape=shape(2 * HALF, WIDTH, F32),
        compiler_params=params(),
        name="grid_grad",
    )(where, w_grid, *parts)

    activation = jax.nn.silu(aggregate).astype(BF16)
    mesh_out = (mesh_latent.astype(F32) + dot(activation, w_node)).astype(BF16)
    return (mesh_out, grid_grad)


def solution(mesh):
    split = Mesh(mesh.devices.reshape(4, 2, 4, 4), ("z", "core", "x", "y"))
    rows = P(("z", "core", "x", "y"))
    placed = (rows,) * 8 + (P(),) * 6 + (rows,)
    return jax.shard_map(per_device, mesh=split, in_specs=placed, out_specs=(rows, rows), check_vma=False)
```

time: 571 us -> 225 us (0.39)
  waiting for transfers between devices: 406 us -> 51.4 us
  starting transfers between devices: 0.2 us -> 122 us
  local copies, waits for them, and re-layouts: 55.5 us -> 4.78 us
  other arithmetic: 49.1 us -> 1.16 us
  Pallas kernels: 0 us -> 38.3 us
  matrix products: 39.1 us -> 1.36 us
  between operations: 13.9 us -> 2.04 us
    reduce_scatter x2 -> x0, waiting for transfers between devices: 274 us -> none  [the longest x1 187 us: per_device(): lax.psum_scatter(grid_partial, 'mesh', scatter_dimension=0, tiled=True)]
    all_gather x3 -> x0, waiting for transfers between devices: 130 us -> none  [the longest x1 72.7 us: per_device(): band_terms = lax.all_gather(grid, 'mesh', axis=0, tiled=True)]
    ppermute x0 -> x77, starting transfers between devices: none -> 122 us  [the longest x34 60.1 us: swap(): return lax.ppermute(value, 'core', [(0, 1), (1, 0)])]
    ppermute x0 -> x77, waiting for transfers between devices: none -> 51.4 us  [the longest x28 40.1 us: shift(): return lax.ppermute(value, CHIP_AXES, along(first, step))]
    scatter-add x4 -> x0, other arithmetic: 48.1 us -> none  [the longest x2 31.4 us: backward(): total.at[senders]]
    gather x10 -> x0, local copies, waits for them, and re-layouts: 44 us -> none  [the longest x4 27.1 us: group_terms(): band_terms[senders]]
    pallas_call x0 -> x16, Pallas kernels: none -> 38.3 us  [the longest x2 14.4 us: forward(): pl.pallas_call(forward_kernel, grid=(groups,), in_specs=[SMEM] * 4 + [off...]
    dot_general x16 -> x2, matrix products: 39.1 us -> 1.36 us  [the longest x1 1.03 us: dot(): return jnp.dot(a, b, preferred_element_type=F32)]
  transfers between devices with their start and end apart: 5 -> 77, of which waited for: 5 -> 27; matrix products, arithmetic and copies ran while one was open for 0% -> 2% of each run, Pallas kernels for 0% -> 16%
where the time goes in v1:
time: 225 us; the launch traced here: 221 us
  starting transfers between devices  122 us (54%)
  waiting for transfers between devices  51.4 us (23%)
  Pallas kernels  38.3 us (17%)
  local copies, waits for them, and re-layouts  4.78 us (2%)
    ppermute x34, starting transfers between devices, swap(): return lax.ppermute(value, 'core', [(0, 1), (1, 0)])  60.1 us
    ppermute x28, waiting for transfers between devices, shift(): return lax.ppermute(value, CHIP_AXES, along(first, step))  40.1 us
    ppermute x28, starting transfers between devices, shift(): return lax.ppermute(value, CHIP_AXES, along(first, step))  38.7 us
    ppermute x15, starting transfers between devices, shift_z(): lax.ppermute(value, 'z', [(i, (i + step) % RING) for i in range(RING)])  23 us
    pallas_call x2, Pallas kernels, forward(): pl.pallas_call(forward_kernel, grid=(groups,), in_specs=[SMEM] * 4 + [off...  14.4 us
    pallas_call x2, Pallas kernels, backward(): pl.pallas_call(backward_kernel, grid=(groups,), in_specs=[SMEM] * 5 + [of...  10.7 us
    ppermute x15, waiting for transfers between devices, shift_z(): lax.ppermute(value, 'z', [(i, (i + step) % RING) for i in range(RING)])  8.16 us
    pallas_call x1, Pallas kernels, per_device(): pl.pallas_call(edge_kernel, grid=(groups,), in_specs=[SMEM, SMEM, SMEM, o...  7.41 us
  transfers between devices with their start and end apart: 77, of which 27 were waited for; matrix products, arithmetic and copies ran while one was open for 2% of the time, Pallas kernels for 16%

profile of v1, /device:TPU:1, one launch (start us, length us, event | category | flops | bytes accessed | tf_op | source)
XLA Modules:
  0.0 220.8 jit_solution(10424148530275275873)
XLA Ops:
  3.8 1.5 collective-permute-start.23
  6.3 1.4 collective-permute-start.24
  8.3 3.8 %collective-permute-start = (bf16[256,512]{1,0:T(8,128)(2,1)}, bf16[256,512]{1,0:T(8,128)(2,1)S(1)}, u32[]{:S(2)}, u32[]{:S(2)}) collective-permute-start(bf16[256,512]{1,0:T(8,128)(2,1)} %rest_0_.1), channel_id=1, source_target_pairs={{0,96},{32,0},{64,32},{96,64},{1,97},{33,1},{65,33},{97,65},{2,98}... | collective-permute-start | bytes 786440 | tf_op jit(solution)/shard_map/ppermute | solution.py:57
  12.8 3.0 %collective-permute-start.25 = (bf16[512,256]{1,0:T(8,128)(2,1)S(1)}, bf16[512,256]{1,0:T(8,128)(2,1)S(1)}, u32[]{:S(2)}, u32[]{:S(2)}) collective-permute-start(bf16[512,256]{1,0:T(8,128)(2,1)S(1)} %constant_dynamic-update-slice_fusion.7), channel_id=1, source_target_pairs={{0,8},{1,9},{2,10},{3,11},{4,12},{5,13},{6,14},{7,15},{8,0},{9,1},... | collective-permute-start | bytes 786440 | tf_op jit(solution)/shard_map/ppermute | solution.py:53
  16.7 3.2 %collective-permute-done.25 = bf16[512,256]{1,0:T(8,128)(2,1)S(1)} collective-permute-done((bf16[512,256]{1,0:T(8,128)(2,1)S(1)}, bf16[512,256]{1,0:T(8,128)(2,1)S(1)}, u32[]{:S(2)}, u32[]{:S(2)}) %collective-permute-start.25) | collective-permute-done | bytes 262176 | tf_op jit(solution)/shard_map/ppermute | solution.py:53
  19.9 1.3 collective-permute-start.8
  21.3 1.8 collective-permute-done.26
  23.1 1.6 collective-permute-start.9
  24.8 2.0 collective-permute-done.8
  26.8 1.5 collective-permute-start.10
  28.2 2.5 %collective-permute-done.9 = bf16[512,256]{1,0:T(8,128)(2,1)S(1)} collective-permute-done((bf16[512,256]{1,0:T(8,128)(2,1)S(1)}, bf16[512,256]{1,0:T(8,128)(2,1)S(1)}, u32[]{:S(2)}, u32[]{:S(2)}) %collective-permute-start.9) | collective-permute-done | bytes 262176 | tf_op jit(solution)/shard_map/ppermute | solution.py:53
  30.8 1.4 collective-permute-start.29
  34.2 5.9 %collective-permute-start.3 = (bf16[256,512]{1,0:T(8,128)(2,1)S(1)}, bf16[256,512]{1,0:T(8,128)(2,1)S(1)}, u32[]{:S(2)}, u32[]{:S(2)}) collective-permute-start(bf16[256,512]{1,0:T(8,128)(2,1)S(1)} %copy-done.8), channel_id=1, source_target_pairs={{0,16},{16,0},{1,17},{17,1},{2,18},{18,2},{3,19},{19,3},{4,20},{20... | collective-permute-start | bytes 786440 | tf_op jit(solution)/shard_map/ppermute | solution.py:61
  40.2 1.9 collective-permute-start.13
  42.3 4.1 %collective-permute-done.29.rest_3_ = bf16[2048,256]{1,0:T(8,128)(2,1)S(1)} collective-permute-done((bf16[2048,256]{1,0:T(8,128)(2,1)S(1)}, bf16[2048,256]{1,0:T(8,128)(2,1)S(1)}, u32[]{:S(2)}, u32[]{:S(2)}) %collective-permute-start.29) | collective-permute-done | bytes 1048608 | tf_op jit(solution)/shard_map/ppermute | solution.py:53
  46.4 1.4 collective-permute-start.5
  49.4 1.7 collective-permute-start.32
  51.3 5.1 %collective-permute-start.31 = (bf16[1024,256]{1,0:T(8,128)(2,1)S(1)}, bf16[1024,256]{1,0:T(8,128)(2,1)S(1)}, u32[]{:S(2)}, u32[]{:S(2)}) collective-permute-start(bf16[1024,256]{1,0:T(8,128)(2,1)S(1)} %get-tuple-element.112), channel_id=1, source_target_pairs={{0,16},{16,0},{1,17},{17,1},{2,18},{18,2},{3,19},{19,3},{4,20},{20... | collective-permute-start | bytes 1572872 | tf_op jit(solution)/shard_map/ppermute | solution.py:61
  56.4 1.2 collective-permute-done.13.rest_3_
  57.7 1.4 collective-permute-start.34
  59.9 1.7 collective-permute-start.16
  61.6 1.7 collective-permute-done.32
  63.3 4.1 %collective-permute-start.33 = (bf16[1024,256]{1,0:T(8,128)(2,1)S(1)}, bf16[1024,256]{1,0:T(8,128)(2,1)S(1)}, u32[]{:S(2)}, u32[]{:S(2)}) collective-permute-start(bf16[1024,256]{1,0:T(8,128)(2,1)S(1)} %collective-permute-done.32), channel_id=1, source_target_pairs={{0,16},{16,0},{1,17},{17,1},{2,18},{18,2},{3,19},{19,3},{4,20},{20... | collective-permute-start | bytes 1572872 | tf_op jit(solution)/shard_map/ppermute | solution.py:61
  68.2 2.7 %collective-permute-start.14 = (bf16[1024,256]{1,0:T(8,128)(2,1)}, bf16[1024,256]{1,0:T(8,128)(2,1)S(1)}, u32[]{:S(2)}, u32[]{:S(2)}) collective-permute-start(bf16[1024,256]{1,0:T(8,128)(2,1)} %pad_maximum_fusion), channel_id=1, source_target_pairs={{0,16},{16,0},{1,17},{17,1},{2,18},{18,2},{3,19},{19,3},{4,20},{20... | collective-permute-start | bytes 1572872 | tf_op jit(solution)/shard_map/ppermute | solution.py:61
  71.2 3.6 %collective-permute-start.15 = (bf16[1024,256]{1,0:T(8,128)(2,1)S(1)}, bf16[1024,256]{1,0:T(8,128)(2,1)S(1)}, u32[]{:S(2)}, u32[]{:S(2)}) collective-permute-start(bf16[1024,256]{1,0:T(8,128)(2,1)S(1)} %get-tuple-element.114), channel_id=1, source_target_pairs={{0,16},{16,0},{1,17},{17,1},{2,18},{18,2},{3,19},{19,3},{4,20},{20... | collective-permute-start | bytes 1572872 | tf_op jit(solution)/shard_map/ppermute | solution.py:61
  75.8 7.4 %edge_terms.1 = (f32[2048,256]{1,0:T(8,128)S(1)}, f32[2048,256]{1,0:T(8,128)}) custom-call(s32[4]{0:T(128)S(1)} %pad_add_fusion.where, s32[1]{0:T(128)S(6)} %copy.33.live, s32[16]{0:T(128)S(1)} %copy-done.11, s32[16,128]{1,0:T(8,128)S(1)} %copy-done.9, bf16[2048,512]{1,0:T(8,128)(2,1)} %edge.1, bf16[512,512]{1,0:T(8,128)(2,1)S(1)} %copy-done.6, ...), custom_call_target="tpu_custom_call" | custom-call | tf_op jit(solution)/shard_map/edge_terms/pallas_call | solution.py:350
  83.2 1.3 copy-done.1
  84.5 7.2 %forward_1.1 = (f32[2048,256]{1,0:T(8,128)}, f32[1024,256]{1,0:T(8,128)S(1)}, bf16[1024,256]{1,0:T(8,128)(2,1)S(1)}) custom-call(s32[4]{0:T(128)S(1)} %pad_add_fusion.where, s32[1]{0:T(128)S(6)} %copy.33.live, s32[16]{0:T(128)S(1)} %copy-done.12, s32[16]{0:T(128)S(1)} %copy-done.11, s32[16,128]{1,0:T(8,128)S(1)} %copy-done.10, s32[16,128]{1,0:T(8,128)S(1)} %copy-done.9, ...), custom_call_target="tpu_custom_call" | custom-call | tf_op jit(solution)/shard_map/forward_1/pallas_call | solution.py:374
  92.6 7.2 %forward_0.1 = (f32[2048,256]{1,0:T(8,128)}, f32[1024,256]{1,0:T(8,128)S(1)}, bf16[1024,256]{1,0:T(8,128)(2,1)S(1)}) custom-call(s32[4]{0:T(128)S(1)} %pad_add_fusion.where, s32[1]{0:T(128)S(6)} %copy.33.live, s32[16]{0:T(128)S(1)} %copy-done.12, s32[16]{0:T(128)S(1)} %copy-done.11, s32[16,128]{1,0:T(8,128)S(1)} %copy-done.10, s32[16,128]{1,0:T(8,128)S(1)} %copy-done.9, ...), custom_call_target="tpu_custom_call" | custom-call | tf_op jit(solution)/shard_map/forward_0/pallas_call | solution.py:374
  100.3 7.3 %collective-permute-start.36 = (bf16[256,256]{1,0:T(8,128)(2,1)S(1)}, bf16[256,256]{1,0:T(8,128)(2,1)S(1)}, u32[]{:S(2)}, u32[]{:S(2)}) collective-permute-start(bf16[256,256]{1,0:T(8,128)(2,1)S(1)} %get-tuple-element.72), channel_id=1, source_target_pairs={{0,32},{32,64},{64,96},{96,0},{1,33},{33,65},{65,97},{97,1},{2,34}... | collective-permute-start | bytes 393224 | tf_op jit(solution)/shard_map/ppermute | solution.py:57
  107.6 1.9 collective-permute-start.38
  109.7 2.7 %collective-permute-start.21 = (bf16[256,256]{1,0:T(8,128)(2,1)S(1)}, bf16[256,256]{1,0:T(8,128)(2,1)S(1)}, u32[]{:S(2)}, u32[]{:S(2)}) collective-permute-start(bf16[256,256]{1,0:T(8,128)(2,1)S(1)} %get-tuple-element.64), channel_id=1, source_target_pairs={{0,96},{32,0},{64,32},{96,64},{1,97},{33,1},{65,33},{97,65},{2,98}... | collective-permute-start | bytes 393224 | tf_op jit(solution)/shard_map/ppermute | solution.py:57
  113.6 3.9 %collective-permute-done.20.rest_1_ = bf16[256,256]{1,0:T(8,128)(2,1)S(1)} collective-permute-done((bf16[256,256]{1,0:T(8,128)(2,1)S(1)}, bf16[256,256]{1,0:T(8,128)(2,1)S(1)}, u32[]{:S(2)}, u32[]{:S(2)}) %collective-permute-start.20) | collective-permute-done | bytes 131104 | tf_op jit(solution)/shard_map/ppermute | solution.py:57
  117.7 1.5 collective-permute-done.22.rest_3_
  120.0 3.8 %collective-permute-start.58 = (bf16[256,256]{1,0:T(8,128)(2,1)S(1)}, bf16[256,256]{1,0:T(8,128)(2,1)S(1)}, u32[]{:S(2)}, u32[]{:S(2)}) collective-permute-start(bf16[256,256]{1,0:T(8,128)(2,1)S(1)} %get-tuple-element.95.rest_0_), channel_id=1, source_target_pairs={{0,96},{32,0},{64,32},{96,64},{1,97},{33,1},{65,33},{97,65},{2,98}... | collective-permute-start | bytes 393224 | tf_op jit(solution)/shard_map/ppermute | solution.py:57
  124.4 2.0 collective-permute-start.61
  126.4 2.3 %collective-permute-done.58.rest_1_ = bf16[256,256]{1,0:T(8,128)(2,1)S(1)} collective-permute-done((bf16[256,256]{1,0:T(8,128)(2,1)S(1)}, bf16[256,256]{1,0:T(8,128)(2,1)S(1)}, u32[]{:S(2)}, u32[]{:S(2)}) %collective-permute-start.58) | collective-permute-done | bytes 131104 | tf_op jit(solution)/shard_map/ppermute | solution.py:57
  128.8 1.5 collective-permute-start.62
  130.3 2.4 %collective-permute-start.63 = (bf16[256,256]{1,0:T(8,128)(2,1)S(1)}, bf16[256,256]{1,0:T(8,128)(2,1)S(1)}, u32[]{:S(2)}, u32[]{:S(2)}) collective-permute-start(bf16[256,256]{1,0:T(8,128)(2,1)S(1)} %collective-permute-done.59.rest_2_), channel_id=1, source_target_pairs={{0,16},{16,0},{1,17},{17,1},{2,18},{18,2},{3,19},{19,3},{4,20},{20... | collective-permute-start | bytes 393224 | tf_op jit(solution)/shard_map/ppermute | solution.py:61
  135.2 10.1 %collective-permute-start.42 = (bf16[256,256]{1,0:T(8,128)(2,1)S(1)}, bf16[256,256]{1,0:T(8,128)(2,1)S(1)}, u32[]{:S(2)}, u32[]{:S(2)}) collective-permute-start(bf16[256,256]{1,0:T(8,128)(2,1)S(1)} %get-tuple-element.77.rest_0_), channel_id=1, source_target_pairs={{0,16},{16,0},{1,17},{17,1},{2,18},{18,2},{3,19},{19,3},{4,20},{20... | collective-permute-start | bytes 393224 | tf_op jit(solution)/shard_map/ppermute | solution.py:61
  145.5 5.0 %backward_1.1 = (bf16[1024,256]{1,0:T(8,128)(2,1)S(1)}, bf16[1024,256]{1,0:T(8,128)(2,1)S(1)}, bf16[1024,256]{1,0:T(8,128)(2,1)S(1)}, bf16[1024,256]{1,0:T(8,128...) custom-call(s32[4]{0:T(128)S(1)} %pad_add_fusion.where, ...), custom_call_target="tpu_custom_call" | custom-call | tf_op jit(solution)/shard_map/backward_1/pallas_call | solution.py:426
  151.8 1.7 collective-permute-done.43.rest_5_
  153.8 5.7 %backward_0.1 = (bf16[1024,256]{1,0:T(8,128)(2,1)S(1)}, bf16[1024,256]{1,0:T(8,128)(2,1)S(1)}, bf16[1024,256]{1,0:T(8,128)(2,1)S(1)}, bf16[1024,256]{1,0:T(8,128...) custom-call(s32[4]{0:T(128)S(1)} %pad_add_fusion.where, ...), custom_call_target="tpu_custom_call" | custom-call | tf_op jit(solution)/shard_map/backward_0/pallas_call | solution.py:426
  160.0 2.4 %collective-permute-start.70 = (bf16[1024,256]{1,0:T(8,128)(2,1)S(1)}, bf16[1024,256]{1,0:T(8,128)(2,1)S(1)}, u32[]{:S(2)}, u32[]{:S(2)}) collective-permute-start(bf16[1024,256]{1,0:T(8,128)(2,1)S(1)} %collective-permute-done.69), channel_id=1, source_target_pairs={{0,3},{1,0},{2,1},{3,2},{4,7},{5,4},{6,5},{7,6},{8,11},{9,8},{10,9... | collective-permute-start | bytes 1572872 | tf_op jit(solution)/shard_map/ppermute | solution.py:53
  162.4 2.6 %collective-permute-start.47 = (bf16[1024,256]{1,0:T(8,128)(2,1)S(1)}, bf16[1024,256]{1,0:T(8,128)(2,1)S(1)}, u32[]{:S(2)}, u32[]{:S(2)}) collective-permute-start(bf16[1024,256]{1,0:T(8,128)(2,1)S(1)} %get-tuple-element.81), channel_id=1, source_target_pairs={{0,16},{16,0},{1,17},{17,1},{2,18},{18,2},{3,19},{19,3},{4,20},{20... | collective-permute-start | bytes 1572872 | tf_op jit(solution)/shard_map/ppermute | solution.py:61
  165.1 1.3 collective-permute-start.49
  166.4 1.5 collective-permute-start.51
  169.3 3.1 %collective-permute-start.72 = (bf16[2048,256]{1,0:T(8,128)(2,1)S(1)}, bf16[2048,256]{1,0:T(8,128)(2,1)S(1)}, u32[]{:S(2)}, u32[]{:S(2)}) collective-permute-start(bf16[2048,256]{1,0:T(8,128)(2,1)S(1)} %get-tuple-element.105), channel_id=1, source_target_pairs={{0,3},{1,0},{2,1},{3,2},{4,7},{5,4},{6,5},{7,6},{8,11},{9,8},{10,9... | collective-permute-start | bytes 3145736 | tf_op jit(solution)/shard_map/ppermute | solution.py:53
  172.4 2.2 collective-permute-done.48.into_up
  174.6 1.3 collective-permute-start.65
  176.3 2.7 %collective-permute-start.53 = (bf16[2048,256]{1,0:T(8,128)(2,1)S(1)}, bf16[2048,256]{1,0:T(8,128)(2,1)S(1)}, u32[]{:S(2)}, u32[]{:S(2)}) collective-permute-start(bf16[2048,256]{1,0:T(8,128)(2,1)S(1)} %get-tuple-element.87), channel_id=1, source_target_pairs={{0,3},{1,0},{2,1},{3,2},{4,7},{5,4},{6,5},{7,6},{8,11},{9,8},{10,9... | collective-permute-start | bytes 3145736 | tf_op jit(solution)/shard_map/ppermute | solution.py:53
  178.9 2.6 %collective-permute-start.46 = (bf16[1024,256]{1,0:T(8,128)(2,1)}, bf16[1024,256]{1,0:T(8,128)(2,1)S(1)}, u32[]{:S(2)}, u32[]{:S(2)}) collective-permute-start(bf16[1024,256]{1,0:T(8,128)(2,1)} %get-tuple-element.79), channel_id=1, source_target_pairs={{0,16},{16,0},{1,17},{17,1},{2,18},{18,2},{3,19},{19,3},{4,20},{20... | collective-permute-start | bytes 1572872 | tf_op jit(solution)/shard_map/ppermute | solution.py:61
  181.5 4.3 %collective-permute-done.71.up = bf16[2048,256]{1,0:T(8,128)(2,1)S(1)} collective-permute-done((bf16[2048,256]{1,0:T(8,128)(2,1)S(1)}, bf16[2048,256]{1,0:T(8,128)(2,1)S(1)}, u32[]{:S(2)}, u32[]{:S(2)}) %collective-permute-start.71) | collective-permute-done | bytes 1048608 | tf_op jit(solution)/shard_map/ppermute | solution.py:53
  186.3 2.7 %collective-permute-start.73 = (bf16[512,256]{1,0:T(8,128)(2,1)S(1)}, bf16[512,256]{1,0:T(8,128)(2,1)S(1)}, u32[]{:S(2)}, u32[]{:S(2)}) collective-permute-start(bf16[512,256]{1,0:T(8,128)(2,1)S(1)} %get-tuple-element.107), channel_id=1, source_target_pairs={{0,4},{1,5},{2,6},{3,7},{4,8},{5,9},{6,10},{7,11},{8,12},{9,13},{1... | collective-permute-start | bytes 786440 | tf_op jit(solution)/shard_map/ppermute | solution.py:53
  189.0 1.3 collective-permute-start.74
  190.2 1.3 collective-permute-start.75
  191.5 8.7 %collective-permute-done.52.up = bf16[2048,256]{1,0:T(8,128)(2,1)S(1)} collective-permute-done((bf16[2048,256]{1,0:T(8,128)(2,1)S(1)}, bf16[2048,256]{1,0:T(8,128)(2,1)S(1)}, u32[]{:S(2)}, u32[]{:S(2)}) %collective-permute-start.52) | collective-permute-done | bytes 1048608 | tf_op jit(solution)/shard_map/ppermute | solution.py:53
  200.2 2.1 collective-permute-done.53.down
  202.6 3.2 %collective-permute-start.54 = (bf16[512,256]{1,0:T(8,128)(2,1)S(1)}, bf16[512,256]{1,0:T(8,128)(2,1)S(1)}, u32[]{:S(2)}, u32[]{:S(2)}) collective-permute-start(bf16[512,256]{1,0:T(8,128)(2,1)S(1)} %get-tuple-element.89), channel_id=1, source_target_pairs={{0,4},{1,5},{2,6},{3,7},{4,8},{5,9},{6,10},{7,11},{8,12},{9,13},{1... | collective-permute-start | bytes 786440 | tf_op jit(solution)/shard_map/ppermute | solution.py:53
  206.6 1.4 collective-permute-start.56
  208.2 1.6 collective-permute-start.76
  211.3 3.3 %collective-permute-done.56.across = bf16[512,256]{1,0:T(8,128)(2,1)S(1)} collective-permute-done((bf16[512,256]{1,0:T(8,128)(2,1)S(1)}, bf16[512,256]{1,0:T(8,128)(2,1)S(1)}, u32[]{:S(2)}, u32[]{:S(2)}) %collective-permute-start.56) | collective-permute-done | bytes 262176 | tf_op jit(solution)/shard_map/ppermute | solution.py:53
  214.7 2.5 %collective-permute-start.57 = (f32[256,256]{1,0:T(8,128)S(1)}, f32[256,256]{1,0:T(8,128)S(1)}, u32[]{:S(2)}, u32[]{:S(2)}) collective-permute-start(f32[256,256]{1,0:T(8,128)S(1)} %get-tuple-element.93), channel_id=1, source_target_pairs={{0,16},{16,0},{1,17},{17,1},{2,18},{18,2},{3,19},{19,3},{4,20},{20... | collective-permute-start | bytes 786440 | tf_op jit(solution)/shard_map/ppermute | solution.py:61
  218.4 2.3 %grid_grad.1 = f32[512,512]{1,0:T(8,128)} custom-call(s32[4]{0:T(128)S(1)} %pad_add_fusion.where, bf16[512,512]{1,0:T(8,128)(2,1)S(1)} %copy-done.3, f32[256,256]{1,0:T(8,128)S(1)} %get-tuple-element.92.rest_0_, f32[256,256]{1,0:T(8,128)S(1)} %collective-permute-done.57.rest_1_, f32[256,256]{1,0:T(8,128)S(1)} %get-tuple-element.110.rest_2_, ...), custom_call_target="tpu_custom_call" | custom-call | tf_op jit(solution)/shard_map/grid_grad/pallas_call | solution.py:470
  (172 shorter events, 28.2 us)
Async XLA Ops:
  6.3 9.5 %collective-permute-start.24 = (bf16[512,256]{1,0:T(8,128)(2,1)S(1)}, bf16[512,256]{1,0:T(8,128)(2,1)S(1)}, u32[]{:S(2)}, u32[]{:S(2)}) collective-permute-start(bf16[512,256]{1,0:T(8,128)(2,1)S(1)} %constant_dynamic-update-slice_fusion.7), channel_id=1, source_target_pairs={{0,4},{1,5},{2,6},{3,7},{4,8},{5,9},{6,10},{7,11},{8,12},{9,13},{1... | collective-permute-start | bytes 786440 | tf_op jit(solution)/shard_map/ppermute | solution.py:53
  8.3 25.9 %collective-permute-start = (bf16[256,512]{1,0:T(8,128)(2,1)}, bf16[256,512]{1,0:T(8,128)(2,1)S(1)}, u32[]{:S(2)}, u32[]{:S(2)}) collective-permute-start(bf16[256,512]{1,0:T(8,128)(2,1)} %rest_0_.1), channel_id=1, source_target_pairs={{0,96},{32,0},{64,32},{96,64},{1,97},{33,1},{65,33},{97,65},{2,98}... | collective-permute-start | bytes 786440 | tf_op jit(solution)/shard_map/ppermute | solution.py:57
  12.1 28.1 %collective-permute-start.1 = (bf16[256,512]{1,0:T(8,128)(2,1)}, bf16[256,512]{1,0:T(8,128)(2,1)S(1)}, u32[]{:S(2)}, u32[]{:S(2)}) collective-permute-start(bf16[256,512]{1,0:T(8,128)(2,1)} %rest_0_.1), channel_id=1, source_target_pairs={{0,64},{32,96},{64,0},{96,32},{1,65},{33,97},{65,1},{97,33},{2,66}... | collective-permute-start | bytes 786440 | tf_op jit(solution)/shard_map/ppermute | solution.py:57
  12.1 30.0 %collective-permute-start.2 = (bf16[256,512]{1,0:T(8,128)(2,1)}, bf16[256,512]{1,0:T(8,128)(2,1)S(1)}, u32[]{:S(2)}, u32[]{:S(2)}) collective-permute-start(bf16[256,512]{1,0:T(8,128)(2,1)} %rest_0_.1), channel_id=1, source_target_pairs={{0,32},{32,64},{64,96},{96,0},{1,33},{33,65},{65,97},{97,1},{2,34}... | collective-permute-start | bytes 786440 | tf_op jit(solution)/shard_map/ppermute | solution.py:57
  12.8 7.1 %collective-permute-start.25 = (bf16[512,256]{1,0:T(8,128)(2,1)S(1)}, bf16[512,256]{1,0:T(8,128)(2,1)S(1)}, u32[]{:S(2)}, u32[]{:S(2)}) collective-permute-start(bf16[512,256]{1,0:T(8,128)(2,1)S(1)} %constant_dynamic-update-slice_fusion.7), channel_id=1, source_target_pairs={{0,8},{1,9},{2,10},{3,11},{4,12},{5,13},{6,14},{7,15},{8,0},{9,1},... | collective-permute-start | bytes 786440 | tf_op jit(solution)/shard_map/ppermute | solution.py:53
  15.9 7.3 %collective-permute-start.26 = (bf16[512,256]{1,0:T(8,128)(2,1)S(1)}, bf16[512,256]{1,0:T(8,128)(2,1)S(1)}, u32[]{:S(2)}, u32[]{:S(2)}) collective-permute-start(bf16[512,256]{1,0:T(8,128)(2,1)S(1)} %constant_dynamic-update-slice_fusion.7), channel_id=1, source_target_pairs={{0,12},{1,13},{2,14},{3,15},{4,0},{5,1},{6,2},{7,3},{8,4},{9,5},{1... | collective-permute-start | bytes 786440 | tf_op jit(solution)/shard_map/ppermute | solution.py:53
  19.9 6.8 %collective-permute-start.8 = (bf16[512,256]{1,0:T(8,128)(2,1)S(1)}, bf16[512,256]{1,0:T(8,128)(2,1)S(1)}, u32[]{:S(2)}, u32[]{:S(2)}) collective-permute-start(bf16[512,256]{1,0:T(8,128)(2,1)S(1)} %constant_dynamic-update-slice_fusion), channel_id=1, source_target_pairs={{0,4},{1,5},{2,6},{3,7},{4,8},{5,9},{6,10},{7,11},{8,12},{9,13},{1... | collective-permute-start | bytes 786440 | tf_op jit(solution)/shard_map/ppermute | solution.py:53
  23.1 7.6 %collective-permute-start.9 = (bf16[512,256]{1,0:T(8,128)(2,1)S(1)}, bf16[512,256]{1,0:T(8,128)(2,1)S(1)}, u32[]{:S(2)}, u32[]{:S(2)}) collective-permute-start(bf16[512,256]{1,0:T(8,128)(2,1)S(1)} %constant_dynamic-update-slice_fusion), channel_id=1, source_target_pairs={{0,8},{1,9},{2,10},{3,11},{4,12},{5,13},{6,14},{7,15},{8,0},{9,1},... | collective-permute-start | bytes 786440 | tf_op jit(solution)/shard_map/ppermute | solution.py:53
  26.8 6.1 %collective-permute-start.10 = (bf16[512,256]{1,0:T(8,128)(2,1)S(1)}, bf16[512,256]{1,0:T(8,128)(2,1)S(1)}, u32[]{:S(2)}, u32[]{:S(2)}) collective-permute-start(bf16[512,256]{1,0:T(8,128)(2,1)S(1)} %constant_dynamic-update-slice_fusion), channel_id=1, source_target_pairs={{0,12},{1,13},{2,14},{3,15},{4,0},{5,1},{6,2},{7,3},{8,4},{9,5},{1... | collective-permute-start | bytes 786440 | tf_op jit(solution)/shard_map/ppermute | solution.py:53
  30.8 15.7 %collective-permute-start.29 = (bf16[2048,256]{1,0:T(8,128)(2,1)S(1)}, bf16[2048,256]{1,0:T(8,128)(2,1)S(1)}, u32[]{:S(2)}, u32[]{:S(2)}) collective-permute-start(bf16[2048,256]{1,0:T(8,128)(2,1)S(1)} %get-tuple-element.121.rest_0_), channel_id=1, source_target_pairs={{0,3},{1,0},{2,1},{3,2},{4,7},{5,4},{6,5},{7,6},{8,11},{9,8},{10,9... | collective-permute-start | bytes 3145736 | tf_op jit(solution)/shard_map/ppermute | solution.py:53
  32.9 16.5 %collective-permute-start.27 = (bf16[2048,256]{1,0:T(8,128)(2,1)S(1)}, bf16[2048,256]{1,0:T(8,128)(2,1)S(1)}, u32[]{:S(2)}, u32[]{:S(2)}) collective-permute-start(bf16[2048,256]{1,0:T(8,128)(2,1)S(1)} %get-tuple-element.121.rest_0_), channel_id=1, source_target_pairs={{0,1},{1,2},{2,3},{3,0},{4,5},{5,6},{6,7},{7,4},{8,9},{9,10},{10,1... | collective-permute-start | bytes 3145736 | tf_op jit(solution)/shard_map/ppermute | solution.py:53
  34.2 7.9 %collective-permute-start.3 = (bf16[256,512]{1,0:T(8,128)(2,1)S(1)}, bf16[256,512]{1,0:T(8,128)(2,1)S(1)}, u32[]{:S(2)}, u32[]{:S(2)}) collective-permute-start(bf16[256,512]{1,0:T(8,128)(2,1)S(1)} %copy-done.8), channel_id=1, source_target_pairs={{0,16},{16,0},{1,17},{17,1},{2,18},{18,2},{3,19},{19,3},{4,20},{20... | collective-permute-start | bytes 786440 | tf_op jit(solution)/shard_map/ppermute | solution.py:61
  40.2 17.5 %collective-permute-start.13 = (bf16[2048,256]{1,0:T(8,128)(2,1)S(1)}, bf16[2048,256]{1,0:T(8,128)(2,1)S(1)}, u32[]{:S(2)}, u32[]{:S(2)}) collective-permute-start(bf16[2048,256]{1,0:T(8,128)(2,1)S(1)} %get-tuple-element.127.rest_0_), channel_id=1, source_target_pairs={{0,3},{1,0},{2,1},{3,2},{4,7},{5,4},{6,5},{7,6},{8,11},{9,8},{10,9... | collective-permute-start | bytes 3145736 | tf_op jit(solution)/shard_map/ppermute | solution.py:53
  42.1 17.8 %collective-permute-start.11 = (bf16[2048,256]{1,0:T(8,128)(2,1)S(1)}, bf16[2048,256]{1,0:T(8,128)(2,1)S(1)}, u32[]{:S(2)}, u32[]{:S(2)}) collective-permute-start(bf16[2048,256]{1,0:T(8,128)(2,1)S(1)} %get-tuple-element.127.rest_0_), channel_id=1, source_target_pairs={{0,1},{1,2},{2,3},{3,0},{4,5},{5,6},{6,7},{7,4},{8,9},{9,10},{10,1... | collective-permute-start | bytes 3145736 | tf_op jit(solution)/shard_map/ppermute | solution.py:53
  42.1 5.8 %collective-permute-start.4 = (bf16[256,512]{1,0:T(8,128)(2,1)S(1)}, bf16[256,512]{1,0:T(8,128)(2,1)S(1)}, u32[]{:S(2)}, u32[]{:S(2)}) collective-permute-start(bf16[256,512]{1,0:T(8,128)(2,1)S(1)} %collective-permute-done.rest_1_), channel_id=1, source_target_pairs={{0,16},{16,0},{1,17},{17,1},{2,18},{18,2},{3,19},{19,3},{4,20},{20... | collective-permute-start | bytes 786440 | tf_op jit(solution)/shard_map/ppermute | solution.py:61
  49.4 13.9 %collective-permute-start.32 = (bf16[1024,256]{1,0:T(8,128)(2,1)S(1)}, bf16[1024,256]{1,0:T(8,128)(2,1)S(1)}, u32[]{:S(2)}, u32[]{:S(2)}) collective-permute-start(bf16[1024,256]{1,0:T(8,128)(2,1)S(1)} %slice.95), channel_id=1, source_target_pairs={{0,3},{1,0},{2,1},{3,2},{4,7},{5,4},{6,5},{7,6},{8,11},{9,8},{10,9... | collective-permute-start | bytes 1572872 | tf_op jit(solution)/shard_map/ppermute | solution.py:53
  51.2 17.1 %collective-permute-start.28 = (bf16[1024,256]{1,0:T(8,128)(2,1)S(1)}, bf16[1024,256]{1,0:T(8,128)(2,1)S(1)}, u32[]{:S(2)}, u32[]{:S(2)}) collective-permute-start(bf16[1024,256]{1,0:T(8,128)(2,1)S(1)} %get-tuple-element.113), channel_id=1, source_target_pairs={{0,1},{1,2},{2,3},{3,0},{4,5},{5,6},{6,7},{7,4},{8,9},{9,10},{10,1... | collective-permute-start | bytes 1572872 | tf_op jit(solution)/shard_map/ppermute | solution.py:53
  51.3 19.7 %collective-permute-start.31 = (bf16[1024,256]{1,0:T(8,128)(2,1)S(1)}, bf16[1024,256]{1,0:T(8,128)(2,1)S(1)}, u32[]{:S(2)}, u32[]{:S(2)}) collective-permute-start(bf16[1024,256]{1,0:T(8,128)(2,1)S(1)} %get-tuple-element.112), channel_id=1, source_target_pairs={{0,16},{16,0},{1,17},{17,1},{2,18},{18,2},{3,19},{19,3},{4,20},{20... | collective-permute-start | bytes 1572872 | tf_op jit(solution)/shard_map/ppermute | solution.py:61
  57.7 13.5 %collective-permute-start.34 = (bf16[1024,256]{1,0:T(8,128)(2,1)S(1)}, bf16[1024,256]{1,0:T(8,128)(2,1)S(1)}, u32[]{:S(2)}, u32[]{:S(2)}) collective-permute-start(bf16[1024,256]{1,0:T(8,128)(2,1)S(1)} %slice.95), channel_id=1, source_target_pairs={{0,16},{16,0},{1,17},{17,1},{2,18},{18,2},{3,19},{19,3},{4,20},{20... | collective-permute-start | bytes 1572872 | tf_op jit(solution)/shard_map/ppermute | solution.py:61
  59.9 11.3 %collective-permute-start.16 = (bf16[1024,256]{1,0:T(8,128)(2,1)}, bf16[1024,256]{1,0:T(8,128)(2,1)}, u32[]{:S(2)}, u32[]{:S(2)}) collective-permute-start(bf16[1024,256]{1,0:T(8,128)(2,1)} %slice.86), channel_id=1, source_target_pairs={{0,3},{1,0},{2,1},{3,2},{4,7},{5,4},{6,5},{7,6},{8,11},{9,8},{10,9... | collective-permute-start | bytes 1572872 | tf_op jit(solution)/shard_map/ppermute | solution.py:53
  63.3 11.6 %collective-permute-start.33 = (bf16[1024,256]{1,0:T(8,128)(2,1)S(1)}, bf16[1024,256]{1,0:T(8,128)(2,1)S(1)}, u32[]{:S(2)}, u32[]{:S(2)}) collective-permute-start(bf16[1024,256]{1,0:T(8,128)(2,1)S(1)} %collective-permute-done.32), channel_id=1, source_target_pairs={{0,16},{16,0},{1,17},{17,1},{2,18},{18,2},{3,19},{19,3},{4,20},{20... | collective-permute-start | bytes 1572872 | tf_op jit(solution)/shard_map/ppermute | solution.py:61
  68.2 23.5 %collective-permute-start.14 = (bf16[1024,256]{1,0:T(8,128)(2,1)}, bf16[1024,256]{1,0:T(8,128)(2,1)S(1)}, u32[]{:S(2)}, u32[]{:S(2)}) collective-permute-start(bf16[1024,256]{1,0:T(8,128)(2,1)} %pad_maximum_fusion), channel_id=1, source_target_pairs={{0,16},{16,0},{1,17},{17,1},{2,18},{18,2},{3,19},{19,3},{4,20},{20... | collective-permute-start | bytes 1572872 | tf_op jit(solution)/shard_map/ppermute | solution.py:61
  71.0 21.6 %collective-permute-start.18 = (bf16[1024,256]{1,0:T(8,128)(2,1)}, bf16[1024,256]{1,0:T(8,128)(2,1)S(1)}, u32[]{:S(2)}, u32[]{:S(2)}) collective-permute-start(bf16[1024,256]{1,0:T(8,128)(2,1)} %slice.86), channel_id=1, source_target_pairs={{0,16},{16,0},{1,17},{17,1},{2,18},{18,2},{3,19},{19,3},{4,20},{20... | collective-permute-start | bytes 1572872 | tf_op jit(solution)/shard_map/ppermute | solution.py:61
  71.1 21.5 %collective-permute-start.12 = (bf16[1024,256]{1,0:T(8,128)(2,1)S(1)}, bf16[1024,256]{1,0:T(8,128)(2,1)S(1)}, u32[]{:S(2)}, u32[]{:S(2)}) collective-permute-start(bf16[1024,256]{1,0:T(8,128)(2,1)S(1)} %get-tuple-element.115), channel_id=1, source_target_pairs={{0,1},{1,2},{2,3},{3,0},{4,5},{5,6},{6,7},{7,4},{8,9},{9,10},{10,1... | collective-permute-start | bytes 1572872 | tf_op jit(solution)/shard_map/ppermute | solution.py:53
  71.2 21.4 %collective-permute-start.15 = (bf16[1024,256]{1,0:T(8,128)(2,1)S(1)}, bf16[1024,256]{1,0:T(8,128)(2,1)S(1)}, u32[]{:S(2)}, u32[]{:S(2)}) collective-permute-start(bf16[1024,256]{1,0:T(8,128)(2,1)S(1)} %get-tuple-element.114), channel_id=1, source_target_pairs={{0,16},{16,0},{1,17},{17,1},{2,18},{18,2},{3,19},{19,3},{4,20},{20... | collective-permute-start | bytes 1572872 | tf_op jit(solution)/shard_map/ppermute | solution.py:61
  74.8 17.8 %collective-permute-start.17 = (bf16[1024,256]{1,0:T(8,128)(2,1)}, bf16[1024,256]{1,0:T(8,128)(2,1)S(1)}, u32[]{:S(2)}, u32[]{:S(2)}) collective-permute-start(bf16[1024,256]{1,0:T(8,128)(2,1)} %collective-permute-done.16), channel_id=1, source_target_pairs={{0,16},{16,0},{1,17},{17,1},{2,18},{18,2},{3,19},{19,3},{4,20},{20... | collective-permute-start | bytes 1572872 | tf_op jit(solution)/shard_map/ppermute | solution.py:61
  91.8 8.5 %collective-permute-start.35 = (bf16[1024,256]{1,0:T(8,128)(2,1)S(1)}, bf16[1024,256]{1,0:T(8,128)(2,1)S(1)}, u32[]{:S(2)}, u32[]{:S(2)}) collective-permute-start(bf16[1024,256]{1,0:T(8,128)(2,1)S(1)} %get-tuple-element.70), channel_id=1, source_target_pairs={{0,16},{16,0},{1,17},{17,1},{2,18},{18,2},{3,19},{19,3},{4,20},{20... | collective-permute-start | bytes 1572872 | tf_op jit(solution)/shard_map/ppermute | solution.py:61
  99.9 9.6 %collective-permute-start.19 = (bf16[1024,256]{1,0:T(8,128)(2,1)S(1)}, bf16[1024,256]{1,0:T(8,128)(2,1)S(1)}, u32[]{:S(2)}, u32[]{:S(2)}) collective-permute-start(bf16[1024,256]{1,0:T(8,128)(2,1)S(1)} %get-tuple-element.61), channel_id=1, source_target_pairs={{0,16},{16,0},{1,17},{17,1},{2,18},{18,2},{3,19},{19,3},{4,20},{20... | collective-permute-start | bytes 1572872 | tf_op jit(solution)/shard_map/ppermute | solution.py:61
  100.3 12.0 %collective-permute-start.36 = (bf16[256,256]{1,0:T(8,128)(2,1)S(1)}, bf16[256,256]{1,0:T(8,128)(2,1)S(1)}, u32[]{:S(2)}, u32[]{:S(2)}) collective-permute-start(bf16[256,256]{1,0:T(8,128)(2,1)S(1)} %get-tuple-element.72), channel_id=1, source_target_pairs={{0,32},{32,64},{64,96},{96,0},{1,33},{33,65},{65,97},{97,1},{2,34}... | collective-permute-start | bytes 393224 | tf_op jit(solution)/shard_map/ppermute | solution.py:57
  107.6 5.8 %collective-permute-start.37 = (bf16[256,256]{1,0:T(8,128)(2,1)S(1)}, bf16[256,256]{1,0:T(8,128)(2,1)S(1)}, u32[]{:S(2)}, u32[]{:S(2)}) collective-permute-start(bf16[256,256]{1,0:T(8,128)(2,1)S(1)} %get-tuple-element.73), channel_id=1, source_target_pairs={{0,96},{32,0},{64,32},{96,64},{1,97},{33,1},{65,33},{97,65},{2,98}... | collective-permute-start | bytes 393224 | tf_op jit(solution)/shard_map/ppermute | solution.py:57
  107.6 6.0 %collective-permute-start.38 = (bf16[256,256]{1,0:T(8,128)(2,1)S(1)}, bf16[256,256]{1,0:T(8,128)(2,1)S(1)}, u32[]{:S(2)}, u32[]{:S(2)}) collective-permute-start(bf16[256,256]{1,0:T(8,128)(2,1)S(1)} %get-tuple-element.74), channel_id=1, source_target_pairs={{0,64},{32,96},{64,0},{96,32},{1,65},{33,97},{65,1},{97,33},{2,66}... | collective-permute-start | bytes 393224 | tf_op jit(solution)/shard_map/ppermute | solution.py:57
  109.6 7.8 %collective-permute-start.20 = (bf16[256,256]{1,0:T(8,128)(2,1)S(1)}, bf16[256,256]{1,0:T(8,128)(2,1)S(1)}, u32[]{:S(2)}, u32[]{:S(2)}) collective-permute-start(bf16[256,256]{1,0:T(8,128)(2,1)S(1)} %get-tuple-element.63), channel_id=1, source_target_pairs={{0,32},{32,64},{64,96},{96,0},{1,33},{33,65},{65,97},{97,1},{2,34}... | collective-permute-start | bytes 393224 | tf_op jit(solution)/shard_map/ppermute | solution.py:57
  109.7 8.0 %collective-permute-start.21 = (bf16[256,256]{1,0:T(8,128)(2,1)S(1)}, bf16[256,256]{1,0:T(8,128)(2,1)S(1)}, u32[]{:S(2)}, u32[]{:S(2)}) collective-permute-start(bf16[256,256]{1,0:T(8,128)(2,1)S(1)} %get-tuple-element.64), channel_id=1, source_target_pairs={{0,96},{32,0},{64,32},{96,64},{1,97},{33,1},{65,33},{97,65},{2,98}... | collective-permute-start | bytes 393224 | tf_op jit(solution)/shard_map/ppermute | solution.py:57
  112.4 6.8 %collective-permute-start.22 = (bf16[256,256]{1,0:T(8,128)(2,1)S(1)}, bf16[256,256]{1,0:T(8,128)(2,1)S(1)}, u32[]{:S(2)}, u32[]{:S(2)}) collective-permute-start(bf16[256,256]{1,0:T(8,128)(2,1)S(1)} %get-tuple-element.65), channel_id=1, source_target_pairs={{0,64},{32,96},{64,0},{96,32},{1,65},{33,97},{65,1},{97,33},{2,66}... | collective-permute-start | bytes 393224 | tf_op jit(solution)/shard_map/ppermute | solution.py:57
  120.0 8.8 %collective-permute-start.58 = (bf16[256,256]{1,0:T(8,128)(2,1)S(1)}, bf16[256,256]{1,0:T(8,128)(2,1)S(1)}, u32[]{:S(2)}, u32[]{:S(2)}) collective-permute-start(bf16[256,256]{1,0:T(8,128)(2,1)S(1)} %get-tuple-element.95.rest_0_), channel_id=1, source_target_pairs={{0,96},{32,0},{64,32},{96,64},{1,97},{33,1},{65,33},{97,65},{2,98}... | collective-permute-start | bytes 393224 | tf_op jit(solution)/shard_map/ppermute | solution.py:57
  123.7 6.5 %collective-permute-start.59 = (bf16[256,256]{1,0:T(8,128)(2,1)S(1)}, bf16[256,256]{1,0:T(8,128)(2,1)S(1)}, u32[]{:S(2)}, u32[]{:S(2)}) collective-permute-start(bf16[256,256]{1,0:T(8,128)(2,1)S(1)} %get-tuple-element.95.rest_0_), channel_id=1, source_target_pairs={{0,64},{32,96},{64,0},{96,32},{1,65},{33,97},{65,1},{97,33},{2,66}... | collective-permute-start | bytes 393224 | tf_op jit(solution)/shard_map/ppermute | solution.py:57
  123.7 8.9 %collective-permute-start.60 = (bf16[256,256]{1,0:T(8,128)(2,1)S(1)}, bf16[256,256]{1,0:T(8,128)(2,1)S(1)}, u32[]{:S(2)}, u32[]{:S(2)}) collective-permute-start(bf16[256,256]{1,0:T(8,128)(2,1)S(1)} %get-tuple-element.95.rest_0_), channel_id=1, source_target_pairs={{0,32},{32,64},{64,96},{96,0},{1,33},{33,65},{65,97},{97,1},{2,34}... | collective-permute-start | bytes 393224 | tf_op jit(solution)/shard_map/ppermute | solution.py:57
  124.4 9.9 %collective-permute-start.61 = (bf16[256,256]{1,0:T(8,128)(2,1)S(1)}, bf16[256,256]{1,0:T(8,128)(2,1)S(1)}, u32[]{:S(2)}, u32[]{:S(2)}) collective-permute-start(bf16[256,256]{1,0:T(8,128)(2,1)S(1)} %get-tuple-element.95.rest_0_), channel_id=1, source_target_pairs={{0,16},{16,0},{1,17},{17,1},{2,18},{18,2},{3,19},{19,3},{4,20},{20... | collective-permute-start | bytes 393224 | tf_op jit(solution)/shard_map/ppermute | solution.py:61
  132.7 12.9 %collective-permute-start.64 = (bf16[256,256]{1,0:T(8,128)(2,1)S(1)}, bf16[256,256]{1,0:T(8,128)(2,1)S(1)}, u32[]{:S(2)}, u32[]{:S(2)}) collective-permute-start(bf16[256,256]{1,0:T(8,128)(2,1)S(1)} %collective-permute-done.60.rest_3_), channel_id=1, source_target_pairs={{0,16},{16,0},{1,17},{17,1},{2,18},{18,2},{3,19},{19,3},{4,20},{20... | collective-permute-start | bytes 393224 | tf_op jit(solution)/shard_map/ppermute | solution.py:61
  133.7 17.1 %collective-permute-start.39 = (bf16[256,256]{1,0:T(8,128)(2,1)S(1)}, bf16[256,256]{1,0:T(8,128)(2,1)S(1)}, u32[]{:S(2)}, u32[]{:S(2)}) collective-permute-start(bf16[256,256]{1,0:T(8,128)(2,1)S(1)} %get-tuple-element.77.rest_0_), channel_id=1, source_target_pairs={{0,96},{32,0},{64,32},{96,64},{1,97},{33,1},{65,33},{97,65},{2,98}... | collective-permute-start | bytes 393224 | tf_op jit(solution)/shard_map/ppermute | solution.py:57
  134.3 16.8 %collective-permute-start.40 = (bf16[256,256]{1,0:T(8,128)(2,1)S(1)}, bf16[256,256]{1,0:T(8,128)(2,1)S(1)}, u32[]{:S(2)}, u32[]{:S(2)}) collective-permute-start(bf16[256,256]{1,0:T(8,128)(2,1)S(1)} %get-tuple-element.77.rest_0_), channel_id=1, source_target_pairs={{0,64},{32,96},{64,0},{96,32},{1,65},{33,97},{65,1},{97,33},{2,66}... | collective-permute-start | bytes 393224 | tf_op jit(solution)/shard_map/ppermute | solution.py:57
  134.3 17.0 %collective-permute-start.41 = (bf16[256,256]{1,0:T(8,128)(2,1)S(1)}, bf16[256,256]{1,0:T(8,128)(2,1)S(1)}, u32[]{:S(2)}, u32[]{:S(2)}) collective-permute-start(bf16[256,256]{1,0:T(8,128)(2,1)S(1)} %get-tuple-element.77.rest_0_), channel_id=1, source_target_pairs={{0,32},{32,64},{64,96},{96,0},{1,33},{33,65},{65,97},{97,1},{2,34}... | collective-permute-start | bytes 393224 | tf_op jit(solution)/shard_map/ppermute | solution.py:57
  135.2 16.4 %collective-permute-start.42 = (bf16[256,256]{1,0:T(8,128)(2,1)S(1)}, bf16[256,256]{1,0:T(8,128)(2,1)S(1)}, u32[]{:S(2)}, u32[]{:S(2)}) collective-permute-start(bf16[256,256]{1,0:T(8,128)(2,1)S(1)} %get-tuple-element.77.rest_0_), channel_id=1, source_target_pairs={{0,16},{16,0},{1,17},{17,1},{2,18},{18,2},{3,19},{19,3},{4,20},{20... | collective-permute-start | bytes 393224 | tf_op jit(solution)/shard_map/ppermute | solution.py:61
  150.5 9.5 %collective-permute-start.69 = (bf16[1024,256]{1,0:T(8,128)(2,1)S(1)}, bf16[1024,256]{1,0:T(8,128)(2,1)S(1)}, u32[]{:S(2)}, u32[]{:S(2)}) collective-permute-start(bf16[1024,256]{1,0:T(8,128)(2,1)S(1)} %get-tuple-element.103), channel_id=1, source_target_pairs={{0,16},{16,0},{1,17},{17,1},{2,18},{18,2},{3,19},{19,3},{4,20},{20... | collective-permute-start | bytes 1572872 | tf_op jit(solution)/shard_map/ppermute | solution.py:61
  150.8 11.7 %collective-permute-start.66 = (bf16[1024,256]{1,0:T(8,128)(2,1)S(1)}, bf16[1024,256]{1,0:T(8,128)(2,1)S(1)}, u32[]{:S(2)}, u32[]{:S(2)}) collective-permute-start(bf16[1024,256]{1,0:T(8,128)(2,1)S(1)} %get-tuple-element.99), channel_id=1, source_target_pairs={{0,16},{16,0},{1,17},{17,1},{2,18},{18,2},{3,19},{19,3},{4,20},{20... | collective-permute-start | bytes 1572872 | tf_op jit(solution)/shard_map/ppermute | solution.py:61
  153.5 11.6 %collective-permute-start.67 = (bf16[1024,256]{1,0:T(8,128)(2,1)S(1)}, bf16[1024,256]{1,0:T(8,128)(2,1)S(1)}, u32[]{:S(2)}, u32[]{:S(2)}) collective-permute-start(bf16[1024,256]{1,0:T(8,128)(2,1)S(1)} %get-tuple-element.100), channel_id=1, source_target_pairs={{0,1},{1,2},{2,3},{3,0},{4,5},{5,6},{6,7},{7,4},{8,9},{9,10},{10,1... | collective-permute-start | bytes 1572872 | tf_op jit(solution)/shard_map/ppermute | solution.py:53
  153.6 11.4 %collective-permute-start.68 = (bf16[1024,256]{1,0:T(8,128)(2,1)S(1)}, bf16[1024,256]{1,0:T(8,128)(2,1)S(1)}, u32[]{:S(2)}, u32[]{:S(2)}) collective-permute-start(bf16[1024,256]{1,0:T(8,128)(2,1)S(1)} %get-tuple-element.102), channel_id=1, source_target_pairs={{0,16},{16,0},{1,17},{17,1},{2,18},{18,2},{3,19},{19,3},{4,20},{20... | collective-permute-start | bytes 1572872 | tf_op jit(solution)/shard_map/ppermute | solution.py:61
  159.5 6.8 %collective-permute-start.50 = (bf16[1024,256]{1,0:T(8,128)(2,1)S(1)}, bf16[1024,256]{1,0:T(8,128)(2,1)S(1)}, u32[]{:S(2)}, u32[]{:S(2)}) collective-permute-start(bf16[1024,256]{1,0:T(8,128)(2,1)S(1)} %get-tuple-element.85), channel_id=1, source_target_pairs={{0,16},{16,0},{1,17},{17,1},{2,18},{18,2},{3,19},{19,3},{4,20},{20... | collective-permute-start | bytes 1572872 | tf_op jit(solution)/shard_map/ppermute | solution.py:61
  160.0 8.5 %collective-permute-start.70 = (bf16[1024,256]{1,0:T(8,128)(2,1)S(1)}, bf16[1024,256]{1,0:T(8,128)(2,1)S(1)}, u32[]{:S(2)}, u32[]{:S(2)}) collective-permute-start(bf16[1024,256]{1,0:T(8,128)(2,1)S(1)} %collective-permute-done.69), channel_id=1, source_target_pairs={{0,3},{1,0},{2,1},{3,2},{4,7},{5,4},{6,5},{7,6},{8,11},{9,8},{10,9... | collective-permute-start | bytes 1572872 | tf_op jit(solution)/shard_map/ppermute | solution.py:53
  162.4 6.9 %collective-permute-start.47 = (bf16[1024,256]{1,0:T(8,128)(2,1)S(1)}, bf16[1024,256]{1,0:T(8,128)(2,1)S(1)}, u32[]{:S(2)}, u32[]{:S(2)}) collective-permute-start(bf16[1024,256]{1,0:T(8,128)(2,1)S(1)} %get-tuple-element.81), channel_id=1, source_target_pairs={{0,16},{16,0},{1,17},{17,1},{2,18},{18,2},{3,19},{19,3},{4,20},{20... | collective-permute-start | bytes 1572872 | tf_op jit(solution)/shard_map/ppermute | solution.py:61
  165.1 9.5 %collective-permute-start.48 = (bf16[1024,256]{1,0:T(8,128)(2,1)S(1)}, bf16[1024,256]{1,0:T(8,128)(2,1)S(1)}, u32[]{:S(2)}, u32[]{:S(2)}) collective-permute-start(bf16[1024,256]{1,0:T(8,128)(2,1)S(1)} %get-tuple-element.82), channel_id=1, source_target_pairs={{0,1},{1,2},{2,3},{3,0},{4,5},{5,6},{6,7},{7,4},{8,9},{9,10},{10,1... | collective-permute-start | bytes 1572872 | tf_op jit(solution)/shard_map/ppermute | solution.py:53
  165.1 10.8 %collective-permute-start.49 = (bf16[1024,256]{1,0:T(8,128)(2,1)S(1)}, bf16[1024,256]{1,0:T(8,128)(2,1)S(1)}, u32[]{:S(2)}, u32[]{:S(2)}) collective-permute-start(bf16[1024,256]{1,0:T(8,128)(2,1)S(1)} %get-tuple-element.84), channel_id=1, source_target_pairs={{0,16},{16,0},{1,17},{17,1},{2,18},{18,2},{3,19},{19,3},{4,20},{20... | collective-permute-start | bytes 1572872 | tf_op jit(solution)/shard_map/ppermute | solution.py:61
  166.4 9.6 %collective-permute-start.51 = (bf16[1024,256]{1,0:T(8,128)(2,1)S(1)}, bf16[1024,256]{1,0:T(8,128)(2,1)S(1)}, u32[]{:S(2)}, u32[]{:S(2)}) collective-permute-start(bf16[1024,256]{1,0:T(8,128)(2,1)S(1)} %collective-permute-done.50), channel_id=1, source_target_pairs={{0,3},{1,0},{2,1},{3,2},{4,7},{5,4},{6,5},{7,6},{8,11},{9,8},{10,9... | collective-permute-start | bytes 1572872 | tf_op jit(solution)/shard_map/ppermute | solution.py:53
  168.8 17.0 %collective-permute-start.71 = (bf16[2048,256]{1,0:T(8,128)(2,1)S(1)}, bf16[2048,256]{1,0:T(8,128)(2,1)S(1)}, u32[]{:S(2)}, u32[]{:S(2)}) collective-permute-start(bf16[2048,256]{1,0:T(8,128)(2,1)S(1)} %get-tuple-element.104), channel_id=1, source_target_pairs={{0,1},{1,2},{2,3},{3,0},{4,5},{5,6},{6,7},{7,4},{8,9},{9,10},{10,1... | collective-permute-start | bytes 3145736 | tf_op jit(solution)/shard_map/ppermute | solution.py:53
  169.3 16.6 %collective-permute-start.72 = (bf16[2048,256]{1,0:T(8,128)(2,1)S(1)}, bf16[2048,256]{1,0:T(8,128)(2,1)S(1)}, u32[]{:S(2)}, u32[]{:S(2)}) collective-permute-start(bf16[2048,256]{1,0:T(8,128)(2,1)S(1)} %get-tuple-element.105), channel_id=1, source_target_pairs={{0,3},{1,0},{2,1},{3,2},{4,7},{5,4},{6,5},{7,6},{8,11},{9,8},{10,9... | collective-permute-start | bytes 3145736 | tf_op jit(solution)/shard_map/ppermute | solution.py:53
  176.2 24.0 %collective-permute-start.52 = (bf16[2048,256]{1,0:T(8,128)(2,1)S(1)}, bf16[2048,256]{1,0:T(8,128)(2,1)S(1)}, u32[]{:S(2)}, u32[]{:S(2)}) collective-permute-start(bf16[2048,256]{1,0:T(8,128)(2,1)S(1)} %get-tuple-element.86), channel_id=1, source_target_pairs={{0,1},{1,2},{2,3},{3,0},{4,5},{5,6},{6,7},{7,4},{8,9},{9,10},{10,1... | collective-permute-start | bytes 3145736 | tf_op jit(solution)/shard_map/ppermute | solution.py:53
  176.3 26.0 %collective-permute-start.53 = (bf16[2048,256]{1,0:T(8,128)(2,1)S(1)}, bf16[2048,256]{1,0:T(8,128)(2,1)S(1)}, u32[]{:S(2)}, u32[]{:S(2)}) collective-permute-start(bf16[2048,256]{1,0:T(8,128)(2,1)S(1)} %get-tuple-element.87), channel_id=1, source_target_pairs={{0,3},{1,0},{2,1},{3,2},{4,7},{5,4},{6,5},{7,6},{8,11},{9,8},{10,9... | collective-permute-start | bytes 3145736 | tf_op jit(solution)/shard_map/ppermute | solution.py:53
  178.9 11.3 %collective-permute-start.46 = (bf16[1024,256]{1,0:T(8,128)(2,1)}, bf16[1024,256]{1,0:T(8,128)(2,1)S(1)}, u32[]{:S(2)}, u32[]{:S(2)}) collective-permute-start(bf16[1024,256]{1,0:T(8,128)(2,1)} %get-tuple-element.79), channel_id=1, source_target_pairs={{0,16},{16,0},{1,17},{17,1},{2,18},{18,2},{3,19},{19,3},{4,20},{20... | collective-permute-start | bytes 1572872 | tf_op jit(solution)/shard_map/ppermute | solution.py:61
  186.3 20.3 %collective-permute-start.73 = (bf16[512,256]{1,0:T(8,128)(2,1)S(1)}, bf16[512,256]{1,0:T(8,128)(2,1)S(1)}, u32[]{:S(2)}, u32[]{:S(2)}) collective-permute-start(bf16[512,256]{1,0:T(8,128)(2,1)S(1)} %get-tuple-element.107), channel_id=1, source_target_pairs={{0,4},{1,5},{2,6},{3,7},{4,8},{5,9},{6,10},{7,11},{8,12},{9,13},{1... | collective-permute-start | bytes 786440 | tf_op jit(solution)/shard_map/ppermute | solution.py:53
  189.0 19.1 %collective-permute-start.74 = (bf16[512,256]{1,0:T(8,128)(2,1)S(1)}, bf16[512,256]{1,0:T(8,128)(2,1)S(1)}, u32[]{:S(2)}, u32[]{:S(2)}) collective-permute-start(bf16[512,256]{1,0:T(8,128)(2,1)S(1)} %get-tuple-element.108), channel_id=1, source_target_pairs={{0,12},{1,13},{2,14},{3,15},{4,0},{5,1},{6,2},{7,3},{8,4},{9,5},{1... | collective-permute-start | bytes 786440 | tf_op jit(solution)/shard_map/ppermute | solution.py:53
  190.2 17.8 %collective-permute-start.75 = (bf16[512,256]{1,0:T(8,128)(2,1)S(1)}, bf16[512,256]{1,0:T(8,128)(2,1)S(1)}, u32[]{:S(2)}, u32[]{:S(2)}) collective-permute-start(bf16[512,256]{1,0:T(8,128)(2,1)S(1)} %get-tuple-element.109), channel_id=1, source_target_pairs={{0,8},{1,9},{2,10},{3,11},{4,12},{5,13},{6,14},{7,15},{8,0},{9,1},... | collective-permute-start | bytes 786440 | tf_op jit(solution)/shard_map/ppermute | solution.py:53
  202.6 8.0 %collective-permute-start.54 = (bf16[512,256]{1,0:T(8,128)(2,1)S(1)}, bf16[512,256]{1,0:T(8,128)(2,1)S(1)}, u32[]{:S(2)}, u32[]{:S(2)}) collective-permute-start(bf16[512,256]{1,0:T(8,128)(2,1)S(1)} %get-tuple-element.89), channel_id=1, source_target_pairs={{0,4},{1,5},{2,6},{3,7},{4,8},{5,9},{6,10},{7,11},{8,12},{9,13},{1... | collective-permute-start | bytes 786440 | tf_op jit(solution)/shard_map/ppermute | solution.py:53
  206.6 8.0 %collective-permute-start.56 = (bf16[512,256]{1,0:T(8,128)(2,1)S(1)}, bf16[512,256]{1,0:T(8,128)(2,1)S(1)}, u32[]{:S(2)}, u32[]{:S(2)}) collective-permute-start(bf16[512,256]{1,0:T(8,128)(2,1)S(1)} %get-tuple-element.91), channel_id=1, source_target_pairs={{0,8},{1,9},{2,10},{3,11},{4,12},{5,13},{6,14},{7,15},{8,0},{9,1},... | collective-permute-start | bytes 786440 | tf_op jit(solution)/shard_map/ppermute | solution.py:53
  208.2 10.1 %collective-permute-start.76 = (f32[256,256]{1,0:T(8,128)S(1)}, f32[256,256]{1,0:T(8,128)S(1)}, u32[]{:S(2)}, u32[]{:S(2)}) collective-permute-start(f32[256,256]{1,0:T(8,128)S(1)} %get-tuple-element.111), channel_id=1, source_target_pairs={{0,16},{16,0},{1,17},{17,1},{2,18},{18,2},{3,19},{19,3},{4,20},{20... | collective-permute-start | bytes 786440 | tf_op jit(solution)/shard_map/ppermute | solution.py:61
  (32 other events, 413.3 us)

commit v2 on v0

v2 whole, which is shorter than its diff:
```python
import functools

import jax
import jax.numpy as jnp
from jax import lax
from jax.experimental import pallas as pl
from jax.experimental.pallas import tpu as pltpu
from jax.sharding import Mesh
from jax.sharding import PartitionSpec as P

F32 = jnp.float32
BF16 = jnp.bfloat16
RING = 4
BLOCK = 128
SLOTS = 16
GROUP = 4
WIDTH = 512
CHUNKS = 2
COLS = WIDTH // CHUNKS
HALF = 256
GATHERED = RING * HALF
VMEM = pl.BlockSpec(memory_space=pltpu.VMEM)
SMEM = pl.BlockSpec(memory_space=pltpu.SMEM)
ANY = pl.BlockSpec(memory_space=pl.ANY)
LIGHT = pl.CostEstimate(flops=0, bytes_accessed=0, transcendentals=0)
LIMIT = 20 * 1024 * 1024


def shape(rows, cols, dtype):
    return jax.ShapeDtypeStruct((rows, cols), dtype)


def params():
    return pltpu.CompilerParams(vmem_limit_bytes=LIMIT)


CHIP_AXES = ("core", "x", "y")


def along(first, step):
    pairs = []
    for core in range(2):
        for x in range(RING):
            for y in range(RING):
                if (core == 0) == first:
                    to = ((x + step) % RING, y)
                else:
                    to = (x, (y + step) % RING)
                pairs.append((core * 16 + x * RING + y, core * 16 + to[0] * RING + to[1]))
    return pairs


def shift(value, first, step):
    return lax.ppermute(value, CHIP_AXES, along(first, step))


def shift_z(value, step):
    return lax.ppermute(value, "z", [(i, (i + step) % RING) for i in range(RING)])


def after(value, *others):
    return lax.optimization_barrier((value, others))[0]


def pair_z(value, flip):
    return lax.ppermute(value, "z", [(i, i ^ flip) for i in range(RING)])


def swap(value):
    return lax.ppermute(value, "core", [(0, 1), (1, 0)])


def dot(a, b):
    return jnp.dot(a, b, preferred_element_type=F32)


def dot_t(a, b):
    return lax.dot_general(a, b, (((1,), (1,)), ((), ())), preferred_element_type=F32)


def t_dot(a, b):
    return lax.dot_general(a, b, (((0,), (0,)), ((), ())), preferred_element_type=F32)


def split_dot(a, b, product):
    high = a.astype(BF16)
    low = (a - high.astype(F32)).astype(BF16)
    return product(high, b) + product(low, b)


def sigmoid(value):
    return 1.0 / (1.0 + jnp.exp(-value))


def one_hot(offsets, slot):
    rows = lax.broadcasted_iota(jnp.int32, (BLOCK, BLOCK), 0)
    return (rows == offsets[pl.ds(slot, 1), :]).astype(BF16)


def grid_place(block, where):
    core, x, y = where[1], where[2], where[3]
    owner = block // 4
    kind = (block % 4) // 2
    dx = lax.rem(x - owner // 4 + RING, RING)
    dy = lax.rem(y - owner % 4 + RING, RING)
    mine = kind == core
    near = jnp.where(kind == 0, dx, dy)
    far = jnp.where(kind == 0, dy, dx)
    return mine, near, far, (block % 2) * BLOCK


def mesh_place(block, where):
    owner = block // 2
    dz = lax.rem(owner // 2 - where[0] + RING, RING)
    return owner % 2 == where[1], dz, (block % 2) * BLOCK


def first_product_kernel(where, grid, w_grid, keep, give):
    core = where[1]
    for out, half in ((give, 1 - core), (keep, core)):
        out[...] = dot(grid[pl.ds(pl.multiple_of(half * HALF, HALF), HALF), :], w_grid[...]).astype(BF16)


def ring_kernel(keep, got, up, across, down, *outs):
    for chunk, out in enumerate(outs):
        cols = pl.ds(chunk * COLS, COLS)
        out[:HALF, :] = keep[:, cols]
        out[GATHERED : GATHERED + HALF, :] = got[:, cols]
        for step, term in enumerate((up, across, down)):
            out[pl.ds((step + 1) * HALF, HALF), :] = term[:HALF, cols]
            out[pl.ds(GATHERED + (step + 1) * HALF, HALF), :] = term[HALF:, cols]


def edge_kernel(where, live, mesh_block, recv, edge, w_mesh, w_edge, bias, *rest):
    pieces, outs, (blocks, rows) = rest[:2], rest[2 : 2 + CHUNKS], rest[-2:]

    @pl.loop(0, live[0])
    def _(group):
        for i in range(GROUP):
            block = mesh_block[group * GROUP + i]
            owner = block // 2
            flip = (owner // 2) ^ where[0]
            mine, far = owner % 2 == where[1], flip // 2
            row = (2 * far + (flip ^ (3 * far))) * HALF + (block % 2) * BLOCK
            for piece in range(2):

                @pl.when(mine == (piece == 0))
                def _():
                    blocks[i] = pieces[piece][pl.ds(pl.multiple_of(row, BLOCK), BLOCK), :]

        for i in range(GROUP):
            rows[pl.ds(i * BLOCK, BLOCK), :] = t_dot(one_hot(recv, group * GROUP + i), blocks[i]).astype(BF16)
        lines = pl.ds(pl.multiple_of(group * GROUP * BLOCK, GROUP * BLOCK), GROUP * BLOCK)
        for chunk in range(CHUNKS):
            cols = pl.ds(chunk * COLS, COLS)
            outs[chunk][lines, :] = dot(rows[...], w_mesh[:, cols]) + dot(edge[lines, :], w_edge[:, cols]) + bias[:, cols]


def forward_kernel(where, live, grid_block, mesh_block, send, recv, rest_in, *rest):
    pieces, (slope, near, far) = rest[:6], rest[6:9]
    total, blocks, sems = rest[9:]

    @pl.loop(0, live[0] * GROUP)
    def _(slot):
        mine, first, second, row = grid_place(grid_block[slot], where)
        start = first * HALF + row
        for piece in range(6):
            if piece < RING:
                here, base = jnp.logical_and(mine, second == piece), 0
            elif piece == RING:
                here, base = jnp.logical_and(jnp.logical_not(mine), second != 2), jnp.minimum(second, 2) * GATHERED
            else:
                here, base = jnp.logical_and(jnp.logical_not(mine), second == 2), 0

            @pl.when(here)
            def _():
                lines = pl.ds(pl.multiple_of(base + start, BLOCK), BLOCK)
                pltpu.make_async_copy(pieces[piece].at[lines, :], blocks.at[slot], sems.at[slot]).start()

    total[...] = jnp.zeros_like(total)

    @pl.loop(0, live[0])
    def _(group):
        hidden = []
        for i in range(GROUP):
            slot = group * GROUP + i
            pltpu.make_async_copy(pieces[0].at[pl.ds(0, BLOCK), :], blocks.at[slot], sems.at[slot]).wait()
            lines = pl.ds(pl.multiple_of(slot * BLOCK, BLOCK), BLOCK)
            pre = rest_in[lines, :] + t_dot(one_hot(send, slot), blocks[slot])
            sig = sigmoid(pre)
            slope[lines, :] = sig * (1.0 + pre * (1.0 - sig))
            hidden.append((pre * sig).astype(BF16))
        for i in range(GROUP):
            slot = group * GROUP + i
            mine, dz, row = mesh_place(mesh_block[slot], where)
            start = jnp.where(mine, 0, RING * HALF) + dz * HALF + row
            lines = pl.ds(pl.multiple_of(start, BLOCK), BLOCK)
            total[lines, :] += dot(one_hot(recv, slot), hidden[i])

    near[...] = total[: RING * HALF, :]
    far[...] = total[RING * HALF :, :].astype(BF16)


def pair_sum_kernel(*refs):
    near, other, outs = refs[:CHUNKS], refs[CHUNKS : 2 * CHUNKS], refs[2 * CHUNKS :]
    for chunk in range(CHUNKS):
        for step in range(RING):
            lines = pl.ds(step * HALF, HALF)
            value = near[chunk][lines, :] + other[chunk][lines, :].astype(F32)
            outs[step][:, pl.ds(chunk * COLS, COLS)] = value.astype(outs[step].dtype)


def node_kernel(cot, w_out, own, a, b, c, aggregate, grads):
    part = own[...] + (a[...].astype(F32) + b[...].astype(F32) + c[...].astype(F32))
    total = split_dot(part, w_out[...], dot)
    aggregate[...] = total
    sig = sigmoid(total)
    grad = (cot[...] * (sig * (1.0 + total * (1.0 - sig)))).astype(BF16)
    grads[...] = dot_t(grad, w_out[...]).astype(BF16)


def backward_kernel(where, live, grid_block, mesh_block, first_of, send, recv, *rest):
    slopes, pieces, outs = rest[:CHUNKS], rest[CHUNKS : CHUNKS + 8], rest[CHUNKS + 8 : -2]
    total, blocks = rest[-2:]
    for out in outs:
        out[...] = jnp.zeros_like(out)

    @pl.loop(0, live[0])
    def _(group):
        for i in range(GROUP):
            mine, dz, row = mesh_place(mesh_block[group * GROUP + i], where)
            for piece in range(8):

                @pl.when(jnp.logical_and(mine == (piece < 4), dz == piece % 4))
                def _():
                    blocks[i] = pieces[piece][pl.ds(pl.multiple_of(row, BLOCK), BLOCK), :]

        parts = []
        for i in range(GROUP):
            slot = group * GROUP + i
            lines = pl.ds(pl.multiple_of(slot * BLOCK, BLOCK), BLOCK)
            grad = t_dot(one_hot(recv, slot), blocks[i])
            grads = [(grad[:, c * COLS : (c + 1) * COLS] * slopes[c][lines, :]).astype(BF16) for c in range(CHUNKS)]
            parts.append([dot(one_hot(send, slot), g) for g in grads])
        for i in range(GROUP):
            slot = group * GROUP + i
            first = first_of[slot]
            for c in range(CHUNKS):
                cols = pl.ds(c * COLS, COLS)

                @pl.when(first == slot)
                def _():
                    total[slot, :, cols] = parts[i][c]

                @pl.when(first != slot)
                def _():
                    total[first, :, cols] += parts[i][c]

    @pl.loop(0, live[0] * GROUP)
    def _(slot):
        @pl.when(first_of[slot] == slot)
        def _():
            mine, near, far, row = grid_place(grid_block[slot], where)
            start = lax.rem(RING - near, RING) * HALF + row
            far = lax.rem(RING - far, RING)
            for c in range(CHUNKS):
                own, (give_across, give_rest) = outs[RING * c : RING * (c + 1)], outs[RING * CHUNKS :]
                for step in range(RING):

                    @pl.when(jnp.logical_and(mine, far == step))
                    def _():
                        own[step][pl.ds(pl.multiple_of(start, BLOCK), BLOCK), :] = total[slot, :, pl.ds(c * COLS, COLS)].astype(BF16)

                    @pl.when(jnp.logical_and(jnp.logical_not(mine), far == step))
                    def _():
                        to, place = (give_across, c) if step == 2 else (give_rest, 3 * c + min(step, 2))
                        place = start + place * GATHERED
                        to[pl.ds(pl.multiple_of(place, BLOCK), BLOCK), :] = total[slot, :, pl.ds(c * COLS, COLS)].astype(BF16)


def add(a, b):
    return (a[...].astype(F32) + b[...].astype(F32)).astype(BF16)


def merge_kernel(base, up, down, other, into_up, into_down, out_up, out_down):
    out_up[:GATHERED, :] = add(up, into_up)
    out_up[GATHERED:, :] = other[pl.ds(base + GATHERED, GATHERED), :]
    out_down[:GATHERED, :] = down[...]
    out_down[GATHERED:, :] = add(other.at[pl.ds(base + 2 * GATHERED, GATHERED), :], into_down)


def column_sum_kernel(base, own, other, up, down, here, *outs):
    for half, (term, first) in enumerate(((own, 0), (other, base))):
        for step in range(RING):
            both = pl.ds(half * GATHERED + step * HALF, HALF)
            value = term[pl.ds(first + step * HALF, HALF), :].astype(F32) + (up[both, :].astype(F32) + down[both, :].astype(F32))
            place = pl.ds(half * HALF, HALF)
            if step == 0:
                here[place, :] = value
            else:
                outs[step - 1][place, :] = value.astype(BF16)


def row_sum_kernel(here, up, down, across, own, other):
    value = here[...] + (up[...].astype(F32) + down[...].astype(F32) + across[...].astype(F32))
    own[...] = value[:HALF, :]
    other[...] = value[HALF:, :]


def grid_grad_kernel(where, w_grid, *rest):
    out = rest[-1]
    core = where[1]
    for which in range(2):
        value = jnp.zeros((HALF, WIDTH), F32)
        for chunk in range(CHUNKS):
            value += split_dot(rest[2 * chunk + which][...], w_grid[:, chunk * COLS : (chunk + 1) * COLS], dot_t)
        place = core if which == 0 else 1 - core
        out[pl.ds(pl.multiple_of(place * HALF, HALF), HALF), :] = value


def per_device(
    grid,
    mesh_latent,
    edge_latent,
    edge_grid_block,
    edge_mesh_block,
    sender_offset,
    receiver_offset,
    live_groups,
    w_grid,
    w_mesh,
    w_edge,
    bias,
    w_out,
    w_node,
    cotangent,
):
    where = jnp.stack([lax.axis_index(a) for a in ("z", "core", "x", "y")]).astype(jnp.int32)
    edges = SLOTS * BLOCK
    both_chunks = range(CHUNKS)

    def call(kernel, name, outs, *args, scalars=0, scratch=(), spec=VMEM):
        whole = [SMEM] * scalars + [VMEM] * (len(args) - scalars)
        if spec is ANY:
            whole[-6:] = [ANY] * 6
        return pl.pallas_call(
            kernel,
            in_specs=whole,
            out_specs=[VMEM] * len(outs),
            out_shape=outs,
            scratch_shapes=scratch,
            compiler_params=params(),
            cost_estimate=LIGHT,
            name=name,
        )(*args)

    keep, give = call(
        first_product_kernel, "first_product", [shape(HALF, WIDTH, BF16)] * 2, where, grid, w_grid, scalars=1
    )
    got = swap(give)
    mine = jnp.concatenate([keep, got], axis=0)
    mesh_pair = pair_z(after(mesh_latent, mine), 1)

    def far_gather(value):
        return shift(value, False, 1), shift(value, False, -1)

    def give_rows(both, up, down):
        return jnp.concatenate([both[GATHERED:], up[GATHERED:], down[GATHERED:]], axis=0)

    near = shift(mine, True, 1), shift(mine, True, 2), shift(mine, True, -1)
    ring_0, ring_1 = call(
        ring_kernel, "ring", [shape(2 * GATHERED, COLS, BF16)] * CHUNKS, keep, got, *after(near, mesh_pair)
    )

    mesh_near = jnp.concatenate([mesh_latent, mesh_pair], axis=0)
    mesh_far = pair_z(after(mesh_near, ring_0), 3)
    (up_0, down_0), mesh_far = lax.optimization_barrier((far_gather(ring_0), mesh_far))
    across_0 = shift(up_0[:GATHERED], False, 1), shift(down_0[GATHERED:], False, -1)
    far_1 = far_gather(after(ring_1, up_0))
    mesh_rows = jnp.concatenate([mesh_near, mesh_far], axis=0)
    mesh_pieces = [mesh_rows, swap(mesh_rows)]
    edge_terms = call(
        edge_kernel,
        "edge_terms",
        [shape(edges, COLS, F32)] * CHUNKS,
        where,
        live_groups,
        edge_mesh_block,
        receiver_offset,
        edge_latent,
        w_mesh,
        w_edge,
        bias.reshape(1, WIDTH),
        *mesh_pieces,
        scalars=3,
        scratch=[pltpu.VMEM((GROUP, BLOCK, WIDTH), BF16), pltpu.VMEM((GROUP * BLOCK, WIDTH), BF16)],
    )
    cot = dot_t(cotangent, w_node)

    got_0 = swap(after(give_rows(ring_0, up_0, down_0), mesh_pieces[1]))
    own_across, other_across = lax.optimization_barrier(across_0)
    far_got_0 = swap(after(other_across, got_0))
    (up_1, down_1), edge_terms, got_0, far_got_0 = lax.optimization_barrier((far_1, edge_terms, got_0, far_got_0))
    across_1 = shift(up_1[:GATHERED], False, 1), shift(down_1[GATHERED:], False, -1)

    def forward(chunk, own, got):
        return call(
            forward_kernel,
            f"forward_{chunk}",
            [shape(edges, COLS, F32), shape(RING * HALF, COLS, F32), shape(RING * HALF, COLS, BF16)],
            where,
            live_groups,
            edge_grid_block,
            edge_mesh_block,
            sender_offset,
            receiver_offset,
            edge_terms[chunk],
            *own,
            *got,
            scalars=4,
            scratch=[
                pltpu.VMEM((2 * RING * HALF, COLS), F32),
                pltpu.VMEM((SLOTS, BLOCK, COLS), BF16),
                pltpu.SemaphoreType.DMA((SLOTS,)),
            ],
            spec=ANY,
        )

    def pair_sum(*terms):
        outs = [shape(HALF, WIDTH, F32)] + [shape(HALF, WIDTH, BF16)] * 3
        return call(pair_sum_kernel, "pair_sum", outs, *terms)

    def band_sum(own, a, b, c):
        return [own, shift_z(a, 1), shift_z(c, -1), shift_z(b, 2)]

    slope_0, near_sum_0, far_sum_0 = forward(0, (ring_0, up_0, own_across, down_0), (got_0, far_got_0))
    got_1 = swap(give_rows(ring_1, up_1, down_1))
    (own_across, other_across), got_1, far_sum_0, cot = lax.optimization_barrier((across_1, got_1, far_sum_0, cot))
    far_got_1, far_sum_0 = swap(other_across), swap(far_sum_0)
    slope_1, near_sum_1, far_sum_1 = forward(
        1, (ring_1, up_1, own_across, down_1), (got_1, after(far_got_1, far_sum_0))
    )
    sums = band_sum(*pair_sum(near_sum_0, near_sum_1, far_sum_0, swap(far_sum_1)))
    slopes = [slope_0, slope_1]

    aggregate, grads = call(
        node_kernel, "node", [shape(HALF, WIDTH, F32), shape(HALF, WIDTH, BF16)], cot, w_out, *sums
    )

    slots = jnp.arange(SLOTS)
    same = edge_grid_block[:, None] == edge_grid_block[None, :]
    first_of = jnp.min(jnp.where(same, slots[None, :], SLOTS), axis=1).astype(jnp.int32)

    band = [grads, shift_z(grads, -1), shift_z(grads, 2), shift_z(grads, 1)]
    partial = call(
        backward_kernel,
        "backward",
        [shape(GATHERED, COLS, BF16)] * (RING * CHUNKS)
        + [shape(CHUNKS * GATHERED, COLS, BF16), shape(3 * CHUNKS * GATHERED, COLS, BF16)],
        where,
        live_groups,
        edge_grid_block,
        edge_mesh_block,
        first_of,
        sender_offset,
        receiver_offset,
        *slopes,
        *band,
        *[swap(p) for p in band],
        scalars=5,
        scratch=[pltpu.VMEM((SLOTS, BLOCK, WIDTH), F32), pltpu.VMEM((GROUP, BLOCK, WIDTH), BF16)],
    )
    own_0, own_1, give_across, give_rest = partial[:RING], partial[RING : 2 * RING], partial[-2], partial[-1]

    def merge(chunk, own, other, into):
        kernel = functools.partial(merge_kernel, 3 * chunk * GATHERED)
        return call(kernel, f"merge_{chunk}", [shape(2 * GATHERED, COLS, BF16)] * 2, own[1], own[3], other, *into)

    def column_sum(chunk, own, other, far):
        outs = [shape(2 * HALF, COLS, F32)] + [shape(2 * HALF, COLS, BF16)] * 3
        kernel = functools.partial(column_sum_kernel, 3 * chunk * GATHERED)
        return call(kernel, f"column_sum_{chunk}", outs, own[0], other, *far)

    def far_send(up, down):
        return shift(up, False, 1), shift(down, False, -1)

    def near_send(here, a, b, c):
        return here, shift(a, True, 1), shift(b, True, 2), shift(c, True, -1)

    def row_sum(chunk, terms):
        return call(row_sum_kernel, f"row_sum_{chunk}", [shape(HALF, COLS, F32)] * 2, *terms)

    across = swap(give_across)
    other = swap(after(give_rest, across))
    into_0 = shift(own_0[2], False, 1), shift(across[:GATHERED], False, -1)
    into_1 = shift(own_1[2], False, 1), shift(across[GATHERED:], False, -1)
    merged = merge(0, own_0, other, into_0)
    far_0 = far_send(*merged)
    merged = merge(1, own_1, after(other, merged), into_1)
    far_1 = far_send(*merged)
    activation = jax.nn.silu(aggregate).astype(BF16)
    mesh_out = (mesh_latent.astype(F32) + dot(activation, w_node)).astype(BF16)
    columns = column_sum(0, own_0, other, after(far_0, merged, mesh_out))
    rows_0 = near_send(*columns)
    columns = column_sum(1, own_1, other, after(far_1, columns))
    rows_1 = near_send(*columns)
    mine_0, give_0 = row_sum(0, after(rows_0, columns))
    got_0 = swap(give_0)
    mine_1, give_1 = row_sum(1, after(rows_1, give_0))
    parts = [mine_0, got_0, mine_1, swap(give_1)]

    grid_grad = call(
        grid_grad_kernel, "grid_grad", [shape(2 * HALF, WIDTH, F32)], where, w_grid, *parts, scalars=1
    )[0]
    return (mesh_out, grid_grad)


def solution(mesh):
    split = Mesh(mesh.devices.reshape(4, 2, 4, 4), ("z", "core", "x", "y"))
    rows = P(("z", "core", "x", "y"))
    placed = (rows,) * 8 + (P(),) * 6 + (rows,)
    return jax.shard_map(per_device, mesh=split, in_specs=placed, out_specs=(rows, rows), check_vma=False)
```

time: 571 us -> 197 us (0.35)
  waiting for transfers between devices: 406 us -> 90.1 us
  starting transfers between devices: 0.2 us -> 73.1 us
  local copies, waits for them, and re-layouts: 55.5 us -> 2.67 us
  other arithmetic: 49.1 us -> 0.5 us
  matrix products: 39.1 us -> 1.36 us
  Pallas kernels: 0 us -> 28.2 us
  between operations: 13.9 us -> 1.73 us
    reduce_scatter x2 -> x0, waiting for transfers between devices: 274 us -> none  [the longest x1 187 us: per_device(): lax.psum_scatter(grid_partial, 'mesh', scatter_dimension=0, tiled=True)]
    all_gather x3 -> x0, waiting for transfers between devices: 130 us -> none  [the longest x1 72.7 us: per_device(): band_terms = lax.all_gather(grid, 'mesh', axis=0, tiled=True)]
    ppermute x0 -> x49, waiting for transfers between devices: none -> 90.1 us  [the longest x25 44.7 us: shift(): return lax.ppermute(value, CHIP_AXES, along(first, step))]
    ppermute x0 -> x49, starting transfers between devices: none -> 73.1 us  [the longest x25 39.4 us: shift(): return lax.ppermute(value, CHIP_AXES, along(first, step))]
    scatter-add x4 -> x0, other arithmetic: 48.1 us -> none  [the longest x2 31.4 us: backward(): total.at[senders]]
    gather x10 -> x0, local copies, waits for them, and re-layouts: 44 us -> none  [the longest x4 27.1 us: group_terms(): band_terms[senders]]
    dot_general x16 -> x2, matrix products: 39.1 us -> 1.36 us  [the longest x1 1.04 us: dot(): return jnp.dot(a, b, preferred_element_type=F32)]
    pallas_call x0 -> x15, Pallas kernels: none -> 28.2 us  [call(): pl.pallas_call(kernel, in_specs=whole, out_specs=[VMEM] * len(outs), out_...]
  transfers between devices with their start and end apart: 5 -> 49, of which waited for: 5 -> 26; matrix products, arithmetic and copies ran while one was open for 0% -> 1% of each run, Pallas kernels for 0% -> 6%
where the time goes in v2:
time: 197 us; the launch traced here: 198 us
  waiting for transfers between devices  90.1 us (46%)
  starting transfers between devices  73.1 us (37%)
  Pallas kernels  28.2 us (14%)
  local copies, waits for them, and re-layouts  2.67 us (1%)
    ppermute x25, waiting for transfers between devices, shift(): return lax.ppermute(value, CHIP_AXES, along(first, step))  44.7 us
    ppermute x25, starting transfers between devices, shift(): return lax.ppermute(value, CHIP_AXES, along(first, step))  39.4 us
    pallas_call x15, Pallas kernels, call(): pl.pallas_call(kernel, in_specs=whole, out_specs=[VMEM] * len(outs), out_...  28.2 us
    ppermute x16, starting transfers between devices, swap(): return lax.ppermute(value, 'core', [(0, 1), (1, 0)])  19.2 us
    ppermute x6, waiting for transfers between devices, shift_z(): lax.ppermute(value, 'z', [(i, (i + step) % RING) for i in range(RING)])  16.9 us
    ppermute x2, waiting for transfers between devices, pair_z(): return lax.ppermute(value, 'z', [(i, i ^ flip) for i in range(RING)])  16.1 us
    ppermute x16, waiting for transfers between devices, swap(): return lax.ppermute(value, 'core', [(0, 1), (1, 0)])  12.3 us
    ppermute x6, starting transfers between devices, shift_z(): lax.ppermute(value, 'z', [(i, (i + step) % RING) for i in range(RING)])  9.07 us
  transfers between devices with their start and end apart: 49, of which 26 were waited for; matrix products, arithmetic and copies ran while one was open for 1% of the time, Pallas kernels for 6%

profile of v2, /device:TPU:1, one launch (start us, length us, event | category | flops | bytes accessed | tf_op | source)
XLA Modules:
  0.0 197.7 jit_solution(9973328410079040617)
XLA Ops:
  0.7 1.1 copy-done.2
  1.8 1.0 copy-done.4
  2.9 1.0 first_product.1
  3.8 1.5 collective-permute-start
  5.4 1.1 collective-permute-done.got
  6.5 1.4 collective-permute-start.1
  8.0 2.6 %collective-permute-start.2 = (bf16[512,512]{1,0:T(8,128)(2,1)S(1)}, bf16[512,512]{1,0:T(8,128)(2,1)S(1)}, u32[]{:S(2)}, u32[]{:S(2)}) collective-permute-start(bf16[512,512]{1,0:T(8,128)(2,1)S(1)} %constant_dynamic-update-slice_fusion), channel_id=1, source_target_pairs={{0,8},{1,9},{2,10},{3,11},{4,12},{5,13},{6,14},{7,15},{8,0},{9,1},... | collective-permute-start | bytes 1572872 | tf_op jit(solution)/shard_map/ppermute | solution.py:54
  10.6 1.1 collective-permute-start.3
  11.7 1.6 collective-permute-start.4
  13.3 5.5 %collective-permute-done.4 = bf16[256,512]{1,0:T(8,128)(2,1)S(1)} collective-permute-done((bf16[256,512]{1,0:T(8,128)(2,1)S(1)}, bf16[256,512]{1,0:T(8,128)(2,1)S(1)}, u32[]{:S(2)}, u32[]{:S(2)}) %collective-permute-start.4) | collective-permute-done | bytes 262176 | tf_op jit(solution)/shard_map/ppermute | solution.py:66
  18.8 4.3 %collective-permute-done.2.across = bf16[512,512]{1,0:T(8,128)(2,1)S(1)} collective-permute-done((bf16[512,512]{1,0:T(8,128)(2,1)S(1)}, bf16[512,512]{1,0:T(8,128)(2,1)S(1)}, u32[]{:S(2)}, u32[]{:S(2)}) %collective-permute-start.2) | collective-permute-done | bytes 524320 | tf_op jit(solution)/shard_map/ppermute | solution.py:54
  23.2 1.0 collective-permute-start.5
  24.2 1.8 collective-permute-start.6
  26.0 3.8 %collective-permute-start.7 = (bf16[512,512]{1,0:T(8,128)(2,1)S(1)}, bf16[512,512]{1,0:T(8,128)(2,1)S(1)}, u32[]{:S(2)}, u32[]{:S(2)}) collective-permute-start(bf16[512,512]{1,0:T(8,128)(2,1)S(1)} %pad_maximum_fusion.2), channel_id=1, source_target_pairs={{0,96},{32,64},{64,32},{96,0},{1,97},{33,65},{65,33},{97,1},{2,98}... | collective-permute-start | bytes 1572872 | tf_op jit(solution)/shard_map/ppermute | solution.py:66
  29.9 10.7 %collective-permute-done.7 = bf16[512,512]{1,0:T(8,128)(2,1)S(1)} collective-permute-done((bf16[512,512]{1,0:T(8,128)(2,1)S(1)}, bf16[512,512]{1,0:T(8,128)(2,1)S(1)}, u32[]{:S(2)}, u32[]{:S(2)}) %collective-permute-start.7) | collective-permute-done | bytes 524320 | tf_op jit(solution)/shard_map/ppermute | solution.py:66
  40.6 2.3 %collective-permute-start.10 = (bf16[1024,512]{1,0:T(8,128)(2,1)S(1)}, bf16[1024,512]{1,0:T(8,128)(2,1)S(1)}, u32[]{:S(2)}, u32[]{:S(2)}) collective-permute-start(bf16[1024,512]{1,0:T(8,128)(2,1)S(1)} %constant_dynamic-update-slice_fusion.2.rest_0_), channel_id=1, source_target_pairs={{0,16},{16,0},{1,17},{17,1},{2,18},{18,2},{3,19},{19,3},{4,20},{20... | collective-permute-start | bytes 3145736 | tf_op jit(solution)/shard_map/ppermute | solution.py:70
  43.2 1.9 collective-permute-done.10.rest_1_
  45.5 2.7 %collective-permute-start.13 = (bf16[1024,256]{1,0:T(8,128)(2,1)S(1)}, bf16[1024,256]{1,0:T(8,128)(2,1)S(1)}, u32[]{:S(2)}, u32[]{:S(2)}) collective-permute-start(bf16[1024,256]{1,0:T(8,128)(2,1)S(1)} %slice.34), channel_id=1, source_target_pairs={{0,3},{1,0},{2,1},{3,2},{4,7},{5,4},{6,5},{7,6},{8,11},{9,8},{10,9... | collective-permute-start | bytes 1572872 | tf_op jit(solution)/shard_map/ppermute | solution.py:54
  48.2 2.7 %collective-permute-start.9 = (bf16[2048,256]{1,0:T(8,128)(2,1)S(1)}, bf16[2048,256]{1,0:T(8,128)(2,1)S(1)}, u32[]{:S(2)}, u32[]{:S(2)}) collective-permute-start(bf16[2048,256]{1,0:T(8,128)(2,1)S(1)} %get-tuple-element.95.rest_0_), channel_id=1, source_target_pairs={{0,3},{1,0},{2,1},{3,2},{4,7},{5,4},{6,5},{7,6},{8,11},{9,8},{10,9... | collective-permute-start | bytes 3145736 | tf_op jit(solution)/shard_map/ppermute | solution.py:54
  50.9 4.2 %collective-permute-done.12.rest_2_ = bf16[1024,256]{1,0:T(8,128)(2,1)S(1)} collective-permute-done((bf16[1024,256]{1,0:T(8,128)(2,1)S(1)}, bf16[1024,256]{1,0:T(8,128)(2,1)S(1)}, u32[]{:S(2)}, u32[]{:S(2)}) %collective-permute-start.12) | collective-permute-done | bytes 524320 | tf_op jit(solution)/shard_map/ppermute | solution.py:54
  55.1 1.0 collective-permute-start.14
  56.8 3.6 %edge_terms.1 = (f32[2048,256]{1,0:T(8,128)S(1)}, f32[2048,256]{1,0:T(8,128)S(1)}) custom-call(s32[4]{0:T(128)S(1)} %pad_add_fusion.where, s32[1]{0:T(128)S(6)} %copy.20.live, s32[16]{0:T(128)S(1)} %copy-done.10, s32[16,128]{1,0:T(8,128)S(1)} %copy-done.8, bf16[2048,512]{1,0:T(8,128)(2,1)S(1)} %copy-done.1, bf16[512,512]{1,0:T(8,128)(2,1)S(1)} %copy-done.6, ...), custom_call_target="tpu_custom_call" | custom-call | tf_op jit(solution)/shard_map/edge_terms/pallas_call | solution.py:346
  60.4 5.9 %collective-permute-done.8.rest_1_ = bf16[2048,256]{1,0:T(8,128)(2,1)S(1)} collective-permute-done((bf16[2048,256]{1,0:T(8,128)(2,1)S(1)}, bf16[2048,256]{1,0:T(8,128)(2,1)S(1)}, u32[]{:S(2)}, u32[]{:S(2)}) %collective-permute-start.8) | collective-permute-done | bytes 1048608 | tf_op jit(solution)/shard_map/ppermute | solution.py:54
  66.6 1.1 collective-permute-start.17
  67.6 2.7 %collective-permute-start.16 = (bf16[1024,256]{1,0:T(8,128)(2,1)S(1)}, bf16[1024,256]{1,0:T(8,128)(2,1)S(1)}, u32[]{:S(2)}, u32[]{:S(2)}) collective-permute-start(bf16[1024,256]{1,0:T(8,128)(2,1)S(1)} %slice.37), channel_id=1, source_target_pairs={{0,3},{1,0},{2,1},{3,2},{4,7},{5,4},{6,5},{7,6},{8,11},{9,8},{10,9... | collective-permute-start | bytes 1572872 | tf_op jit(solution)/shard_map/ppermute | solution.py:54
  70.7 6.1 %forward_0.1 = (f32[2048,256]{1,0:T(8,128)S(1)}, f32[1024,256]{1,0:T(8,128)S(1)}, bf16[1024,256]{1,0:T(8,128)(2,1)S(1)}) custom-call(s32[4]{0:T(128)S(1)} %pad_add_fusion.where, s32[1]{0:T(128)S(6)} %copy.20.live, s32[16]{0:T(128)S(1)} %copy-done.11, s32[16]{0:T(128)S(1)} %copy-done.10, s32[16,128]{1,0:T(8,128)S(1)} %copy-done.9, s32[16,128]{1,0:T(8,128)S(1)} %copy-done.8, ...), custom_call_target="tpu_custom_call" | custom-call | tf_op jit(solution)/shard_map/forward_0/pallas_call | solution.py:346
  77.2 1.0 collective-permute-start.18
  78.2 1.5 collective-permute-done.18.rest_5_
  80.5 6.1 %forward_1.1 = (f32[2048,256]{1,0:T(8,128)S(1)}, f32[1024,256]{1,0:T(8,128)S(1)}, bf16[1024,256]{1,0:T(8,128)(2,1)S(1)}) custom-call(s32[4]{0:T(128)S(1)} %pad_add_fusion.where, s32[1]{0:T(128)S(6)} %copy.20.live, s32[16]{0:T(128)S(1)} %copy-done.11, s32[16]{0:T(128)S(1)} %copy-done.10, s32[16,128]{1,0:T(8,128)S(1)} %copy-done.9, s32[16,128]{1,0:T(8,128)S(1)} %copy-done.8, ...), custom_call_target="tpu_custom_call" | custom-call | tf_op jit(solution)/shard_map/forward_1/pallas_call | solution.py:346
  86.7 1.9 collective-permute-done.20.refs_3_
  88.8 5.5 %collective-permute-start.22 = (bf16[256,512]{1,0:T(8,128)(2,1)S(1)}, bf16[256,512]{1,0:T(8,128)(2,1)S(1)}, u32[]{:S(2)}, u32[]{:S(2)}) collective-permute-start(bf16[256,512]{1,0:T(8,128)(2,1)S(1)} %get-tuple-element.122), channel_id=1, source_target_pairs={{0,96},{32,0},{64,32},{96,64},{1,97},{33,1},{65,33},{97,65},{2,98}... | collective-permute-start | bytes 786440 | tf_op jit(solution)/shard_map/ppermute | solution.py:58
  94.3 1.1 collective-permute-start.23
  95.4 5.2 %collective-permute-done.21.a = bf16[256,512]{1,0:T(8,128)(2,1)S(1)} collective-permute-done((bf16[256,512]{1,0:T(8,128)(2,1)S(1)}, bf16[256,512]{1,0:T(8,128)(2,1)S(1)}, u32[]{:S(2)}, u32[]{:S(2)}) %collective-permute-start.21) | collective-permute-done | bytes 262176 | tf_op jit(solution)/shard_map/ppermute | solution.py:58
  100.6 4.6 %collective-permute-done.22.b = bf16[256,512]{1,0:T(8,128)(2,1)S(1)} collective-permute-done((bf16[256,512]{1,0:T(8,128)(2,1)S(1)}, bf16[256,512]{1,0:T(8,128)(2,1)S(1)}, u32[]{:S(2)}, u32[]{:S(2)}) %collective-permute-start.22) | collective-permute-done | bytes 262176 | tf_op jit(solution)/shard_map/ppermute | solution.py:58
  105.3 1.8 collective-permute-done.23.c
  107.1 0.8 node.1
  107.9 1.7 collective-permute-start.24
  110.3 2.1 %collective-permute-start.27 = (bf16[256,512]{1,0:T(8,128)(2,1)S(1)}, bf16[256,512]{1,0:T(8,128)(2,1)S(1)}, u32[]{:S(2)}, u32[]{:S(2)}) collective-permute-start(bf16[256,512]{1,0:T(8,128)(2,1)S(1)} %get-tuple-element.127.rest_2_), channel_id=1, source_target_pairs={{0,16},{16,0},{1,17},{17,1},{2,18},{18,2},{3,19},{19,3},{4,20},{20... | collective-permute-start | bytes 786440 | tf_op jit(solution)/shard_map/ppermute | solution.py:70
  112.4 2.2 %collective-permute-done.24.rest_3_ = bf16[256,512]{1,0:T(8,128)(2,1)S(1)} collective-permute-done((bf16[256,512]{1,0:T(8,128)(2,1)S(1)}, bf16[256,512]{1,0:T(8,128)(2,1)S(1)}, u32[]{:S(2)}, u32[]{:S(2)}) %collective-permute-start.24) | collective-permute-done | bytes 262176 | tf_op jit(solution)/shard_map/ppermute | solution.py:58
  114.6 7.2 %collective-permute-start.28 = (bf16[256,512]{1,0:T(8,128)(2,1)S(1)}, bf16[256,512]{1,0:T(8,128)(2,1)S(1)}, u32[]{:S(2)}, u32[]{:S(2)}) collective-permute-start(bf16[256,512]{1,0:T(8,128)(2,1)S(1)} %collective-permute-done.24.rest_3_), channel_id=1, source_target_pairs={{0,16},{16,0},{1,17},{17,1},{2,18},{18,2},{3,19},{19,3},{4,20},{20... | collective-permute-start | bytes 786440 | tf_op jit(solution)/shard_map/ppermute | solution.py:70
  121.9 3.1 %collective-permute-done.26.rest_5_ = bf16[256,512]{1,0:T(8,128)(2,1)S(1)} collective-permute-done((bf16[256,512]{1,0:T(8,128)(2,1)S(1)}, bf16[256,512]{1,0:T(8,128)(2,1)S(1)}, u32[]{:S(2)}, u32[]{:S(2)}) %collective-permute-start.26) | collective-permute-done | bytes 262176 | tf_op jit(solution)/shard_map/ppermute | solution.py:58
  125.7 1.0 collective-permute-done.30.rest_9_
  126.6 6.6 %backward.1 = (bf16[1024,256]{1,0:T(8,128)(2,1)S(1)}, bf16[1024,256]{1,0:T(8,128)(2,1)S(1)}, bf16[1024,256]{1,0:T(8,128)(2,1)S(1)}, bf16[1024,256]{1,0:T(8,128)(...) custom-call(s32[4]{0:T(128)S(1)} %pad_add_fusion.where, ...), custom_call_target="tpu_custom_call" | custom-call | tf_op jit(solution)/shard_map/backward/pallas_call | solution.py:346
  133.3 2.6 %collective-permute-done.31 = bf16[2048,256]{1,0:T(8,128)(2,1)S(1)} collective-permute-done((bf16[2048,256]{1,0:T(8,128)(2,1)S(1)}, bf16[2048,256]{1,0:T(8,128)(2,1)S(1)}, u32[]{:S(2)}, u32[]{:S(2)}) %collective-permute-start.31) | collective-permute-done | bytes 1048608 | tf_op jit(solution)/shard_map/ppermute | solution.py:70
  136.2 2.7 %collective-permute-start.34 = (bf16[1024,256]{1,0:T(8,128)(2,1)S(1)}, bf16[1024,256]{1,0:T(8,128)(2,1)S(1)}, u32[]{:S(2)}, u32[]{:S(2)}) collective-permute-start(bf16[1024,256]{1,0:T(8,128)(2,1)S(1)} %get-tuple-element.169), channel_id=1, source_target_pairs={{0,3},{1,0},{2,1},{3,2},{4,7},{5,4},{6,5},{7,6},{8,11},{9,8},{10,9... | collective-permute-start | bytes 1572872 | tf_op jit(solution)/shard_map/ppermute | solution.py:54
  138.9 2.7 %collective-permute-start.38 = (bf16[1024,256]{1,0:T(8,128)(2,1)S(1)}, bf16[1024,256]{1,0:T(8,128)(2,1)S(1)}, u32[]{:S(2)}, u32[]{:S(2)}) collective-permute-start(bf16[1024,256]{1,0:T(8,128)(2,1)S(1)} %get-tuple-element.168), channel_id=1, source_target_pairs={{0,3},{1,0},{2,1},{3,2},{4,7},{5,4},{6,5},{7,6},{8,11},{9,8},{10,9... | collective-permute-start | bytes 1572872 | tf_op jit(solution)/shard_map/ppermute | solution.py:54
  141.6 4.0 %collective-permute-done.33.into_up = bf16[1024,256]{1,0:T(8,128)(2,1)S(1)} collective-permute-done((bf16[1024,256]{1,0:T(8,128)(2,1)S(1)}, bf16[1024,256]{1,0:T(8,128)(2,1)S(1)}, u32[]{:S(2)}, u32[]{:S(2)}) %collective-permute-start.33) | collective-permute-done | bytes 524320 | tf_op jit(solution)/shard_map/ppermute | solution.py:54
  146.0 1.5 collective-permute-start.35
  147.5 1.4 collective-permute-start.36
  148.9 2.4 %collective-permute-done.37.into_up = bf16[1024,256]{1,0:T(8,128)(2,1)S(1)} collective-permute-done((bf16[1024,256]{1,0:T(8,128)(2,1)S(1)}, bf16[1024,256]{1,0:T(8,128)(2,1)S(1)}, u32[]{:S(2)}, u32[]{:S(2)}) %collective-permute-start.37) | collective-permute-done | bytes 524320 | tf_op jit(solution)/shard_map/ppermute | solution.py:54
  151.6 1.5 collective-permute-start.42
  153.1 1.4 collective-permute-start.43
  154.5 1.0 fusion
  155.5 7.0 %collective-permute-done.35.up = bf16[2048,256]{1,0:T(8,128)(2,1)S(1)} collective-permute-done((bf16[2048,256]{1,0:T(8,128)(2,1)S(1)}, bf16[2048,256]{1,0:T(8,128)(2,1)S(1)}, u32[]{:S(2)}, u32[]{:S(2)}) %collective-permute-start.35) | collective-permute-done | bytes 1048608 | tf_op jit(solution)/shard_map/ppermute | solution.py:54
  162.9 2.3 %collective-permute-start.39 = (bf16[512,256]{1,0:T(8,128)(2,1)S(1)}, bf16[512,256]{1,0:T(8,128)(2,1)S(1)}, u32[]{:S(2)}, u32[]{:S(2)}) collective-permute-start(bf16[512,256]{1,0:T(8,128)(2,1)S(1)} %get-tuple-element.146), channel_id=1, source_target_pairs={{0,4},{1,5},{2,6},{3,7},{4,8},{5,9},{6,10},{7,11},{8,12},{9,13},{1... | collective-permute-start | bytes 786440 | tf_op jit(solution)/shard_map/ppermute | solution.py:54
  165.3 3.4 %collective-permute-start.40 = (bf16[512,256]{1,0:T(8,128)(2,1)S(1)}, bf16[512,256]{1,0:T(8,128)(2,1)S(1)}, u32[]{:S(2)}, u32[]{:S(2)}) collective-permute-start(bf16[512,256]{1,0:T(8,128)(2,1)S(1)} %get-tuple-element.147), channel_id=1, source_target_pairs={{0,8},{1,9},{2,10},{3,11},{4,12},{5,13},{6,14},{7,15},{8,0},{9,1},... | collective-permute-start | bytes 786440 | tf_op jit(solution)/shard_map/ppermute | solution.py:54
  168.7 10.1 %collective-permute-done.42.up = bf16[2048,256]{1,0:T(8,128)(2,1)S(1)} collective-permute-done((bf16[2048,256]{1,0:T(8,128)(2,1)S(1)}, bf16[2048,256]{1,0:T(8,128)(2,1)S(1)}, u32[]{:S(2)}, u32[]{:S(2)}) %collective-permute-start.42) | collective-permute-done | bytes 1048608 | tf_op jit(solution)/shard_map/ppermute | solution.py:54
  179.1 1.8 collective-permute-start.45
  180.9 4.6 %collective-permute-start.46 = (bf16[512,256]{1,0:T(8,128)(2,1)S(1)}, bf16[512,256]{1,0:T(8,128)(2,1)S(1)}, u32[]{:S(2)}, u32[]{:S(2)}) collective-permute-start(bf16[512,256]{1,0:T(8,128)(2,1)S(1)} %get-tuple-element.154), channel_id=1, source_target_pairs={{0,8},{1,9},{2,10},{3,11},{4,12},{5,13},{6,14},{7,15},{8,0},{9,1},... | collective-permute-start | bytes 786440 | tf_op jit(solution)/shard_map/ppermute | solution.py:54
  185.7 2.7 %collective-permute-done.45.up = bf16[512,256]{1,0:T(8,128)(2,1)S(1)} collective-permute-done((bf16[512,256]{1,0:T(8,128)(2,1)S(1)}, bf16[512,256]{1,0:T(8,128)(2,1)S(1)}, u32[]{:S(2)}, u32[]{:S(2)}) %collective-permute-start.45) | collective-permute-done | bytes 262176 | tf_op jit(solution)/shard_map/ppermute | solution.py:54
  188.4 3.7 %collective-permute-done.46.down = bf16[512,256]{1,0:T(8,128)(2,1)S(1)} collective-permute-done((bf16[512,256]{1,0:T(8,128)(2,1)S(1)}, bf16[512,256]{1,0:T(8,128)(2,1)S(1)}, u32[]{:S(2)}, u32[]{:S(2)}) %collective-permute-start.46) | collective-permute-done | bytes 262176 | tf_op jit(solution)/shard_map/ppermute | solution.py:54
  192.2 1.6 collective-permute-start.48
  194.0 1.1 collective-permute-done.48.rest_3_
  195.4 2.3 %grid_grad.1 = f32[512,512]{1,0:T(8,128)} custom-call(s32[4]{0:T(128)S(1)} %pad_add_fusion.where, bf16[512,512]{1,0:T(8,128)(2,1)S(1)} %copy-done.3, f32[256,256]{1,0:T(8,128)S(1)} %get-tuple-element.160.rest_0_, f32[256,256]{1,0:T(8,128)S(1)} %collective-permute-done.44.rest_1_, f32[256,256]{1,0:T(8,128)S(1)} %get-tuple-element.166.rest_2_, ...), custom_call_target="tpu_custom_call" | custom-call | tf_op jit(solution)/shard_map/grid_grad/pallas_call | solution.py:346
  (98 shorter events, 7.2 us)
Async XLA Ops:
  0.6 69.7 %copy-start = (bf16[512,512]{1,0:T(8,128)(2,1)S(1)}, bf16[512,512]{1,0:T(8,128)(2,1)}, u32[]{:S(2)}) copy-start(bf16[512,512]{1,0:T(8,128)(2,1)} %param.28) | copy-start | bytes 1572868
  0.7 1.1 copy-start.2
  1.8 1.0 copy-start.4
  2.9 8.8 %copy-start.13 = (bf16[256,512]{1,0:T(8,128)(2,1)S(1)}, bf16[256,512]{1,0:T(8,128)(2,1)}, u32[]{:S(2)}) copy-start(bf16[256,512]{1,0:T(8,128)(2,1)} %param.16) | copy-start | bytes 786436
  3.8 2.7 %collective-permute-start = (bf16[256,512]{1,0:T(8,128)(2,1)S(1)}, bf16[256,512]{1,0:T(8,128)(2,1)S(1)}, u32[]{:S(2)}, u32[]{:S(2)}) collective-permute-start(bf16[256,512]{1,0:T(8,128)(2,1)S(1)} %get-tuple-element.86), channel_id=1, source_target_pairs={{0,16},{16,0},{1,17},{17,1},{2,18},{18,2},{3,19},{19,3},{4,20},{20... | collective-permute-start | bytes 786440 | tf_op jit(solution)/shard_map/ppermute | solution.py:70
  6.5 12.3 %collective-permute-start.1 = (bf16[512,512]{1,0:T(8,128)(2,1)S(1)}, bf16[512,512]{1,0:T(8,128)(2,1)S(1)}, u32[]{:S(2)}, u32[]{:S(2)}) collective-permute-start(bf16[512,512]{1,0:T(8,128)(2,1)S(1)} %constant_dynamic-update-slice_fusion), channel_id=1, source_target_pairs={{0,4},{1,5},{2,6},{3,7},{4,8},{5,9},{6,10},{7,11},{8,12},{9,13},{1... | collective-permute-start | bytes 1572872 | tf_op jit(solution)/shard_map/ppermute | solution.py:54
  8.0 15.1 %collective-permute-start.2 = (bf16[512,512]{1,0:T(8,128)(2,1)S(1)}, bf16[512,512]{1,0:T(8,128)(2,1)S(1)}, u32[]{:S(2)}, u32[]{:S(2)}) collective-permute-start(bf16[512,512]{1,0:T(8,128)(2,1)S(1)} %constant_dynamic-update-slice_fusion), channel_id=1, source_target_pairs={{0,8},{1,9},{2,10},{3,11},{4,12},{5,13},{6,14},{7,15},{8,0},{9,1},... | collective-permute-start | bytes 1572872 | tf_op jit(solution)/shard_map/ppermute | solution.py:54
  10.6 12.5 %collective-permute-start.3 = (bf16[512,512]{1,0:T(8,128)(2,1)S(1)}, bf16[512,512]{1,0:T(8,128)(2,1)S(1)}, u32[]{:S(2)}, u32[]{:S(2)}) collective-permute-start(bf16[512,512]{1,0:T(8,128)(2,1)S(1)} %constant_dynamic-update-slice_fusion), channel_id=1, source_target_pairs={{0,12},{1,13},{2,14},{3,15},{4,0},{5,1},{6,2},{7,3},{8,4},{9,5},{1... | collective-permute-start | bytes 1572872 | tf_op jit(solution)/shard_map/ppermute | solution.py:54
  11.7 7.1 %collective-permute-start.4 = (bf16[256,512]{1,0:T(8,128)(2,1)S(1)}, bf16[256,512]{1,0:T(8,128)(2,1)S(1)}, u32[]{:S(2)}, u32[]{:S(2)}) collective-permute-start(bf16[256,512]{1,0:T(8,128)(2,1)S(1)} %copy-done.13), channel_id=1, source_target_pairs={{0,32},{32,0},{64,96},{96,64},{1,33},{33,1},{65,97},{97,65},{2,34}... | collective-permute-start | bytes 786440 | tf_op jit(solution)/shard_map/ppermute | solution.py:66
  23.2 17.3 %collective-permute-start.5 = (bf16[2048,256]{1,0:T(8,128)(2,1)S(1)}, bf16[2048,256]{1,0:T(8,128)(2,1)S(1)}, u32[]{:S(2)}, u32[]{:S(2)}) collective-permute-start(bf16[2048,256]{1,0:T(8,128)(2,1)S(1)} %get-tuple-element.92.rest_0_), channel_id=1, source_target_pairs={{0,1},{1,2},{2,3},{3,0},{4,5},{5,6},{6,7},{7,4},{8,9},{9,10},{10,1... | collective-permute-start | bytes 3145736 | tf_op jit(solution)/shard_map/ppermute | solution.py:54
  24.2 16.3 %collective-permute-start.6 = (bf16[2048,256]{1,0:T(8,128)(2,1)S(1)}, bf16[2048,256]{1,0:T(8,128)(2,1)S(1)}, u32[]{:S(2)}, u32[]{:S(2)}) collective-permute-start(bf16[2048,256]{1,0:T(8,128)(2,1)S(1)} %get-tuple-element.92.rest_0_), channel_id=1, source_target_pairs={{0,3},{1,0},{2,1},{3,2},{4,7},{5,4},{6,5},{7,6},{8,11},{9,8},{10,9... | collective-permute-start | bytes 3145736 | tf_op jit(solution)/shard_map/ppermute | solution.py:54
  26.0 14.5 %collective-permute-start.7 = (bf16[512,512]{1,0:T(8,128)(2,1)S(1)}, bf16[512,512]{1,0:T(8,128)(2,1)S(1)}, u32[]{:S(2)}, u32[]{:S(2)}) collective-permute-start(bf16[512,512]{1,0:T(8,128)(2,1)S(1)} %pad_maximum_fusion.2), channel_id=1, source_target_pairs={{0,96},{32,64},{64,32},{96,0},{1,97},{33,65},{65,33},{97,1},{2,98}... | collective-permute-start | bytes 1572872 | tf_op jit(solution)/shard_map/ppermute | solution.py:66
  40.6 4.5 %collective-permute-start.10 = (bf16[1024,512]{1,0:T(8,128)(2,1)S(1)}, bf16[1024,512]{1,0:T(8,128)(2,1)S(1)}, u32[]{:S(2)}, u32[]{:S(2)}) collective-permute-start(bf16[1024,512]{1,0:T(8,128)(2,1)S(1)} %constant_dynamic-update-slice_fusion.2.rest_0_), channel_id=1, source_target_pairs={{0,16},{16,0},{1,17},{17,1},{2,18},{18,2},{3,19},{19,3},{4,20},{20... | collective-permute-start | bytes 3145736 | tf_op jit(solution)/shard_map/ppermute | solution.py:70
  43.0 13.8 %copy-start.1 = (bf16[2048,512]{1,0:T(8,128)(2,1)S(1)}, bf16[2048,512]{1,0:T(8,128)(2,1)}, u32[]{:S(2)}) copy-start(bf16[2048,512]{1,0:T(8,128)(2,1)} %edge.1) | copy-start | bytes 6291460
  43.0 13.8 %copy-start.6 = (bf16[512,512]{1,0:T(8,128)(2,1)S(1)}, bf16[512,512]{1,0:T(8,128)(2,1)}, u32[]{:S(2)}) copy-start(bf16[512,512]{1,0:T(8,128)(2,1)} %w_mesh.1) | copy-start | bytes 1572868
  43.0 13.7 %copy-start.7 = (bf16[512,512]{1,0:T(8,128)(2,1)S(1)}, bf16[512,512]{1,0:T(8,128)(2,1)}, u32[]{:S(2)}) copy-start(bf16[512,512]{1,0:T(8,128)(2,1)} %w_edge.1) | copy-start | bytes 1572868
  43.0 13.7 %copy-start.8 = (s32[16,128]{1,0:T(8,128)S(1)}, s32[16,128]{1,0:T(8,128)}, u32[]{:S(2)}) copy-start(s32[16,128]{1,0:T(8,128)} %recv.7) | copy-start | bytes 24580
  43.1 13.7 %copy-start.10 = (s32[16]{0:T(128)S(1)}, s32[16]{0:T(128)}, u32[]{:S(2)}) copy-start(s32[16]{0:T(128)} %mesh_block.7) | copy-start | bytes 196
  43.1 13.7 %copy-start.12 = (f32[512]{0:T(512)S(1)}, f32[512]{0:T(512)}, u32[]{:S(2)}) copy-start(f32[512]{0:T(512)} %param.26) | copy-start | bytes 6148
  45.1 9.9 %collective-permute-start.11 = (bf16[3072,256]{1,0:T(8,128)(2,1)S(1)}, bf16[3072,256]{1,0:T(8,128)(2,1)S(1)}, u32[]{:S(2)}, u32[]{:S(2)}) collective-permute-start(bf16[3072,256]{1,0:T(8,128)(2,1)S(1)} %pad_maximum_fusion), channel_id=1, source_target_pairs={{0,16},{16,0},{1,17},{17,1},{2,18},{18,2},{3,19},{19,3},{4,20},{20... | collective-permute-start | bytes 4718600 | tf_op jit(solution)/shard_map/ppermute | solution.py:70
  45.5 9.5 %collective-permute-start.12 = (bf16[1024,256]{1,0:T(8,128)(2,1)S(1)}, bf16[1024,256]{1,0:T(8,128)(2,1)S(1)}, u32[]{:S(2)}, u32[]{:S(2)}) collective-permute-start(bf16[1024,256]{1,0:T(8,128)(2,1)S(1)} %get-tuple-element.172), channel_id=1, source_target_pairs={{0,1},{1,2},{2,3},{3,0},{4,5},{5,6},{6,7},{7,4},{8,9},{9,10},{10,1... | collective-permute-start | bytes 1572872 | tf_op jit(solution)/shard_map/ppermute | solution.py:54
  45.5 9.5 %collective-permute-start.13 = (bf16[1024,256]{1,0:T(8,128)(2,1)S(1)}, bf16[1024,256]{1,0:T(8,128)(2,1)S(1)}, u32[]{:S(2)}, u32[]{:S(2)}) collective-permute-start(bf16[1024,256]{1,0:T(8,128)(2,1)S(1)} %slice.34), channel_id=1, source_target_pairs={{0,3},{1,0},{2,1},{3,2},{4,7},{5,4},{6,5},{7,6},{8,11},{9,8},{10,9... | collective-permute-start | bytes 1572872 | tf_op jit(solution)/shard_map/ppermute | solution.py:54
  48.2 18.1 %collective-permute-start.8 = (bf16[2048,256]{1,0:T(8,128)(2,1)S(1)}, bf16[2048,256]{1,0:T(8,128)(2,1)S(1)}, u32[]{:S(2)}, u32[]{:S(2)}) collective-permute-start(bf16[2048,256]{1,0:T(8,128)(2,1)S(1)} %get-tuple-element.95.rest_0_), channel_id=1, source_target_pairs={{0,1},{1,2},{2,3},{3,0},{4,5},{5,6},{6,7},{7,4},{8,9},{9,10},{10,1... | collective-permute-start | bytes 3145736 | tf_op jit(solution)/shard_map/ppermute | solution.py:54
  48.2 18.1 %collective-permute-start.9 = (bf16[2048,256]{1,0:T(8,128)(2,1)S(1)}, bf16[2048,256]{1,0:T(8,128)(2,1)S(1)}, u32[]{:S(2)}, u32[]{:S(2)}) collective-permute-start(bf16[2048,256]{1,0:T(8,128)(2,1)S(1)} %get-tuple-element.95.rest_0_), channel_id=1, source_target_pairs={{0,3},{1,0},{2,1},{3,2},{4,7},{5,4},{6,5},{7,6},{8,11},{9,8},{10,9... | collective-permute-start | bytes 3145736 | tf_op jit(solution)/shard_map/ppermute | solution.py:54
  55.1 11.2 %collective-permute-start.14 = (bf16[1024,256]{1,0:T(8,128)(2,1)S(1)}, bf16[1024,256]{1,0:T(8,128)(2,1)S(1)}, u32[]{:S(2)}, u32[]{:S(2)}) collective-permute-start(bf16[1024,256]{1,0:T(8,128)(2,1)S(1)} %collective-permute-done.13), channel_id=1, source_target_pairs={{0,16},{16,0},{1,17},{17,1},{2,18},{18,2},{3,19},{19,3},{4,20},{20... | collective-permute-start | bytes 1572872 | tf_op jit(solution)/shard_map/ppermute | solution.py:70
  66.4 4.0 %copy-start.14 = (bf16[256,512]{1,0:T(8,128)(2,1)S(1)}, bf16[256,512]{1,0:T(8,128)(2,1)}, u32[]{:S(2)}) copy-start(bf16[256,512]{1,0:T(8,128)(2,1)} %param.29) | copy-start | bytes 786436
  66.4 4.2 %copy-start.9 = (s32[16,128]{1,0:T(8,128)S(1)}, s32[16,128]{1,0:T(8,128)}, u32[]{:S(2)}) copy-start(s32[16,128]{1,0:T(8,128)} %send.5) | copy-start | bytes 24580
  66.4 4.2 %copy-start.11 = (s32[16]{0:T(128)S(1)}, s32[16]{0:T(128)}, u32[]{:S(2)}) copy-start(s32[16]{0:T(128)} %grid_block.5) | copy-start | bytes 196
  66.6 10.6 %collective-permute-start.17 = (bf16[3072,256]{1,0:T(8,128)(2,1)S(1)}, bf16[3072,256]{1,0:T(8,128)(2,1)S(1)}, u32[]{:S(2)}, u32[]{:S(2)}) collective-permute-start(bf16[3072,256]{1,0:T(8,128)(2,1)S(1)} %pad_maximum_fusion.1), channel_id=1, source_target_pairs={{0,16},{16,0},{1,17},{17,1},{2,18},{18,2},{3,19},{19,3},{4,20},{20... | collective-permute-start | bytes 4718600 | tf_op jit(solution)/shard_map/ppermute | solution.py:70
  67.6 9.5 %collective-permute-start.15 = (bf16[1024,256]{1,0:T(8,128)(2,1)S(1)}, bf16[1024,256]{1,0:T(8,128)(2,1)S(1)}, u32[]{:S(2)}, u32[]{:S(2)}) collective-permute-start(bf16[1024,256]{1,0:T(8,128)(2,1)S(1)} %get-tuple-element.171), channel_id=1, source_target_pairs={{0,1},{1,2},{2,3},{3,0},{4,5},{5,6},{6,7},{7,4},{8,9},{9,10},{10,1... | collective-permute-start | bytes 1572872 | tf_op jit(solution)/shard_map/ppermute | solution.py:54
  67.6 9.5 %collective-permute-start.16 = (bf16[1024,256]{1,0:T(8,128)(2,1)S(1)}, bf16[1024,256]{1,0:T(8,128)(2,1)S(1)}, u32[]{:S(2)}, u32[]{:S(2)}) collective-permute-start(bf16[1024,256]{1,0:T(8,128)(2,1)S(1)} %slice.37), channel_id=1, source_target_pairs={{0,3},{1,0},{2,1},{3,2},{4,7},{5,4},{6,5},{7,6},{8,11},{9,8},{10,9... | collective-permute-start | bytes 1572872 | tf_op jit(solution)/shard_map/ppermute | solution.py:54
  77.2 2.6 %collective-permute-start.18 = (bf16[1024,256]{1,0:T(8,128)(2,1)S(1)}, bf16[1024,256]{1,0:T(8,128)(2,1)S(1)}, u32[]{:S(2)}, u32[]{:S(2)}) collective-permute-start(bf16[1024,256]{1,0:T(8,128)(2,1)S(1)} %collective-permute-done.16), channel_id=1, source_target_pairs={{0,16},{16,0},{1,17},{17,1},{2,18},{18,2},{3,19},{19,3},{4,20},{20... | collective-permute-start | bytes 1572872 | tf_op jit(solution)/shard_map/ppermute | solution.py:70
  78.2 2.3 %collective-permute-start.19 = (bf16[1024,256]{1,0:T(8,128)(2,1)S(1)}, bf16[1024,256]{1,0:T(8,128)(2,1)S(1)}, u32[]{:S(2)}, u32[]{:S(2)}) collective-permute-start(bf16[1024,256]{1,0:T(8,128)(2,1)S(1)} %get-tuple-element.116), channel_id=1, source_target_pairs={{0,16},{16,0},{1,17},{17,1},{2,18},{18,2},{3,19},{19,3},{4,20},{20... | collective-permute-start | bytes 1572872 | tf_op jit(solution)/shard_map/ppermute | solution.py:70
  86.6 20.5 %copy-start.5 = (bf16[512,512]{1,0:T(8,128)(2,1)S(1)}, bf16[512,512]{1,0:T(8,128)(2,1)}, u32[]{:S(2)}) copy-start(bf16[512,512]{1,0:T(8,128)(2,1)} %w_out.1) | copy-start | bytes 1572868
  86.6 2.0 %collective-permute-start.20 = (bf16[1024,256]{1,0:T(8,128)(2,1)S(1)}, bf16[1024,256]{1,0:T(8,128)(2,1)S(1)}, u32[]{:S(2)}, u32[]{:S(2)}) collective-permute-start(bf16[1024,256]{1,0:T(8,128)(2,1)S(1)} %get-tuple-element.119), channel_id=1, source_target_pairs={{0,16},{16,0},{1,17},{17,1},{2,18},{18,2},{3,19},{19,3},{4,20},{20... | collective-permute-start | bytes 1572872 | tf_op jit(solution)/shard_map/ppermute | solution.py:70
  88.8 11.9 %collective-permute-start.21 = (bf16[256,512]{1,0:T(8,128)(2,1)S(1)}, bf16[256,512]{1,0:T(8,128)(2,1)S(1)}, u32[]{:S(2)}, u32[]{:S(2)}) collective-permute-start(bf16[256,512]{1,0:T(8,128)(2,1)S(1)} %get-tuple-element.121), channel_id=1, source_target_pairs={{0,32},{32,64},{64,96},{96,0},{1,33},{33,65},{65,97},{97,1},{2,34}... | collective-permute-start | bytes 786440 | tf_op jit(solution)/shard_map/ppermute | solution.py:58
  88.8 16.4 %collective-permute-start.22 = (bf16[256,512]{1,0:T(8,128)(2,1)S(1)}, bf16[256,512]{1,0:T(8,128)(2,1)S(1)}, u32[]{:S(2)}, u32[]{:S(2)}) collective-permute-start(bf16[256,512]{1,0:T(8,128)(2,1)S(1)} %get-tuple-element.122), channel_id=1, source_target_pairs={{0,96},{32,0},{64,32},{96,64},{1,97},{33,1},{65,33},{97,65},{2,98}... | collective-permute-start | bytes 786440 | tf_op jit(solution)/shard_map/ppermute | solution.py:58
  94.3 12.8 %collective-permute-start.23 = (bf16[256,512]{1,0:T(8,128)(2,1)S(1)}, bf16[256,512]{1,0:T(8,128)(2,1)S(1)}, u32[]{:S(2)}, u32[]{:S(2)}) collective-permute-start(bf16[256,512]{1,0:T(8,128)(2,1)S(1)} %get-tuple-element.123), channel_id=1, source_target_pairs={{0,64},{32,96},{64,0},{96,32},{1,65},{33,97},{65,1},{97,33},{2,66}... | collective-permute-start | bytes 786440 | tf_op jit(solution)/shard_map/ppermute | solution.py:58
  107.9 6.7 %collective-permute-start.24 = (bf16[256,512]{1,0:T(8,128)(2,1)S(1)}, bf16[256,512]{1,0:T(8,128)(2,1)S(1)}, u32[]{:S(2)}, u32[]{:S(2)}) collective-permute-start(bf16[256,512]{1,0:T(8,128)(2,1)S(1)} %get-tuple-element.127.rest_2_), channel_id=1, source_target_pairs={{0,96},{32,0},{64,32},{96,64},{1,97},{33,1},{65,33},{97,65},{2,98}... | collective-permute-start | bytes 786440 | tf_op jit(solution)/shard_map/ppermute | solution.py:58
  109.6 12.2 %collective-permute-start.25 = (bf16[256,512]{1,0:T(8,128)(2,1)S(1)}, bf16[256,512]{1,0:T(8,128)(2,1)S(1)}, u32[]{:S(2)}, u32[]{:S(2)}) collective-permute-start(bf16[256,512]{1,0:T(8,128)(2,1)S(1)} %get-tuple-element.127.rest_2_), channel_id=1, source_target_pairs={{0,64},{32,96},{64,0},{96,32},{1,65},{33,97},{65,1},{97,33},{2,66}... | collective-permute-start | bytes 786440 | tf_op jit(solution)/shard_map/ppermute | solution.py:58
  110.3 14.6 %collective-permute-start.26 = (bf16[256,512]{1,0:T(8,128)(2,1)S(1)}, bf16[256,512]{1,0:T(8,128)(2,1)S(1)}, u32[]{:S(2)}, u32[]{:S(2)}) collective-permute-start(bf16[256,512]{1,0:T(8,128)(2,1)S(1)} %get-tuple-element.127.rest_2_), channel_id=1, source_target_pairs={{0,32},{32,64},{64,96},{96,0},{1,33},{33,65},{65,97},{97,1},{2,34}... | collective-permute-start | bytes 786440 | tf_op jit(solution)/shard_map/ppermute | solution.py:58
  110.3 15.3 %collective-permute-start.27 = (bf16[256,512]{1,0:T(8,128)(2,1)S(1)}, bf16[256,512]{1,0:T(8,128)(2,1)S(1)}, u32[]{:S(2)}, u32[]{:S(2)}) collective-permute-start(bf16[256,512]{1,0:T(8,128)(2,1)S(1)} %get-tuple-element.127.rest_2_), channel_id=1, source_target_pairs={{0,16},{16,0},{1,17},{17,1},{2,18},{18,2},{3,19},{19,3},{4,20},{20... | collective-permute-start | bytes 786440 | tf_op jit(solution)/shard_map/ppermute | solution.py:70
  114.6 11.0 %collective-permute-start.28 = (bf16[256,512]{1,0:T(8,128)(2,1)S(1)}, bf16[256,512]{1,0:T(8,128)(2,1)S(1)}, u32[]{:S(2)}, u32[]{:S(2)}) collective-permute-start(bf16[256,512]{1,0:T(8,128)(2,1)S(1)} %collective-permute-done.24.rest_3_), channel_id=1, source_target_pairs={{0,16},{16,0},{1,17},{17,1},{2,18},{18,2},{3,19},{19,3},{4,20},{20... | collective-permute-start | bytes 786440 | tf_op jit(solution)/shard_map/ppermute | solution.py:70
  121.8 3.9 %collective-permute-start.29 = (bf16[256,512]{1,0:T(8,128)(2,1)S(1)}, bf16[256,512]{1,0:T(8,128)(2,1)S(1)}, u32[]{:S(2)}, u32[]{:S(2)}) collective-permute-start(bf16[256,512]{1,0:T(8,128)(2,1)S(1)} %collective-permute-done.25.rest_4_), channel_id=1, source_target_pairs={{0,16},{16,0},{1,17},{17,1},{2,18},{18,2},{3,19},{19,3},{4,20},{20... | collective-permute-start | bytes 786440 | tf_op jit(solution)/shard_map/ppermute | solution.py:70
  124.9 1.7 collective-permute-start.30
  133.2 2.7 %collective-permute-start.31 = (bf16[2048,256]{1,0:T(8,128)(2,1)S(1)}, bf16[2048,256]{1,0:T(8,128)(2,1)S(1)}, u32[]{:S(2)}, u32[]{:S(2)}) collective-permute-start(bf16[2048,256]{1,0:T(8,128)(2,1)S(1)} %get-tuple-element.130), channel_id=1, source_target_pairs={{0,16},{16,0},{1,17},{17,1},{2,18},{18,2},{3,19},{19,3},{4,20},{20... | collective-permute-start | bytes 3145736 | tf_op jit(solution)/shard_map/ppermute | solution.py:70
  136.0 9.7 %collective-permute-start.32 = (bf16[6144,256]{1,0:T(8,128)(2,1)S(1)}, bf16[6144,256]{1,0:T(8,128)(2,1)S(1)}, u32[]{:S(2)}, u32[]{:S(2)}) collective-permute-start(bf16[6144,256]{1,0:T(8,128)(2,1)S(1)} %get-tuple-element.131), channel_id=1, source_target_pairs={{0,16},{16,0},{1,17},{17,1},{2,18},{18,2},{3,19},{19,3},{4,20},{20... | collective-permute-start | bytes 9437192 | tf_op jit(solution)/shard_map/ppermute | solution.py:70
  136.1 9.5 %collective-permute-start.33 = (bf16[1024,256]{1,0:T(8,128)(2,1)S(1)}, bf16[1024,256]{1,0:T(8,128)(2,1)S(1)}, u32[]{:S(2)}, u32[]{:S(2)}) collective-permute-start(bf16[1024,256]{1,0:T(8,128)(2,1)S(1)} %get-tuple-element.134), channel_id=1, source_target_pairs={{0,1},{1,2},{2,3},{3,0},{4,5},{5,6},{6,7},{7,4},{8,9},{9,10},{10,1... | collective-permute-start | bytes 1572872 | tf_op jit(solution)/shard_map/ppermute | solution.py:54
  136.2 9.5 %collective-permute-start.34 = (bf16[1024,256]{1,0:T(8,128)(2,1)S(1)}, bf16[1024,256]{1,0:T(8,128)(2,1)S(1)}, u32[]{:S(2)}, u32[]{:S(2)}) collective-permute-start(bf16[1024,256]{1,0:T(8,128)(2,1)S(1)} %get-tuple-element.169), channel_id=1, source_target_pairs={{0,3},{1,0},{2,1},{3,2},{4,7},{5,4},{6,5},{7,6},{8,11},{9,8},{10,9... | collective-permute-start | bytes 1572872 | tf_op jit(solution)/shard_map/ppermute | solution.py:54
  138.9 12.3 %collective-permute-start.37 = (bf16[1024,256]{1,0:T(8,128)(2,1)S(1)}, bf16[1024,256]{1,0:T(8,128)(2,1)S(1)}, u32[]{:S(2)}, u32[]{:S(2)}) collective-permute-start(bf16[1024,256]{1,0:T(8,128)(2,1)S(1)} %get-tuple-element.140), channel_id=1, source_target_pairs={{0,1},{1,2},{2,3},{3,0},{4,5},{5,6},{6,7},{7,4},{8,9},{9,10},{10,1... | collective-permute-start | bytes 1572872 | tf_op jit(solution)/shard_map/ppermute | solution.py:54
  138.9 12.4 %collective-permute-start.38 = (bf16[1024,256]{1,0:T(8,128)(2,1)S(1)}, bf16[1024,256]{1,0:T(8,128)(2,1)S(1)}, u32[]{:S(2)}, u32[]{:S(2)}) collective-permute-start(bf16[1024,256]{1,0:T(8,128)(2,1)S(1)} %get-tuple-element.168), channel_id=1, source_target_pairs={{0,3},{1,0},{2,1},{3,2},{4,7},{5,4},{6,5},{7,6},{8,11},{9,8},{10,9... | collective-permute-start | bytes 1572872 | tf_op jit(solution)/shard_map/ppermute | solution.py:54
  146.0 16.5 %collective-permute-start.35 = (bf16[2048,256]{1,0:T(8,128)(2,1)S(1)}, bf16[2048,256]{1,0:T(8,128)(2,1)S(1)}, u32[]{:S(2)}, u32[]{:S(2)}) collective-permute-start(bf16[2048,256]{1,0:T(8,128)(2,1)S(1)} %get-tuple-element.135), channel_id=1, source_target_pairs={{0,1},{1,2},{2,3},{3,0},{4,5},{5,6},{6,7},{7,4},{8,9},{9,10},{10,1... | collective-permute-start | bytes 3145736 | tf_op jit(solution)/shard_map/ppermute | solution.py:54
  147.5 15.0 %collective-permute-start.36 = (bf16[2048,256]{1,0:T(8,128)(2,1)S(1)}, bf16[2048,256]{1,0:T(8,128)(2,1)S(1)}, u32[]{:S(2)}, u32[]{:S(2)}) collective-permute-start(bf16[2048,256]{1,0:T(8,128)(2,1)S(1)} %get-tuple-element.136), channel_id=1, source_target_pairs={{0,3},{1,0},{2,1},{3,2},{4,7},{5,4},{6,5},{7,6},{8,11},{9,8},{10,9... | collective-permute-start | bytes 3145736 | tf_op jit(solution)/shard_map/ppermute | solution.py:54
  151.6 27.2 %collective-permute-start.42 = (bf16[2048,256]{1,0:T(8,128)(2,1)S(1)}, bf16[2048,256]{1,0:T(8,128)(2,1)S(1)}, u32[]{:S(2)}, u32[]{:S(2)}) collective-permute-start(bf16[2048,256]{1,0:T(8,128)(2,1)S(1)} %get-tuple-element.141), channel_id=1, source_target_pairs={{0,1},{1,2},{2,3},{3,0},{4,5},{5,6},{6,7},{7,4},{8,9},{9,10},{10,1... | collective-permute-start | bytes 3145736 | tf_op jit(solution)/shard_map/ppermute | solution.py:54
  153.1 25.6 %collective-permute-start.43 = (bf16[2048,256]{1,0:T(8,128)(2,1)S(1)}, bf16[2048,256]{1,0:T(8,128)(2,1)S(1)}, u32[]{:S(2)}, u32[]{:S(2)}) collective-permute-start(bf16[2048,256]{1,0:T(8,128)(2,1)S(1)} %get-tuple-element.142), channel_id=1, source_target_pairs={{0,3},{1,0},{2,1},{3,2},{4,7},{5,4},{6,5},{7,6},{8,11},{9,8},{10,9... | collective-permute-start | bytes 3145736 | tf_op jit(solution)/shard_map/ppermute | solution.py:54
  162.9 22.6 %collective-permute-start.39 = (bf16[512,256]{1,0:T(8,128)(2,1)S(1)}, bf16[512,256]{1,0:T(8,128)(2,1)S(1)}, u32[]{:S(2)}, u32[]{:S(2)}) collective-permute-start(bf16[512,256]{1,0:T(8,128)(2,1)S(1)} %get-tuple-element.146), channel_id=1, source_target_pairs={{0,4},{1,5},{2,6},{3,7},{4,8},{5,9},{6,10},{7,11},{8,12},{9,13},{1... | collective-permute-start | bytes 786440 | tf_op jit(solution)/shard_map/ppermute | solution.py:54
  165.3 20.3 %collective-permute-start.40 = (bf16[512,256]{1,0:T(8,128)(2,1)S(1)}, bf16[512,256]{1,0:T(8,128)(2,1)S(1)}, u32[]{:S(2)}, u32[]{:S(2)}) collective-permute-start(bf16[512,256]{1,0:T(8,128)(2,1)S(1)} %get-tuple-element.147), channel_id=1, source_target_pairs={{0,8},{1,9},{2,10},{3,11},{4,12},{5,13},{6,14},{7,15},{8,0},{9,1},... | collective-permute-start | bytes 786440 | tf_op jit(solution)/shard_map/ppermute | solution.py:54
  168.7 16.9 %collective-permute-start.41 = (bf16[512,256]{1,0:T(8,128)(2,1)S(1)}, bf16[512,256]{1,0:T(8,128)(2,1)S(1)}, u32[]{:S(2)}, u32[]{:S(2)}) collective-permute-start(bf16[512,256]{1,0:T(8,128)(2,1)S(1)} %get-tuple-element.148), channel_id=1, source_target_pairs={{0,12},{1,13},{2,14},{3,15},{4,0},{5,1},{6,2},{7,3},{8,4},{9,5},{1... | collective-permute-start | bytes 786440 | tf_op jit(solution)/shard_map/ppermute | solution.py:54
  179.1 16.3 %copy-start.3 = (bf16[512,512]{1,0:T(8,128)(2,1)S(1)}, bf16[512,512]{1,0:T(8,128)(2,1)}, u32[]{:S(2)}) copy-start(bf16[512,512]{1,0:T(8,128)(2,1)} %w_grid.3) | copy-start | bytes 1572868
  179.1 9.3 %collective-permute-start.45 = (bf16[512,256]{1,0:T(8,128)(2,1)S(1)}, bf16[512,256]{1,0:T(8,128)(2,1)S(1)}, u32[]{:S(2)}, u32[]{:S(2)}) collective-permute-start(bf16[512,256]{1,0:T(8,128)(2,1)S(1)} %get-tuple-element.153), channel_id=1, source_target_pairs={{0,4},{1,5},{2,6},{3,7},{4,8},{5,9},{6,10},{7,11},{8,12},{9,13},{1... | collective-permute-start | bytes 786440 | tf_op jit(solution)/shard_map/ppermute | solution.py:54
  180.9 11.2 %collective-permute-start.46 = (bf16[512,256]{1,0:T(8,128)(2,1)S(1)}, bf16[512,256]{1,0:T(8,128)(2,1)S(1)}, u32[]{:S(2)}, u32[]{:S(2)}) collective-permute-start(bf16[512,256]{1,0:T(8,128)(2,1)S(1)} %get-tuple-element.154), channel_id=1, source_target_pairs={{0,8},{1,9},{2,10},{3,11},{4,12},{5,13},{6,14},{7,15},{8,0},{9,1},... | collective-permute-start | bytes 786440 | tf_op jit(solution)/shard_map/ppermute | solution.py:54
  185.6 6.6 %collective-permute-start.47 = (bf16[512,256]{1,0:T(8,128)(2,1)S(1)}, bf16[512,256]{1,0:T(8,128)(2,1)S(1)}, u32[]{:S(2)}, u32[]{:S(2)}) collective-permute-start(bf16[512,256]{1,0:T(8,128)(2,1)S(1)} %get-tuple-element.155), channel_id=1, source_target_pairs={{0,12},{1,13},{2,14},{3,15},{4,0},{5,1},{6,2},{7,3},{8,4},{9,5},{1... | collective-permute-start | bytes 786440 | tf_op jit(solution)/shard_map/ppermute | solution.py:54
  192.2 2.8 %collective-permute-start.48 = (f32[256,256]{1,0:T(8,128)S(1)}, f32[256,256]{1,0:T(8,128)S(1)}, u32[]{:S(2)}, u32[]{:S(2)}) collective-permute-start(f32[256,256]{1,0:T(8,128)S(1)} %get-tuple-element.167), channel_id=1, source_target_pairs={{0,16},{16,0},{1,17},{17,1},{2,18},{18,2},{3,19},{19,3},{4,20},{20... | collective-permute-start | bytes 786440 | tf_op jit(solution)/shard_map/ppermute | solution.py:70
  193.9 1.5 collective-permute-start.44

commit v3 on v2

v3 whole, which is shorter than its diff:
```python
import functools

import jax
import jax.numpy as jnp
from jax import lax
from jax.experimental import pallas as pl
from jax.experimental.pallas import tpu as pltpu
from jax.sharding import Mesh
from jax.sharding import PartitionSpec as P

F32 = jnp.float32
BF16 = jnp.bfloat16
RING = 4
BLOCK = 128
SLOTS = 16
GROUP = 4
WIDTH = 512
CHUNKS = 2
COLS = WIDTH // CHUNKS
HALF = 256
GATHERED = RING * HALF
VMEM = pl.BlockSpec(memory_space=pltpu.VMEM)
SMEM = pl.BlockSpec(memory_space=pltpu.SMEM)
ANY = pl.BlockSpec(memory_space=pl.ANY)
LIGHT = pl.CostEstimate(flops=0, bytes_accessed=0, transcendentals=0)
LIMIT = 20 * 1024 * 1024


def shape(rows, cols, dtype):
    return jax.ShapeDtypeStruct((rows, cols), dtype)


def params():
    return pltpu.CompilerParams(vmem_limit_bytes=LIMIT)


CHIP_AXES = ("core", "x", "y")


def along(first, step):
    pairs = []
    for core in range(2):
        for x in range(RING):
            for y in range(RING):
                if (core == 0) == first:
                    to = ((x + step) % RING, y)
                else:
                    to = (x, (y + step) % RING)
                pairs.append((core * 16 + x * RING + y, core * 16 + to[0] * RING + to[1]))
    return pairs


def shift(value, first, step):
    return lax.ppermute(value, CHIP_AXES, along(first, step))


def shift_z(value, step):
    return lax.ppermute(value, "z", [(i, (i + step) % RING) for i in range(RING)])


def after(value, *others):
    return lax.optimization_barrier((value, others))[0]


def pair_z(value, flip):
    return lax.ppermute(value, "z", [(i, i ^ flip) for i in range(RING)])


def swap(value):
    return lax.ppermute(value, "core", [(0, 1), (1, 0)])


def dot(a, b):
    return jnp.dot(a, b, preferred_element_type=F32)


def dot_t(a, b):
    return lax.dot_general(a, b, (((1,), (1,)), ((), ())), preferred_element_type=F32)


def split_dot(a, b, product):
    high = a.astype(BF16)
    low = (a - high.astype(F32)).astype(BF16)
    return product(high, b) + product(low, b)


def sigmoid(value):
    return 1.0 / (1.0 + jnp.exp(-value))


def one_hot(offsets, slot):
    rows = lax.broadcasted_iota(jnp.int32, (BLOCK, BLOCK), 0)
    return (rows == offsets[pl.ds(slot, 1), :]).astype(BF16)


def grid_place(block, where):
    core, x, y = where[1], where[2], where[3]
    owner = block // 4
    kind = (block % 4) // 2
    dx = lax.rem(x - owner // 4 + RING, RING)
    dy = lax.rem(y - owner % 4 + RING, RING)
    mine = kind == core
    near = jnp.where(kind == 0, dx, dy)
    far = jnp.where(kind == 0, dy, dx)
    return mine, near, far, (block % 2) * BLOCK


def mesh_place(block, where):
    owner = block // 2
    dz = lax.rem(owner // 2 - where[0] + RING, RING)
    return owner % 2 == where[1], dz, (block % 2) * BLOCK


def first_product_kernel(where, grid, w_grid, keep, give):
    core = where[1]
    for out, half in ((give, 1 - core), (keep, core)):
        out[...] = dot(grid[pl.ds(pl.multiple_of(half * HALF, HALF), HALF), :], w_grid[...]).astype(BF16)


def ring_kernel(keep, got, up, across, down, *outs):
    for chunk, out in enumerate(outs):
        cols = pl.ds(chunk * COLS, COLS)
        out[:HALF, :] = keep[:, cols]
        out[GATHERED : GATHERED + HALF, :] = got[:, cols]
        for step, term in enumerate((up, across, down)):
            out[pl.ds((step + 1) * HALF, HALF), :] = term[:HALF, cols]
            out[pl.ds(GATHERED + (step + 1) * HALF, HALF), :] = term[HALF:, cols]


def edge_kernel(where, live, mesh_block, pick, edge, w_mesh, w_edge, bias, *rest):
    pieces, outs, (blocks, rows) = rest[:2], rest[2 : 2 + CHUNKS], rest[-2:]

    @pl.loop(0, live[0])
    def _(group):
        for i in range(GROUP):
            block = mesh_block[group * GROUP + i]
            owner = block // 2
            flip = (owner // 2) ^ where[0]
            mine = owner % 2 == where[1]
            row = flip * HALF + (block % 2) * BLOCK

            @pl.when(mine)
            def _():
                blocks[i] = pieces[0][pl.ds(pl.multiple_of(row, BLOCK), BLOCK), :]

            @pl.when(jnp.logical_not(mine))
            def _():
                for chunk in range(CHUNKS):
                    lines = pl.ds(pl.multiple_of((3 + chunk) * GATHERED + row, BLOCK), BLOCK)
                    blocks[i, :, pl.ds(chunk * COLS, COLS)] = pieces[1][lines, :]

        first = group * GROUP * BLOCK
        for i in range(GROUP):
            at = pl.ds(pl.multiple_of(first + i * BLOCK, BLOCK), BLOCK)
            rows[pl.ds(i * BLOCK, BLOCK), :] = dot(pick[at, :], blocks[i]).astype(BF16)
        lines = pl.ds(pl.multiple_of(first, GROUP * BLOCK), GROUP * BLOCK)
        for chunk in range(CHUNKS):
            cols = pl.ds(chunk * COLS, COLS)
            outs[chunk][lines, :] = dot(rows[...], w_mesh[:, cols]) + dot(edge[lines, :], w_edge[:, cols]) + bias[:, cols]


def forward_kernel(where, live, grid_block, mesh_block, pick, recv, rest_in, *rest):
    pieces, (slope, near, far) = rest[:6], rest[6:9]
    total, blocks, sems = rest[9:]

    @pl.loop(0, live[0] * GROUP)
    def _(slot):
        mine, first, second, row = grid_place(grid_block[slot], where)
        start = first * HALF + row

        def fetch(piece, base):
            lines = pl.ds(pl.multiple_of(base + start, BLOCK), BLOCK)
            pltpu.make_async_copy(pieces[piece].at[lines, :], blocks.at[slot], sems.at[slot]).start()

        for piece in range(RING):

            @pl.when(jnp.logical_and(mine, second == piece))
            def _():
                fetch(piece, 0)

        @pl.when(jnp.logical_and(jnp.logical_not(mine), second != 2))
        def _():
            fetch(RING, jnp.minimum(second, 2) * GATHERED)

        @pl.when(jnp.logical_and(jnp.logical_not(mine), second == 2))
        def _():
            fetch(RING + 1, 0)

    total[...] = jnp.zeros_like(total)

    @pl.loop(0, live[0])
    def _(group):
        slots = [group * GROUP + i for i in range(GROUP)]
        for slot in slots:
            pltpu.make_async_copy(pieces[0].at[pl.ds(0, BLOCK), :], blocks.at[slot], sems.at[slot]).wait()
        lines = [pl.ds(pl.multiple_of(slot * BLOCK, BLOCK), BLOCK) for slot in slots]
        pres = [rest_in[at, :] + dot(pick[at, :], blocks[slot]) for at, slot in zip(lines, slots)]
        sigs = [sigmoid(pre) for pre in pres]
        for at, pre, sig in zip(lines, pres, sigs):
            slope[at, :] = sig * (1.0 + pre * (1.0 - sig))
        sums = [dot(one_hot(recv, slot), (pre * sig).astype(BF16)) for slot, pre, sig in zip(slots, pres, sigs)]
        for slot, value in zip(slots, sums):
            mine, dz, row = mesh_place(mesh_block[slot], where)
            start = jnp.where(mine, 0, RING * HALF) + dz * HALF + row
            total[pl.ds(pl.multiple_of(start, BLOCK), BLOCK), :] += value

    near[...] = total[: RING * HALF, :]
    far[...] = total[RING * HALF :, :].astype(BF16)


def pair_sum_kernel(*refs):
    near, other, outs = refs[:CHUNKS], refs[CHUNKS : 2 * CHUNKS], refs[2 * CHUNKS :]
    for chunk in range(CHUNKS):
        for step in range(RING):
            lines = pl.ds(step * HALF, HALF)
            value = near[chunk][lines, :] + other[chunk][lines, :].astype(F32)
            outs[step][:, pl.ds(chunk * COLS, COLS)] = value.astype(outs[step].dtype)


def node_kernel(cot, w_out, own, a, b, c, aggregate, grads):
    part = own[...] + (a[...].astype(F32) + b[...].astype(F32) + c[...].astype(F32))
    total = split_dot(part, w_out[...], dot)
    aggregate[...] = total
    sig = sigmoid(total)
    grad = (cot[...] * (sig * (1.0 + total * (1.0 - sig)))).astype(BF16)
    grads[...] = dot_t(grad, w_out[...]).astype(BF16)


def backward_kernel(where, live, grid_block, mesh_block, first_of, pick, send, *rest):
    slopes, pieces, outs = rest[:CHUNKS], rest[CHUNKS : CHUNKS + 8], rest[CHUNKS + 8 : -2]
    total, blocks = rest[-2:]
    for out in outs:
        out[...] = jnp.zeros_like(out)

    @pl.loop(0, live[0])
    def _(group):
        slots = [group * GROUP + i for i in range(GROUP)]
        for i, slot in enumerate(slots):
            mine, dz, row = mesh_place(mesh_block[slot], where)
            at = jnp.where(mine, dz, dz + RING)
            for piece in range(8):

                @pl.when(at == piece)
                def _():
                    blocks[i] = pieces[piece][pl.ds(pl.multiple_of(row, BLOCK), BLOCK), :]

        lines = [pl.ds(pl.multiple_of(slot * BLOCK, BLOCK), BLOCK) for slot in slots]
        hot = [one_hot(send, slot) for slot in slots]
        for c in range(CHUNKS):
            cols = pl.ds(c * COLS, COLS)
            grads = [dot(pick[at, :], blocks[i, :, cols]) * slopes[c][at, :] for i, at in enumerate(lines)]
            parts = [dot(hot[i], grad.astype(BF16)) for i, grad in enumerate(grads)]
            for slot, part in zip(slots, parts):
                first = first_of[slot]
                total[first, :, cols] = jnp.where(first == slot, 0.0, total[first, :, cols]) + part

    @pl.loop(0, live[0] * GROUP)
    def _(slot):
        mine, near, far, row = grid_place(grid_block[slot], where)
        start = lax.rem(RING - near, RING) * HALF + row
        far = lax.rem(RING - far, RING)
        at = jnp.where(first_of[slot] == slot, jnp.where(mine, far, jnp.where(far == 2, RING, RING + 1)), -1)
        for step in range(RING + 2):

            @pl.when(at == step)
            def _():
                for c in range(CHUNKS):
                    if step < RING:
                        to, place = outs[RING * c + step], start
                    elif step == RING:
                        to, place = outs[-2], start + c * GATHERED
                    else:
                        to, place = outs[-1], start + (3 * c + jnp.minimum(far, 2)) * GATHERED
                    to[pl.ds(pl.multiple_of(place, BLOCK), BLOCK), :] = total[slot, :, pl.ds(c * COLS, COLS)].astype(BF16)


def add(a, b):
    return (a[...].astype(F32) + b[...].astype(F32)).astype(BF16)


def merge_kernel(terms, *refs):
    into_up, into_down, out_up, out_down = refs[-4:]
    up_0, up_1, down_0, down_1 = [refs[i].at[pl.ds(base, GATHERED), :] for i, base in terms]
    out_up[:GATHERED, :] = add(up_0, into_up)
    out_up[GATHERED:, :] = up_1[...]
    out_down[:GATHERED, :] = down_0[...]
    out_down[GATHERED:, :] = add(down_1, into_down)


def column_sum_kernel(terms, *refs):
    up, down, here, *outs = refs[-6:]
    for chunk, (i, base) in enumerate(terms):
        cols = pl.ds(chunk * COLS, COLS)
        for step in range(RING):
            both = pl.ds(chunk * GATHERED + step * HALF, HALF)
            value = refs[i][pl.ds(base + step * HALF, HALF), :].astype(F32) + (up[both, :].astype(F32) + down[both, :].astype(F32))
            if step == 0:
                here[:, cols] = value
            else:
                outs[step - 1][:, cols] = value.astype(BF16)


def row_sum_kernel(w_grid, here, up, down, across, out):
    value = here[...] + (up[...].astype(F32) + down[...].astype(F32) + across[...].astype(F32))
    out[...] = split_dot(value, w_grid[...], dot_t)


def place_kernel(other, where, value, *rest):
    out, sem = rest[-2:]
    place = 1 - where[1] if other else where[1]
    copy = pltpu.make_async_copy(value, out.at[pl.ds(pl.multiple_of(place * HALF, HALF), HALF), :], sem)
    copy.start()
    copy.wait()


def per_device(
    grid,
    mesh_latent,
    edge_latent,
    edge_grid_block,
    edge_mesh_block,
    sender_offset,
    receiver_offset,
    live_groups,
    w_grid,
    w_mesh,
    w_edge,
    bias,
    w_out,
    w_node,
    cotangent,
):
    def picks(offsets):
        return (offsets.reshape(-1, 1) == jnp.arange(BLOCK, dtype=jnp.int32)).astype(BF16)

    pick_send, pick_recv = picks(sender_offset), picks(receiver_offset)
    where = jnp.stack([lax.axis_index(a) for a in ("z", "core", "x", "y")]).astype(jnp.int32)
    edges = SLOTS * BLOCK
    both_chunks = range(CHUNKS)

    def call(kernel, name, outs, *args, scalars=0, scratch=(), spec=VMEM):
        whole = [SMEM] * scalars + [VMEM] * (len(args) - scalars)
        if spec is ANY:
            whole[-6:] = [ANY] * 6
        return pl.pallas_call(
            kernel,
            in_specs=whole,
            out_specs=[VMEM] * len(outs),
            out_shape=outs,
            scratch_shapes=scratch,
            compiler_params=params(),
            cost_estimate=LIGHT,
            name=name,
        )(*args)

    keep, give = call(
        first_product_kernel, "first_product", [shape(HALF, WIDTH, BF16)] * 2, where, grid, w_grid, scalars=1
    )
    got = swap(give)
    mine = jnp.concatenate([keep, got], axis=0)
    mesh_first = after(mesh_latent, mine)
    mesh_pair = pair_z(mesh_first, 1), pair_z(mesh_first, 3)

    def far_gather(value):
        return shift(value, False, 1), shift(value, False, -1)

    def give_rows(both, up, down):
        return jnp.concatenate([both[GATHERED:], up[GATHERED:], down[GATHERED:]], axis=0)

    near = shift(mine, True, 1), shift(mine, True, 2), shift(mine, True, -1)
    ring_0, ring_1 = call(
        ring_kernel, "ring", [shape(2 * GATHERED, COLS, BF16)] * CHUNKS, keep, got, *after(near, mesh_pair)
    )

    mesh_far = pair_z(after(mesh_pair[1], ring_0), 1)
    (up_0, down_0), mesh_far = lax.optimization_barrier((far_gather(ring_0), mesh_far))
    mesh_rows = jnp.concatenate([mesh_latent, mesh_pair[0], mesh_far, mesh_pair[1]], axis=0)
    give = [give_rows(ring_0, up_0, down_0)] + [mesh_rows[:, c * COLS : (c + 1) * COLS] for c in both_chunks]
    got_0 = swap(jnp.concatenate(give, axis=0))
    across_0 = shift(up_0[:GATHERED], False, 1), shift(down_0[GATHERED:], False, -1)
    far_1 = far_gather(after(ring_1, up_0))
    edge_terms = call(
        edge_kernel,
        "edge_terms",
        [shape(edges, COLS, F32)] * CHUNKS,
        where,
        live_groups,
        edge_mesh_block,
        pick_recv,
        edge_latent,
        w_mesh,
        w_edge,
        bias.reshape(1, WIDTH),
        mesh_rows,
        got_0,
        scalars=3,
        scratch=[pltpu.VMEM((GROUP, BLOCK, WIDTH), BF16), pltpu.VMEM((GROUP * BLOCK, WIDTH), BF16)],
    )
    cot = dot_t(cotangent, w_node)

    own_across, other_across = lax.optimization_barrier(across_0)
    far_got_0 = swap(other_across)
    (up_1, down_1), edge_terms, got_0, far_got_0 = lax.optimization_barrier((far_1, edge_terms, got_0, far_got_0))
    across_1 = shift(up_1[:GATHERED], False, 1), shift(down_1[GATHERED:], False, -1)

    def forward(chunk, own, got):
        return call(
            forward_kernel,
            f"forward_{chunk}",
            [shape(edges, COLS, F32), shape(RING * HALF, COLS, F32), shape(RING * HALF, COLS, BF16)],
            where,
            live_groups,
            edge_grid_block,
            edge_mesh_block,
            pick_send,
            receiver_offset,
            edge_terms[chunk],
            *own,
            *got,
            scalars=4,
            scratch=[
                pltpu.VMEM((2 * RING * HALF, COLS), F32),
                pltpu.VMEM((SLOTS, BLOCK, COLS), BF16),
                pltpu.SemaphoreType.DMA((SLOTS,)),
            ],
            spec=ANY,
        )

    def pair_sum(*terms):
        outs = [shape(HALF, WIDTH, F32)] + [shape(HALF, WIDTH, BF16)] * 3
        return call(pair_sum_kernel, "pair_sum", outs, *terms)

    def band_sum(own, a, b, c):
        return [own, shift_z(a, 1), shift_z(c, -1), shift_z(b, 2)]

    slope_0, near_sum_0, far_sum_0 = forward(0, (ring_0, up_0, own_across, down_0), (got_0, far_got_0))
    got_1 = swap(give_rows(ring_1, up_1, down_1))
    (own_across, other_across), got_1, far_sum_0, cot = lax.optimization_barrier((across_1, got_1, far_sum_0, cot))
    far_got_1, far_sum_0 = swap(other_across), swap(far_sum_0)
    slope_1, near_sum_1, far_sum_1 = forward(
        1, (ring_1, up_1, own_across, down_1), (got_1, after(far_got_1, far_sum_0))
    )
    sums = band_sum(*pair_sum(near_sum_0, near_sum_1, far_sum_0, swap(far_sum_1)))
    slopes = [slope_0, slope_1]

    aggregate, grads = call(
        node_kernel, "node", [shape(HALF, WIDTH, F32), shape(HALF, WIDTH, BF16)], cot, w_out, *sums
    )

    slots = jnp.arange(SLOTS)
    same = edge_grid_block[:, None] == edge_grid_block[None, :]
    first_of = jnp.min(jnp.where(same, slots[None, :], SLOTS), axis=1).astype(jnp.int32)

    band = [grads, shift_z(grads, -1), shift_z(grads, 2), shift_z(grads, 1)]
    partial = call(
        backward_kernel,
        "backward",
        [shape(GATHERED, COLS, BF16)] * (RING * CHUNKS)
        + [shape(CHUNKS * GATHERED, COLS, BF16), shape(3 * CHUNKS * GATHERED, COLS, BF16)],
        where,
        live_groups,
        edge_grid_block,
        edge_mesh_block,
        first_of,
        pick_recv,
        sender_offset,
        *slopes,
        *band,
        *[swap(p) for p in band],
        scalars=5,
        scratch=[pltpu.VMEM((SLOTS, BLOCK, WIDTH), F32), pltpu.VMEM((GROUP, BLOCK, WIDTH), BF16)],
    )
    own_0, own_1, give_across, give_rest = partial[:RING], partial[RING : 2 * RING], partial[-2], partial[-1]

    def far_send(into, name, terms, *refs):
        kernel = functools.partial(merge_kernel, terms)
        up, down = call(kernel, name, [shape(2 * GATHERED, COLS, BF16)] * 2, *refs, *into)
        return (shift(up, False, 1), shift(down, False, -1)), up

    def column_sum(far, name, terms, *refs):
        kernel = functools.partial(column_sum_kernel, terms)
        outs = [shape(HALF, WIDTH, F32)] + [shape(HALF, WIDTH, BF16)] * 3
        return call(kernel, name, outs, *refs, *far)

    def near_send(here, a, b, c):
        return here, shift(a, True, 1), shift(b, True, 2), shift(c, True, -1)

    def row_sum(name, terms):
        return call(row_sum_kernel, name, [shape(HALF, WIDTH, F32)], w_grid, *terms)[0]

    into_mine = shift(own_0[2], False, 1), shift(own_1[2], False, -1)
    across = swap(give_across)
    rest = swap(after(give_rest, across))
    into_other = shift(across[:GATHERED], False, 1), shift(across[GATHERED:], False, -1)
    far_mine, merged = far_send(
        into_mine, "merge_mine", ((0, 0), (1, 0), (2, 0), (3, 0)), own_0[1], own_1[1], own_0[3], own_1[3]
    )
    step = GATHERED
    far_other, merged = far_send(
        into_other, "merge_other", ((0, step), (0, 4 * step), (0, 2 * step), (0, 5 * step)), after(rest, merged)
    )
    activation = jax.nn.silu(aggregate).astype(BF16)
    mesh_out = (mesh_latent.astype(F32) + dot(activation, w_node)).astype(BF16)
    columns = column_sum(after(far_mine, (mesh_out, merged)), "column_sum_mine", ((0, 0), (1, 0)), own_0[0], own_1[0])
    near_mine = near_send(*columns)
    columns = column_sum(after(far_other, columns), "column_sum_other", ((0, 0), (0, 3 * step)), rest)
    near_other = near_send(*columns)
    mine = row_sum("row_sum_mine", after(near_mine, columns))

    def place(name, other, value, *into):
        return pl.pallas_call(
            functools.partial(place_kernel, other),
            in_specs=[SMEM, VMEM] + [ANY] * len(into),
            out_specs=ANY,
            out_shape=shape(2 * HALF, WIDTH, F32),
            input_output_aliases={2: 0} if into else {},
            scratch_shapes=[pltpu.SemaphoreType.DMA],
            compiler_params=params(),
            cost_estimate=LIGHT,
            name=name,
        )(where, value, *into)

    half_done = place("place_mine", False, mine)
    other = row_sum("row_sum_other", after(near_other, half_done))
    grid_grad = place("place_other", True, swap(other), half_done)
    return (mesh_out, grid_grad)


def solution(mesh):
    split = Mesh(mesh.devices.reshape(4, 2, 4, 4), ("z", "core", "x", "y"))
    rows = P(("z", "core", "x", "y"))
    placed = (rows,) * 8 + (P(),) * 6 + (rows,)
    return jax.shard_map(per_device, mesh=split, in_specs=placed, out_specs=(rows, rows), check_vma=False)
```

time: 197 us -> 193 us (0.980)
  starting transfers between devices: 73.1 us -> 65.3 us
    ppermute x25, waiting for transfers between devices: 44.7 us -> 53.2 us  [shift(): return lax.ppermute(value, CHIP_AXES, along(first, step))]
    ppermute x25, starting transfers between devices: 39.4 us -> 31.1 us  [shift(): return lax.ppermute(value, CHIP_AXES, along(first, step))]
    ppermute x2 -> x3, waiting for transfers between devices: 16.1 us -> 11.3 us  [pair_z(): return lax.ppermute(value, 'z', [(i, i ^ flip) for i in range(RING)])]
    pallas_call x0 -> x2, Pallas kernels: none -> 2.69 us  [place(): pl.pallas_call(functools.partial(place_kernel, other), in_specs=[SMEM, VM...]
    pallas_call x15 -> x14, Pallas kernels: 28.2 us -> 26 us  [call(): pl.pallas_call(kernel, in_specs=whole, out_specs=[VMEM] * len(outs), out_...]
    ppermute x16 -> x14, waiting for transfers between devices: 12.3 us -> 10.4 us  [swap(): return lax.ppermute(value, 'core', [(0, 1), (1, 0)])]
    ppermute x16 -> x14, starting transfers between devices: 19.2 us -> 20.9 us  [swap(): return lax.ppermute(value, 'core', [(0, 1), (1, 0)])]
    ppermute x2 -> x3, starting transfers between devices: 5.47 us -> 5.48 us  [pair_z(): return lax.ppermute(value, 'z', [(i, i ^ flip) for i in range(RING)])]
  transfers between devices with their start and end apart: 49 -> 48, of which waited for: 26 -> 32; matrix products, arithmetic and copies ran while one was open for 1% -> 1% of each run, Pallas kernels for 6% -> 7%
where the time goes in v3:
time: 193 us; the launch traced here: 192 us
  waiting for transfers between devices  91 us (47%)
  starting transfers between devices  65.3 us (34%)
  Pallas kernels  28.7 us (15%)
  local copies, waits for them, and re-layouts  2.78 us (1%)
  between operations  1.93 us (1%)
    ppermute x25, waiting for transfers between devices, shift(): return lax.ppermute(value, CHIP_AXES, along(first, step))  53.2 us
    ppermute x25, starting transfers between devices, shift(): return lax.ppermute(value, CHIP_AXES, along(first, step))  31.1 us
    pallas_call x14, Pallas kernels, call(): pl.pallas_call(kernel, in_specs=whole, out_specs=[VMEM] * len(outs), out_...  26 us
    ppermute x14, starting transfers between devices, swap(): return lax.ppermute(value, 'core', [(0, 1), (1, 0)])  20.9 us
    ppermute x6, waiting for transfers between devices, shift_z(): lax.ppermute(value, 'z', [(i, (i + step) % RING) for i in range(RING)])  16.2 us
    ppermute x3, waiting for transfers between devices, pair_z(): return lax.ppermute(value, 'z', [(i, i ^ flip) for i in range(RING)])  11.3 us
    ppermute x14, waiting for transfers between devices, swap(): return lax.ppermute(value, 'core', [(0, 1), (1, 0)])  10.4 us
    ppermute x6, starting transfers between devices, shift_z(): lax.ppermute(value, 'z', [(i, (i + step) % RING) for i in range(RING)])  7.88 us
  transfers between devices with their start and end apart: 48, of which 32 were waited for; matrix products, arithmetic and copies ran while one was open for 1% of the time, Pallas kernels for 7%

profile of v3, /device:TPU:1, one launch (start us, length us, event | category | flops | bytes accessed | tf_op | source)
XLA Modules:
  0.0 192.1 jit_solution(6654286757579623933)
XLA Ops:
  0.7 1.1 copy-done.1
  1.8 1.0 copy-done.6
  2.9 1.0 first_product.1
  3.8 1.5 collective-permute-start
  5.4 1.1 collective-permute-done.got
  6.5 1.4 collective-permute-start.1
  8.0 2.6 %collective-permute-start.2 = (bf16[512,512]{1,0:T(8,128)(2,1)S(1)}, bf16[512,512]{1,0:T(8,128)(2,1)S(1)}, u32[]{:S(2)}, u32[]{:S(2)}) collective-permute-start(bf16[512,512]{1,0:T(8,128)(2,1)S(1)} %constant_dynamic-update-slice_fusion), channel_id=1, source_target_pairs={{0,8},{1,9},{2,10},{3,11},{4,12},{5,13},{6,14},{7,15},{8,0},{9,1},... | collective-permute-start | bytes 1572872 | tf_op jit(solution)/shard_map/ppermute | solution.py:54
  10.6 1.1 collective-permute-start.3
  11.7 3.8 %collective-permute-start.5 = (bf16[256,512]{1,0:T(8,128)(2,1)}, bf16[256,512]{1,0:T(8,128)(2,1)S(1)}, u32[]{:S(2)}, u32[]{:S(2)}) collective-permute-start(bf16[256,512]{1,0:T(8,128)(2,1)} %param.16), channel_id=1, source_target_pairs={{0,96},{32,64},{64,32},{96,0},{1,97},{33,65},{65,33},{97,1},{2,98}... | collective-permute-start | bytes 786440 | tf_op jit(solution)/shard_map/ppermute | solution.py:66
  15.4 5.8 %collective-permute-done.5 = bf16[256,512]{1,0:T(8,128)(2,1)S(1)} collective-permute-done((bf16[256,512]{1,0:T(8,128)(2,1)}, bf16[256,512]{1,0:T(8,128)(2,1)S(1)}, u32[]{:S(2)}, u32[]{:S(2)}) %collective-permute-start.5) | collective-permute-done | bytes 262176 | tf_op jit(solution)/shard_map/ppermute | solution.py:66
  21.2 0.9 collective-permute-done.4
  22.1 1.0 collective-permute-done.2.across
  23.2 1.3 collective-permute-start.6
  24.5 1.4 collective-permute-start.7
  26.0 1.7 collective-permute-start.8
  27.8 4.6 %collective-permute-done.8 = bf16[256,512]{1,0:T(8,128)(2,1)S(1)} collective-permute-done((bf16[256,512]{1,0:T(8,128)(2,1)S(1)}, bf16[256,512]{1,0:T(8,128)(2,1)S(1)}, u32[]{:S(2)}, u32[]{:S(2)}) %collective-permute-start.8) | collective-permute-done | bytes 262176 | tf_op jit(solution)/shard_map/ppermute | solution.py:66
  32.4 6.1 %collective-permute-done.6.rest_1_ = bf16[2048,256]{1,0:T(8,128)(2,1)S(1)} collective-permute-done((bf16[2048,256]{1,0:T(8,128)(2,1)S(1)}, bf16[2048,256]{1,0:T(8,128)(2,1)S(1)}, u32[]{:S(2)}, u32[]{:S(2)}) %collective-permute-start.6) | collective-permute-done | bytes 1048608 | tf_op jit(solution)/shard_map/ppermute | solution.py:54
  38.8 2.3 %collective-permute-start.11 = (bf16[5120,256]{1,0:T(8,128)(2,1)S(1)}, bf16[5120,256]{1,0:T(8,128)(2,1)S(1)}, u32[]{:S(2)}, u32[]{:S(2)}) collective-permute-start(bf16[5120,256]{1,0:T(8,128)(2,1)S(1)} %slice_dynamic-update-slice_fusion), channel_id=1, source_target_pairs={{0,16},{16,0},{1,17},{17,1},{2,18},{18,2},{3,19},{19,3},{4,20},{20... | collective-permute-start | bytes 7864328 | tf_op jit(solution)/shard_map/ppermute | solution.py:70
  41.1 2.3 %collective-permute-start.13 = (bf16[1024,256]{1,0:T(8,128)(2,1)S(1)}, bf16[1024,256]{1,0:T(8,128)(2,1)S(1)}, u32[]{:S(2)}, u32[]{:S(2)}) collective-permute-start(bf16[1024,256]{1,0:T(8,128)(2,1)S(1)} %get-tuple-element.160), channel_id=1, source_target_pairs={{0,3},{1,0},{2,1},{3,2},{4,7},{5,4},{6,5},{7,6},{8,11},{9,8},{10,9... | collective-permute-start | bytes 1572872 | tf_op jit(solution)/shard_map/ppermute | solution.py:54
  43.3 2.7 %collective-permute-start.10 = (bf16[2048,256]{1,0:T(8,128)(2,1)S(1)}, bf16[2048,256]{1,0:T(8,128)(2,1)S(1)}, u32[]{:S(2)}, u32[]{:S(2)}) collective-permute-start(bf16[2048,256]{1,0:T(8,128)(2,1)S(1)} %get-tuple-element.89.rest_0_), channel_id=1, source_target_pairs={{0,3},{1,0},{2,1},{3,2},{4,7},{5,4},{6,5},{7,6},{8,11},{9,8},{10,9... | collective-permute-start | bytes 3145736 | tf_op jit(solution)/shard_map/ppermute | solution.py:54
  46.0 3.5 %collective-permute-done.13 = bf16[1024,256]{1,0:T(8,128)(2,1)S(1)} collective-permute-done((bf16[1024,256]{1,0:T(8,128)(2,1)S(1)}, bf16[1024,256]{1,0:T(8,128)(2,1)S(1)}, u32[]{:S(2)}, u32[]{:S(2)}) %collective-permute-start.13) | collective-permute-done | bytes 524320 | tf_op jit(solution)/shard_map/ppermute | solution.py:54
  49.6 3.3 %collective-permute-done.12.rest_2_ = bf16[1024,256]{1,0:T(8,128)(2,1)S(1)} collective-permute-done((bf16[1024,256]{1,0:T(8,128)(2,1)S(1)}, bf16[1024,256]{1,0:T(8,128)(2,1)S(1)}, u32[]{:S(2)}, u32[]{:S(2)}) %collective-permute-start.12) | collective-permute-done | bytes 524320 | tf_op jit(solution)/shard_map/ppermute | solution.py:54
  52.9 1.9 collective-permute-start.14
  55.9 4.4 %edge_terms.1 = (f32[2048,256]{1,0:T(8,128)S(1)}, f32[2048,256]{1,0:T(8,128)S(1)}) custom-call(s32[4]{0:T(128)S(1)} %pad_add_fusion.where, s32[1]{0:T(128)S(6)} %copy.27.live, s32[16]{0:T(128)S(1)} %copy-done.10, bf16[2048,128]{1,0:T(8,128)(2,1)S(1)} %fusion.1.pick, bf16[2048,512]{1,0:T(8,128)(2,1)S(1)} %copy-done.3, bf16[512,512]{1,0:T(8,128)(2,1)S(1)} %copy-done.4, ...), custom_call_target="tpu_custom_call" | custom-call | tf_op jit(solution)/shard_map/edge_terms/pallas_call | solution.py:345
  60.8 3.3 %collective-permute-done.9.rest_1_ = bf16[2048,256]{1,0:T(8,128)(2,1)S(1)} collective-permute-done((bf16[2048,256]{1,0:T(8,128)(2,1)S(1)}, bf16[2048,256]{1,0:T(8,128)(2,1)S(1)}, u32[]{:S(2)}, u32[]{:S(2)}) %collective-permute-start.9) | collective-permute-done | bytes 1048608 | tf_op jit(solution)/shard_map/ppermute | solution.py:54
  64.4 1.9 %collective-permute-start.17 = (bf16[3072,256]{1,0:T(8,128)(2,1)S(1)}, bf16[3072,256]{1,0:T(8,128)(2,1)S(1)}, u32[]{:S(2)}, u32[]{:S(2)}) collective-permute-start(bf16[3072,256]{1,0:T(8,128)(2,1)S(1)} %pad_maximum_fusion), channel_id=1, source_target_pairs={{0,16},{16,0},{1,17},{17,1},{2,18},{18,2},{3,19},{19,3},{4,20},{20... | collective-permute-start | bytes 4718600 | tf_op jit(solution)/shard_map/ppermute | solution.py:70
  66.3 1.9 collective-permute-start.16
  68.9 5.6 %forward_0.1 = (f32[2048,256]{1,0:T(8,128)S(1)}, f32[1024,256]{1,0:T(8,128)S(1)}, bf16[1024,256]{1,0:T(8,128)(2,1)S(1)}) custom-call(s32[4]{0:T(128)S(1)} %pad_add_fusion.where, s32[1]{0:T(128)S(6)} %copy.27.live, s32[16]{0:T(128)S(1)} %copy-done.11, s32[16]{0:T(128)S(1)} %copy-done.10, bf16[2048,128]{1,0:T(8,128)(2,1)S(1)} %fusion.2.pick, ...), custom_call_target="tpu_custom_call" | custom-call | tf_op jit(solution)/shard_map/forward_0/pallas_call | solution.py:345
  74.5 3.0 %collective-permute-done.15.rest_2_ = bf16[1024,256]{1,0:T(8,128)(2,1)S(1)} collective-permute-done((bf16[1024,256]{1,0:T(8,128)(2,1)S(1)}, bf16[1024,256]{1,0:T(8,128)(2,1)S(1)}, u32[]{:S(2)}, u32[]{:S(2)}) %collective-permute-start.15) | collective-permute-done | bytes 524320 | tf_op jit(solution)/shard_map/ppermute | solution.py:54
  78.0 1.4 collective-permute-done.18.rest_5_
  80.2 5.6 %forward_1.1 = (f32[2048,256]{1,0:T(8,128)S(1)}, f32[1024,256]{1,0:T(8,128)S(1)}, bf16[1024,256]{1,0:T(8,128)(2,1)S(1)}) custom-call(s32[4]{0:T(128)S(1)} %pad_add_fusion.where, s32[1]{0:T(128)S(6)} %copy.27.live, s32[16]{0:T(128)S(1)} %copy-done.11, s32[16]{0:T(128)S(1)} %copy-done.10, bf16[2048,128]{1,0:T(8,128)(2,1)S(1)} %fusion.2.pick, ...), custom_call_target="tpu_custom_call" | custom-call | tf_op jit(solution)/shard_map/forward_1/pallas_call | solution.py:345
  85.8 1.9 collective-permute-done.20.refs_3_
  87.9 1.8 collective-permute-start.21
  89.7 1.0 collective-permute-start.22
  90.7 2.5 %collective-permute-start.23 = (bf16[256,512]{1,0:T(8,128)(2,1)S(1)}, bf16[256,512]{1,0:T(8,128)(2,1)S(1)}, u32[]{:S(2)}, u32[]{:S(2)}) collective-permute-start(bf16[256,512]{1,0:T(8,128)(2,1)S(1)} %get-tuple-element.115), channel_id=1, source_target_pairs={{0,64},{32,96},{64,0},{96,32},{1,65},{33,97},{65,1},{97,33},{2,66}... | collective-permute-start | bytes 786440 | tf_op jit(solution)/shard_map/ppermute | solution.py:58
  93.2 3.8 %collective-permute-done.21.a = bf16[256,512]{1,0:T(8,128)(2,1)S(1)} collective-permute-done((bf16[256,512]{1,0:T(8,128)(2,1)S(1)}, bf16[256,512]{1,0:T(8,128)(2,1)S(1)}, u32[]{:S(2)}, u32[]{:S(2)}) %collective-permute-start.21) | collective-permute-done | bytes 262176 | tf_op jit(solution)/shard_map/ppermute | solution.py:58
  97.4 6.3 %collective-permute-done.23.c = bf16[256,512]{1,0:T(8,128)(2,1)S(1)} collective-permute-done((bf16[256,512]{1,0:T(8,128)(2,1)S(1)}, bf16[256,512]{1,0:T(8,128)(2,1)S(1)}, u32[]{:S(2)}, u32[]{:S(2)}) %collective-permute-start.23) | collective-permute-done | bytes 262176 | tf_op jit(solution)/shard_map/ppermute | solution.py:58
  104.5 1.8 collective-permute-start.24
  106.3 0.8 collective-permute-start.25
  107.2 1.8 collective-permute-start.27
  109.0 2.6 %collective-permute-done.24.rest_3_ = bf16[256,512]{1,0:T(8,128)(2,1)S(1)} collective-permute-done((bf16[256,512]{1,0:T(8,128)(2,1)S(1)}, bf16[256,512]{1,0:T(8,128)(2,1)S(1)}, u32[]{:S(2)}, u32[]{:S(2)}) %collective-permute-start.24) | collective-permute-done | bytes 262176 | tf_op jit(solution)/shard_map/ppermute | solution.py:58
  111.5 7.0 %collective-permute-start.28 = (bf16[256,512]{1,0:T(8,128)(2,1)S(1)}, bf16[256,512]{1,0:T(8,128)(2,1)S(1)}, u32[]{:S(2)}, u32[]{:S(2)}) collective-permute-start(bf16[256,512]{1,0:T(8,128)(2,1)S(1)} %collective-permute-done.24.rest_3_), channel_id=1, source_target_pairs={{0,16},{16,0},{1,17},{17,1},{2,18},{18,2},{3,19},{19,3},{4,20},{20... | collective-permute-start | bytes 786440 | tf_op jit(solution)/shard_map/ppermute | solution.py:70
  118.6 3.1 %collective-permute-done.26.rest_5_ = bf16[256,512]{1,0:T(8,128)(2,1)S(1)} collective-permute-done((bf16[256,512]{1,0:T(8,128)(2,1)S(1)}, bf16[256,512]{1,0:T(8,128)(2,1)S(1)}, u32[]{:S(2)}, u32[]{:S(2)}) %collective-permute-start.26) | collective-permute-done | bytes 262176 | tf_op jit(solution)/shard_map/ppermute | solution.py:58
  122.4 1.0 collective-permute-done.30.rest_9_
  123.4 6.1 %backward.1 = (bf16[1024,256]{1,0:T(8,128)(2,1)S(1)}, bf16[1024,256]{1,0:T(8,128)(2,1)S(1)}, bf16[1024,256]{1,0:T(8,128)(2,1)S(1)}, bf16[1024,256]{1,0:T(8,128)(...) custom-call(s32[4]{0:T(128)S(1)} %pad_add_fusion.where, ...), custom_call_target="tpu_custom_call" | custom-call | tf_op jit(solution)/shard_map/backward/pallas_call | solution.py:345
  129.5 2.6 %collective-permute-done.31 = bf16[2048,256]{1,0:T(8,128)(2,1)S(1)} collective-permute-done((bf16[2048,256]{1,0:T(8,128)(2,1)S(1)}, bf16[2048,256]{1,0:T(8,128)(2,1)S(1)}, u32[]{:S(2)}, u32[]{:S(2)}) %collective-permute-start.31) | collective-permute-done | bytes 1048608 | tf_op jit(solution)/shard_map/ppermute | solution.py:70
  132.3 1.5 collective-permute-start.33
  133.8 1.2 collective-permute-start.34
  135.4 2.4 %collective-permute-start.36 = (bf16[1024,256]{1,0:T(8,128)(2,1)S(1)}, bf16[1024,256]{1,0:T(8,128)(2,1)S(1)}, u32[]{:S(2)}, u32[]{:S(2)}) collective-permute-start(bf16[1024,256]{1,0:T(8,128)(2,1)S(1)} %get-tuple-element.156), channel_id=1, source_target_pairs={{0,3},{1,0},{2,1},{3,2},{4,7},{5,4},{6,5},{7,6},{8,11},{9,8},{10,9... | collective-permute-start | bytes 1572872 | tf_op jit(solution)/shard_map/ppermute | solution.py:54
  137.8 4.0 %collective-permute-done.33.refs_4_ = bf16[1024,256]{1,0:T(8,128)(2,1)S(1)} collective-permute-done((bf16[1024,256]{1,0:T(8,128)(2,1)S(1)}, bf16[1024,256]{1,0:T(8,128)(2,1)S(1)}, u32[]{:S(2)}, u32[]{:S(2)}) %collective-permute-start.33) | collective-permute-done | bytes 524320 | tf_op jit(solution)/shard_map/ppermute | solution.py:54
  143.0 2.2 %collective-permute-start.40 = (bf16[2048,256]{1,0:T(8,128)(2,1)S(1)}, bf16[2048,256]{1,0:T(8,128)(2,1)S(1)}, u32[]{:S(2)}, u32[]{:S(2)}) collective-permute-start(bf16[2048,256]{1,0:T(8,128)(2,1)S(1)} %get-tuple-element.135), channel_id=1, source_target_pairs={{0,3},{1,0},{2,1},{3,2},{4,7},{5,4},{6,5},{7,6},{8,11},{9,8},{10,9... | collective-permute-start | bytes 3145736 | tf_op jit(solution)/shard_map/ppermute | solution.py:54
  145.2 2.3 %collective-permute-done.35.refs_1_ = bf16[1024,256]{1,0:T(8,128)(2,1)S(1)} collective-permute-done((bf16[1024,256]{1,0:T(8,128)(2,1)S(1)}, bf16[1024,256]{1,0:T(8,128)(2,1)S(1)}, u32[]{:S(2)}, u32[]{:S(2)}) %collective-permute-start.35) | collective-permute-done | bytes 524320 | tf_op jit(solution)/shard_map/ppermute | solution.py:54
  148.6 2.2 %collective-permute-start.38 = (bf16[2048,256]{1,0:T(8,128)(2,1)S(1)}, bf16[2048,256]{1,0:T(8,128)(2,1)S(1)}, u32[]{:S(2)}, u32[]{:S(2)}) collective-permute-start(bf16[2048,256]{1,0:T(8,128)(2,1)S(1)} %get-tuple-element.132), channel_id=1, source_target_pairs={{0,3},{1,0},{2,1},{3,2},{4,7},{5,4},{6,5},{7,6},{8,11},{9,8},{10,9... | collective-permute-start | bytes 3145736 | tf_op jit(solution)/shard_map/ppermute | solution.py:54
  150.8 1.0 fusion
  151.8 6.9 %collective-permute-done.39.refs_2_ = bf16[2048,256]{1,0:T(8,128)(2,1)S(1)} collective-permute-done((bf16[2048,256]{1,0:T(8,128)(2,1)S(1)}, bf16[2048,256]{1,0:T(8,128)(2,1)S(1)}, u32[]{:S(2)}, u32[]{:S(2)}) %collective-permute-start.39) | collective-permute-done | bytes 1048608 | tf_op jit(solution)/shard_map/ppermute | solution.py:54
  159.6 2.6 %collective-permute-start.46 = (bf16[256,512]{1,0:T(8,128)(2,1)S(1)}, bf16[256,512]{1,0:T(8,128)(2,1)S(1)}, u32[]{:S(2)}, u32[]{:S(2)}) collective-permute-start(bf16[256,512]{1,0:T(8,128)(2,1)S(1)} %get-tuple-element.141), channel_id=1, source_target_pairs={{0,12},{1,13},{2,14},{3,15},{4,0},{5,1},{6,2},{7,3},{8,4},{9,5},{1... | collective-permute-start | bytes 786440 | tf_op jit(solution)/shard_map/ppermute | solution.py:54
  162.1 12.5 %collective-permute-done.37.refs_1_ = bf16[2048,256]{1,0:T(8,128)(2,1)S(1)} collective-permute-done((bf16[2048,256]{1,0:T(8,128)(2,1)S(1)}, bf16[2048,256]{1,0:T(8,128)(2,1)S(1)}, u32[]{:S(2)}, u32[]{:S(2)}) %collective-permute-start.37) | collective-permute-done | bytes 1048608 | tf_op jit(solution)/shard_map/ppermute | solution.py:54
  175.4 2.5 %collective-permute-start.43 = (bf16[256,512]{1,0:T(8,128)(2,1)S(1)}, bf16[256,512]{1,0:T(8,128)(2,1)S(1)}, u32[]{:S(2)}, u32[]{:S(2)}) collective-permute-start(bf16[256,512]{1,0:T(8,128)(2,1)S(1)} %get-tuple-element.147), channel_id=1, source_target_pairs={{0,12},{1,13},{2,14},{3,15},{4,0},{5,1},{6,2},{7,3},{8,4},{9,5},{1... | collective-permute-start | bytes 786440 | tf_op jit(solution)/shard_map/ppermute | solution.py:54
  178.5 1.3 place_mine.1.rest_0_
  179.8 4.7 %collective-permute-done.41.up = bf16[256,512]{1,0:T(8,128)(2,1)S(1)} collective-permute-done((bf16[256,512]{1,0:T(8,128)(2,1)S(1)}, bf16[256,512]{1,0:T(8,128)(2,1)S(1)}, u32[]{:S(2)}, u32[]{:S(2)}) %collective-permute-start.41) | collective-permute-done | bytes 262176 | tf_op jit(solution)/shard_map/ppermute | solution.py:54
  184.5 0.9 collective-permute-done.43.across
  185.9 3.1 %collective-permute-start.47 = (f32[256,512]{1,0:T(8,128)S(1)}, f32[256,512]{1,0:T(8,128)S(1)}, u32[]{:S(2)}, u32[]{:S(2)}) collective-permute-start(f32[256,512]{1,0:T(8,128)S(1)} %row_sum_other.1), channel_id=1, source_target_pairs={{0,16},{16,0},{1,17},{17,1},{2,18},{18,2},{3,19},{19,3},{4,20},{20... | collective-permute-start | bytes 1572872 | tf_op jit(solution)/shard_map/ppermute | solution.py:70
  189.1 1.5 collective-permute-done.47.value
  190.6 1.3 place_other.1
  (100 shorter events, 11.5 us)
Async XLA Ops:
  0.6 67.6 %copy-start = (bf16[512,512]{1,0:T(8,128)(2,1)S(1)}, bf16[512,512]{1,0:T(8,128)(2,1)}, u32[]{:S(2)}) copy-start(bf16[512,512]{1,0:T(8,128)(2,1)} %param.28) | copy-start | bytes 1572868
  0.7 1.1 copy-start.1
  1.8 1.0 copy-start.6
  2.9 23.1 %copy-start.14 = (bf16[256,512]{1,0:T(8,128)(2,1)S(1)}, bf16[256,512]{1,0:T(8,128)(2,1)}, u32[]{:S(2)}) copy-start(bf16[256,512]{1,0:T(8,128)(2,1)} %param.16) | copy-start | bytes 786436
  3.8 2.7 %collective-permute-start = (bf16[256,512]{1,0:T(8,128)(2,1)S(1)}, bf16[256,512]{1,0:T(8,128)(2,1)S(1)}, u32[]{:S(2)}, u32[]{:S(2)}) collective-permute-start(bf16[256,512]{1,0:T(8,128)(2,1)S(1)} %get-tuple-element.80), channel_id=1, source_target_pairs={{0,16},{16,0},{1,17},{17,1},{2,18},{18,2},{3,19},{19,3},{4,20},{20... | collective-permute-start | bytes 786440 | tf_op jit(solution)/shard_map/ppermute | solution.py:70
  6.5 15.6 %collective-permute-start.1 = (bf16[512,512]{1,0:T(8,128)(2,1)S(1)}, bf16[512,512]{1,0:T(8,128)(2,1)S(1)}, u32[]{:S(2)}, u32[]{:S(2)}) collective-permute-start(bf16[512,512]{1,0:T(8,128)(2,1)S(1)} %constant_dynamic-update-slice_fusion), channel_id=1, source_target_pairs={{0,4},{1,5},{2,6},{3,7},{4,8},{5,9},{6,10},{7,11},{8,12},{9,13},{1... | collective-permute-start | bytes 1572872 | tf_op jit(solution)/shard_map/ppermute | solution.py:54
  8.0 15.1 %collective-permute-start.2 = (bf16[512,512]{1,0:T(8,128)(2,1)S(1)}, bf16[512,512]{1,0:T(8,128)(2,1)S(1)}, u32[]{:S(2)}, u32[]{:S(2)}) collective-permute-start(bf16[512,512]{1,0:T(8,128)(2,1)S(1)} %constant_dynamic-update-slice_fusion), channel_id=1, source_target_pairs={{0,8},{1,9},{2,10},{3,11},{4,12},{5,13},{6,14},{7,15},{8,0},{9,1},... | collective-permute-start | bytes 1572872 | tf_op jit(solution)/shard_map/ppermute | solution.py:54
  10.6 12.5 %collective-permute-start.3 = (bf16[512,512]{1,0:T(8,128)(2,1)S(1)}, bf16[512,512]{1,0:T(8,128)(2,1)S(1)}, u32[]{:S(2)}, u32[]{:S(2)}) collective-permute-start(bf16[512,512]{1,0:T(8,128)(2,1)S(1)} %constant_dynamic-update-slice_fusion), channel_id=1, source_target_pairs={{0,12},{1,13},{2,14},{3,15},{4,0},{5,1},{6,2},{7,3},{8,4},{9,5},{1... | collective-permute-start | bytes 1572872 | tf_op jit(solution)/shard_map/ppermute | solution.py:54
  11.7 9.6 %collective-permute-start.5 = (bf16[256,512]{1,0:T(8,128)(2,1)}, bf16[256,512]{1,0:T(8,128)(2,1)S(1)}, u32[]{:S(2)}, u32[]{:S(2)}) collective-permute-start(bf16[256,512]{1,0:T(8,128)(2,1)} %param.16), channel_id=1, source_target_pairs={{0,96},{32,64},{64,32},{96,0},{1,97},{33,65},{65,33},{97,1},{2,98}... | collective-permute-start | bytes 786440 | tf_op jit(solution)/shard_map/ppermute | solution.py:66
  15.4 6.7 %collective-permute-start.4 = (bf16[256,512]{1,0:T(8,128)(2,1)}, bf16[256,512]{1,0:T(8,128)(2,1)S(1)}, u32[]{:S(2)}, u32[]{:S(2)}) collective-permute-start(bf16[256,512]{1,0:T(8,128)(2,1)} %param.16), channel_id=1, source_target_pairs={{0,32},{32,0},{64,96},{96,64},{1,33},{33,1},{65,97},{97,65},{2,34}... | collective-permute-start | bytes 786440 | tf_op jit(solution)/shard_map/ppermute | solution.py:66
  23.2 15.2 %collective-permute-start.6 = (bf16[2048,256]{1,0:T(8,128)(2,1)S(1)}, bf16[2048,256]{1,0:T(8,128)(2,1)S(1)}, u32[]{:S(2)}, u32[]{:S(2)}) collective-permute-start(bf16[2048,256]{1,0:T(8,128)(2,1)S(1)} %get-tuple-element.86.rest_0_), channel_id=1, source_target_pairs={{0,1},{1,2},{2,3},{3,0},{4,5},{5,6},{6,7},{7,4},{8,9},{9,10},{10,1... | collective-permute-start | bytes 3145736 | tf_op jit(solution)/shard_map/ppermute | solution.py:54
  24.5 13.9 %collective-permute-start.7 = (bf16[2048,256]{1,0:T(8,128)(2,1)S(1)}, bf16[2048,256]{1,0:T(8,128)(2,1)S(1)}, u32[]{:S(2)}, u32[]{:S(2)}) collective-permute-start(bf16[2048,256]{1,0:T(8,128)(2,1)S(1)} %get-tuple-element.86.rest_0_), channel_id=1, source_target_pairs={{0,3},{1,0},{2,1},{3,2},{4,7},{5,4},{6,5},{7,6},{8,11},{9,8},{10,9... | collective-permute-start | bytes 3145736 | tf_op jit(solution)/shard_map/ppermute | solution.py:54
  26.0 6.4 %collective-permute-start.8 = (bf16[256,512]{1,0:T(8,128)(2,1)S(1)}, bf16[256,512]{1,0:T(8,128)(2,1)S(1)}, u32[]{:S(2)}, u32[]{:S(2)}) collective-permute-start(bf16[256,512]{1,0:T(8,128)(2,1)S(1)} %collective-permute-done.5), channel_id=1, source_target_pairs={{0,32},{32,0},{64,96},{96,64},{1,33},{33,1},{65,97},{97,65},{2,34}... | collective-permute-start | bytes 786440 | tf_op jit(solution)/shard_map/ppermute | solution.py:66
  38.5 16.9 %copy-start.8 = (s32[16,128]{1,0:T(8,128)S(1)}, s32[16,128]{1,0:T(8,128)}, u32[]{:S(2)}) copy-start(s32[16,128]{1,0:T(8,128)} %recv.3) | copy-start | bytes 24580
  38.6 17.2 %copy-start.3 = (bf16[2048,512]{1,0:T(8,128)(2,1)S(1)}, bf16[2048,512]{1,0:T(8,128)(2,1)}, u32[]{:S(2)}) copy-start(bf16[2048,512]{1,0:T(8,128)(2,1)} %edge.1) | copy-start | bytes 6291460
  38.6 17.2 %copy-start.4 = (bf16[512,512]{1,0:T(8,128)(2,1)S(1)}, bf16[512,512]{1,0:T(8,128)(2,1)}, u32[]{:S(2)}) copy-start(bf16[512,512]{1,0:T(8,128)(2,1)} %w_mesh.1) | copy-start | bytes 1572868
  38.6 17.2 %copy-start.5 = (bf16[512,512]{1,0:T(8,128)(2,1)S(1)}, bf16[512,512]{1,0:T(8,128)(2,1)}, u32[]{:S(2)}) copy-start(bf16[512,512]{1,0:T(8,128)(2,1)} %w_edge.1) | copy-start | bytes 1572868
  38.7 17.2 %copy-start.10 = (s32[16]{0:T(128)S(1)}, s32[16]{0:T(128)}, u32[]{:S(2)}) copy-start(s32[16]{0:T(128)} %mesh_block.7) | copy-start | bytes 196
  38.7 17.2 %copy-start.12 = (f32[512]{0:T(512)S(1)}, f32[512]{0:T(512)}, u32[]{:S(2)}) copy-start(f32[512]{0:T(512)} %param.26) | copy-start | bytes 6148
  38.8 17.0 %collective-permute-start.11 = (bf16[5120,256]{1,0:T(8,128)(2,1)S(1)}, bf16[5120,256]{1,0:T(8,128)(2,1)S(1)}, u32[]{:S(2)}, u32[]{:S(2)}) collective-permute-start(bf16[5120,256]{1,0:T(8,128)(2,1)S(1)} %slice_dynamic-update-slice_fusion), channel_id=1, source_target_pairs={{0,16},{16,0},{1,17},{17,1},{2,18},{18,2},{3,19},{19,3},{4,20},{20... | collective-permute-start | bytes 7864328 | tf_op jit(solution)/shard_map/ppermute | solution.py:70
  41.1 8.5 %collective-permute-start.13 = (bf16[1024,256]{1,0:T(8,128)(2,1)S(1)}, bf16[1024,256]{1,0:T(8,128)(2,1)S(1)}, u32[]{:S(2)}, u32[]{:S(2)}) collective-permute-start(bf16[1024,256]{1,0:T(8,128)(2,1)S(1)} %get-tuple-element.160), channel_id=1, source_target_pairs={{0,3},{1,0},{2,1},{3,2},{4,7},{5,4},{6,5},{7,6},{8,11},{9,8},{10,9... | collective-permute-start | bytes 1572872 | tf_op jit(solution)/shard_map/ppermute | solution.py:54
  43.3 9.5 %collective-permute-start.12 = (bf16[1024,256]{1,0:T(8,128)(2,1)S(1)}, bf16[1024,256]{1,0:T(8,128)(2,1)S(1)}, u32[]{:S(2)}, u32[]{:S(2)}) collective-permute-start(bf16[1024,256]{1,0:T(8,128)(2,1)S(1)} %get-tuple-element.162), channel_id=1, source_target_pairs={{0,1},{1,2},{2,3},{3,0},{4,5},{5,6},{6,7},{7,4},{8,9},{9,10},{10,1... | collective-permute-start | bytes 1572872 | tf_op jit(solution)/shard_map/ppermute | solution.py:54
  43.3 17.4 %collective-permute-start.10 = (bf16[2048,256]{1,0:T(8,128)(2,1)S(1)}, bf16[2048,256]{1,0:T(8,128)(2,1)S(1)}, u32[]{:S(2)}, u32[]{:S(2)}) collective-permute-start(bf16[2048,256]{1,0:T(8,128)(2,1)S(1)} %get-tuple-element.89.rest_0_), channel_id=1, source_target_pairs={{0,3},{1,0},{2,1},{3,2},{4,7},{5,4},{6,5},{7,6},{8,11},{9,8},{10,9... | collective-permute-start | bytes 3145736 | tf_op jit(solution)/shard_map/ppermute | solution.py:54
  46.0 18.1 %collective-permute-start.9 = (bf16[2048,256]{1,0:T(8,128)(2,1)S(1)}, bf16[2048,256]{1,0:T(8,128)(2,1)S(1)}, u32[]{:S(2)}, u32[]{:S(2)}) collective-permute-start(bf16[2048,256]{1,0:T(8,128)(2,1)S(1)} %get-tuple-element.89.rest_0_), channel_id=1, source_target_pairs={{0,1},{1,2},{2,3},{3,0},{4,5},{5,6},{6,7},{7,4},{8,9},{9,10},{10,1... | collective-permute-start | bytes 3145736 | tf_op jit(solution)/shard_map/ppermute | solution.py:54
  52.9 7.4 %collective-permute-start.14 = (bf16[1024,256]{1,0:T(8,128)(2,1)S(1)}, bf16[1024,256]{1,0:T(8,128)(2,1)S(1)}, u32[]{:S(2)}, u32[]{:S(2)}) collective-permute-start(bf16[1024,256]{1,0:T(8,128)(2,1)S(1)} %collective-permute-done.13), channel_id=1, source_target_pairs={{0,16},{16,0},{1,17},{17,1},{2,18},{18,2},{3,19},{19,3},{4,20},{20... | collective-permute-start | bytes 1572872 | tf_op jit(solution)/shard_map/ppermute | solution.py:70
  64.2 4.0 %copy-start.13 = (bf16[256,512]{1,0:T(8,128)(2,1)S(1)}, bf16[256,512]{1,0:T(8,128)(2,1)}, u32[]{:S(2)}) copy-start(bf16[256,512]{1,0:T(8,128)(2,1)} %param.29) | copy-start | bytes 786436
  64.2 4.3 %copy-start.9 = (s32[16,128]{1,0:T(8,128)S(1)}, s32[16,128]{1,0:T(8,128)}, u32[]{:S(2)}) copy-start(s32[16,128]{1,0:T(8,128)} %send.1) | copy-start | bytes 24580
  64.3 4.6 %copy-start.11 = (s32[16]{0:T(128)S(1)}, s32[16]{0:T(128)}, u32[]{:S(2)}) copy-start(s32[16]{0:T(128)} %grid_block.5) | copy-start | bytes 196
  64.4 13.1 %collective-permute-start.17 = (bf16[3072,256]{1,0:T(8,128)(2,1)S(1)}, bf16[3072,256]{1,0:T(8,128)(2,1)S(1)}, u32[]{:S(2)}, u32[]{:S(2)}) collective-permute-start(bf16[3072,256]{1,0:T(8,128)(2,1)S(1)} %pad_maximum_fusion), channel_id=1, source_target_pairs={{0,16},{16,0},{1,17},{17,1},{2,18},{18,2},{3,19},{19,3},{4,20},{20... | collective-permute-start | bytes 4718600 | tf_op jit(solution)/shard_map/ppermute | solution.py:70
  66.3 11.1 %collective-permute-start.16 = (bf16[1024,256]{1,0:T(8,128)(2,1)S(1)}, bf16[1024,256]{1,0:T(8,128)(2,1)S(1)}, u32[]{:S(2)}, u32[]{:S(2)}) collective-permute-start(bf16[1024,256]{1,0:T(8,128)(2,1)S(1)} %slice.45), channel_id=1, source_target_pairs={{0,3},{1,0},{2,1},{3,2},{4,7},{5,4},{6,5},{7,6},{8,11},{9,8},{10,9... | collective-permute-start | bytes 1572872 | tf_op jit(solution)/shard_map/ppermute | solution.py:54
  68.2 9.3 %collective-permute-start.15 = (bf16[1024,256]{1,0:T(8,128)(2,1)S(1)}, bf16[1024,256]{1,0:T(8,128)(2,1)S(1)}, u32[]{:S(2)}, u32[]{:S(2)}) collective-permute-start(bf16[1024,256]{1,0:T(8,128)(2,1)S(1)} %get-tuple-element.159), channel_id=1, source_target_pairs={{0,1},{1,2},{2,3},{3,0},{4,5},{5,6},{6,7},{7,4},{8,9},{9,10},{10,1... | collective-permute-start | bytes 1572872 | tf_op jit(solution)/shard_map/ppermute | solution.py:54
  77.5 1.9 %collective-permute-start.18 = (bf16[1024,256]{1,0:T(8,128)(2,1)S(1)}, bf16[1024,256]{1,0:T(8,128)(2,1)S(1)}, u32[]{:S(2)}, u32[]{:S(2)}) collective-permute-start(bf16[1024,256]{1,0:T(8,128)(2,1)S(1)} %collective-permute-done.16), channel_id=1, source_target_pairs={{0,16},{16,0},{1,17},{17,1},{2,18},{18,2},{3,19},{19,3},{4,20},{20... | collective-permute-start | bytes 1572872 | tf_op jit(solution)/shard_map/ppermute | solution.py:70
  77.9 2.3 %collective-permute-start.19 = (bf16[1024,256]{1,0:T(8,128)(2,1)S(1)}, bf16[1024,256]{1,0:T(8,128)(2,1)S(1)}, u32[]{:S(2)}, u32[]{:S(2)}) collective-permute-start(bf16[1024,256]{1,0:T(8,128)(2,1)S(1)} %get-tuple-element.108), channel_id=1, source_target_pairs={{0,16},{16,0},{1,17},{17,1},{2,18},{18,2},{3,19},{19,3},{4,20},{20... | collective-permute-start | bytes 1572872 | tf_op jit(solution)/shard_map/ppermute | solution.py:70
  85.7 18.0 %copy-start.7 = (bf16[512,512]{1,0:T(8,128)(2,1)S(1)}, bf16[512,512]{1,0:T(8,128)(2,1)}, u32[]{:S(2)}) copy-start(bf16[512,512]{1,0:T(8,128)(2,1)} %w_out.1) | copy-start | bytes 1572868
  85.7 2.0 %collective-permute-start.20 = (bf16[1024,256]{1,0:T(8,128)(2,1)S(1)}, bf16[1024,256]{1,0:T(8,128)(2,1)S(1)}, u32[]{:S(2)}, u32[]{:S(2)}) collective-permute-start(bf16[1024,256]{1,0:T(8,128)(2,1)S(1)} %get-tuple-element.111), channel_id=1, source_target_pairs={{0,16},{16,0},{1,17},{17,1},{2,18},{18,2},{3,19},{19,3},{4,20},{20... | collective-permute-start | bytes 1572872 | tf_op jit(solution)/shard_map/ppermute | solution.py:70
  87.9 9.0 %collective-permute-start.21 = (bf16[256,512]{1,0:T(8,128)(2,1)S(1)}, bf16[256,512]{1,0:T(8,128)(2,1)S(1)}, u32[]{:S(2)}, u32[]{:S(2)}) collective-permute-start(bf16[256,512]{1,0:T(8,128)(2,1)S(1)} %get-tuple-element.113), channel_id=1, source_target_pairs={{0,32},{32,64},{64,96},{96,0},{1,33},{33,65},{65,97},{97,1},{2,34}... | collective-permute-start | bytes 786440 | tf_op jit(solution)/shard_map/ppermute | solution.py:58
  89.7 7.7 %collective-permute-start.22 = (bf16[256,512]{1,0:T(8,128)(2,1)S(1)}, bf16[256,512]{1,0:T(8,128)(2,1)S(1)}, u32[]{:S(2)}, u32[]{:S(2)}) collective-permute-start(bf16[256,512]{1,0:T(8,128)(2,1)S(1)} %get-tuple-element.114), channel_id=1, source_target_pairs={{0,96},{32,0},{64,32},{96,64},{1,97},{33,1},{65,33},{97,65},{2,98}... | collective-permute-start | bytes 786440 | tf_op jit(solution)/shard_map/ppermute | solution.py:58
  90.7 13.0 %collective-permute-start.23 = (bf16[256,512]{1,0:T(8,128)(2,1)S(1)}, bf16[256,512]{1,0:T(8,128)(2,1)S(1)}, u32[]{:S(2)}, u32[]{:S(2)}) collective-permute-start(bf16[256,512]{1,0:T(8,128)(2,1)S(1)} %get-tuple-element.115), channel_id=1, source_target_pairs={{0,64},{32,96},{64,0},{96,32},{1,65},{33,97},{65,1},{97,33},{2,66}... | collective-permute-start | bytes 786440 | tf_op jit(solution)/shard_map/ppermute | solution.py:58
  104.5 7.0 %collective-permute-start.24 = (bf16[256,512]{1,0:T(8,128)(2,1)S(1)}, bf16[256,512]{1,0:T(8,128)(2,1)S(1)}, u32[]{:S(2)}, u32[]{:S(2)}) collective-permute-start(bf16[256,512]{1,0:T(8,128)(2,1)S(1)} %get-tuple-element.119.rest_2_), channel_id=1, source_target_pairs={{0,96},{32,0},{64,32},{96,64},{1,97},{33,1},{65,33},{97,65},{2,98}... | collective-permute-start | bytes 786440 | tf_op jit(solution)/shard_map/ppermute | solution.py:58
  106.3 12.2 %collective-permute-start.25 = (bf16[256,512]{1,0:T(8,128)(2,1)S(1)}, bf16[256,512]{1,0:T(8,128)(2,1)S(1)}, u32[]{:S(2)}, u32[]{:S(2)}) collective-permute-start(bf16[256,512]{1,0:T(8,128)(2,1)S(1)} %get-tuple-element.119.rest_2_), channel_id=1, source_target_pairs={{0,64},{32,96},{64,0},{96,32},{1,65},{33,97},{65,1},{97,33},{2,66}... | collective-permute-start | bytes 786440 | tf_op jit(solution)/shard_map/ppermute | solution.py:58
  107.2 14.5 %collective-permute-start.26 = (bf16[256,512]{1,0:T(8,128)(2,1)S(1)}, bf16[256,512]{1,0:T(8,128)(2,1)S(1)}, u32[]{:S(2)}, u32[]{:S(2)}) collective-permute-start(bf16[256,512]{1,0:T(8,128)(2,1)S(1)} %get-tuple-element.119.rest_2_), channel_id=1, source_target_pairs={{0,32},{32,64},{64,96},{96,0},{1,33},{33,65},{65,97},{97,1},{2,34}... | collective-permute-start | bytes 786440 | tf_op jit(solution)/shard_map/ppermute | solution.py:58
  107.2 15.2 %collective-permute-start.27 = (bf16[256,512]{1,0:T(8,128)(2,1)S(1)}, bf16[256,512]{1,0:T(8,128)(2,1)S(1)}, u32[]{:S(2)}, u32[]{:S(2)}) collective-permute-start(bf16[256,512]{1,0:T(8,128)(2,1)S(1)} %get-tuple-element.119.rest_2_), channel_id=1, source_target_pairs={{0,16},{16,0},{1,17},{17,1},{2,18},{18,2},{3,19},{19,3},{4,20},{20... | collective-permute-start | bytes 786440 | tf_op jit(solution)/shard_map/ppermute | solution.py:70
  111.5 10.8 %collective-permute-start.28 = (bf16[256,512]{1,0:T(8,128)(2,1)S(1)}, bf16[256,512]{1,0:T(8,128)(2,1)S(1)}, u32[]{:S(2)}, u32[]{:S(2)}) collective-permute-start(bf16[256,512]{1,0:T(8,128)(2,1)S(1)} %collective-permute-done.24.rest_3_), channel_id=1, source_target_pairs={{0,16},{16,0},{1,17},{17,1},{2,18},{18,2},{3,19},{19,3},{4,20},{20... | collective-permute-start | bytes 786440 | tf_op jit(solution)/shard_map/ppermute | solution.py:70
  118.5 3.9 %collective-permute-start.29 = (bf16[256,512]{1,0:T(8,128)(2,1)S(1)}, bf16[256,512]{1,0:T(8,128)(2,1)S(1)}, u32[]{:S(2)}, u32[]{:S(2)}) collective-permute-start(bf16[256,512]{1,0:T(8,128)(2,1)S(1)} %collective-permute-done.25.rest_4_), channel_id=1, source_target_pairs={{0,16},{16,0},{1,17},{17,1},{2,18},{18,2},{3,19},{19,3},{4,20},{20... | collective-permute-start | bytes 786440 | tf_op jit(solution)/shard_map/ppermute | solution.py:70
  121.7 1.7 collective-permute-start.30
  129.5 2.7 %collective-permute-start.31 = (bf16[2048,256]{1,0:T(8,128)(2,1)S(1)}, bf16[2048,256]{1,0:T(8,128)(2,1)S(1)}, u32[]{:S(2)}, u32[]{:S(2)}) collective-permute-start(bf16[2048,256]{1,0:T(8,128)(2,1)S(1)} %get-tuple-element.121), channel_id=1, source_target_pairs={{0,16},{16,0},{1,17},{17,1},{2,18},{18,2},{3,19},{19,3},{4,20},{20... | collective-permute-start | bytes 3145736 | tf_op jit(solution)/shard_map/ppermute | solution.py:70
  132.2 13.0 %collective-permute-start.32 = (bf16[6144,256]{1,0:T(8,128)(2,1)S(1)}, bf16[6144,256]{1,0:T(8,128)(2,1)S(1)}, u32[]{:S(2)}, u32[]{:S(2)}) collective-permute-start(bf16[6144,256]{1,0:T(8,128)(2,1)S(1)} %get-tuple-element.122), channel_id=1, source_target_pairs={{0,16},{16,0},{1,17},{17,1},{2,18},{18,2},{3,19},{19,3},{4,20},{20... | collective-permute-start | bytes 9437192 | tf_op jit(solution)/shard_map/ppermute | solution.py:70
  132.3 9.5 %collective-permute-start.33 = (bf16[1024,256]{1,0:T(8,128)(2,1)S(1)}, bf16[1024,256]{1,0:T(8,128)(2,1)S(1)}, u32[]{:S(2)}, u32[]{:S(2)}) collective-permute-start(bf16[1024,256]{1,0:T(8,128)(2,1)S(1)} %get-tuple-element.127), channel_id=1, source_target_pairs={{0,1},{1,2},{2,3},{3,0},{4,5},{5,6},{6,7},{7,4},{8,9},{9,10},{10,1... | collective-permute-start | bytes 1572872 | tf_op jit(solution)/shard_map/ppermute | solution.py:54
  133.8 8.3 %collective-permute-start.34 = (bf16[1024,256]{1,0:T(8,128)(2,1)S(1)}, bf16[1024,256]{1,0:T(8,128)(2,1)S(1)}, u32[]{:S(2)}, u32[]{:S(2)}) collective-permute-start(bf16[1024,256]{1,0:T(8,128)(2,1)S(1)} %get-tuple-element.128), channel_id=1, source_target_pairs={{0,3},{1,0},{2,1},{3,2},{4,7},{5,4},{6,5},{7,6},{8,11},{9,8},{10,9... | collective-permute-start | bytes 1572872 | tf_op jit(solution)/shard_map/ppermute | solution.py:54
  135.1 12.4 %collective-permute-start.35 = (bf16[1024,256]{1,0:T(8,128)(2,1)S(1)}, bf16[1024,256]{1,0:T(8,128)(2,1)S(1)}, u32[]{:S(2)}, u32[]{:S(2)}) collective-permute-start(bf16[1024,256]{1,0:T(8,128)(2,1)S(1)} %get-tuple-element.157), channel_id=1, source_target_pairs={{0,1},{1,2},{2,3},{3,0},{4,5},{5,6},{6,7},{7,4},{8,9},{9,10},{10,1... | collective-permute-start | bytes 1572872 | tf_op jit(solution)/shard_map/ppermute | solution.py:54
  135.4 12.3 %collective-permute-start.36 = (bf16[1024,256]{1,0:T(8,128)(2,1)S(1)}, bf16[1024,256]{1,0:T(8,128)(2,1)S(1)}, u32[]{:S(2)}, u32[]{:S(2)}) collective-permute-start(bf16[1024,256]{1,0:T(8,128)(2,1)S(1)} %get-tuple-element.156), channel_id=1, source_target_pairs={{0,3},{1,0},{2,1},{3,2},{4,7},{5,4},{6,5},{7,6},{8,11},{9,8},{10,9... | collective-permute-start | bytes 1572872 | tf_op jit(solution)/shard_map/ppermute | solution.py:54
  142.4 16.3 %collective-permute-start.39 = (bf16[2048,256]{1,0:T(8,128)(2,1)S(1)}, bf16[2048,256]{1,0:T(8,128)(2,1)S(1)}, u32[]{:S(2)}, u32[]{:S(2)}) collective-permute-start(bf16[2048,256]{1,0:T(8,128)(2,1)S(1)} %get-tuple-element.129), channel_id=1, source_target_pairs={{0,1},{1,2},{2,3},{3,0},{4,5},{5,6},{6,7},{7,4},{8,9},{9,10},{10,1... | collective-permute-start | bytes 3145736 | tf_op jit(solution)/shard_map/ppermute | solution.py:54
  143.0 16.0 %collective-permute-start.40 = (bf16[2048,256]{1,0:T(8,128)(2,1)S(1)}, bf16[2048,256]{1,0:T(8,128)(2,1)S(1)}, u32[]{:S(2)}, u32[]{:S(2)}) collective-permute-start(bf16[2048,256]{1,0:T(8,128)(2,1)S(1)} %get-tuple-element.135), channel_id=1, source_target_pairs={{0,3},{1,0},{2,1},{3,2},{4,7},{5,4},{6,5},{7,6},{8,11},{9,8},{10,9... | collective-permute-start | bytes 3145736 | tf_op jit(solution)/shard_map/ppermute | solution.py:54
  148.1 26.6 %collective-permute-start.37 = (bf16[2048,256]{1,0:T(8,128)(2,1)S(1)}, bf16[2048,256]{1,0:T(8,128)(2,1)S(1)}, u32[]{:S(2)}, u32[]{:S(2)}) collective-permute-start(bf16[2048,256]{1,0:T(8,128)(2,1)S(1)} %get-tuple-element.131), channel_id=1, source_target_pairs={{0,1},{1,2},{2,3},{3,0},{4,5},{5,6},{6,7},{7,4},{8,9},{9,10},{10,1... | collective-permute-start | bytes 3145736 | tf_op jit(solution)/shard_map/ppermute | solution.py:54
  148.6 26.3 %collective-permute-start.38 = (bf16[2048,256]{1,0:T(8,128)(2,1)S(1)}, bf16[2048,256]{1,0:T(8,128)(2,1)S(1)}, u32[]{:S(2)}, u32[]{:S(2)}) collective-permute-start(bf16[2048,256]{1,0:T(8,128)(2,1)S(1)} %get-tuple-element.132), channel_id=1, source_target_pairs={{0,3},{1,0},{2,1},{3,2},{4,7},{5,4},{6,5},{7,6},{8,11},{9,8},{10,9... | collective-permute-start | bytes 3145736 | tf_op jit(solution)/shard_map/ppermute | solution.py:54
  159.4 16.0 %collective-permute-start.44 = (bf16[256,512]{1,0:T(8,128)(2,1)S(1)}, bf16[256,512]{1,0:T(8,128)(2,1)S(1)}, u32[]{:S(2)}, u32[]{:S(2)}) collective-permute-start(bf16[256,512]{1,0:T(8,128)(2,1)S(1)} %get-tuple-element.139), channel_id=1, source_target_pairs={{0,4},{1,5},{2,6},{3,7},{4,8},{5,9},{6,10},{7,11},{8,12},{9,13},{1... | collective-permute-start | bytes 786440 | tf_op jit(solution)/shard_map/ppermute | solution.py:54
  159.5 18.5 %collective-permute-start.45 = (bf16[256,512]{1,0:T(8,128)(2,1)S(1)}, bf16[256,512]{1,0:T(8,128)(2,1)S(1)}, u32[]{:S(2)}, u32[]{:S(2)}) collective-permute-start(bf16[256,512]{1,0:T(8,128)(2,1)S(1)} %get-tuple-element.140), channel_id=1, source_target_pairs={{0,8},{1,9},{2,10},{3,11},{4,12},{5,13},{6,14},{7,15},{8,0},{9,1},... | collective-permute-start | bytes 786440 | tf_op jit(solution)/shard_map/ppermute | solution.py:54
  159.6 18.4 %collective-permute-start.46 = (bf16[256,512]{1,0:T(8,128)(2,1)S(1)}, bf16[256,512]{1,0:T(8,128)(2,1)S(1)}, u32[]{:S(2)}, u32[]{:S(2)}) collective-permute-start(bf16[256,512]{1,0:T(8,128)(2,1)S(1)} %get-tuple-element.141), channel_id=1, source_target_pairs={{0,12},{1,13},{2,14},{3,15},{4,0},{5,1},{6,2},{7,3},{8,4},{9,5},{1... | collective-permute-start | bytes 786440 | tf_op jit(solution)/shard_map/ppermute | solution.py:54
  174.8 3.1 %copy-start.2 = (bf16[512,512]{1,0:T(8,128)(2,1)S(1)}, bf16[512,512]{1,0:T(8,128)(2,1)}, u32[]{:S(2)}) copy-start(bf16[512,512]{1,0:T(8,128)(2,1)} %w_grid.5) | copy-start | bytes 1572868
  175.2 9.3 %collective-permute-start.41 = (bf16[256,512]{1,0:T(8,128)(2,1)S(1)}, bf16[256,512]{1,0:T(8,128)(2,1)S(1)}, u32[]{:S(2)}, u32[]{:S(2)}) collective-permute-start(bf16[256,512]{1,0:T(8,128)(2,1)S(1)} %get-tuple-element.145), channel_id=1, source_target_pairs={{0,4},{1,5},{2,6},{3,7},{4,8},{5,9},{6,10},{7,11},{8,12},{9,13},{1... | collective-permute-start | bytes 786440 | tf_op jit(solution)/shard_map/ppermute | solution.py:54
  175.4 9.1 %collective-permute-start.42 = (bf16[256,512]{1,0:T(8,128)(2,1)S(1)}, bf16[256,512]{1,0:T(8,128)(2,1)S(1)}, u32[]{:S(2)}, u32[]{:S(2)}) collective-permute-start(bf16[256,512]{1,0:T(8,128)(2,1)S(1)} %get-tuple-element.146), channel_id=1, source_target_pairs={{0,8},{1,9},{2,10},{3,11},{4,12},{5,13},{6,14},{7,15},{8,0},{9,1},... | collective-permute-start | bytes 786440 | tf_op jit(solution)/shard_map/ppermute | solution.py:54
  175.4 10.0 %collective-permute-start.43 = (bf16[256,512]{1,0:T(8,128)(2,1)S(1)}, bf16[256,512]{1,0:T(8,128)(2,1)S(1)}, u32[]{:S(2)}, u32[]{:S(2)}) collective-permute-start(bf16[256,512]{1,0:T(8,128)(2,1)S(1)} %get-tuple-element.147), channel_id=1, source_target_pairs={{0,12},{1,13},{2,14},{3,15},{4,0},{5,1},{6,2},{7,3},{8,4},{9,5},{1... | collective-permute-start | bytes 786440 | tf_op jit(solution)/shard_map/ppermute | solution.py:54
  185.9 4.7 %collective-permute-start.47 = (f32[256,512]{1,0:T(8,128)S(1)}, f32[256,512]{1,0:T(8,128)S(1)}, u32[]{:S(2)}, u32[]{:S(2)}) collective-permute-start(f32[256,512]{1,0:T(8,128)S(1)} %row_sum_other.1), channel_id=1, source_target_pairs={{0,16},{16,0},{1,17},{17,1},{2,18},{18,2},{3,19},{19,3},{4,20},{20... | collective-permute-start | bytes 1572872 | tf_op jit(solution)/shard_map/ppermute | solution.py:70

commit v4 on v3

--- a/solution.py
+++ b/solution.py
@@ -85,7 +85,7 @@
 
 
 def sigmoid(value):
-    return 1.0 / (1.0 + jnp.exp(-value))
+    return 0.5 * jnp.tanh(0.5 * value) + 0.5
 
 
 def one_hot(offsets, slot):
@@ -117,7 +117,7 @@
         out[...] = dot(grid[pl.ds(pl.multiple_of(half * HALF, HALF), HALF), :], w_grid[...]).astype(BF16)
 
 
-def ring_kernel(keep, got, up, across, down, *outs):
+def ring_kernel(keep, got, down, across, up, *outs):
     for chunk, out in enumerate(outs):
         cols = pl.ds(chunk * COLS, COLS)
         out[:HALF, :] = keep[:, cols]
@@ -193,13 +193,12 @@
         slots = [group * GROUP + i for i in range(GROUP)]
         for slot in slots:
             pltpu.make_async_copy(pieces[0].at[pl.ds(0, BLOCK), :], blocks.at[slot], sems.at[slot]).wait()
-        lines = [pl.ds(pl.multiple_of(slot * BLOCK, BLOCK), BLOCK) for slot in slots]
-        pres = [rest_in[at, :] + dot(pick[at, :], blocks[slot]) for at, slot in zip(lines, slots)]
-        sigs = [sigmoid(pre) for pre in pres]
-        for at, pre, sig in zip(lines, pres, sigs):
+        for slot in slots:
+            at = pl.ds(pl.multiple_of(slot * BLOCK, BLOCK), BLOCK)
+            pre = rest_in[at, :] + dot(pick[at, :], blocks[slot])
+            sig = sigmoid(pre)
             slope[at, :] = sig * (1.0 + pre * (1.0 - sig))
-        sums = [dot(one_hot(recv, slot), (pre * sig).astype(BF16)) for slot, pre, sig in zip(slots, pres, sigs)]
-        for slot, value in zip(slots, sums):
+            value = dot(one_hot(recv, slot), (pre * sig).astype(BF16))
             mine, dz, row = mesh_place(mesh_block[slot], where)
             start = jnp.where(mine, 0, RING * HALF) + dz * HALF + row
             total[pl.ds(pl.multiple_of(start, BLOCK), BLOCK), :] += value
@@ -226,11 +225,14 @@
     grads[...] = dot_t(grad, w_out[...]).astype(BF16)
 
 
-def backward_kernel(where, live, grid_block, mesh_block, first_of, pick, send, *rest):
-    slopes, pieces, outs = rest[:CHUNKS], rest[CHUNKS : CHUNKS + 8], rest[CHUNKS + 8 : -2]
-    total, blocks = rest[-2:]
+def zeros_kernel(*outs):
     for out in outs:
         out[...] = jnp.zeros_like(out)
+
+
+def backward_kernel(where, live, grid_block, mesh_block, first_of, pick, send, *rest):
+    slopes, pieces = rest[:CHUNKS], rest[CHUNKS : CHUNKS + 8]
+    outs, (total, blocks) = rest[-2 - RING * CHUNKS - 2 : -2], rest[-2:]
 
     @pl.loop(0, live[0])
     def _(group):
@@ -244,14 +246,14 @@
                 def _():
                     blocks[i] = pieces[piece][pl.ds(pl.multiple_of(row, BLOCK), BLOCK), :]
 
-        lines = [pl.ds(pl.multiple_of(slot * BLOCK, BLOCK), BLOCK) for slot in slots]
-        hot = [one_hot(send, slot) for slot in slots]
-        for c in range(CHUNKS):
-            cols = pl.ds(c * COLS, COLS)
-            grads = [dot(pick[at, :], blocks[i, :, cols]) * slopes[c][at, :] for i, at in enumerate(lines)]
-            parts = [dot(hot[i], grad.astype(BF16)) for i, grad in enumerate(grads)]
-            for slot, part in zip(slots, parts):
-                first = first_of[slot]
+        for i, slot in enumerate(slots):
+            at = pl.ds(pl.multiple_of(slot * BLOCK, BLOCK), BLOCK)
+            hot = one_hot(send, slot)
+            first = first_of[slot]
+            for c in range(CHUNKS):
+                cols = pl.ds(c * COLS, COLS)
+                grad = dot(pick[at, :], blocks[i, :, cols]) * slopes[c][at, :]
+                part = dot(hot, grad.astype(BF16))
                 total[first, :, cols] = jnp.where(first == slot, 0.0, total[first, :, cols]) + part
 
     @pl.loop(0, live[0] * GROUP)
@@ -305,12 +307,19 @@
     out[...] = split_dot(value, w_grid[...], dot_t)
 
 
-def place_kernel(other, where, value, *rest):
-    out, sem = rest[-2:]
-    place = 1 - where[1] if other else where[1]
-    copy = pltpu.make_async_copy(value, out.at[pl.ds(pl.multiple_of(place * HALF, HALF), HALF), :], sem)
+def place(row, value, out, sem):
+    copy = pltpu.make_async_copy(value, out.at[pl.ds(pl.multiple_of(row, HALF), HALF), :], sem)
     copy.start()
     copy.wait()
+
+
+def place_other_kernel(where, value, out, sem):
+    place((1 - where[1]) * HALF, value, out, sem)
+
+
+def place_mine_kernel(where, w_grid, here, up, down, across, placed, out, value, sem):
+    row_sum_kernel(w_grid, here, up, down, across, value)
+    place(where[1] * HALF, value, out, sem)
 
 
 def per_device(
@@ -358,23 +367,23 @@
     )
     got = swap(give)
     mine = jnp.concatenate([keep, got], axis=0)
-    mesh_first = after(mesh_latent, mine)
-    mesh_pair = pair_z(mesh_first, 1), pair_z(mesh_first, 3)
+    mesh_then = after(mesh_latent, mine)
+    mesh_first, mesh_third = pair_z(mesh_then, 1), pair_z(mesh_then, 3)
 
     def far_gather(value):
-        return shift(value, False, 1), shift(value, False, -1)
+        return shift(value, False, -1), shift(value, False, 1)
 
     def give_rows(both, up, down):
         return jnp.concatenate([both[GATHERED:], up[GATHERED:], down[GATHERED:]], axis=0)
 
-    near = shift(mine, True, 1), shift(mine, True, 2), shift(mine, True, -1)
+    near = [shift(mine, True, step) for step in (-1, 2, 1)]
     ring_0, ring_1 = call(
-        ring_kernel, "ring", [shape(2 * GATHERED, COLS, BF16)] * CHUNKS, keep, got, *after(near, mesh_pair)
-    )
-
-    mesh_far = pair_z(after(mesh_pair[1], ring_0), 1)
-    (up_0, down_0), mesh_far = lax.optimization_barrier((far_gather(ring_0), mesh_far))
-    mesh_rows = jnp.concatenate([mesh_latent, mesh_pair[0], mesh_far, mesh_pair[1]], axis=0)
+        ring_kernel, "ring", [shape(2 * GATHERED, COLS, BF16)] * CHUNKS, keep, got, *after(near, (mesh_first, mesh_third))
+    )
+
+    mesh_far = pair_z(after(mesh_third, ring_0), 1)
+    (down_0, up_0), mesh_far = lax.optimization_barrier((far_gather(ring_0), mesh_far))
+    mesh_rows = jnp.concatenate([mesh_latent, mesh_first, mesh_far, mesh_third], axis=0)
     give = [give_rows(ring_0, up_0, down_0)] + [mesh_rows[:, c * COLS : (c + 1) * COLS] for c in both_chunks]
     got_0 = swap(jnp.concatenate(give, axis=0))
     across_0 = shift(up_0[:GATHERED], False, 1), shift(down_0[GATHERED:], False, -1)
@@ -400,7 +409,7 @@
 
     own_across, other_across = lax.optimization_barrier(across_0)
     far_got_0 = swap(other_across)
-    (up_1, down_1), edge_terms, got_0, far_got_0 = lax.optimization_barrier((far_1, edge_terms, got_0, far_got_0))
+    (down_1, up_1), edge_terms, got_0, far_got_0 = lax.optimization_barrier((far_1, edge_terms, got_0, far_got_0))
     across_1 = shift(up_1[:GATHERED], False, 1), shift(down_1[GATHERED:], False, -1)
 
     def forward(chunk, own, got):
@@ -451,12 +460,13 @@
     same = edge_grid_block[:, None] == edge_grid_block[None, :]
     first_of = jnp.min(jnp.where(same, slots[None, :], SLOTS), axis=1).astype(jnp.int32)
 
-    band = [grads, shift_z(grads, -1), shift_z(grads, 2), shift_z(grads, 1)]
-    partial = call(
-        backward_kernel,
-        "backward",
-        [shape(GATHERED, COLS, BF16)] * (RING * CHUNKS)
-        + [shape(CHUNKS * GATHERED, COLS, BF16), shape(3 * CHUNKS * GATHERED, COLS, BF16)],
+    partial_shapes = [shape(GATHERED, COLS, BF16)] * (RING * CHUNKS)
+    partial_shapes += [shape(CHUNKS * GATHERED, COLS, BF16), shape(3 * CHUNKS * GATHERED, COLS, BF16)]
+    zeros = call(zeros_kernel, "zeros", partial_shapes)
+    up, down, across = shift_z(grads, -1), shift_z(grads, 1), shift_z(grads, 2)
+    down, zeros = after((down, zeros), up)
+    band = [grads, up, across, down]
+    inputs = [
         where,
         live_groups,
         edge_grid_block,
@@ -467,9 +477,18 @@
         *slopes,
         *band,
         *[swap(p) for p in band],
-        scalars=5,
-        scratch=[pltpu.VMEM((SLOTS, BLOCK, WIDTH), F32), pltpu.VMEM((GROUP, BLOCK, WIDTH), BF16)],
-    )
+    ]
+    partial = pl.pallas_call(
+        backward_kernel,
+        in_specs=[SMEM] * 5 + [VMEM] * (len(inputs) - 5) + [VMEM] * len(zeros),
+        out_specs=[VMEM] * len(zeros),
+        out_shape=partial_shapes,
+        input_output_aliases={len(inputs) + i: i for i in range(len(zeros))},
+        scratch_shapes=[pltpu.VMEM((SLOTS, BLOCK, WIDTH), F32), pltpu.VMEM((GROUP, BLOCK, WIDTH), BF16)],
+        compiler_params=params(),
+        cost_estimate=LIGHT,
+        name="backward",
+    )(*inputs, *zeros)
     own_0, own_1, give_across, give_rest = partial[:RING], partial[RING : 2 * RING], partial[-2], partial[-1]
 
     def far_send(into, name, terms, *refs):
@@ -488,41 +507,45 @@
     def row_sum(name, terms):
         return call(row_sum_kernel, name, [shape(HALF, WIDTH, F32)], w_grid, *terms)[0]
 
-    into_mine = shift(own_0[2], False, 1), shift(own_1[2], False, -1)
     across = swap(give_across)
     rest = swap(after(give_rest, across))
     into_other = shift(across[:GATHERED], False, 1), shift(across[GATHERED:], False, -1)
-    far_mine, merged = far_send(
-        into_mine, "merge_mine", ((0, 0), (1, 0), (2, 0), (3, 0)), own_0[1], own_1[1], own_0[3], own_1[3]
-    )
+    into_mine = shift(own_0[2], False, 1), shift(own_1[2], False, -1)
     step = GATHERED
     far_other, merged = far_send(
-        into_other, "merge_other", ((0, step), (0, 4 * step), (0, 2 * step), (0, 5 * step)), after(rest, merged)
+        into_other, "merge_other", ((0, step), (0, 4 * step), (0, 2 * step), (0, 5 * step)), rest
+    )
+    far_mine, merged = far_send(
+        after(into_mine, merged), "merge_mine", ((0, 0), (1, 0), (2, 0), (3, 0)), own_0[1], own_1[1], own_0[3], own_1[3]
     )
     activation = jax.nn.silu(aggregate).astype(BF16)
     mesh_out = (mesh_latent.astype(F32) + dot(activation, w_node)).astype(BF16)
-    columns = column_sum(after(far_mine, (mesh_out, merged)), "column_sum_mine", ((0, 0), (1, 0)), own_0[0], own_1[0])
+    columns = column_sum(after(far_other, (mesh_out, merged)), "column_sum_other", ((0, 0), (0, 3 * step)), rest)
+    near_other = near_send(*columns)
+    columns = column_sum(after(far_mine, columns), "column_sum_mine", ((0, 0), (1, 0)), own_0[0], own_1[0])
     near_mine = near_send(*columns)
-    columns = column_sum(after(far_other, columns), "column_sum_other", ((0, 0), (0, 3 * step)), rest)
-    near_other = near_send(*columns)
-    mine = row_sum("row_sum_mine", after(near_mine, columns))
-
-    def place(name, other, value, *into):
-        return pl.pallas_call(
-            functools.partial(place_kernel, other),
-            in_specs=[SMEM, VMEM] + [ANY] * len(into),
-            out_specs=ANY,
-            out_shape=shape(2 * HALF, WIDTH, F32),
-            input_output_aliases={2: 0} if into else {},
-            scratch_shapes=[pltpu.SemaphoreType.DMA],
-            compiler_params=params(),
-            cost_estimate=LIGHT,
-            name=name,
-        )(where, value, *into)
-
-    half_done = place("place_mine", False, mine)
-    other = row_sum("row_sum_other", after(near_other, half_done))
-    grid_grad = place("place_other", True, swap(other), half_done)
+    other = swap(row_sum("row_sum_other", after(near_other, columns)))
+    placed = pl.pallas_call(
+        place_other_kernel,
+        in_specs=[SMEM, VMEM],
+        out_specs=ANY,
+        out_shape=shape(2 * HALF, WIDTH, F32),
+        scratch_shapes=[pltpu.SemaphoreType.DMA],
+        compiler_params=params(),
+        cost_estimate=LIGHT,
+        name="place_other",
+    )(where, other)
+    grid_grad = pl.pallas_call(
+        place_mine_kernel,
+        in_specs=[SMEM] + [VMEM] * 5 + [ANY],
+        out_specs=ANY,
+        out_shape=shape(2 * HALF, WIDTH, F32),
+        input_output_aliases={6: 0},
+        scratch_shapes=[pltpu.VMEM((HALF, WIDTH), F32), pltpu.SemaphoreType.DMA],
+        compiler_params=params(),
+        cost_estimate=LIGHT,
+        name="place_mine",
+    )(where, w_grid, *after(near_mine, placed), placed)
     return (mesh_out, grid_grad)
 
 

time: 193 us -> 188 us (0.974)
  Pallas kernels: 28.7 us -> 23.5 us
    pallas_call x14 -> x13, Pallas kernels: 26 us -> 16.3 us  [call(): pl.pallas_call(kernel, in_specs=whole, out_specs=[VMEM] * len(outs), out_...]
    ppermute x25, waiting for transfers between devices: 53.2 us -> 60.6 us  [shift(): return lax.ppermute(value, CHIP_AXES, along(first, step))]
    pallas_call x2 -> x3, Pallas kernels: 2.69 us -> 7.19 us  [the longest x1 4.02 us: per_device(): pl.pallas_call(backward_kernel, in_specs=[SMEM] * 5 + [VMEM] * (len(input...]
    ppermute x6, waiting for transfers between devices: 16.2 us -> 12 us  [shift_z(): lax.ppermute(value, 'z', [(i, (i + step) % RING) for i in range(RING)])]
  transfers between devices with their start and end apart: 48 -> 48, of which waited for: 32 -> 31; matrix products, arithmetic and copies ran while one was open for 1% -> 1% of each run, Pallas kernels for 7% -> 6%
where the time goes in v4:
time: 188 us; the launch traced here: 189 us
  waiting for transfers between devices  92.4 us (49%)
  starting transfers between devices  65.5 us (35%)
  Pallas kernels  23.5 us (12%)
  local copies, waits for them, and re-layouts  2.78 us (1%)
  between operations  1.94 us (1%)
    ppermute x25, waiting for transfers between devices, shift(): return lax.ppermute(value, CHIP_AXES, along(first, step))  60.6 us
    ppermute x25, starting transfers between devices, shift(): return lax.ppermute(value, CHIP_AXES, along(first, step))  30.6 us
    ppermute x14, starting transfers between devices, swap(): return lax.ppermute(value, 'core', [(0, 1), (1, 0)])  21.8 us
    pallas_call x13, Pallas kernels, call(): pl.pallas_call(kernel, in_specs=whole, out_specs=[VMEM] * len(outs), out_...  16.3 us
    ppermute x6, waiting for transfers between devices, shift_z(): lax.ppermute(value, 'z', [(i, (i + step) % RING) for i in range(RING)])  12 us
    ppermute x3, waiting for transfers between devices, pair_z(): return lax.ppermute(value, 'z', [(i, i ^ flip) for i in range(RING)])  11.3 us
    ppermute x14, waiting for transfers between devices, swap(): return lax.ppermute(value, 'core', [(0, 1), (1, 0)])  8.6 us
    ppermute x6, starting transfers between devices, shift_z(): lax.ppermute(value, 'z', [(i, (i + step) % RING) for i in range(RING)])  7.67 us
  transfers between devices with their start and end apart: 48, of which 31 were waited for; matrix products, arithmetic and copies ran while one was open for 1% of the time, Pallas kernels for 6%

profile of v4, /device:TPU:1, one launch (start us, length us, event | category | flops | bytes accessed | tf_op | source)
XLA Modules:
  0.0 188.6 jit_solution(16925024839318547718)
XLA Ops:
  0.7 1.1 copy-done.1
  1.8 1.0 copy-done.6
  2.9 1.0 first_product.1
  3.8 1.5 collective-permute-start
  5.4 1.1 collective-permute-done.got
  6.5 1.4 collective-permute-start.3
  8.0 2.6 %collective-permute-start.2 = (bf16[512,512]{1,0:T(8,128)(2,1)S(1)}, bf16[512,512]{1,0:T(8,128)(2,1)S(1)}, u32[]{:S(2)}, u32[]{:S(2)}) collective-permute-start(bf16[512,512]{1,0:T(8,128)(2,1)S(1)} %constant_dynamic-update-slice_fusion), channel_id=1, source_target_pairs={{0,8},{1,9},{2,10},{3,11},{4,12},{5,13},{6,14},{7,15},{8,0},{9,1},... | collective-permute-start | bytes 1572872 | tf_op jit(solution)/shard_map/ppermute | solution.py:54
  10.6 1.1 collective-permute-start.1
  11.7 3.8 %collective-permute-start.5 = (bf16[256,512]{1,0:T(8,128)(2,1)}, bf16[256,512]{1,0:T(8,128)(2,1)S(1)}, u32[]{:S(2)}, u32[]{:S(2)}) collective-permute-start(bf16[256,512]{1,0:T(8,128)(2,1)} %param.16), channel_id=1, source_target_pairs={{0,96},{32,64},{64,32},{96,0},{1,97},{33,65},{65,33},{97,1},{2,98}... | collective-permute-start | bytes 786440 | tf_op jit(solution)/shard_map/ppermute | solution.py:66
  15.4 5.8 %collective-permute-done.5 = bf16[256,512]{1,0:T(8,128)(2,1)S(1)} collective-permute-done((bf16[256,512]{1,0:T(8,128)(2,1)}, bf16[256,512]{1,0:T(8,128)(2,1)S(1)}, u32[]{:S(2)}, u32[]{:S(2)}) %collective-permute-start.5) | collective-permute-done | bytes 262176 | tf_op jit(solution)/shard_map/ppermute | solution.py:66
  22.1 1.0 collective-permute-done.2.across
  23.2 1.3 collective-permute-start.7
  24.5 1.4 collective-permute-start.6
  26.0 1.7 collective-permute-start.8
  27.8 4.6 %collective-permute-done.8 = bf16[256,512]{1,0:T(8,128)(2,1)S(1)} collective-permute-done((bf16[256,512]{1,0:T(8,128)(2,1)S(1)}, bf16[256,512]{1,0:T(8,128)(2,1)S(1)}, u32[]{:S(2)}, u32[]{:S(2)}) %collective-permute-start.8) | collective-permute-done | bytes 262176 | tf_op jit(solution)/shard_map/ppermute | solution.py:66
  32.4 6.1 %collective-permute-done.7.rest_1_ = bf16[2048,256]{1,0:T(8,128)(2,1)S(1)} collective-permute-done((bf16[2048,256]{1,0:T(8,128)(2,1)S(1)}, bf16[2048,256]{1,0:T(8,128)(2,1)S(1)}, u32[]{:S(2)}, u32[]{:S(2)}) %collective-permute-start.7) | collective-permute-done | bytes 1048608 | tf_op jit(solution)/shard_map/ppermute | solution.py:54
  38.8 2.3 %collective-permute-start.11 = (bf16[5120,256]{1,0:T(8,128)(2,1)S(1)}, bf16[5120,256]{1,0:T(8,128)(2,1)S(1)}, u32[]{:S(2)}, u32[]{:S(2)}) collective-permute-start(bf16[5120,256]{1,0:T(8,128)(2,1)S(1)} %slice_dynamic-update-slice_fusion), channel_id=1, source_target_pairs={{0,16},{16,0},{1,17},{17,1},{2,18},{18,2},{3,19},{19,3},{4,20},{20... | collective-permute-start | bytes 7864328 | tf_op jit(solution)/shard_map/ppermute | solution.py:70
  41.1 1.6 collective-permute-start.12
  42.7 1.1 collective-permute-start.13
  44.2 2.3 %collective-permute-start.9 = (bf16[2048,256]{1,0:T(8,128)(2,1)S(1)}, bf16[2048,256]{1,0:T(8,128)(2,1)S(1)}, u32[]{:S(2)}, u32[]{:S(2)}) collective-permute-start(bf16[2048,256]{1,0:T(8,128)(2,1)S(1)} %get-tuple-element.111.rest_0_), channel_id=1, source_target_pairs={{0,3},{1,0},{2,1},{3,2},{4,7},{5,4},{6,5},{7,6},{8,11},{9,8},{10,9... | collective-permute-start | bytes 3145736 | tf_op jit(solution)/shard_map/ppermute | solution.py:54
  46.4 4.2 %collective-permute-done.12.rest_2_ = bf16[1024,256]{1,0:T(8,128)(2,1)S(1)} collective-permute-done((bf16[1024,256]{1,0:T(8,128)(2,1)S(1)}, bf16[1024,256]{1,0:T(8,128)(2,1)S(1)}, u32[]{:S(2)}, u32[]{:S(2)}) %collective-permute-start.12) | collective-permute-done | bytes 524320 | tf_op jit(solution)/shard_map/ppermute | solution.py:54
  53.0 3.4 %edge_terms.1 = (f32[2048,256]{1,0:T(8,128)S(1)}, f32[2048,256]{1,0:T(8,128)S(1)}) custom-call(s32[4]{0:T(128)S(1)} %pad_add_fusion.where, s32[1]{0:T(128)S(6)} %copy.47.live, s32[16]{0:T(128)S(1)} %copy-done.10, bf16[2048,128]{1,0:T(8,128)(2,1)S(1)} %fusion.1.pick, bf16[2048,512]{1,0:T(8,128)(2,1)S(1)} %copy-done.3, bf16[512,512]{1,0:T(8,128)(2,1)S(1)} %copy-done.4, ...), custom_call_target="tpu_custom_call" | custom-call | tf_op jit(solution)/shard_map/edge_terms/pallas_call | solution.py:354
  56.5 5.4 %collective-permute-done.10.rest_1_ = bf16[2048,256]{1,0:T(8,128)(2,1)S(1)} collective-permute-done((bf16[2048,256]{1,0:T(8,128)(2,1)S(1)}, bf16[2048,256]{1,0:T(8,128)(2,1)S(1)}, u32[]{:S(2)}, u32[]{:S(2)}) %collective-permute-start.10) | collective-permute-done | bytes 1048608 | tf_op jit(solution)/shard_map/ppermute | solution.py:54
  62.5 1.0 collective-permute-start.17
  63.5 2.3 %collective-permute-start.16 = (bf16[1024,256]{1,0:T(8,128)(2,1)S(1)}, bf16[1024,256]{1,0:T(8,128)(2,1)S(1)}, u32[]{:S(2)}, u32[]{:S(2)}) collective-permute-start(bf16[1024,256]{1,0:T(8,128)(2,1)S(1)} %slice.45), channel_id=1, source_target_pairs={{0,3},{1,0},{2,1},{3,2},{4,7},{5,4},{6,5},{7,6},{8,11},{9,8},{10,9... | collective-permute-start | bytes 1572872 | tf_op jit(solution)/shard_map/ppermute | solution.py:54
  66.5 4.2 %forward_0.1 = (f32[2048,256]{1,0:T(8,128)S(1)}, f32[1024,256]{1,0:T(8,128)S(1)}, bf16[1024,256]{1,0:T(8,128)(2,1)S(1)}) custom-call(s32[4]{0:T(128)S(1)} %pad_add_fusion.where, s32[1]{0:T(128)S(6)} %copy.47.live, s32[16]{0:T(128)S(1)} %copy-done.11, s32[16]{0:T(128)S(1)} %copy-done.10, bf16[2048,128]{1,0:T(8,128)(2,1)S(1)} %fusion.2.pick, ...), custom_call_target="tpu_custom_call" | custom-call | tf_op jit(solution)/shard_map/forward_0/pallas_call | solution.py:354
  70.7 1.3 collective-permute-done.16
  72.0 3.3 %collective-permute-done.15.rest_2_ = bf16[1024,256]{1,0:T(8,128)(2,1)S(1)} collective-permute-done((bf16[1024,256]{1,0:T(8,128)(2,1)S(1)}, bf16[1024,256]{1,0:T(8,128)(2,1)S(1)}, u32[]{:S(2)}, u32[]{:S(2)}) %collective-permute-start.15) | collective-permute-done | bytes 524320 | tf_op jit(solution)/shard_map/ppermute | solution.py:54
  75.3 1.6 collective-permute-start.18
  76.9 1.5 collective-permute-done.18.rest_5_
  79.2 4.2 %forward_1.1 = (f32[2048,256]{1,0:T(8,128)S(1)}, f32[1024,256]{1,0:T(8,128)S(1)}, bf16[1024,256]{1,0:T(8,128)(2,1)S(1)}) custom-call(s32[4]{0:T(128)S(1)} %pad_add_fusion.where, s32[1]{0:T(128)S(6)} %copy.47.live, s32[16]{0:T(128)S(1)} %copy-done.11, s32[16]{0:T(128)S(1)} %copy-done.10, bf16[2048,128]{1,0:T(8,128)(2,1)S(1)} %fusion.2.pick, ...), custom_call_target="tpu_custom_call" | custom-call | tf_op jit(solution)/shard_map/forward_1/pallas_call | solution.py:354
  83.4 1.5 collective-permute-start.20
  85.0 1.5 collective-permute-done.20.refs_3_
  86.7 1.7 collective-permute-start.21
  88.4 1.1 collective-permute-start.22
  89.5 1.3 collective-permute-start.23
  90.7 4.8 %collective-permute-done.21.a = bf16[256,512]{1,0:T(8,128)(2,1)S(1)} collective-permute-done((bf16[256,512]{1,0:T(8,128)(2,1)S(1)}, bf16[256,512]{1,0:T(8,128)(2,1)S(1)}, u32[]{:S(2)}, u32[]{:S(2)}) %collective-permute-start.21) | collective-permute-done | bytes 262176 | tf_op jit(solution)/shard_map/ppermute | solution.py:58
  95.6 5.6 %collective-permute-done.23.c = bf16[256,512]{1,0:T(8,128)(2,1)S(1)} collective-permute-done((bf16[256,512]{1,0:T(8,128)(2,1)S(1)}, bf16[256,512]{1,0:T(8,128)(2,1)S(1)}, u32[]{:S(2)}, u32[]{:S(2)}) %collective-permute-start.23) | collective-permute-done | bytes 262176 | tf_op jit(solution)/shard_map/ppermute | solution.py:58
  102.6 2.1 %collective-permute-start.24 = (bf16[256,512]{1,0:T(8,128)(2,1)S(1)}, bf16[256,512]{1,0:T(8,128)(2,1)S(1)}, u32[]{:S(2)}, u32[]{:S(2)}) collective-permute-start(bf16[256,512]{1,0:T(8,128)(2,1)S(1)} %get-tuple-element.141.rest_2_), channel_id=1, source_target_pairs={{0,96},{32,0},{64,32},{96,64},{1,97},{33,1},{65,33},{97,65},{2,98}... | collective-permute-start | bytes 786440 | tf_op jit(solution)/shard_map/ppermute | solution.py:58
  106.2 2.2 %collective-permute-start.27 = (bf16[256,512]{1,0:T(8,128)(2,1)S(1)}, bf16[256,512]{1,0:T(8,128)(2,1)S(1)}, u32[]{:S(2)}, u32[]{:S(2)}) collective-permute-start(bf16[256,512]{1,0:T(8,128)(2,1)S(1)} %get-tuple-element.141.rest_2_), channel_id=1, source_target_pairs={{0,16},{16,0},{1,17},{17,1},{2,18},{18,2},{3,19},{19,3},{4,20},{20... | collective-permute-start | bytes 786440 | tf_op jit(solution)/shard_map/ppermute | solution.py:70
  108.4 1.5 collective-permute-done.26.rest_5_
  109.9 7.1 %collective-permute-start.28 = (bf16[256,512]{1,0:T(8,128)(2,1)S(1)}, bf16[256,512]{1,0:T(8,128)(2,1)S(1)}, u32[]{:S(2)}, u32[]{:S(2)}) collective-permute-start(bf16[256,512]{1,0:T(8,128)(2,1)S(1)} %collective-permute-done.24.rest_3_), channel_id=1, source_target_pairs={{0,16},{16,0},{1,17},{17,1},{2,18},{18,2},{3,19},{19,3},{4,20},{20... | collective-permute-start | bytes 786440 | tf_op jit(solution)/shard_map/ppermute | solution.py:70
  116.9 1.6 collective-permute-start.29
  118.7 1.0 collective-permute-done.29.rest_8_
  120.1 4.0 %backward.1 = (bf16[1024,256]{1,0:T(8,128)(2,1)S(1)}, bf16[1024,256]{1,0:T(8,128)(2,1)S(1)}, bf16[1024,256]{1,0:T(8,128)(2,1)S(1)}, bf16[1024,256]{1,0:T(8,128)(...) custom-call(s32[4]{0:T(128)S(1)} %pad_add_fusion.where, ...), custom_call_target="tpu_custom_call", output_to_operand_aliasing={{0}: (17, {}), {1}: (18, {}), {2}: (19, {}), {3}: (20, {}),... | custom-call | tf_op jit(solution)/shard_map/backward/pallas_call | solution.py:481
  124.1 1.6 collective-permute-start.33
  125.7 2.3 %collective-permute-done.33 = bf16[2048,256]{1,0:T(8,128)(2,1)S(1)} collective-permute-done((bf16[2048,256]{1,0:T(8,128)(2,1)S(1)}, bf16[2048,256]{1,0:T(8,128)(2,1)S(1)}, u32[]{:S(2)}, u32[]{:S(2)}) %collective-permute-start.33) | collective-permute-done | bytes 1048608 | tf_op jit(solution)/shard_map/ppermute | solution.py:70
  128.4 3.9 %collective-permute-start.36 = (bf16[1024,256]{1,0:T(8,128)(2,1)S(1)}, bf16[1024,256]{1,0:T(8,128)(2,1)S(1)}, u32[]{:S(2)}, u32[]{:S(2)}) collective-permute-start(bf16[1024,256]{1,0:T(8,128)(2,1)S(1)} %get-tuple-element.200), channel_id=1, source_target_pairs={{0,3},{1,0},{2,1},{3,2},{4,7},{5,4},{6,5},{7,6},{8,11},{9,8},{10,9... | collective-permute-start | bytes 1572872 | tf_op jit(solution)/shard_map/ppermute | solution.py:54
  133.1 1.9 collective-permute-start.32
  135.0 3.5 %collective-permute-done.36.refs_2_ = bf16[1024,256]{1,0:T(8,128)(2,1)S(1)} collective-permute-done((bf16[1024,256]{1,0:T(8,128)(2,1)S(1)}, bf16[1024,256]{1,0:T(8,128)(2,1)S(1)}, u32[]{:S(2)}, u32[]{:S(2)}) %collective-permute-start.36) | collective-permute-done | bytes 524320 | tf_op jit(solution)/shard_map/ppermute | solution.py:54
  138.5 3.3 %collective-permute-done.35.refs_1_ = bf16[1024,256]{1,0:T(8,128)(2,1)S(1)} collective-permute-done((bf16[1024,256]{1,0:T(8,128)(2,1)S(1)}, bf16[1024,256]{1,0:T(8,128)(2,1)S(1)}, u32[]{:S(2)}, u32[]{:S(2)}) %collective-permute-start.35) | collective-permute-done | bytes 524320 | tf_op jit(solution)/shard_map/ppermute | solution.py:54
  142.2 1.5 collective-permute-start.39
  143.6 3.8 %collective-permute-done.31.refs_4_ = bf16[1024,256]{1,0:T(8,128)(2,1)S(1)} collective-permute-done((bf16[1024,256]{1,0:T(8,128)(2,1)S(1)}, bf16[1024,256]{1,0:T(8,128)(2,1)S(1)}, u32[]{:S(2)}, u32[]{:S(2)}) %collective-permute-start.31) | collective-permute-done | bytes 524320 | tf_op jit(solution)/shard_map/ppermute | solution.py:54
  147.8 1.5 collective-permute-start.37
  149.3 1.0 fusion
  150.3 5.8 %collective-permute-done.40.refs_2_ = bf16[2048,256]{1,0:T(8,128)(2,1)S(1)} collective-permute-done((bf16[2048,256]{1,0:T(8,128)(2,1)S(1)}, bf16[2048,256]{1,0:T(8,128)(2,1)S(1)}, u32[]{:S(2)}, u32[]{:S(2)}) %collective-permute-start.40) | collective-permute-done | bytes 1048608 | tf_op jit(solution)/shard_map/ppermute | solution.py:54
  156.1 2.6 %collective-permute-done.39.refs_1_ = bf16[2048,256]{1,0:T(8,128)(2,1)S(1)} collective-permute-done((bf16[2048,256]{1,0:T(8,128)(2,1)S(1)}, bf16[2048,256]{1,0:T(8,128)(2,1)S(1)}, u32[]{:S(2)}, u32[]{:S(2)}) %collective-permute-start.39) | collective-permute-done | bytes 1048608 | tf_op jit(solution)/shard_map/ppermute | solution.py:54
  160.1 1.8 collective-permute-start.46
  161.8 10.3 %collective-permute-done.38.refs_3_ = bf16[2048,256]{1,0:T(8,128)(2,1)S(1)} collective-permute-done((bf16[2048,256]{1,0:T(8,128)(2,1)S(1)}, bf16[2048,256]{1,0:T(8,128)(2,1)S(1)}, u32[]{:S(2)}, u32[]{:S(2)}) %collective-permute-start.38) | collective-permute-done | bytes 1048608 | tf_op jit(solution)/shard_map/ppermute | solution.py:54
  172.1 3.1 %collective-permute-done.37.refs_2_ = bf16[2048,256]{1,0:T(8,128)(2,1)S(1)} collective-permute-done((bf16[2048,256]{1,0:T(8,128)(2,1)S(1)}, bf16[2048,256]{1,0:T(8,128)(2,1)S(1)}, u32[]{:S(2)}, u32[]{:S(2)}) %collective-permute-start.37) | collective-permute-done | bytes 1048608 | tf_op jit(solution)/shard_map/ppermute | solution.py:54
  177.3 1.8 collective-permute-start.43
  179.1 1.3 place_other.1.placed
  180.5 5.5 %collective-permute-done.41.up = bf16[256,512]{1,0:T(8,128)(2,1)S(1)} collective-permute-done((bf16[256,512]{1,0:T(8,128)(2,1)S(1)}, bf16[256,512]{1,0:T(8,128)(2,1)S(1)}, u32[]{:S(2)}, u32[]{:S(2)}) %collective-permute-start.41) | collective-permute-done | bytes 262176 | tf_op jit(solution)/shard_map/ppermute | solution.py:54
  186.6 1.8 place_mine.1
  (100 shorter events, 15.4 us)
Async XLA Ops:
  0.6 65.1 %copy-start = (bf16[512,512]{1,0:T(8,128)(2,1)S(1)}, bf16[512,512]{1,0:T(8,128)(2,1)}, u32[]{:S(2)}) copy-start(bf16[512,512]{1,0:T(8,128)(2,1)} %param.28) | copy-start | bytes 1572868
  0.7 1.1 copy-start.1
  1.8 1.0 copy-start.6
  2.9 23.1 %copy-start.14 = (bf16[256,512]{1,0:T(8,128)(2,1)S(1)}, bf16[256,512]{1,0:T(8,128)(2,1)}, u32[]{:S(2)}) copy-start(bf16[256,512]{1,0:T(8,128)(2,1)} %param.16) | copy-start | bytes 786436
  3.8 2.7 %collective-permute-start = (bf16[256,512]{1,0:T(8,128)(2,1)S(1)}, bf16[256,512]{1,0:T(8,128)(2,1)S(1)}, u32[]{:S(2)}, u32[]{:S(2)}) collective-permute-start(bf16[256,512]{1,0:T(8,128)(2,1)S(1)} %get-tuple-element.102), channel_id=1, source_target_pairs={{0,16},{16,0},{1,17},{17,1},{2,18},{18,2},{3,19},{19,3},{4,20},{20... | collective-permute-start | bytes 786440 | tf_op jit(solution)/shard_map/ppermute | solution.py:70
  6.5 15.6 %collective-permute-start.3 = (bf16[512,512]{1,0:T(8,128)(2,1)S(1)}, bf16[512,512]{1,0:T(8,128)(2,1)S(1)}, u32[]{:S(2)}, u32[]{:S(2)}) collective-permute-start(bf16[512,512]{1,0:T(8,128)(2,1)S(1)} %constant_dynamic-update-slice_fusion), channel_id=1, source_target_pairs={{0,4},{1,5},{2,6},{3,7},{4,8},{5,9},{6,10},{7,11},{8,12},{9,13},{1... | collective-permute-start | bytes 1572872 | tf_op jit(solution)/shard_map/ppermute | solution.py:54
  8.0 15.1 %collective-permute-start.2 = (bf16[512,512]{1,0:T(8,128)(2,1)S(1)}, bf16[512,512]{1,0:T(8,128)(2,1)S(1)}, u32[]{:S(2)}, u32[]{:S(2)}) collective-permute-start(bf16[512,512]{1,0:T(8,128)(2,1)S(1)} %constant_dynamic-update-slice_fusion), channel_id=1, source_target_pairs={{0,8},{1,9},{2,10},{3,11},{4,12},{5,13},{6,14},{7,15},{8,0},{9,1},... | collective-permute-start | bytes 1572872 | tf_op jit(solution)/shard_map/ppermute | solution.py:54
  10.6 12.5 %collective-permute-start.1 = (bf16[512,512]{1,0:T(8,128)(2,1)S(1)}, bf16[512,512]{1,0:T(8,128)(2,1)S(1)}, u32[]{:S(2)}, u32[]{:S(2)}) collective-permute-start(bf16[512,512]{1,0:T(8,128)(2,1)S(1)} %constant_dynamic-update-slice_fusion), channel_id=1, source_target_pairs={{0,12},{1,13},{2,14},{3,15},{4,0},{5,1},{6,2},{7,3},{8,4},{9,5},{1... | collective-permute-start | bytes 1572872 | tf_op jit(solution)/shard_map/ppermute | solution.py:54
  11.7 9.6 %collective-permute-start.5 = (bf16[256,512]{1,0:T(8,128)(2,1)}, bf16[256,512]{1,0:T(8,128)(2,1)S(1)}, u32[]{:S(2)}, u32[]{:S(2)}) collective-permute-start(bf16[256,512]{1,0:T(8,128)(2,1)} %param.16), channel_id=1, source_target_pairs={{0,96},{32,64},{64,32},{96,0},{1,97},{33,65},{65,33},{97,1},{2,98}... | collective-permute-start | bytes 786440 | tf_op jit(solution)/shard_map/ppermute | solution.py:66
  15.4 6.7 %collective-permute-start.4 = (bf16[256,512]{1,0:T(8,128)(2,1)}, bf16[256,512]{1,0:T(8,128)(2,1)S(1)}, u32[]{:S(2)}, u32[]{:S(2)}) collective-permute-start(bf16[256,512]{1,0:T(8,128)(2,1)} %param.16), channel_id=1, source_target_pairs={{0,32},{32,0},{64,96},{96,64},{1,33},{33,1},{65,97},{97,65},{2,34}... | collective-permute-start | bytes 786440 | tf_op jit(solution)/shard_map/ppermute | solution.py:66
  23.2 15.2 %collective-permute-start.7 = (bf16[2048,256]{1,0:T(8,128)(2,1)S(1)}, bf16[2048,256]{1,0:T(8,128)(2,1)S(1)}, u32[]{:S(2)}, u32[]{:S(2)}) collective-permute-start(bf16[2048,256]{1,0:T(8,128)(2,1)S(1)} %get-tuple-element.108.rest_0_), channel_id=1, source_target_pairs={{0,1},{1,2},{2,3},{3,0},{4,5},{5,6},{6,7},{7,4},{8,9},{9,10},{10,1... | collective-permute-start | bytes 3145736 | tf_op jit(solution)/shard_map/ppermute | solution.py:54
  24.5 13.9 %collective-permute-start.6 = (bf16[2048,256]{1,0:T(8,128)(2,1)S(1)}, bf16[2048,256]{1,0:T(8,128)(2,1)S(1)}, u32[]{:S(2)}, u32[]{:S(2)}) collective-permute-start(bf16[2048,256]{1,0:T(8,128)(2,1)S(1)} %get-tuple-element.108.rest_0_), channel_id=1, source_target_pairs={{0,3},{1,0},{2,1},{3,2},{4,7},{5,4},{6,5},{7,6},{8,11},{9,8},{10,9... | collective-permute-start | bytes 3145736 | tf_op jit(solution)/shard_map/ppermute | solution.py:54
  26.0 6.4 %collective-permute-start.8 = (bf16[256,512]{1,0:T(8,128)(2,1)S(1)}, bf16[256,512]{1,0:T(8,128)(2,1)S(1)}, u32[]{:S(2)}, u32[]{:S(2)}) collective-permute-start(bf16[256,512]{1,0:T(8,128)(2,1)S(1)} %collective-permute-done.5), channel_id=1, source_target_pairs={{0,32},{32,0},{64,96},{96,64},{1,33},{33,1},{65,97},{97,65},{2,34}... | collective-permute-start | bytes 786440 | tf_op jit(solution)/shard_map/ppermute | solution.py:66
  38.6 14.0 %copy-start.8 = (s32[16,128]{1,0:T(8,128)S(1)}, s32[16,128]{1,0:T(8,128)}, u32[]{:S(2)}) copy-start(s32[16,128]{1,0:T(8,128)} %recv.3) | copy-start | bytes 24580
  38.6 14.4 %copy-start.3 = (bf16[2048,512]{1,0:T(8,128)(2,1)S(1)}, bf16[2048,512]{1,0:T(8,128)(2,1)}, u32[]{:S(2)}) copy-start(bf16[2048,512]{1,0:T(8,128)(2,1)} %edge.1) | copy-start | bytes 6291460
  38.6 14.4 %copy-start.4 = (bf16[512,512]{1,0:T(8,128)(2,1)S(1)}, bf16[512,512]{1,0:T(8,128)(2,1)}, u32[]{:S(2)}) copy-start(bf16[512,512]{1,0:T(8,128)(2,1)} %w_mesh.1) | copy-start | bytes 1572868
  38.6 14.4 %copy-start.5 = (bf16[512,512]{1,0:T(8,128)(2,1)S(1)}, bf16[512,512]{1,0:T(8,128)(2,1)}, u32[]{:S(2)}) copy-start(bf16[512,512]{1,0:T(8,128)(2,1)} %w_edge.1) | copy-start | bytes 1572868
  38.6 14.4 %copy-start.10 = (s32[16]{0:T(128)S(1)}, s32[16]{0:T(128)}, u32[]{:S(2)}) copy-start(s32[16]{0:T(128)} %mesh_block.7) | copy-start | bytes 196
  38.6 14.4 %copy-start.12 = (f32[512]{0:T(512)S(1)}, f32[512]{0:T(512)}, u32[]{:S(2)}) copy-start(f32[512]{0:T(512)} %param.26) | copy-start | bytes 6148
  38.8 14.1 %collective-permute-start.11 = (bf16[5120,256]{1,0:T(8,128)(2,1)S(1)}, bf16[5120,256]{1,0:T(8,128)(2,1)S(1)}, u32[]{:S(2)}, u32[]{:S(2)}) collective-permute-start(bf16[5120,256]{1,0:T(8,128)(2,1)S(1)} %slice_dynamic-update-slice_fusion), channel_id=1, source_target_pairs={{0,16},{16,0},{1,17},{17,1},{2,18},{18,2},{3,19},{19,3},{4,20},{20... | collective-permute-start | bytes 7864328 | tf_op jit(solution)/shard_map/ppermute | solution.py:70
  41.1 9.5 %collective-permute-start.12 = (bf16[1024,256]{1,0:T(8,128)(2,1)S(1)}, bf16[1024,256]{1,0:T(8,128)(2,1)S(1)}, u32[]{:S(2)}, u32[]{:S(2)}) collective-permute-start(bf16[1024,256]{1,0:T(8,128)(2,1)S(1)} %get-tuple-element.206), channel_id=1, source_target_pairs={{0,1},{1,2},{2,3},{3,0},{4,5},{5,6},{6,7},{7,4},{8,9},{9,10},{10,1... | collective-permute-start | bytes 1572872 | tf_op jit(solution)/shard_map/ppermute | solution.py:54
  42.7 8.3 %collective-permute-start.13 = (bf16[1024,256]{1,0:T(8,128)(2,1)S(1)}, bf16[1024,256]{1,0:T(8,128)(2,1)S(1)}, u32[]{:S(2)}, u32[]{:S(2)}) collective-permute-start(bf16[1024,256]{1,0:T(8,128)(2,1)S(1)} %get-tuple-element.204), channel_id=1, source_target_pairs={{0,3},{1,0},{2,1},{3,2},{4,7},{5,4},{6,5},{7,6},{8,11},{9,8},{10,9... | collective-permute-start | bytes 1572872 | tf_op jit(solution)/shard_map/ppermute | solution.py:54
  43.8 18.1 %collective-permute-start.10 = (bf16[2048,256]{1,0:T(8,128)(2,1)S(1)}, bf16[2048,256]{1,0:T(8,128)(2,1)S(1)}, u32[]{:S(2)}, u32[]{:S(2)}) collective-permute-start(bf16[2048,256]{1,0:T(8,128)(2,1)S(1)} %get-tuple-element.111.rest_0_), channel_id=1, source_target_pairs={{0,1},{1,2},{2,3},{3,0},{4,5},{5,6},{6,7},{7,4},{8,9},{9,10},{10,1... | collective-permute-start | bytes 3145736 | tf_op jit(solution)/shard_map/ppermute | solution.py:54
  44.2 18.1 %collective-permute-start.9 = (bf16[2048,256]{1,0:T(8,128)(2,1)S(1)}, bf16[2048,256]{1,0:T(8,128)(2,1)S(1)}, u32[]{:S(2)}, u32[]{:S(2)}) collective-permute-start(bf16[2048,256]{1,0:T(8,128)(2,1)S(1)} %get-tuple-element.111.rest_0_), channel_id=1, source_target_pairs={{0,3},{1,0},{2,1},{3,2},{4,7},{5,4},{6,5},{7,6},{8,11},{9,8},{10,9... | collective-permute-start | bytes 3145736 | tf_op jit(solution)/shard_map/ppermute | solution.py:54
  51.0 11.2 %collective-permute-start.14 = (bf16[1024,256]{1,0:T(8,128)(2,1)S(1)}, bf16[1024,256]{1,0:T(8,128)(2,1)S(1)}, u32[]{:S(2)}, u32[]{:S(2)}) collective-permute-start(bf16[1024,256]{1,0:T(8,128)(2,1)S(1)} %collective-permute-done.13), channel_id=1, source_target_pairs={{0,16},{16,0},{1,17},{17,1},{2,18},{18,2},{3,19},{19,3},{4,20},{20... | collective-permute-start | bytes 1572872 | tf_op jit(solution)/shard_map/ppermute | solution.py:70
  62.3 3.5 %copy-start.13 = (bf16[256,512]{1,0:T(8,128)(2,1)S(1)}, bf16[256,512]{1,0:T(8,128)(2,1)}, u32[]{:S(2)}) copy-start(bf16[256,512]{1,0:T(8,128)(2,1)} %param.29) | copy-start | bytes 786436
  62.4 3.7 %copy-start.9 = (s32[16,128]{1,0:T(8,128)S(1)}, s32[16,128]{1,0:T(8,128)}, u32[]{:S(2)}) copy-start(s32[16,128]{1,0:T(8,128)} %send.1) | copy-start | bytes 24580
  62.4 4.1 %copy-start.11 = (s32[16]{0:T(128)S(1)}, s32[16]{0:T(128)}, u32[]{:S(2)}) copy-start(s32[16]{0:T(128)} %grid_block.5) | copy-start | bytes 196
  62.5 12.8 %collective-permute-start.17 = (bf16[3072,256]{1,0:T(8,128)(2,1)S(1)}, bf16[3072,256]{1,0:T(8,128)(2,1)S(1)}, u32[]{:S(2)}, u32[]{:S(2)}) collective-permute-start(bf16[3072,256]{1,0:T(8,128)(2,1)S(1)} %pad_maximum_fusion), channel_id=1, source_target_pairs={{0,16},{16,0},{1,17},{17,1},{2,18},{18,2},{3,19},{19,3},{4,20},{20... | collective-permute-start | bytes 4718600 | tf_op jit(solution)/shard_map/ppermute | solution.py:70
  63.5 8.5 %collective-permute-start.16 = (bf16[1024,256]{1,0:T(8,128)(2,1)S(1)}, bf16[1024,256]{1,0:T(8,128)(2,1)S(1)}, u32[]{:S(2)}, u32[]{:S(2)}) collective-permute-start(bf16[1024,256]{1,0:T(8,128)(2,1)S(1)} %slice.45), channel_id=1, source_target_pairs={{0,3},{1,0},{2,1},{3,2},{4,7},{5,4},{6,5},{7,6},{8,11},{9,8},{10,9... | collective-permute-start | bytes 1572872 | tf_op jit(solution)/shard_map/ppermute | solution.py:54
  65.8 9.5 %collective-permute-start.15 = (bf16[1024,256]{1,0:T(8,128)(2,1)S(1)}, bf16[1024,256]{1,0:T(8,128)(2,1)S(1)}, u32[]{:S(2)}, u32[]{:S(2)}) collective-permute-start(bf16[1024,256]{1,0:T(8,128)(2,1)S(1)} %get-tuple-element.203), channel_id=1, source_target_pairs={{0,1},{1,2},{2,3},{3,0},{4,5},{5,6},{6,7},{7,4},{8,9},{9,10},{10,1... | collective-permute-start | bytes 1572872 | tf_op jit(solution)/shard_map/ppermute | solution.py:54
  75.3 3.1 %collective-permute-start.18 = (bf16[1024,256]{1,0:T(8,128)(2,1)S(1)}, bf16[1024,256]{1,0:T(8,128)(2,1)S(1)}, u32[]{:S(2)}, u32[]{:S(2)}) collective-permute-start(bf16[1024,256]{1,0:T(8,128)(2,1)S(1)} %collective-permute-done.16), channel_id=1, source_target_pairs={{0,16},{16,0},{1,17},{17,1},{2,18},{18,2},{3,19},{19,3},{4,20},{20... | collective-permute-start | bytes 1572872 | tf_op jit(solution)/shard_map/ppermute | solution.py:70
  76.9 2.3 %collective-permute-start.19 = (bf16[1024,256]{1,0:T(8,128)(2,1)S(1)}, bf16[1024,256]{1,0:T(8,128)(2,1)S(1)}, u32[]{:S(2)}, u32[]{:S(2)}) collective-permute-start(bf16[1024,256]{1,0:T(8,128)(2,1)S(1)} %get-tuple-element.130), channel_id=1, source_target_pairs={{0,16},{16,0},{1,17},{17,1},{2,18},{18,2},{3,19},{19,3},{4,20},{20... | collective-permute-start | bytes 1572872 | tf_op jit(solution)/shard_map/ppermute | solution.py:70
  83.4 17.8 %copy-start.7 = (bf16[512,512]{1,0:T(8,128)(2,1)S(1)}, bf16[512,512]{1,0:T(8,128)(2,1)}, u32[]{:S(2)}) copy-start(bf16[512,512]{1,0:T(8,128)(2,1)} %w_out.1) | copy-start | bytes 1572868
  83.4 3.1 %collective-permute-start.20 = (bf16[1024,256]{1,0:T(8,128)(2,1)S(1)}, bf16[1024,256]{1,0:T(8,128)(2,1)S(1)}, u32[]{:S(2)}, u32[]{:S(2)}) collective-permute-start(bf16[1024,256]{1,0:T(8,128)(2,1)S(1)} %get-tuple-element.133), channel_id=1, source_target_pairs={{0,16},{16,0},{1,17},{17,1},{2,18},{18,2},{3,19},{19,3},{4,20},{20... | collective-permute-start | bytes 1572872 | tf_op jit(solution)/shard_map/ppermute | solution.py:70
  86.7 8.8 %collective-permute-start.21 = (bf16[256,512]{1,0:T(8,128)(2,1)S(1)}, bf16[256,512]{1,0:T(8,128)(2,1)S(1)}, u32[]{:S(2)}, u32[]{:S(2)}) collective-permute-start(bf16[256,512]{1,0:T(8,128)(2,1)S(1)} %get-tuple-element.135), channel_id=1, source_target_pairs={{0,32},{32,64},{64,96},{96,0},{1,33},{33,65},{65,97},{97,1},{2,34}... | collective-permute-start | bytes 786440 | tf_op jit(solution)/shard_map/ppermute | solution.py:58
  88.4 7.2 %collective-permute-start.22 = (bf16[256,512]{1,0:T(8,128)(2,1)S(1)}, bf16[256,512]{1,0:T(8,128)(2,1)S(1)}, u32[]{:S(2)}, u32[]{:S(2)}) collective-permute-start(bf16[256,512]{1,0:T(8,128)(2,1)S(1)} %get-tuple-element.136), channel_id=1, source_target_pairs={{0,96},{32,0},{64,32},{96,64},{1,97},{33,1},{65,33},{97,65},{2,98}... | collective-permute-start | bytes 786440 | tf_op jit(solution)/shard_map/ppermute | solution.py:58
  89.5 11.7 %collective-permute-start.23 = (bf16[256,512]{1,0:T(8,128)(2,1)S(1)}, bf16[256,512]{1,0:T(8,128)(2,1)S(1)}, u32[]{:S(2)}, u32[]{:S(2)}) collective-permute-start(bf16[256,512]{1,0:T(8,128)(2,1)S(1)} %get-tuple-element.137), channel_id=1, source_target_pairs={{0,64},{32,96},{64,0},{96,32},{1,65},{33,97},{65,1},{97,33},{2,66}... | collective-permute-start | bytes 786440 | tf_op jit(solution)/shard_map/ppermute | solution.py:58
  102.0 7.9 %collective-permute-start.26 = (bf16[256,512]{1,0:T(8,128)(2,1)S(1)}, bf16[256,512]{1,0:T(8,128)(2,1)S(1)}, u32[]{:S(2)}, u32[]{:S(2)}) collective-permute-start(bf16[256,512]{1,0:T(8,128)(2,1)S(1)} %get-tuple-element.141.rest_2_), channel_id=1, source_target_pairs={{0,32},{32,64},{64,96},{96,0},{1,33},{33,65},{65,97},{97,1},{2,34}... | collective-permute-start | bytes 786440 | tf_op jit(solution)/shard_map/ppermute | solution.py:58
  102.6 7.2 %collective-permute-start.24 = (bf16[256,512]{1,0:T(8,128)(2,1)S(1)}, bf16[256,512]{1,0:T(8,128)(2,1)S(1)}, u32[]{:S(2)}, u32[]{:S(2)}) collective-permute-start(bf16[256,512]{1,0:T(8,128)(2,1)S(1)} %get-tuple-element.141.rest_2_), channel_id=1, source_target_pairs={{0,96},{32,0},{64,32},{96,64},{1,97},{33,1},{65,33},{97,65},{2,98}... | collective-permute-start | bytes 786440 | tf_op jit(solution)/shard_map/ppermute | solution.py:58
  104.7 12.2 %collective-permute-start.25 = (bf16[256,512]{1,0:T(8,128)(2,1)S(1)}, bf16[256,512]{1,0:T(8,128)(2,1)S(1)}, u32[]{:S(2)}, u32[]{:S(2)}) collective-permute-start(bf16[256,512]{1,0:T(8,128)(2,1)S(1)} %get-tuple-element.141.rest_2_), channel_id=1, source_target_pairs={{0,64},{32,96},{64,0},{96,32},{1,65},{33,97},{65,1},{97,33},{2,66}... | collective-permute-start | bytes 786440 | tf_op jit(solution)/shard_map/ppermute | solution.py:58
  106.2 12.5 %collective-permute-start.27 = (bf16[256,512]{1,0:T(8,128)(2,1)S(1)}, bf16[256,512]{1,0:T(8,128)(2,1)S(1)}, u32[]{:S(2)}, u32[]{:S(2)}) collective-permute-start(bf16[256,512]{1,0:T(8,128)(2,1)S(1)} %get-tuple-element.141.rest_2_), channel_id=1, source_target_pairs={{0,16},{16,0},{1,17},{17,1},{2,18},{18,2},{3,19},{19,3},{4,20},{20... | collective-permute-start | bytes 786440 | tf_op jit(solution)/shard_map/ppermute | solution.py:70
  109.9 9.8 %collective-permute-start.28 = (bf16[256,512]{1,0:T(8,128)(2,1)S(1)}, bf16[256,512]{1,0:T(8,128)(2,1)S(1)}, u32[]{:S(2)}, u32[]{:S(2)}) collective-permute-start(bf16[256,512]{1,0:T(8,128)(2,1)S(1)} %collective-permute-done.24.rest_3_), channel_id=1, source_target_pairs={{0,16},{16,0},{1,17},{17,1},{2,18},{18,2},{3,19},{19,3},{4,20},{20... | collective-permute-start | bytes 786440 | tf_op jit(solution)/shard_map/ppermute | solution.py:70
  116.9 2.8 %collective-permute-start.29 = (bf16[256,512]{1,0:T(8,128)(2,1)S(1)}, bf16[256,512]{1,0:T(8,128)(2,1)S(1)}, u32[]{:S(2)}, u32[]{:S(2)}) collective-permute-start(bf16[256,512]{1,0:T(8,128)(2,1)S(1)} %collective-permute-done.25.rest_4_), channel_id=1, source_target_pairs={{0,16},{16,0},{1,17},{17,1},{2,18},{18,2},{3,19},{19,3},{4,20},{20... | collective-permute-start | bytes 786440 | tf_op jit(solution)/shard_map/ppermute | solution.py:70
  118.5 1.5 collective-permute-start.30
  124.1 3.9 %collective-permute-start.33 = (bf16[2048,256]{1,0:T(8,128)(2,1)S(1)}, bf16[2048,256]{1,0:T(8,128)(2,1)S(1)}, u32[]{:S(2)}, u32[]{:S(2)}) collective-permute-start(bf16[2048,256]{1,0:T(8,128)(2,1)S(1)} %get-tuple-element.172), channel_id=1, source_target_pairs={{0,16},{16,0},{1,17},{17,1},{2,18},{18,2},{3,19},{19,3},{4,20},{20... | collective-permute-start | bytes 3145736 | tf_op jit(solution)/shard_map/ppermute | solution.py:70
  128.0 13.9 %collective-permute-start.34 = (bf16[6144,256]{1,0:T(8,128)(2,1)S(1)}, bf16[6144,256]{1,0:T(8,128)(2,1)S(1)}, u32[]{:S(2)}, u32[]{:S(2)}) collective-permute-start(bf16[6144,256]{1,0:T(8,128)(2,1)S(1)} %get-tuple-element.173), channel_id=1, source_target_pairs={{0,16},{16,0},{1,17},{17,1},{2,18},{18,2},{3,19},{19,3},{4,20},{20... | collective-permute-start | bytes 9437192 | tf_op jit(solution)/shard_map/ppermute | solution.py:70
  128.4 10.1 %collective-permute-start.36 = (bf16[1024,256]{1,0:T(8,128)(2,1)S(1)}, bf16[1024,256]{1,0:T(8,128)(2,1)S(1)}, u32[]{:S(2)}, u32[]{:S(2)}) collective-permute-start(bf16[1024,256]{1,0:T(8,128)(2,1)S(1)} %get-tuple-element.200), channel_id=1, source_target_pairs={{0,3},{1,0},{2,1},{3,2},{4,7},{5,4},{6,5},{7,6},{8,11},{9,8},{10,9... | collective-permute-start | bytes 1572872 | tf_op jit(solution)/shard_map/ppermute | solution.py:54
  132.3 9.5 %collective-permute-start.35 = (bf16[1024,256]{1,0:T(8,128)(2,1)S(1)}, bf16[1024,256]{1,0:T(8,128)(2,1)S(1)}, u32[]{:S(2)}, u32[]{:S(2)}) collective-permute-start(bf16[1024,256]{1,0:T(8,128)(2,1)S(1)} %get-tuple-element.201), channel_id=1, source_target_pairs={{0,1},{1,2},{2,3},{3,0},{4,5},{5,6},{6,7},{7,4},{8,9},{9,10},{10,1... | collective-permute-start | bytes 1572872 | tf_op jit(solution)/shard_map/ppermute | solution.py:54
  132.3 15.2 %collective-permute-start.31 = (bf16[1024,256]{1,0:T(8,128)(2,1)S(1)}, bf16[1024,256]{1,0:T(8,128)(2,1)S(1)}, u32[]{:S(2)}, u32[]{:S(2)}) collective-permute-start(bf16[1024,256]{1,0:T(8,128)(2,1)S(1)} %get-tuple-element.169), channel_id=1, source_target_pairs={{0,1},{1,2},{2,3},{3,0},{4,5},{5,6},{6,7},{7,4},{8,9},{9,10},{10,1... | collective-permute-start | bytes 1572872 | tf_op jit(solution)/shard_map/ppermute | solution.py:54
  133.1 14.3 %collective-permute-start.32 = (bf16[1024,256]{1,0:T(8,128)(2,1)S(1)}, bf16[1024,256]{1,0:T(8,128)(2,1)S(1)}, u32[]{:S(2)}, u32[]{:S(2)}) collective-permute-start(bf16[1024,256]{1,0:T(8,128)(2,1)S(1)} %get-tuple-element.170), channel_id=1, source_target_pairs={{0,3},{1,0},{2,1},{3,2},{4,7},{5,4},{6,5},{7,6},{8,11},{9,8},{10,9... | collective-permute-start | bytes 1572872 | tf_op jit(solution)/shard_map/ppermute | solution.py:54
  142.1 14.0 %collective-permute-start.40 = (bf16[2048,256]{1,0:T(8,128)(2,1)S(1)}, bf16[2048,256]{1,0:T(8,128)(2,1)S(1)}, u32[]{:S(2)}, u32[]{:S(2)}) collective-permute-start(bf16[2048,256]{1,0:T(8,128)(2,1)S(1)} %get-tuple-element.179), channel_id=1, source_target_pairs={{0,3},{1,0},{2,1},{3,2},{4,7},{5,4},{6,5},{7,6},{8,11},{9,8},{10,9... | collective-permute-start | bytes 3145736 | tf_op jit(solution)/shard_map/ppermute | solution.py:54
  142.2 16.5 %collective-permute-start.39 = (bf16[2048,256]{1,0:T(8,128)(2,1)S(1)}, bf16[2048,256]{1,0:T(8,128)(2,1)S(1)}, u32[]{:S(2)}, u32[]{:S(2)}) collective-permute-start(bf16[2048,256]{1,0:T(8,128)(2,1)S(1)} %get-tuple-element.174), channel_id=1, source_target_pairs={{0,1},{1,2},{2,3},{3,0},{4,5},{5,6},{6,7},{7,4},{8,9},{9,10},{10,1... | collective-permute-start | bytes 3145736 | tf_op jit(solution)/shard_map/ppermute | solution.py:54
  147.7 24.4 %collective-permute-start.38 = (bf16[2048,256]{1,0:T(8,128)(2,1)S(1)}, bf16[2048,256]{1,0:T(8,128)(2,1)S(1)}, u32[]{:S(2)}, u32[]{:S(2)}) collective-permute-start(bf16[2048,256]{1,0:T(8,128)(2,1)S(1)} %get-tuple-element.178), channel_id=1, source_target_pairs={{0,3},{1,0},{2,1},{3,2},{4,7},{5,4},{6,5},{7,6},{8,11},{9,8},{10,9... | collective-permute-start | bytes 3145736 | tf_op jit(solution)/shard_map/ppermute | solution.py:54
  147.8 27.4 %collective-permute-start.37 = (bf16[2048,256]{1,0:T(8,128)(2,1)S(1)}, bf16[2048,256]{1,0:T(8,128)(2,1)S(1)}, u32[]{:S(2)}, u32[]{:S(2)}) collective-permute-start(bf16[2048,256]{1,0:T(8,128)(2,1)S(1)} %get-tuple-element.177), channel_id=1, source_target_pairs={{0,1},{1,2},{2,3},{3,0},{4,5},{5,6},{6,7},{7,4},{8,9},{9,10},{10,1... | collective-permute-start | bytes 3145736 | tf_op jit(solution)/shard_map/ppermute | solution.py:54
  159.1 16.6 %copy-start.2 = (bf16[512,512]{1,0:T(8,128)(2,1)S(1)}, bf16[512,512]{1,0:T(8,128)(2,1)}, u32[]{:S(2)}) copy-start(bf16[512,512]{1,0:T(8,128)(2,1)} %w_grid.5) | copy-start | bytes 1572868
  159.1 16.6 %collective-permute-start.44 = (bf16[256,512]{1,0:T(8,128)(2,1)S(1)}, bf16[256,512]{1,0:T(8,128)(2,1)S(1)}, u32[]{:S(2)}, u32[]{:S(2)}) collective-permute-start(bf16[256,512]{1,0:T(8,128)(2,1)S(1)} %get-tuple-element.183), channel_id=1, source_target_pairs={{0,4},{1,5},{2,6},{3,7},{4,8},{5,9},{6,10},{7,11},{8,12},{9,13},{1... | collective-permute-start | bytes 786440 | tf_op jit(solution)/shard_map/ppermute | solution.py:54
  159.1 16.5 %collective-permute-start.45 = (bf16[256,512]{1,0:T(8,128)(2,1)S(1)}, bf16[256,512]{1,0:T(8,128)(2,1)S(1)}, u32[]{:S(2)}, u32[]{:S(2)}) collective-permute-start(bf16[256,512]{1,0:T(8,128)(2,1)S(1)} %get-tuple-element.184), channel_id=1, source_target_pairs={{0,8},{1,9},{2,10},{3,11},{4,12},{5,13},{6,14},{7,15},{8,0},{9,1},... | collective-permute-start | bytes 786440 | tf_op jit(solution)/shard_map/ppermute | solution.py:54
  160.1 15.6 %collective-permute-start.46 = (bf16[256,512]{1,0:T(8,128)(2,1)S(1)}, bf16[256,512]{1,0:T(8,128)(2,1)S(1)}, u32[]{:S(2)}, u32[]{:S(2)}) collective-permute-start(bf16[256,512]{1,0:T(8,128)(2,1)S(1)} %get-tuple-element.185), channel_id=1, source_target_pairs={{0,12},{1,13},{2,14},{3,15},{4,0},{5,1},{6,2},{7,3},{8,4},{9,5},{1... | collective-permute-start | bytes 786440 | tf_op jit(solution)/shard_map/ppermute | solution.py:54
  176.1 3.0 %collective-permute-start.47 = (f32[256,512]{1,0:T(8,128)S(1)}, f32[256,512]{1,0:T(8,128)S(1)}, u32[]{:S(2)}, u32[]{:S(2)}) collective-permute-start(f32[256,512]{1,0:T(8,128)S(1)} %row_sum_other.1), channel_id=1, source_target_pairs={{0,16},{16,0},{1,17},{17,1},{2,18},{18,2},{3,19},{19,3},{4,20},{20... | collective-permute-start | bytes 1572872 | tf_op jit(solution)/shard_map/ppermute | solution.py:70
  176.4 9.5 %collective-permute-start.41 = (bf16[256,512]{1,0:T(8,128)(2,1)S(1)}, bf16[256,512]{1,0:T(8,128)(2,1)S(1)}, u32[]{:S(2)}, u32[]{:S(2)}) collective-permute-start(bf16[256,512]{1,0:T(8,128)(2,1)S(1)} %get-tuple-element.189), channel_id=1, source_target_pairs={{0,4},{1,5},{2,6},{3,7},{4,8},{5,9},{6,10},{7,11},{8,12},{9,13},{1... | collective-permute-start | bytes 786440 | tf_op jit(solution)/shard_map/ppermute | solution.py:54
  176.5 9.5 %collective-permute-start.42 = (bf16[256,512]{1,0:T(8,128)(2,1)S(1)}, bf16[256,512]{1,0:T(8,128)(2,1)S(1)}, u32[]{:S(2)}, u32[]{:S(2)}) collective-permute-start(bf16[256,512]{1,0:T(8,128)(2,1)S(1)} %get-tuple-element.190), channel_id=1, source_target_pairs={{0,8},{1,9},{2,10},{3,11},{4,12},{5,13},{6,14},{7,15},{8,0},{9,1},... | collective-permute-start | bytes 786440 | tf_op jit(solution)/shard_map/ppermute | solution.py:54
  177.3 9.2 %collective-permute-start.43 = (bf16[256,512]{1,0:T(8,128)(2,1)S(1)}, bf16[256,512]{1,0:T(8,128)(2,1)S(1)}, u32[]{:S(2)}, u32[]{:S(2)}) collective-permute-start(bf16[256,512]{1,0:T(8,128)(2,1)S(1)} %get-tuple-element.191), channel_id=1, source_target_pairs={{0,12},{1,13},{2,14},{3,15},{4,0},{5,1},{6,2},{7,3},{8,4},{9,5},{1... | collective-permute-start | bytes 786440 | tf_op jit(solution)/shard_map/ppermute | solution.py:54

commit v5 on v4

--- a/solution.py
+++ b/solution.py
@@ -261,7 +261,7 @@
         mine, near, far, row = grid_place(grid_block[slot], where)
         start = lax.rem(RING - near, RING) * HALF + row
         far = lax.rem(RING - far, RING)
-        at = jnp.where(first_of[slot] == slot, jnp.where(mine, far, jnp.where(far == 2, RING, RING + 1)), -1)
+        at = jnp.where(first_of[slot] == slot, jnp.where(mine, far, jnp.where(far == 0, RING, RING + 1)), -1)
         for step in range(RING + 2):
 
             @pl.when(at == step)
@@ -272,7 +272,7 @@
                     elif step == RING:
                         to, place = outs[-2], start + c * GATHERED
                     else:
-                        to, place = outs[-1], start + (3 * c + jnp.minimum(far, 2)) * GATHERED
+                        to, place = outs[-1], start + (3 * c + far - 1) * GATHERED
                     to[pl.ds(pl.multiple_of(place, BLOCK), BLOCK), :] = total[slot, :, pl.ds(c * COLS, COLS)].astype(BF16)
 
 
@@ -281,7 +281,7 @@
 
 
 def merge_kernel(terms, *refs):
-    into_up, into_down, out_up, out_down = refs[-4:]
+    into_down, into_up, out_up, out_down = refs[-4:]
     up_0, up_1, down_0, down_1 = [refs[i].at[pl.ds(base, GATHERED), :] for i, base in terms]
     out_up[:GATHERED, :] = add(up_0, into_up)
     out_up[GATHERED:, :] = up_1[...]
@@ -313,11 +313,11 @@
     copy.wait()
 
 
-def place_other_kernel(where, value, out, sem):
+def place_other_kernel(where, value, placed, out, sem):
     place((1 - where[1]) * HALF, value, out, sem)
 
 
-def place_mine_kernel(where, w_grid, here, up, down, across, placed, out, value, sem):
+def place_mine_kernel(where, w_grid, here, up, down, across, out, value, sem):
     row_sum_kernel(w_grid, here, up, down, across, value)
     place(where[1] * HALF, value, out, sem)
 
@@ -410,7 +410,7 @@
     own_across, other_across = lax.optimization_barrier(across_0)
     far_got_0 = swap(other_across)
     (down_1, up_1), edge_terms, got_0, far_got_0 = lax.optimization_barrier((far_1, edge_terms, got_0, far_got_0))
-    across_1 = shift(up_1[:GATHERED], False, 1), shift(down_1[GATHERED:], False, -1)
+    across_1 = shift(down_1[GATHERED:], False, -1), shift(up_1[:GATHERED], False, 1)
 
     def forward(chunk, own, got):
         return call(
@@ -444,7 +444,7 @@
 
     slope_0, near_sum_0, far_sum_0 = forward(0, (ring_0, up_0, own_across, down_0), (got_0, far_got_0))
     got_1 = swap(give_rows(ring_1, up_1, down_1))
-    (own_across, other_across), got_1, far_sum_0, cot = lax.optimization_barrier((across_1, got_1, far_sum_0, cot))
+    (other_across, own_across), got_1, far_sum_0, cot = lax.optimization_barrier((across_1, got_1, far_sum_0, cot))
     far_got_1, far_sum_0 = swap(other_across), swap(far_sum_0)
     slope_1, near_sum_1, far_sum_1 = forward(
         1, (ring_1, up_1, own_across, down_1), (got_1, after(far_got_1, far_sum_0))
@@ -489,12 +489,12 @@
         cost_estimate=LIGHT,
         name="backward",
     )(*inputs, *zeros)
-    own_0, own_1, give_across, give_rest = partial[:RING], partial[RING : 2 * RING], partial[-2], partial[-1]
+    own_0, own_1, give_here, give_far = partial[:RING], partial[RING : 2 * RING], partial[-2], partial[-1]
 
     def far_send(into, name, terms, *refs):
         kernel = functools.partial(merge_kernel, terms)
         up, down = call(kernel, name, [shape(2 * GATHERED, COLS, BF16)] * 2, *refs, *into)
-        return (shift(up, False, 1), shift(down, False, -1)), up
+        return (shift(down, False, -1), shift(up, False, 1)), up
 
     def column_sum(far, name, terms, *refs):
         kernel = functools.partial(column_sum_kernel, terms)
@@ -507,45 +507,45 @@
     def row_sum(name, terms):
         return call(row_sum_kernel, name, [shape(HALF, WIDTH, F32)], w_grid, *terms)[0]
 
-    across = swap(give_across)
-    rest = swap(after(give_rest, across))
-    into_other = shift(across[:GATHERED], False, 1), shift(across[GATHERED:], False, -1)
-    into_mine = shift(own_0[2], False, 1), shift(own_1[2], False, -1)
     step = GATHERED
+    into_mine = shift(own_1[2], False, -1), shift(own_0[2], False, 1)
+    given = swap(give_far)
+    into_other = [shift(given[step : 2 * step], False, 1), shift(given[4 * step : 5 * step], False, -1)]
+    far_mine, merged = far_send(
+        into_mine, "merge_mine", ((0, 0), (1, 0), (2, 0), (3, 0)), own_0[1], own_1[1], own_0[3], own_1[3]
+    )
     far_other, merged = far_send(
-        into_other, "merge_other", ((0, step), (0, 4 * step), (0, 2 * step), (0, 5 * step)), rest
-    )
-    far_mine, merged = far_send(
-        after(into_mine, merged), "merge_mine", ((0, 0), (1, 0), (2, 0), (3, 0)), own_0[1], own_1[1], own_0[3], own_1[3]
-    )
+        after(into_other, merged)[::-1], "merge_other", ((0, 0), (0, 3 * step), (0, 2 * step), (0, 5 * step)), given
+    )
+    given_here = swap(after(give_here, merged))
     activation = jax.nn.silu(aggregate).astype(BF16)
     mesh_out = (mesh_latent.astype(F32) + dot(activation, w_node)).astype(BF16)
-    columns = column_sum(after(far_other, (mesh_out, merged)), "column_sum_other", ((0, 0), (0, 3 * step)), rest)
+    columns = column_sum(after(far_mine, (mesh_out, merged, given_here)), "column_sum_mine", ((0, 0), (1, 0)), own_0[0], own_1[0])
+    near_mine = near_send(*columns)
+    columns = column_sum(after(far_other, columns), "column_sum_other", ((0, 0), (0, step)), given_here)
     near_other = near_send(*columns)
-    columns = column_sum(after(far_mine, columns), "column_sum_mine", ((0, 0), (1, 0)), own_0[0], own_1[0])
-    near_mine = near_send(*columns)
-    other = swap(row_sum("row_sum_other", after(near_other, columns)))
     placed = pl.pallas_call(
-        place_other_kernel,
-        in_specs=[SMEM, VMEM],
+        place_mine_kernel,
+        in_specs=[SMEM] + [VMEM] * 5,
         out_specs=ANY,
         out_shape=shape(2 * HALF, WIDTH, F32),
+        scratch_shapes=[pltpu.VMEM((HALF, WIDTH), F32), pltpu.SemaphoreType.DMA],
+        compiler_params=params(),
+        cost_estimate=LIGHT,
+        name="place_mine",
+    )(where, w_grid, *after(near_mine, columns))
+    other = swap(row_sum("row_sum_other", after(near_other, placed)))
+    grid_grad = pl.pallas_call(
+        place_other_kernel,
+        in_specs=[SMEM, VMEM, ANY],
+        out_specs=ANY,
+        out_shape=shape(2 * HALF, WIDTH, F32),
+        input_output_aliases={2: 0},
         scratch_shapes=[pltpu.SemaphoreType.DMA],
         compiler_params=params(),
         cost_estimate=LIGHT,
         name="place_other",
-    )(where, other)
-    grid_grad = pl.pallas_call(
-        place_mine_kernel,
-        in_specs=[SMEM] + [VMEM] * 5 + [ANY],
-        out_specs=ANY,
-        out_shape=shape(2 * HALF, WIDTH, F32),
-        input_output_aliases={6: 0},
-        scratch_shapes=[pltpu.VMEM((HALF, WIDTH), F32), pltpu.SemaphoreType.DMA],
-        compiler_params=params(),
-        cost_estimate=LIGHT,
-        name="place_mine",
-    )(where, w_grid, *after(near_mine, placed), placed)
+    )(where, other, placed)
     return (mesh_out, grid_grad)
 
 

time: 188 us -> 187 us (level)
  starting transfers between devices: 65.5 us -> 60.3 us
  waiting for transfers between devices: 92.4 us -> 95.1 us
    ppermute x14, waiting for transfers between devices: 8.6 us -> 12.3 us  [swap(): return lax.ppermute(value, 'core', [(0, 1), (1, 0)])]
    ppermute x14, starting transfers between devices: 21.8 us -> 18.4 us  [swap(): return lax.ppermute(value, 'core', [(0, 1), (1, 0)])]
    ppermute x25, starting transfers between devices: 30.6 us -> 27.3 us  [shift(): return lax.ppermute(value, CHIP_AXES, along(first, step))]
    ppermute x25, waiting for transfers between devices: 60.6 us -> 57.4 us  [shift(): return lax.ppermute(value, CHIP_AXES, along(first, step))]
    ppermute x6, waiting for transfers between devices: 12 us -> 14.1 us  [shift_z(): lax.ppermute(value, 'z', [(i, (i + step) % RING) for i in range(RING)])]
  transfers between devices with their start and end apart: 48 -> 48, of which waited for: 31 -> 33; matrix products, arithmetic and copies ran while one was open for 1% -> 1% of each run, Pallas kernels for 6% -> 6%
where the time goes in v5:
time: 187 us; the launch traced here: 186 us
  waiting for transfers between devices  95.1 us (51%)
  starting transfers between devices  60.3 us (32%)
  Pallas kernels  23.6 us (13%)
  local copies, waits for them, and re-layouts  2.78 us (1%)
  between operations  1.92 us (1%)
    ppermute x25, waiting for transfers between devices, shift(): return lax.ppermute(value, CHIP_AXES, along(first, step))  57.4 us
    ppermute x25, starting transfers between devices, shift(): return lax.ppermute(value, CHIP_AXES, along(first, step))  27.3 us
    ppermute x14, starting transfers between devices, swap(): return lax.ppermute(value, 'core', [(0, 1), (1, 0)])  18.4 us
    pallas_call x13, Pallas kernels, call(): pl.pallas_call(kernel, in_specs=whole, out_specs=[VMEM] * len(outs), out_...  16.3 us
    ppermute x6, waiting for transfers between devices, shift_z(): lax.ppermute(value, 'z', [(i, (i + step) % RING) for i in range(RING)])  14.1 us
    ppermute x14, waiting for transfers between devices, swap(): return lax.ppermute(value, 'core', [(0, 1), (1, 0)])  12.3 us
    ppermute x3, waiting for transfers between devices, pair_z(): return lax.ppermute(value, 'z', [(i, i ^ flip) for i in range(RING)])  11.3 us
    ppermute x6, starting transfers between devices, shift_z(): lax.ppermute(value, 'z', [(i, (i + step) % RING) for i in range(RING)])  9.09 us
  transfers between devices with their start and end apart: 48, of which 33 were waited for; matrix products, arithmetic and copies ran while one was open for 1% of the time, Pallas kernels for 6%

profile of v5, /device:TPU:1, one launch (start us, length us, event | category | flops | bytes accessed | tf_op | source)
XLA Modules:
  0.0 186.1 jit_solution(2649783830349941900)
XLA Ops:
  0.7 1.1 copy-done.1
  1.8 1.0 copy-done.6
  2.9 1.0 first_product.1
  3.8 1.5 collective-permute-start
  5.4 1.1 collective-permute-done.got
  6.5 1.4 collective-permute-start.3
  8.0 2.6 %collective-permute-start.2 = (bf16[512,512]{1,0:T(8,128)(2,1)S(1)}, bf16[512,512]{1,0:T(8,128)(2,1)S(1)}, u32[]{:S(2)}, u32[]{:S(2)}) collective-permute-start(bf16[512,512]{1,0:T(8,128)(2,1)S(1)} %constant_dynamic-update-slice_fusion), channel_id=1, source_target_pairs={{0,8},{1,9},{2,10},{3,11},{4,12},{5,13},{6,14},{7,15},{8,0},{9,1},... | collective-permute-start | bytes 1572872 | tf_op jit(solution)/shard_map/ppermute | solution.py:54
  10.6 1.1 collective-permute-start.1
  11.7 3.8 %collective-permute-start.5 = (bf16[256,512]{1,0:T(8,128)(2,1)}, bf16[256,512]{1,0:T(8,128)(2,1)S(1)}, u32[]{:S(2)}, u32[]{:S(2)}) collective-permute-start(bf16[256,512]{1,0:T(8,128)(2,1)} %param.16), channel_id=1, source_target_pairs={{0,96},{32,64},{64,32},{96,0},{1,97},{33,65},{65,33},{97,1},{2,98}... | collective-permute-start | bytes 786440 | tf_op jit(solution)/shard_map/ppermute | solution.py:66
  15.4 5.8 %collective-permute-done.5 = bf16[256,512]{1,0:T(8,128)(2,1)S(1)} collective-permute-done((bf16[256,512]{1,0:T(8,128)(2,1)}, bf16[256,512]{1,0:T(8,128)(2,1)S(1)}, u32[]{:S(2)}, u32[]{:S(2)}) %collective-permute-start.5) | collective-permute-done | bytes 262176 | tf_op jit(solution)/shard_map/ppermute | solution.py:66
  23.2 1.3 collective-permute-start.7
  24.5 1.4 collective-permute-start.6
  26.0 1.7 collective-permute-start.8
  27.8 4.6 %collective-permute-done.8 = bf16[256,512]{1,0:T(8,128)(2,1)S(1)} collective-permute-done((bf16[256,512]{1,0:T(8,128)(2,1)S(1)}, bf16[256,512]{1,0:T(8,128)(2,1)S(1)}, u32[]{:S(2)}, u32[]{:S(2)}) %collective-permute-start.8) | collective-permute-done | bytes 262176 | tf_op jit(solution)/shard_map/ppermute | solution.py:66
  32.4 6.1 %collective-permute-done.7.rest_1_ = bf16[2048,256]{1,0:T(8,128)(2,1)S(1)} collective-permute-done((bf16[2048,256]{1,0:T(8,128)(2,1)S(1)}, bf16[2048,256]{1,0:T(8,128)(2,1)S(1)}, u32[]{:S(2)}, u32[]{:S(2)}) %collective-permute-start.7) | collective-permute-done | bytes 1048608 | tf_op jit(solution)/shard_map/ppermute | solution.py:54
  38.8 2.3 %collective-permute-start.11 = (bf16[5120,256]{1,0:T(8,128)(2,1)S(1)}, bf16[5120,256]{1,0:T(8,128)(2,1)S(1)}, u32[]{:S(2)}, u32[]{:S(2)}) collective-permute-start(bf16[5120,256]{1,0:T(8,128)(2,1)S(1)} %slice_dynamic-update-slice_fusion), channel_id=1, source_target_pairs={{0,16},{16,0},{1,17},{17,1},{2,18},{18,2},{3,19},{19,3},{4,20},{20... | collective-permute-start | bytes 7864328 | tf_op jit(solution)/shard_map/ppermute | solution.py:70
  41.1 1.6 collective-permute-start.12
  42.7 1.1 collective-permute-start.13
  44.2 2.3 %collective-permute-start.9 = (bf16[2048,256]{1,0:T(8,128)(2,1)S(1)}, bf16[2048,256]{1,0:T(8,128)(2,1)S(1)}, u32[]{:S(2)}, u32[]{:S(2)}) collective-permute-start(bf16[2048,256]{1,0:T(8,128)(2,1)S(1)} %get-tuple-element.111.rest_0_), channel_id=1, source_target_pairs={{0,3},{1,0},{2,1},{3,2},{4,7},{5,4},{6,5},{7,6},{8,11},{9,8},{10,9... | collective-permute-start | bytes 3145736 | tf_op jit(solution)/shard_map/ppermute | solution.py:54
  46.4 4.2 %collective-permute-done.12.rest_2_ = bf16[1024,256]{1,0:T(8,128)(2,1)S(1)} collective-permute-done((bf16[1024,256]{1,0:T(8,128)(2,1)S(1)}, bf16[1024,256]{1,0:T(8,128)(2,1)S(1)}, u32[]{:S(2)}, u32[]{:S(2)}) %collective-permute-start.12) | collective-permute-done | bytes 524320 | tf_op jit(solution)/shard_map/ppermute | solution.py:54
  53.0 3.4 %edge_terms.1 = (f32[2048,256]{1,0:T(8,128)S(1)}, f32[2048,256]{1,0:T(8,128)S(1)}) custom-call(s32[4]{0:T(128)S(1)} %pad_add_fusion.where, s32[1]{0:T(128)S(6)} %copy.47.live, s32[16]{0:T(128)S(1)} %copy-done.10, bf16[2048,128]{1,0:T(8,128)(2,1)S(1)} %fusion.1.pick, bf16[2048,512]{1,0:T(8,128)(2,1)S(1)} %copy-done.3, bf16[512,512]{1,0:T(8,128)(2,1)S(1)} %copy-done.4, ...), custom_call_target="tpu_custom_call" | custom-call | tf_op jit(solution)/shard_map/edge_terms/pallas_call | solution.py:354
  56.5 5.4 %collective-permute-done.10.rest_1_ = bf16[2048,256]{1,0:T(8,128)(2,1)S(1)} collective-permute-done((bf16[2048,256]{1,0:T(8,128)(2,1)S(1)}, bf16[2048,256]{1,0:T(8,128)(2,1)S(1)}, u32[]{:S(2)}, u32[]{:S(2)}) %collective-permute-start.10) | collective-permute-done | bytes 1048608 | tf_op jit(solution)/shard_map/ppermute | solution.py:54
  62.5 1.0 collective-permute-start.17
  63.5 2.3 %collective-permute-start.15 = (bf16[1024,256]{1,0:T(8,128)(2,1)S(1)}, bf16[1024,256]{1,0:T(8,128)(2,1)S(1)}, u32[]{:S(2)}, u32[]{:S(2)}) collective-permute-start(bf16[1024,256]{1,0:T(8,128)(2,1)S(1)} %slice.44), channel_id=1, source_target_pairs={{0,3},{1,0},{2,1},{3,2},{4,7},{5,4},{6,5},{7,6},{8,11},{9,8},{10,9... | collective-permute-start | bytes 1572872 | tf_op jit(solution)/shard_map/ppermute | solution.py:54
  66.5 4.2 %forward_0.1 = (f32[2048,256]{1,0:T(8,128)S(1)}, f32[1024,256]{1,0:T(8,128)S(1)}, bf16[1024,256]{1,0:T(8,128)(2,1)S(1)}) custom-call(s32[4]{0:T(128)S(1)} %pad_add_fusion.where, s32[1]{0:T(128)S(6)} %copy.47.live, s32[16]{0:T(128)S(1)} %copy-done.11, s32[16]{0:T(128)S(1)} %copy-done.10, bf16[2048,128]{1,0:T(8,128)(2,1)S(1)} %fusion.2.pick, ...), custom_call_target="tpu_custom_call" | custom-call | tf_op jit(solution)/shard_map/forward_0/pallas_call | solution.py:354
  70.7 1.3 collective-permute-done.15
  72.0 3.3 %collective-permute-done.16.rest_2_ = bf16[1024,256]{1,0:T(8,128)(2,1)S(1)} collective-permute-done((bf16[1024,256]{1,0:T(8,128)(2,1)S(1)}, bf16[1024,256]{1,0:T(8,128)(2,1)S(1)}, u32[]{:S(2)}, u32[]{:S(2)}) %collective-permute-start.16) | collective-permute-done | bytes 524320 | tf_op jit(solution)/shard_map/ppermute | solution.py:54
  75.3 1.6 collective-permute-start.18
  76.9 1.5 collective-permute-done.18.rest_5_
  79.2 4.2 %forward_1.1 = (f32[2048,256]{1,0:T(8,128)S(1)}, f32[1024,256]{1,0:T(8,128)S(1)}, bf16[1024,256]{1,0:T(8,128)(2,1)S(1)}) custom-call(s32[4]{0:T(128)S(1)} %pad_add_fusion.where, s32[1]{0:T(128)S(6)} %copy.47.live, s32[16]{0:T(128)S(1)} %copy-done.11, s32[16]{0:T(128)S(1)} %copy-done.10, bf16[2048,128]{1,0:T(8,128)(2,1)S(1)} %fusion.2.pick, ...), custom_call_target="tpu_custom_call" | custom-call | tf_op jit(solution)/shard_map/forward_1/pallas_call | solution.py:354
  83.5 1.9 %collective-permute-done.20.refs_3_ = bf16[1024,256]{1,0:T(8,128)(2,1)S(1)} collective-permute-done((bf16[1024,256]{1,0:T(8,128)(2,1)S(1)}, bf16[1024,256]{1,0:T(8,128)(2,1)S(1)}, u32[]{:S(2)}, u32[]{:S(2)}) %collective-permute-start.20) | collective-permute-done | bytes 524320 | tf_op jit(solution)/shard_map/ppermute | solution.py:70
  85.6 1.7 collective-permute-start.21
  87.3 3.5 %collective-permute-start.22 = (bf16[256,512]{1,0:T(8,128)(2,1)S(1)}, bf16[256,512]{1,0:T(8,128)(2,1)S(1)}, u32[]{:S(2)}, u32[]{:S(2)}) collective-permute-start(bf16[256,512]{1,0:T(8,128)(2,1)S(1)} %get-tuple-element.136), channel_id=1, source_target_pairs={{0,96},{32,0},{64,32},{96,64},{1,97},{33,1},{65,33},{97,65},{2,98}... | collective-permute-start | bytes 786440 | tf_op jit(solution)/shard_map/ppermute | solution.py:58
  91.7 5.2 %collective-permute-done.21.a = bf16[256,512]{1,0:T(8,128)(2,1)S(1)} collective-permute-done((bf16[256,512]{1,0:T(8,128)(2,1)S(1)}, bf16[256,512]{1,0:T(8,128)(2,1)S(1)}, u32[]{:S(2)}, u32[]{:S(2)}) %collective-permute-start.21) | collective-permute-done | bytes 262176 | tf_op jit(solution)/shard_map/ppermute | solution.py:58
  96.9 4.7 %collective-permute-done.22.b = bf16[256,512]{1,0:T(8,128)(2,1)S(1)} collective-permute-done((bf16[256,512]{1,0:T(8,128)(2,1)S(1)}, bf16[256,512]{1,0:T(8,128)(2,1)S(1)}, u32[]{:S(2)}, u32[]{:S(2)}) %collective-permute-start.22) | collective-permute-done | bytes 262176 | tf_op jit(solution)/shard_map/ppermute | solution.py:58
  101.6 1.8 collective-permute-done.23.c
  104.8 2.1 %collective-permute-start.24 = (bf16[256,512]{1,0:T(8,128)(2,1)S(1)}, bf16[256,512]{1,0:T(8,128)(2,1)S(1)}, u32[]{:S(2)}, u32[]{:S(2)}) collective-permute-start(bf16[256,512]{1,0:T(8,128)(2,1)S(1)} %get-tuple-element.141.rest_2_), channel_id=1, source_target_pairs={{0,96},{32,0},{64,32},{96,64},{1,97},{33,1},{65,33},{97,65},{2,98}... | collective-permute-start | bytes 786440 | tf_op jit(solution)/shard_map/ppermute | solution.py:58
  107.7 1.8 collective-permute-start.27
  109.6 2.5 %collective-permute-done.26.rest_5_ = bf16[256,512]{1,0:T(8,128)(2,1)S(1)} collective-permute-done((bf16[256,512]{1,0:T(8,128)(2,1)S(1)}, bf16[256,512]{1,0:T(8,128)(2,1)S(1)}, u32[]{:S(2)}, u32[]{:S(2)}) %collective-permute-start.26) | collective-permute-done | bytes 262176 | tf_op jit(solution)/shard_map/ppermute | solution.py:58
  112.0 7.1 %collective-permute-start.28 = (bf16[256,512]{1,0:T(8,128)(2,1)S(1)}, bf16[256,512]{1,0:T(8,128)(2,1)S(1)}, u32[]{:S(2)}, u32[]{:S(2)}) collective-permute-start(bf16[256,512]{1,0:T(8,128)(2,1)S(1)} %collective-permute-done.24.rest_3_), channel_id=1, source_target_pairs={{0,16},{16,0},{1,17},{17,1},{2,18},{18,2},{3,19},{19,3},{4,20},{20... | collective-permute-start | bytes 786440 | tf_op jit(solution)/shard_map/ppermute | solution.py:70
  119.1 1.0 collective-permute-start.29
  121.6 4.0 %backward.1 = (bf16[1024,256]{1,0:T(8,128)(2,1)S(1)}, bf16[1024,256]{1,0:T(8,128)(2,1)S(1)}, bf16[1024,256]{1,0:T(8,128)(2,1)S(1)}, bf16[1024,256]{1,0:T(8,128)(...) custom-call(s32[4]{0:T(128)S(1)} %pad_add_fusion.where, ...), custom_call_target="tpu_custom_call", output_to_operand_aliasing={{0}: (17, {}), {1}: (18, {}), {2}: (19, {}), {3}: (20, {}),... | custom-call | tf_op jit(solution)/shard_map/backward/pallas_call | solution.py:481
  125.7 1.5 collective-permute-start.34
  127.3 4.1 %collective-permute-done.31.refs_0_ = bf16[6144,256]{1,0:T(8,128)(2,1)S(1)} collective-permute-done((bf16[6144,256]{1,0:T(8,128)(2,1)S(1)}, bf16[6144,256]{1,0:T(8,128)(2,1)S(1)}, u32[]{:S(2)}, u32[]{:S(2)}) %collective-permute-start.31) | collective-permute-done | bytes 3145760 | tf_op jit(solution)/shard_map/ppermute | solution.py:70
  131.4 1.2 collective-permute-start.33
  133.0 1.1 collective-permute-done.34.refs_4_
  134.1 3.2 %collective-permute-done.35.refs_5_ = bf16[1024,256]{1,0:T(8,128)(2,1)S(1)} collective-permute-done((bf16[1024,256]{1,0:T(8,128)(2,1)S(1)}, bf16[1024,256]{1,0:T(8,128)(2,1)S(1)}, u32[]{:S(2)}, u32[]{:S(2)}) %collective-permute-start.35) | collective-permute-done | bytes 524320 | tf_op jit(solution)/shard_map/ppermute | solution.py:54
  137.6 1.5 collective-permute-start.39
  139.8 3.1 %collective-permute-done.32.refs_2_ = bf16[1024,256]{1,0:T(8,128)(2,1)S(1)} collective-permute-done((bf16[1024,256]{1,0:T(8,128)(2,1)S(1)}, bf16[1024,256]{1,0:T(8,128)(2,1)S(1)}, u32[]{:S(2)}, u32[]{:S(2)}) %collective-permute-start.32) | collective-permute-done | bytes 524320 | tf_op jit(solution)/shard_map/ppermute | solution.py:54
  143.3 1.7 collective-permute-start.37
  145.0 1.0 fusion
  146.1 5.5 %collective-permute-done.39.refs_2_ = bf16[2048,256]{1,0:T(8,128)(2,1)S(1)} collective-permute-done((bf16[2048,256]{1,0:T(8,128)(2,1)S(1)}, bf16[2048,256]{1,0:T(8,128)(2,1)S(1)}, u32[]{:S(2)}, u32[]{:S(2)}) %collective-permute-start.39) | collective-permute-done | bytes 1048608 | tf_op jit(solution)/shard_map/ppermute | solution.py:54
  151.6 2.7 %collective-permute-done.40.refs_3_ = bf16[2048,256]{1,0:T(8,128)(2,1)S(1)} collective-permute-done((bf16[2048,256]{1,0:T(8,128)(2,1)S(1)}, bf16[2048,256]{1,0:T(8,128)(2,1)S(1)}, u32[]{:S(2)}, u32[]{:S(2)}) %collective-permute-start.40) | collective-permute-done | bytes 1048608 | tf_op jit(solution)/shard_map/ppermute | solution.py:54
  154.7 1.5 collective-permute-start.45
  156.2 1.2 collective-permute-start.46
  157.4 9.4 %collective-permute-done.37.refs_1_ = bf16[2048,256]{1,0:T(8,128)(2,1)S(1)} collective-permute-done((bf16[2048,256]{1,0:T(8,128)(2,1)S(1)}, bf16[2048,256]{1,0:T(8,128)(2,1)S(1)}, u32[]{:S(2)}, u32[]{:S(2)}) %collective-permute-start.37) | collective-permute-done | bytes 1048608 | tf_op jit(solution)/shard_map/ppermute | solution.py:54
  166.8 4.1 %collective-permute-done.38.refs_2_ = bf16[2048,256]{1,0:T(8,128)(2,1)S(1)} collective-permute-done((bf16[2048,256]{1,0:T(8,128)(2,1)S(1)}, bf16[2048,256]{1,0:T(8,128)(2,1)S(1)}, u32[]{:S(2)}, u32[]{:S(2)}) %collective-permute-start.38) | collective-permute-done | bytes 1048608 | tf_op jit(solution)/shard_map/ppermute | solution.py:54
  171.3 1.5 collective-permute-start.42
  172.8 1.2 collective-permute-start.43
  174.0 1.8 place_mine.1.placed
  175.8 5.0 %collective-permute-done.41.up = bf16[256,512]{1,0:T(8,128)(2,1)S(1)} collective-permute-done((bf16[256,512]{1,0:T(8,128)(2,1)S(1)}, bf16[256,512]{1,0:T(8,128)(2,1)S(1)}, u32[]{:S(2)}, u32[]{:S(2)}) %collective-permute-start.41) | collective-permute-done | bytes 262176 | tf_op jit(solution)/shard_map/ppermute | solution.py:54
  181.9 1.1 collective-permute-start.47
  183.0 1.5 collective-permute-done.47.value
  184.6 1.3 place_other.1
  (100 shorter events, 15.5 us)
Async XLA Ops:
  0.6 65.1 %copy-start = (bf16[512,512]{1,0:T(8,128)(2,1)S(1)}, bf16[512,512]{1,0:T(8,128)(2,1)}, u32[]{:S(2)}) copy-start(bf16[512,512]{1,0:T(8,128)(2,1)} %param.28) | copy-start | bytes 1572868
  0.7 1.1 copy-start.1
  1.8 1.0 copy-start.6
  2.9 23.1 %copy-start.14 = (bf16[256,512]{1,0:T(8,128)(2,1)S(1)}, bf16[256,512]{1,0:T(8,128)(2,1)}, u32[]{:S(2)}) copy-start(bf16[256,512]{1,0:T(8,128)(2,1)} %param.16) | copy-start | bytes 786436
  3.8 2.7 %collective-permute-start = (bf16[256,512]{1,0:T(8,128)(2,1)S(1)}, bf16[256,512]{1,0:T(8,128)(2,1)S(1)}, u32[]{:S(2)}, u32[]{:S(2)}) collective-permute-start(bf16[256,512]{1,0:T(8,128)(2,1)S(1)} %get-tuple-element.102), channel_id=1, source_target_pairs={{0,16},{16,0},{1,17},{17,1},{2,18},{18,2},{3,19},{19,3},{4,20},{20... | collective-permute-start | bytes 786440 | tf_op jit(solution)/shard_map/ppermute | solution.py:70
  6.5 15.6 %collective-permute-start.3 = (bf16[512,512]{1,0:T(8,128)(2,1)S(1)}, bf16[512,512]{1,0:T(8,128)(2,1)S(1)}, u32[]{:S(2)}, u32[]{:S(2)}) collective-permute-start(bf16[512,512]{1,0:T(8,128)(2,1)S(1)} %constant_dynamic-update-slice_fusion), channel_id=1, source_target_pairs={{0,4},{1,5},{2,6},{3,7},{4,8},{5,9},{6,10},{7,11},{8,12},{9,13},{1... | collective-permute-start | bytes 1572872 | tf_op jit(solution)/shard_map/ppermute | solution.py:54
  8.0 15.1 %collective-permute-start.2 = (bf16[512,512]{1,0:T(8,128)(2,1)S(1)}, bf16[512,512]{1,0:T(8,128)(2,1)S(1)}, u32[]{:S(2)}, u32[]{:S(2)}) collective-permute-start(bf16[512,512]{1,0:T(8,128)(2,1)S(1)} %constant_dynamic-update-slice_fusion), channel_id=1, source_target_pairs={{0,8},{1,9},{2,10},{3,11},{4,12},{5,13},{6,14},{7,15},{8,0},{9,1},... | collective-permute-start | bytes 1572872 | tf_op jit(solution)/shard_map/ppermute | solution.py:54
  10.6 12.5 %collective-permute-start.1 = (bf16[512,512]{1,0:T(8,128)(2,1)S(1)}, bf16[512,512]{1,0:T(8,128)(2,1)S(1)}, u32[]{:S(2)}, u32[]{:S(2)}) collective-permute-start(bf16[512,512]{1,0:T(8,128)(2,1)S(1)} %constant_dynamic-update-slice_fusion), channel_id=1, source_target_pairs={{0,12},{1,13},{2,14},{3,15},{4,0},{5,1},{6,2},{7,3},{8,4},{9,5},{1... | collective-permute-start | bytes 1572872 | tf_op jit(solution)/shard_map/ppermute | solution.py:54
  11.7 9.6 %collective-permute-start.5 = (bf16[256,512]{1,0:T(8,128)(2,1)}, bf16[256,512]{1,0:T(8,128)(2,1)S(1)}, u32[]{:S(2)}, u32[]{:S(2)}) collective-permute-start(bf16[256,512]{1,0:T(8,128)(2,1)} %param.16), channel_id=1, source_target_pairs={{0,96},{32,64},{64,32},{96,0},{1,97},{33,65},{65,33},{97,1},{2,98}... | collective-permute-start | bytes 786440 | tf_op jit(solution)/shard_map/ppermute | solution.py:66
  15.4 6.7 %collective-permute-start.4 = (bf16[256,512]{1,0:T(8,128)(2,1)}, bf16[256,512]{1,0:T(8,128)(2,1)S(1)}, u32[]{:S(2)}, u32[]{:S(2)}) collective-permute-start(bf16[256,512]{1,0:T(8,128)(2,1)} %param.16), channel_id=1, source_target_pairs={{0,32},{32,0},{64,96},{96,64},{1,33},{33,1},{65,97},{97,65},{2,34}... | collective-permute-start | bytes 786440 | tf_op jit(solution)/shard_map/ppermute | solution.py:66
  23.2 15.2 %collective-permute-start.7 = (bf16[2048,256]{1,0:T(8,128)(2,1)S(1)}, bf16[2048,256]{1,0:T(8,128)(2,1)S(1)}, u32[]{:S(2)}, u32[]{:S(2)}) collective-permute-start(bf16[2048,256]{1,0:T(8,128)(2,1)S(1)} %get-tuple-element.108.rest_0_), channel_id=1, source_target_pairs={{0,1},{1,2},{2,3},{3,0},{4,5},{5,6},{6,7},{7,4},{8,9},{9,10},{10,1... | collective-permute-start | bytes 3145736 | tf_op jit(solution)/shard_map/ppermute | solution.py:54
  24.5 13.9 %collective-permute-start.6 = (bf16[2048,256]{1,0:T(8,128)(2,1)S(1)}, bf16[2048,256]{1,0:T(8,128)(2,1)S(1)}, u32[]{:S(2)}, u32[]{:S(2)}) collective-permute-start(bf16[2048,256]{1,0:T(8,128)(2,1)S(1)} %get-tuple-element.108.rest_0_), channel_id=1, source_target_pairs={{0,3},{1,0},{2,1},{3,2},{4,7},{5,4},{6,5},{7,6},{8,11},{9,8},{10,9... | collective-permute-start | bytes 3145736 | tf_op jit(solution)/shard_map/ppermute | solution.py:54
  26.0 6.4 %collective-permute-start.8 = (bf16[256,512]{1,0:T(8,128)(2,1)S(1)}, bf16[256,512]{1,0:T(8,128)(2,1)S(1)}, u32[]{:S(2)}, u32[]{:S(2)}) collective-permute-start(bf16[256,512]{1,0:T(8,128)(2,1)S(1)} %collective-permute-done.5), channel_id=1, source_target_pairs={{0,32},{32,0},{64,96},{96,64},{1,33},{33,1},{65,97},{97,65},{2,34}... | collective-permute-start | bytes 786440 | tf_op jit(solution)/shard_map/ppermute | solution.py:66
  38.6 14.0 %copy-start.8 = (s32[16,128]{1,0:T(8,128)S(1)}, s32[16,128]{1,0:T(8,128)}, u32[]{:S(2)}) copy-start(s32[16,128]{1,0:T(8,128)} %recv.3) | copy-start | bytes 24580
  38.6 14.4 %copy-start.3 = (bf16[2048,512]{1,0:T(8,128)(2,1)S(1)}, bf16[2048,512]{1,0:T(8,128)(2,1)}, u32[]{:S(2)}) copy-start(bf16[2048,512]{1,0:T(8,128)(2,1)} %edge.1) | copy-start | bytes 6291460
  38.6 14.4 %copy-start.4 = (bf16[512,512]{1,0:T(8,128)(2,1)S(1)}, bf16[512,512]{1,0:T(8,128)(2,1)}, u32[]{:S(2)}) copy-start(bf16[512,512]{1,0:T(8,128)(2,1)} %w_mesh.1) | copy-start | bytes 1572868
  38.6 14.4 %copy-start.5 = (bf16[512,512]{1,0:T(8,128)(2,1)S(1)}, bf16[512,512]{1,0:T(8,128)(2,1)}, u32[]{:S(2)}) copy-start(bf16[512,512]{1,0:T(8,128)(2,1)} %w_edge.1) | copy-start | bytes 1572868
  38.6 14.4 %copy-start.10 = (s32[16]{0:T(128)S(1)}, s32[16]{0:T(128)}, u32[]{:S(2)}) copy-start(s32[16]{0:T(128)} %mesh_block.7) | copy-start | bytes 196
  38.6 14.4 %copy-start.12 = (f32[512]{0:T(512)S(1)}, f32[512]{0:T(512)}, u32[]{:S(2)}) copy-start(f32[512]{0:T(512)} %param.26) | copy-start | bytes 6148
  38.8 14.1 %collective-permute-start.11 = (bf16[5120,256]{1,0:T(8,128)(2,1)S(1)}, bf16[5120,256]{1,0:T(8,128)(2,1)S(1)}, u32[]{:S(2)}, u32[]{:S(2)}) collective-permute-start(bf16[5120,256]{1,0:T(8,128)(2,1)S(1)} %slice_dynamic-update-slice_fusion), channel_id=1, source_target_pairs={{0,16},{16,0},{1,17},{17,1},{2,18},{18,2},{3,19},{19,3},{4,20},{20... | collective-permute-start | bytes 7864328 | tf_op jit(solution)/shard_map/ppermute | solution.py:70
  41.1 9.5 %collective-permute-start.12 = (bf16[1024,256]{1,0:T(8,128)(2,1)S(1)}, bf16[1024,256]{1,0:T(8,128)(2,1)S(1)}, u32[]{:S(2)}, u32[]{:S(2)}) collective-permute-start(bf16[1024,256]{1,0:T(8,128)(2,1)S(1)} %get-tuple-element.206), channel_id=1, source_target_pairs={{0,1},{1,2},{2,3},{3,0},{4,5},{5,6},{6,7},{7,4},{8,9},{9,10},{10,1... | collective-permute-start | bytes 1572872 | tf_op jit(solution)/shard_map/ppermute | solution.py:54
  42.7 8.3 %collective-permute-start.13 = (bf16[1024,256]{1,0:T(8,128)(2,1)S(1)}, bf16[1024,256]{1,0:T(8,128)(2,1)S(1)}, u32[]{:S(2)}, u32[]{:S(2)}) collective-permute-start(bf16[1024,256]{1,0:T(8,128)(2,1)S(1)} %get-tuple-element.204), channel_id=1, source_target_pairs={{0,3},{1,0},{2,1},{3,2},{4,7},{5,4},{6,5},{7,6},{8,11},{9,8},{10,9... | collective-permute-start | bytes 1572872 | tf_op jit(solution)/shard_map/ppermute | solution.py:54
  43.8 18.1 %collective-permute-start.10 = (bf16[2048,256]{1,0:T(8,128)(2,1)S(1)}, bf16[2048,256]{1,0:T(8,128)(2,1)S(1)}, u32[]{:S(2)}, u32[]{:S(2)}) collective-permute-start(bf16[2048,256]{1,0:T(8,128)(2,1)S(1)} %get-tuple-element.111.rest_0_), channel_id=1, source_target_pairs={{0,1},{1,2},{2,3},{3,0},{4,5},{5,6},{6,7},{7,4},{8,9},{9,10},{10,1... | collective-permute-start | bytes 3145736 | tf_op jit(solution)/shard_map/ppermute | solution.py:54
  44.2 18.1 %collective-permute-start.9 = (bf16[2048,256]{1,0:T(8,128)(2,1)S(1)}, bf16[2048,256]{1,0:T(8,128)(2,1)S(1)}, u32[]{:S(2)}, u32[]{:S(2)}) collective-permute-start(bf16[2048,256]{1,0:T(8,128)(2,1)S(1)} %get-tuple-element.111.rest_0_), channel_id=1, source_target_pairs={{0,3},{1,0},{2,1},{3,2},{4,7},{5,4},{6,5},{7,6},{8,11},{9,8},{10,9... | collective-permute-start | bytes 3145736 | tf_op jit(solution)/shard_map/ppermute | solution.py:54
  51.0 11.2 %collective-permute-start.14 = (bf16[1024,256]{1,0:T(8,128)(2,1)S(1)}, bf16[1024,256]{1,0:T(8,128)(2,1)S(1)}, u32[]{:S(2)}, u32[]{:S(2)}) collective-permute-start(bf16[1024,256]{1,0:T(8,128)(2,1)S(1)} %collective-permute-done.13), channel_id=1, source_target_pairs={{0,16},{16,0},{1,17},{17,1},{2,18},{18,2},{3,19},{19,3},{4,20},{20... | collective-permute-start | bytes 1572872 | tf_op jit(solution)/shard_map/ppermute | solution.py:70
  62.3 3.5 %copy-start.13 = (bf16[256,512]{1,0:T(8,128)(2,1)S(1)}, bf16[256,512]{1,0:T(8,128)(2,1)}, u32[]{:S(2)}) copy-start(bf16[256,512]{1,0:T(8,128)(2,1)} %param.29) | copy-start | bytes 786436
  62.4 3.7 %copy-start.9 = (s32[16,128]{1,0:T(8,128)S(1)}, s32[16,128]{1,0:T(8,128)}, u32[]{:S(2)}) copy-start(s32[16,128]{1,0:T(8,128)} %send.1) | copy-start | bytes 24580
  62.4 4.1 %copy-start.11 = (s32[16]{0:T(128)S(1)}, s32[16]{0:T(128)}, u32[]{:S(2)}) copy-start(s32[16]{0:T(128)} %grid_block.5) | copy-start | bytes 196
  62.5 12.8 %collective-permute-start.17 = (bf16[3072,256]{1,0:T(8,128)(2,1)S(1)}, bf16[3072,256]{1,0:T(8,128)(2,1)S(1)}, u32[]{:S(2)}, u32[]{:S(2)}) collective-permute-start(bf16[3072,256]{1,0:T(8,128)(2,1)S(1)} %pad_maximum_fusion), channel_id=1, source_target_pairs={{0,16},{16,0},{1,17},{17,1},{2,18},{18,2},{3,19},{19,3},{4,20},{20... | collective-permute-start | bytes 4718600 | tf_op jit(solution)/shard_map/ppermute | solution.py:70
  63.5 8.5 %collective-permute-start.15 = (bf16[1024,256]{1,0:T(8,128)(2,1)S(1)}, bf16[1024,256]{1,0:T(8,128)(2,1)S(1)}, u32[]{:S(2)}, u32[]{:S(2)}) collective-permute-start(bf16[1024,256]{1,0:T(8,128)(2,1)S(1)} %slice.44), channel_id=1, source_target_pairs={{0,3},{1,0},{2,1},{3,2},{4,7},{5,4},{6,5},{7,6},{8,11},{9,8},{10,9... | collective-permute-start | bytes 1572872 | tf_op jit(solution)/shard_map/ppermute | solution.py:54
  65.8 9.5 %collective-permute-start.16 = (bf16[1024,256]{1,0:T(8,128)(2,1)S(1)}, bf16[1024,256]{1,0:T(8,128)(2,1)S(1)}, u32[]{:S(2)}, u32[]{:S(2)}) collective-permute-start(bf16[1024,256]{1,0:T(8,128)(2,1)S(1)} %get-tuple-element.203), channel_id=1, source_target_pairs={{0,1},{1,2},{2,3},{3,0},{4,5},{5,6},{6,7},{7,4},{8,9},{9,10},{10,1... | collective-permute-start | bytes 1572872 | tf_op jit(solution)/shard_map/ppermute | solution.py:54
  75.3 3.1 %collective-permute-start.18 = (bf16[1024,256]{1,0:T(8,128)(2,1)S(1)}, bf16[1024,256]{1,0:T(8,128)(2,1)S(1)}, u32[]{:S(2)}, u32[]{:S(2)}) collective-permute-start(bf16[1024,256]{1,0:T(8,128)(2,1)S(1)} %collective-permute-done.15), channel_id=1, source_target_pairs={{0,16},{16,0},{1,17},{17,1},{2,18},{18,2},{3,19},{19,3},{4,20},{20... | collective-permute-start | bytes 1572872 | tf_op jit(solution)/shard_map/ppermute | solution.py:70
  76.9 2.3 %collective-permute-start.19 = (bf16[1024,256]{1,0:T(8,128)(2,1)S(1)}, bf16[1024,256]{1,0:T(8,128)(2,1)S(1)}, u32[]{:S(2)}, u32[]{:S(2)}) collective-permute-start(bf16[1024,256]{1,0:T(8,128)(2,1)S(1)} %get-tuple-element.130), channel_id=1, source_target_pairs={{0,16},{16,0},{1,17},{17,1},{2,18},{18,2},{3,19},{19,3},{4,20},{20... | collective-permute-start | bytes 1572872 | tf_op jit(solution)/shard_map/ppermute | solution.py:70
  83.4 19.9 %copy-start.7 = (bf16[512,512]{1,0:T(8,128)(2,1)S(1)}, bf16[512,512]{1,0:T(8,128)(2,1)}, u32[]{:S(2)}) copy-start(bf16[512,512]{1,0:T(8,128)(2,1)} %w_out.1) | copy-start | bytes 1572868
  83.4 2.0 %collective-permute-start.20 = (bf16[1024,256]{1,0:T(8,128)(2,1)S(1)}, bf16[1024,256]{1,0:T(8,128)(2,1)S(1)}, u32[]{:S(2)}, u32[]{:S(2)}) collective-permute-start(bf16[1024,256]{1,0:T(8,128)(2,1)S(1)} %get-tuple-element.133), channel_id=1, source_target_pairs={{0,16},{16,0},{1,17},{17,1},{2,18},{18,2},{3,19},{19,3},{4,20},{20... | collective-permute-start | bytes 1572872 | tf_op jit(solution)/shard_map/ppermute | solution.py:70
  85.6 11.3 %collective-permute-start.21 = (bf16[256,512]{1,0:T(8,128)(2,1)S(1)}, bf16[256,512]{1,0:T(8,128)(2,1)S(1)}, u32[]{:S(2)}, u32[]{:S(2)}) collective-permute-start(bf16[256,512]{1,0:T(8,128)(2,1)S(1)} %get-tuple-element.135), channel_id=1, source_target_pairs={{0,32},{32,64},{64,96},{96,0},{1,33},{33,65},{65,97},{97,1},{2,34}... | collective-permute-start | bytes 786440 | tf_op jit(solution)/shard_map/ppermute | solution.py:58
  87.3 14.3 %collective-permute-start.22 = (bf16[256,512]{1,0:T(8,128)(2,1)S(1)}, bf16[256,512]{1,0:T(8,128)(2,1)S(1)}, u32[]{:S(2)}, u32[]{:S(2)}) collective-permute-start(bf16[256,512]{1,0:T(8,128)(2,1)S(1)} %get-tuple-element.136), channel_id=1, source_target_pairs={{0,96},{32,0},{64,32},{96,64},{1,97},{33,1},{65,33},{97,65},{2,98}... | collective-permute-start | bytes 786440 | tf_op jit(solution)/shard_map/ppermute | solution.py:58
  90.8 12.6 %collective-permute-start.23 = (bf16[256,512]{1,0:T(8,128)(2,1)S(1)}, bf16[256,512]{1,0:T(8,128)(2,1)S(1)}, u32[]{:S(2)}, u32[]{:S(2)}) collective-permute-start(bf16[256,512]{1,0:T(8,128)(2,1)S(1)} %get-tuple-element.137), channel_id=1, source_target_pairs={{0,64},{32,96},{64,0},{96,32},{1,65},{33,97},{65,1},{97,33},{2,66}... | collective-permute-start | bytes 786440 | tf_op jit(solution)/shard_map/ppermute | solution.py:58
  104.2 7.9 %collective-permute-start.26 = (bf16[256,512]{1,0:T(8,128)(2,1)S(1)}, bf16[256,512]{1,0:T(8,128)(2,1)S(1)}, u32[]{:S(2)}, u32[]{:S(2)}) collective-permute-start(bf16[256,512]{1,0:T(8,128)(2,1)S(1)} %get-tuple-element.141.rest_2_), channel_id=1, source_target_pairs={{0,32},{32,64},{64,96},{96,0},{1,33},{33,65},{65,97},{97,1},{2,34}... | collective-permute-start | bytes 786440 | tf_op jit(solution)/shard_map/ppermute | solution.py:58
  104.8 7.2 %collective-permute-start.24 = (bf16[256,512]{1,0:T(8,128)(2,1)S(1)}, bf16[256,512]{1,0:T(8,128)(2,1)S(1)}, u32[]{:S(2)}, u32[]{:S(2)}) collective-permute-start(bf16[256,512]{1,0:T(8,128)(2,1)S(1)} %get-tuple-element.141.rest_2_), channel_id=1, source_target_pairs={{0,96},{32,0},{64,32},{96,64},{1,97},{33,1},{65,33},{97,65},{2,98}... | collective-permute-start | bytes 786440 | tf_op jit(solution)/shard_map/ppermute | solution.py:58
  106.9 12.2 %collective-permute-start.25 = (bf16[256,512]{1,0:T(8,128)(2,1)S(1)}, bf16[256,512]{1,0:T(8,128)(2,1)S(1)}, u32[]{:S(2)}, u32[]{:S(2)}) collective-permute-start(bf16[256,512]{1,0:T(8,128)(2,1)S(1)} %get-tuple-element.141.rest_2_), channel_id=1, source_target_pairs={{0,64},{32,96},{64,0},{96,32},{1,65},{33,97},{65,1},{97,33},{2,66}... | collective-permute-start | bytes 786440 | tf_op jit(solution)/shard_map/ppermute | solution.py:58
  107.7 12.5 %collective-permute-start.27 = (bf16[256,512]{1,0:T(8,128)(2,1)S(1)}, bf16[256,512]{1,0:T(8,128)(2,1)S(1)}, u32[]{:S(2)}, u32[]{:S(2)}) collective-permute-start(bf16[256,512]{1,0:T(8,128)(2,1)S(1)} %get-tuple-element.141.rest_2_), channel_id=1, source_target_pairs={{0,16},{16,0},{1,17},{17,1},{2,18},{18,2},{3,19},{19,3},{4,20},{20... | collective-permute-start | bytes 786440 | tf_op jit(solution)/shard_map/ppermute | solution.py:70
  112.0 9.2 %collective-permute-start.28 = (bf16[256,512]{1,0:T(8,128)(2,1)S(1)}, bf16[256,512]{1,0:T(8,128)(2,1)S(1)}, u32[]{:S(2)}, u32[]{:S(2)}) collective-permute-start(bf16[256,512]{1,0:T(8,128)(2,1)S(1)} %collective-permute-done.24.rest_3_), channel_id=1, source_target_pairs={{0,16},{16,0},{1,17},{17,1},{2,18},{18,2},{3,19},{19,3},{4,20},{20... | collective-permute-start | bytes 786440 | tf_op jit(solution)/shard_map/ppermute | solution.py:70
  119.1 2.1 %collective-permute-start.29 = (bf16[256,512]{1,0:T(8,128)(2,1)S(1)}, bf16[256,512]{1,0:T(8,128)(2,1)S(1)}, u32[]{:S(2)}, u32[]{:S(2)}) collective-permute-start(bf16[256,512]{1,0:T(8,128)(2,1)S(1)} %collective-permute-done.25.rest_4_), channel_id=1, source_target_pairs={{0,16},{16,0},{1,17},{17,1},{2,18},{18,2},{3,19},{19,3},{4,20},{20... | collective-permute-start | bytes 786440 | tf_op jit(solution)/shard_map/ppermute | solution.py:70
  120.1 1.5 collective-permute-start.30
  125.6 5.7 %collective-permute-start.31 = (bf16[6144,256]{1,0:T(8,128)(2,1)S(1)}, bf16[6144,256]{1,0:T(8,128)(2,1)S(1)}, u32[]{:S(2)}, u32[]{:S(2)}) collective-permute-start(bf16[6144,256]{1,0:T(8,128)(2,1)S(1)} %get-tuple-element.164), channel_id=1, source_target_pairs={{0,16},{16,0},{1,17},{17,1},{2,18},{18,2},{3,19},{19,3},{4,20},{20... | collective-permute-start | bytes 9437192 | tf_op jit(solution)/shard_map/ppermute | solution.py:70
  125.7 8.4 %collective-permute-start.34 = (bf16[1024,256]{1,0:T(8,128)(2,1)S(1)}, bf16[1024,256]{1,0:T(8,128)(2,1)S(1)}, u32[]{:S(2)}, u32[]{:S(2)}) collective-permute-start(bf16[1024,256]{1,0:T(8,128)(2,1)S(1)} %get-tuple-element.169), channel_id=1, source_target_pairs={{0,3},{1,0},{2,1},{3,2},{4,7},{5,4},{6,5},{7,6},{8,11},{9,8},{10,9... | collective-permute-start | bytes 1572872 | tf_op jit(solution)/shard_map/ppermute | solution.py:54
  127.2 10.1 %collective-permute-start.35 = (bf16[1024,256]{1,0:T(8,128)(2,1)S(1)}, bf16[1024,256]{1,0:T(8,128)(2,1)S(1)}, u32[]{:S(2)}, u32[]{:S(2)}) collective-permute-start(bf16[1024,256]{1,0:T(8,128)(2,1)S(1)} %get-tuple-element.170), channel_id=1, source_target_pairs={{0,1},{1,2},{2,3},{3,0},{4,5},{5,6},{6,7},{7,4},{8,9},{9,10},{10,1... | collective-permute-start | bytes 1572872 | tf_op jit(solution)/shard_map/ppermute | solution.py:54
  131.4 8.4 %collective-permute-start.33 = (bf16[1024,256]{1,0:T(8,128)(2,1)S(1)}, bf16[1024,256]{1,0:T(8,128)(2,1)S(1)}, u32[]{:S(2)}, u32[]{:S(2)}) collective-permute-start(bf16[1024,256]{1,0:T(8,128)(2,1)S(1)} %get-tuple-element.200), channel_id=1, source_target_pairs={{0,3},{1,0},{2,1},{3,2},{4,7},{5,4},{6,5},{7,6},{8,11},{9,8},{10,9... | collective-permute-start | bytes 1572872 | tf_op jit(solution)/shard_map/ppermute | solution.py:54
  132.7 10.3 %collective-permute-start.32 = (bf16[1024,256]{1,0:T(8,128)(2,1)S(1)}, bf16[1024,256]{1,0:T(8,128)(2,1)S(1)}, u32[]{:S(2)}, u32[]{:S(2)}) collective-permute-start(bf16[1024,256]{1,0:T(8,128)(2,1)S(1)} %get-tuple-element.201), channel_id=1, source_target_pairs={{0,1},{1,2},{2,3},{3,0},{4,5},{5,6},{6,7},{7,4},{8,9},{9,10},{10,1... | collective-permute-start | bytes 1572872 | tf_op jit(solution)/shard_map/ppermute | solution.py:54
  137.6 14.0 %collective-permute-start.39 = (bf16[2048,256]{1,0:T(8,128)(2,1)S(1)}, bf16[2048,256]{1,0:T(8,128)(2,1)S(1)}, u32[]{:S(2)}, u32[]{:S(2)}) collective-permute-start(bf16[2048,256]{1,0:T(8,128)(2,1)S(1)} %get-tuple-element.179), channel_id=1, source_target_pairs={{0,3},{1,0},{2,1},{3,2},{4,7},{5,4},{6,5},{7,6},{8,11},{9,8},{10,9... | collective-permute-start | bytes 3145736 | tf_op jit(solution)/shard_map/ppermute | solution.py:54
  139.1 15.2 %collective-permute-start.40 = (bf16[2048,256]{1,0:T(8,128)(2,1)S(1)}, bf16[2048,256]{1,0:T(8,128)(2,1)S(1)}, u32[]{:S(2)}, u32[]{:S(2)}) collective-permute-start(bf16[2048,256]{1,0:T(8,128)(2,1)S(1)} %get-tuple-element.171), channel_id=1, source_target_pairs={{0,1},{1,2},{2,3},{3,0},{4,5},{5,6},{6,7},{7,4},{8,9},{9,10},{10,1... | collective-permute-start | bytes 3145736 | tf_op jit(solution)/shard_map/ppermute | solution.py:54
  143.2 11.1 %collective-permute-start.36 = (bf16[2048,256]{1,0:T(8,128)(2,1)S(1)}, bf16[2048,256]{1,0:T(8,128)(2,1)S(1)}, u32[]{:S(2)}, u32[]{:S(2)}) collective-permute-start(bf16[2048,256]{1,0:T(8,128)(2,1)S(1)} %get-tuple-element.175), channel_id=1, source_target_pairs={{0,16},{16,0},{1,17},{17,1},{2,18},{18,2},{3,19},{19,3},{4,20},{20... | collective-permute-start | bytes 3145736 | tf_op jit(solution)/shard_map/ppermute | solution.py:70
  143.3 23.5 %collective-permute-start.37 = (bf16[2048,256]{1,0:T(8,128)(2,1)S(1)}, bf16[2048,256]{1,0:T(8,128)(2,1)S(1)}, u32[]{:S(2)}, u32[]{:S(2)}) collective-permute-start(bf16[2048,256]{1,0:T(8,128)(2,1)S(1)} %get-tuple-element.176), channel_id=1, source_target_pairs={{0,3},{1,0},{2,1},{3,2},{4,7},{5,4},{6,5},{7,6},{8,11},{9,8},{10,9... | collective-permute-start | bytes 3145736 | tf_op jit(solution)/shard_map/ppermute | solution.py:54
  145.0 25.8 %collective-permute-start.38 = (bf16[2048,256]{1,0:T(8,128)(2,1)S(1)}, bf16[2048,256]{1,0:T(8,128)(2,1)S(1)}, u32[]{:S(2)}, u32[]{:S(2)}) collective-permute-start(bf16[2048,256]{1,0:T(8,128)(2,1)S(1)} %get-tuple-element.174), channel_id=1, source_target_pairs={{0,1},{1,2},{2,3},{3,0},{4,5},{5,6},{6,7},{7,4},{8,9},{9,10},{10,1... | collective-permute-start | bytes 3145736 | tf_op jit(solution)/shard_map/ppermute | solution.py:54
  154.3 19.7 %copy-start.2 = (bf16[512,512]{1,0:T(8,128)(2,1)S(1)}, bf16[512,512]{1,0:T(8,128)(2,1)}, u32[]{:S(2)}) copy-start(bf16[512,512]{1,0:T(8,128)(2,1)} %w_grid.5) | copy-start | bytes 1572868
  154.6 18.1 %collective-permute-start.44 = (bf16[256,512]{1,0:T(8,128)(2,1)S(1)}, bf16[256,512]{1,0:T(8,128)(2,1)S(1)}, u32[]{:S(2)}, u32[]{:S(2)}) collective-permute-start(bf16[256,512]{1,0:T(8,128)(2,1)S(1)} %get-tuple-element.183), channel_id=1, source_target_pairs={{0,4},{1,5},{2,6},{3,7},{4,8},{5,9},{6,10},{7,11},{8,12},{9,13},{1... | collective-permute-start | bytes 786440 | tf_op jit(solution)/shard_map/ppermute | solution.py:54
  154.7 19.2 %collective-permute-start.45 = (bf16[256,512]{1,0:T(8,128)(2,1)S(1)}, bf16[256,512]{1,0:T(8,128)(2,1)S(1)}, u32[]{:S(2)}, u32[]{:S(2)}) collective-permute-start(bf16[256,512]{1,0:T(8,128)(2,1)S(1)} %get-tuple-element.184), channel_id=1, source_target_pairs={{0,8},{1,9},{2,10},{3,11},{4,12},{5,13},{6,14},{7,15},{8,0},{9,1},... | collective-permute-start | bytes 786440 | tf_op jit(solution)/shard_map/ppermute | solution.py:54
  156.2 17.8 %collective-permute-start.46 = (bf16[256,512]{1,0:T(8,128)(2,1)S(1)}, bf16[256,512]{1,0:T(8,128)(2,1)S(1)}, u32[]{:S(2)}, u32[]{:S(2)}) collective-permute-start(bf16[256,512]{1,0:T(8,128)(2,1)S(1)} %get-tuple-element.185), channel_id=1, source_target_pairs={{0,12},{1,13},{2,14},{3,15},{4,0},{5,1},{6,2},{7,3},{8,4},{9,5},{1... | collective-permute-start | bytes 786440 | tf_op jit(solution)/shard_map/ppermute | solution.py:54
  171.2 9.6 %collective-permute-start.41 = (bf16[256,512]{1,0:T(8,128)(2,1)S(1)}, bf16[256,512]{1,0:T(8,128)(2,1)S(1)}, u32[]{:S(2)}, u32[]{:S(2)}) collective-permute-start(bf16[256,512]{1,0:T(8,128)(2,1)S(1)} %get-tuple-element.189), channel_id=1, source_target_pairs={{0,4},{1,5},{2,6},{3,7},{4,8},{5,9},{6,10},{7,11},{8,12},{9,13},{1... | collective-permute-start | bytes 786440 | tf_op jit(solution)/shard_map/ppermute | solution.py:54
  171.3 9.5 %collective-permute-start.42 = (bf16[256,512]{1,0:T(8,128)(2,1)S(1)}, bf16[256,512]{1,0:T(8,128)(2,1)S(1)}, u32[]{:S(2)}, u32[]{:S(2)}) collective-permute-start(bf16[256,512]{1,0:T(8,128)(2,1)S(1)} %get-tuple-element.190), channel_id=1, source_target_pairs={{0,8},{1,9},{2,10},{3,11},{4,12},{5,13},{6,14},{7,15},{8,0},{9,1},... | collective-permute-start | bytes 786440 | tf_op jit(solution)/shard_map/ppermute | solution.py:54
  172.8 8.7 %collective-permute-start.43 = (bf16[256,512]{1,0:T(8,128)(2,1)S(1)}, bf16[256,512]{1,0:T(8,128)(2,1)S(1)}, u32[]{:S(2)}, u32[]{:S(2)}) collective-permute-start(bf16[256,512]{1,0:T(8,128)(2,1)S(1)} %get-tuple-element.191), channel_id=1, source_target_pairs={{0,12},{1,13},{2,14},{3,15},{4,0},{5,1},{6,2},{7,3},{8,4},{9,5},{1... | collective-permute-start | bytes 786440 | tf_op jit(solution)/shard_map/ppermute | solution.py:54
  181.9 2.6 %collective-permute-start.47 = (f32[256,512]{1,0:T(8,128)S(1)}, f32[256,512]{1,0:T(8,128)S(1)}, u32[]{:S(2)}, u32[]{:S(2)}) collective-permute-start(f32[256,512]{1,0:T(8,128)S(1)} %row_sum_other.1), channel_id=1, source_target_pairs={{0,16},{16,0},{1,17},{17,1},{2,18},{18,2},{3,19},{19,3},{4,20},{20... | collective-permute-start | bytes 1572872 | tf_op jit(solution)/shard_map/ppermute | solution.py:70

commit v6 on v5

--- a/solution.py
+++ b/solution.py
@@ -447,7 +447,7 @@
     (other_across, own_across), got_1, far_sum_0, cot = lax.optimization_barrier((across_1, got_1, far_sum_0, cot))
     far_got_1, far_sum_0 = swap(other_across), swap(far_sum_0)
     slope_1, near_sum_1, far_sum_1 = forward(
-        1, (ring_1, up_1, own_across, down_1), (got_1, after(far_got_1, far_sum_0))
+        1, (ring_1, up_1, own_across, down_1), (got_1, far_got_1)
     )
     sums = band_sum(*pair_sum(near_sum_0, near_sum_1, far_sum_0, swap(far_sum_1)))
     slopes = [slope_0, slope_1]

time: 187 us -> 186 us (level)
  starting transfers between devices: 60.3 us -> 63.1 us
  waiting for transfers between devices: 95.1 us -> 92.4 us
    ppermute x25, starting transfers between devices: 27.3 us -> 30.6 us  [shift(): return lax.ppermute(value, CHIP_AXES, along(first, step))]
    ppermute x14, waiting for transfers between devices: 12.3 us -> 9.3 us  [swap(): return lax.ppermute(value, 'core', [(0, 1), (1, 0)])]
  transfers between devices with their start and end apart: 48 -> 48, of which waited for: 33 -> 32; matrix products, arithmetic and copies ran while one was open for 1% -> 1% of each run, Pallas kernels for 6% -> 8%
where the time goes in v6:
time: 186 us
  waiting for transfers between devices  92.4 us (50%)
  starting transfers between devices  63.1 us (34%)
  Pallas kernels  23.6 us (13%)
  local copies, waits for them, and re-layouts  2.78 us (1%)
  between operations  1.93 us (1%)
    ppermute x25, waiting for transfers between devices, shift(): return lax.ppermute(value, CHIP_AXES, along(first, step))  56.9 us
    ppermute x25, starting transfers between devices, shift(): return lax.ppermute(value, CHIP_AXES, along(first, step))  30.6 us
    ppermute x14, starting transfers between devices, swap(): return lax.ppermute(value, 'core', [(0, 1), (1, 0)])  18 us
    pallas_call x13, Pallas kernels, call(): pl.pallas_call(kernel, in_specs=whole, out_specs=[VMEM] * len(outs), out_...  16.4 us
    ppermute x6, waiting for transfers between devices, shift_z(): lax.ppermute(value, 'z', [(i, (i + step) % RING) for i in range(RING)])  14.9 us
    ppermute x3, waiting for transfers between devices, pair_z(): return lax.ppermute(value, 'z', [(i, i ^ flip) for i in range(RING)])  11.3 us
    ppermute x14, waiting for transfers between devices, swap(): return lax.ppermute(value, 'core', [(0, 1), (1, 0)])  9.3 us
    ppermute x6, starting transfers between devices, shift_z(): lax.ppermute(value, 'z', [(i, (i + step) % RING) for i in range(RING)])  9.07 us
  transfers between devices with their start and end apart: 48, of which 32 were waited for; matrix products, arithmetic and copies ran while one was open for 1% of the time, Pallas kernels for 8%

profile of v6, /device:TPU:1, one launch (start us, length us, event | category | flops | bytes accessed | tf_op | source)
XLA Modules:
  0.0 186.2 jit_solution(15336318602597227686)
XLA Ops:
  0.7 1.1 copy-done.1
  1.8 1.0 copy-done.6
  2.9 1.0 first_product.1
  3.8 1.5 collective-permute-start
  5.4 1.1 collective-permute-done.got
  6.5 1.4 collective-permute-start.3
  8.0 2.6 %collective-permute-start.2 = (bf16[512,512]{1,0:T(8,128)(2,1)S(1)}, bf16[512,512]{1,0:T(8,128)(2,1)S(1)}, u32[]{:S(2)}, u32[]{:S(2)}) collective-permute-start(bf16[512,512]{1,0:T(8,128)(2,1)S(1)} %constant_dynamic-update-slice_fusion), channel_id=1, source_target_pairs={{0,8},{1,9},{2,10},{3,11},{4,12},{5,13},{6,14},{7,15},{8,0},{9,1},... | collective-permute-start | bytes 1572872 | tf_op jit(solution)/shard_map/ppermute | solution.py:54
  10.6 1.1 collective-permute-start.1
  11.7 3.8 %collective-permute-start.5 = (bf16[256,512]{1,0:T(8,128)(2,1)}, bf16[256,512]{1,0:T(8,128)(2,1)S(1)}, u32[]{:S(2)}, u32[]{:S(2)}) collective-permute-start(bf16[256,512]{1,0:T(8,128)(2,1)} %param.16), channel_id=1, source_target_pairs={{0,96},{32,64},{64,32},{96,0},{1,97},{33,65},{65,33},{97,1},{2,98}... | collective-permute-start | bytes 786440 | tf_op jit(solution)/shard_map/ppermute | solution.py:66
  15.4 5.8 %collective-permute-done.5 = bf16[256,512]{1,0:T(8,128)(2,1)S(1)} collective-permute-done((bf16[256,512]{1,0:T(8,128)(2,1)}, bf16[256,512]{1,0:T(8,128)(2,1)S(1)}, u32[]{:S(2)}, u32[]{:S(2)}) %collective-permute-start.5) | collective-permute-done | bytes 262176 | tf_op jit(solution)/shard_map/ppermute | solution.py:66
  21.2 0.9 collective-permute-done.4
  22.1 1.0 collective-permute-done.2.across
  23.2 1.3 collective-permute-start.7
  24.5 1.4 collective-permute-start.6
  26.0 1.7 collective-permute-start.8
  27.8 4.6 %collective-permute-done.8 = bf16[256,512]{1,0:T(8,128)(2,1)S(1)} collective-permute-done((bf16[256,512]{1,0:T(8,128)(2,1)S(1)}, bf16[256,512]{1,0:T(8,128)(2,1)S(1)}, u32[]{:S(2)}, u32[]{:S(2)}) %collective-permute-start.8) | collective-permute-done | bytes 262176 | tf_op jit(solution)/shard_map/ppermute | solution.py:66
  32.4 6.1 %collective-permute-done.7.rest_1_ = bf16[2048,256]{1,0:T(8,128)(2,1)S(1)} collective-permute-done((bf16[2048,256]{1,0:T(8,128)(2,1)S(1)}, bf16[2048,256]{1,0:T(8,128)(2,1)S(1)}, u32[]{:S(2)}, u32[]{:S(2)}) %collective-permute-start.7) | collective-permute-done | bytes 1048608 | tf_op jit(solution)/shard_map/ppermute | solution.py:54
  38.8 2.3 %collective-permute-start.11 = (bf16[5120,256]{1,0:T(8,128)(2,1)S(1)}, bf16[5120,256]{1,0:T(8,128)(2,1)S(1)}, u32[]{:S(2)}, u32[]{:S(2)}) collective-permute-start(bf16[5120,256]{1,0:T(8,128)(2,1)S(1)} %slice_dynamic-update-slice_fusion), channel_id=1, source_target_pairs={{0,16},{16,0},{1,17},{17,1},{2,18},{18,2},{3,19},{19,3},{4,20},{20... | collective-permute-start | bytes 7864328 | tf_op jit(solution)/shard_map/ppermute | solution.py:70
  41.1 1.6 collective-permute-start.12
  42.7 1.1 collective-permute-start.13
  44.2 2.3 %collective-permute-start.9 = (bf16[2048,256]{1,0:T(8,128)(2,1)S(1)}, bf16[2048,256]{1,0:T(8,128)(2,1)S(1)}, u32[]{:S(2)}, u32[]{:S(2)}) collective-permute-start(bf16[2048,256]{1,0:T(8,128)(2,1)S(1)} %get-tuple-element.110.rest_0_), channel_id=1, source_target_pairs={{0,3},{1,0},{2,1},{3,2},{4,7},{5,4},{6,5},{7,6},{8,11},{9,8},{10,9... | collective-permute-start | bytes 3145736 | tf_op jit(solution)/shard_map/ppermute | solution.py:54
  46.4 4.2 %collective-permute-done.12.rest_2_ = bf16[1024,256]{1,0:T(8,128)(2,1)S(1)} collective-permute-done((bf16[1024,256]{1,0:T(8,128)(2,1)S(1)}, bf16[1024,256]{1,0:T(8,128)(2,1)S(1)}, u32[]{:S(2)}, u32[]{:S(2)}) %collective-permute-start.12) | collective-permute-done | bytes 524320 | tf_op jit(solution)/shard_map/ppermute | solution.py:54
  51.0 0.9 collective-permute-start.14
  53.0 3.4 %edge_terms.1 = (f32[2048,256]{1,0:T(8,128)S(1)}, f32[2048,256]{1,0:T(8,128)S(1)}) custom-call(s32[4]{0:T(128)S(1)} %pad_add_fusion.where, s32[1]{0:T(128)S(6)} %copy.47.live, s32[16]{0:T(128)S(1)} %copy-done.10, bf16[2048,128]{1,0:T(8,128)(2,1)S(1)} %fusion.1.pick, bf16[2048,512]{1,0:T(8,128)(2,1)S(1)} %copy-done.3, bf16[512,512]{1,0:T(8,128)(2,1)S(1)} %copy-done.4, ...), custom_call_target="tpu_custom_call" | custom-call | tf_op jit(solution)/shard_map/edge_terms/pallas_call | solution.py:354
  56.5 5.4 %collective-permute-done.10.rest_1_ = bf16[2048,256]{1,0:T(8,128)(2,1)S(1)} collective-permute-done((bf16[2048,256]{1,0:T(8,128)(2,1)S(1)}, bf16[2048,256]{1,0:T(8,128)(2,1)S(1)}, u32[]{:S(2)}, u32[]{:S(2)}) %collective-permute-start.10) | collective-permute-done | bytes 1048608 | tf_op jit(solution)/shard_map/ppermute | solution.py:54
  62.5 1.0 collective-permute-start.17
  63.5 2.3 %collective-permute-start.15 = (bf16[1024,256]{1,0:T(8,128)(2,1)S(1)}, bf16[1024,256]{1,0:T(8,128)(2,1)S(1)}, u32[]{:S(2)}, u32[]{:S(2)}) collective-permute-start(bf16[1024,256]{1,0:T(8,128)(2,1)S(1)} %slice.44), channel_id=1, source_target_pairs={{0,3},{1,0},{2,1},{3,2},{4,7},{5,4},{6,5},{7,6},{8,11},{9,8},{10,9... | collective-permute-start | bytes 1572872 | tf_op jit(solution)/shard_map/ppermute | solution.py:54
  66.5 4.2 %forward_0.1 = (f32[2048,256]{1,0:T(8,128)S(1)}, f32[1024,256]{1,0:T(8,128)S(1)}, bf16[1024,256]{1,0:T(8,128)(2,1)S(1)}) custom-call(s32[4]{0:T(128)S(1)} %pad_add_fusion.where, s32[1]{0:T(128)S(6)} %copy.47.live, s32[16]{0:T(128)S(1)} %copy-done.11, s32[16]{0:T(128)S(1)} %copy-done.10, bf16[2048,128]{1,0:T(8,128)(2,1)S(1)} %fusion.2.pick, ...), custom_call_target="tpu_custom_call" | custom-call | tf_op jit(solution)/shard_map/forward_0/pallas_call | solution.py:354
  70.7 1.3 collective-permute-done.15
  72.0 3.3 %collective-permute-done.16.rest_2_ = bf16[1024,256]{1,0:T(8,128)(2,1)S(1)} collective-permute-done((bf16[1024,256]{1,0:T(8,128)(2,1)S(1)}, bf16[1024,256]{1,0:T(8,128)(2,1)S(1)}, u32[]{:S(2)}, u32[]{:S(2)}) %collective-permute-start.16) | collective-permute-done | bytes 524320 | tf_op jit(solution)/shard_map/ppermute | solution.py:54
  75.3 1.6 collective-permute-start.18
  76.9 1.5 collective-permute-done.18.rest_5_
  78.4 4.2 %forward_1.1 = (f32[2048,256]{1,0:T(8,128)S(1)}, f32[1024,256]{1,0:T(8,128)S(1)}, bf16[1024,256]{1,0:T(8,128)(2,1)S(1)}) custom-call(s32[4]{0:T(128)S(1)} %pad_add_fusion.where, s32[1]{0:T(128)S(6)} %copy.47.live, s32[16]{0:T(128)S(1)} %copy-done.11, s32[16]{0:T(128)S(1)} %copy-done.10, bf16[2048,128]{1,0:T(8,128)(2,1)S(1)} %fusion.2.pick, ...), custom_call_target="tpu_custom_call" | custom-call | tf_op jit(solution)/shard_map/forward_1/pallas_call | solution.py:354
  83.1 1.5 collective-permute-done.20.refs_3_
  85.5 4.5 %collective-permute-start.22 = (bf16[256,512]{1,0:T(8,128)(2,1)S(1)}, bf16[256,512]{1,0:T(8,128)(2,1)S(1)}, u32[]{:S(2)}, u32[]{:S(2)}) collective-permute-start(bf16[256,512]{1,0:T(8,128)(2,1)S(1)} %get-tuple-element.134), channel_id=1, source_target_pairs={{0,96},{32,0},{64,32},{96,64},{1,97},{33,1},{65,33},{97,65},{2,98}... | collective-permute-start | bytes 786440 | tf_op jit(solution)/shard_map/ppermute | solution.py:58
  90.0 0.9 collective-permute-start.23
  90.9 5.4 %collective-permute-done.21.a = bf16[256,512]{1,0:T(8,128)(2,1)S(1)} collective-permute-done((bf16[256,512]{1,0:T(8,128)(2,1)S(1)}, bf16[256,512]{1,0:T(8,128)(2,1)S(1)}, u32[]{:S(2)}, u32[]{:S(2)}) %collective-permute-start.21) | collective-permute-done | bytes 262176 | tf_op jit(solution)/shard_map/ppermute | solution.py:58
  96.3 4.9 %collective-permute-done.22.b = bf16[256,512]{1,0:T(8,128)(2,1)S(1)} collective-permute-done((bf16[256,512]{1,0:T(8,128)(2,1)S(1)}, bf16[256,512]{1,0:T(8,128)(2,1)S(1)}, u32[]{:S(2)}, u32[]{:S(2)}) %collective-permute-start.22) | collective-permute-done | bytes 262176 | tf_op jit(solution)/shard_map/ppermute | solution.py:58
  101.2 1.7 collective-permute-done.23.c
  104.3 2.1 %collective-permute-start.24 = (bf16[256,512]{1,0:T(8,128)(2,1)S(1)}, bf16[256,512]{1,0:T(8,128)(2,1)S(1)}, u32[]{:S(2)}, u32[]{:S(2)}) collective-permute-start(bf16[256,512]{1,0:T(8,128)(2,1)S(1)} %get-tuple-element.139.rest_2_), channel_id=1, source_target_pairs={{0,96},{32,0},{64,32},{96,64},{1,97},{33,1},{65,33},{97,65},{2,98}... | collective-permute-start | bytes 786440 | tf_op jit(solution)/shard_map/ppermute | solution.py:58
  107.2 1.6 collective-permute-start.27
  108.8 3.0 %collective-permute-done.26.rest_5_ = bf16[256,512]{1,0:T(8,128)(2,1)S(1)} collective-permute-done((bf16[256,512]{1,0:T(8,128)(2,1)S(1)}, bf16[256,512]{1,0:T(8,128)(2,1)S(1)}, u32[]{:S(2)}, u32[]{:S(2)}) %collective-permute-start.26) | collective-permute-done | bytes 262176 | tf_op jit(solution)/shard_map/ppermute | solution.py:58
  111.8 6.8 %collective-permute-start.28 = (bf16[256,512]{1,0:T(8,128)(2,1)S(1)}, bf16[256,512]{1,0:T(8,128)(2,1)S(1)}, u32[]{:S(2)}, u32[]{:S(2)}) collective-permute-start(bf16[256,512]{1,0:T(8,128)(2,1)S(1)} %collective-permute-done.24.rest_3_), channel_id=1, source_target_pairs={{0,16},{16,0},{1,17},{17,1},{2,18},{18,2},{3,19},{19,3},{4,20},{20... | collective-permute-start | bytes 786440 | tf_op jit(solution)/shard_map/ppermute | solution.py:70
  118.6 1.0 collective-permute-start.29
  119.8 1.0 collective-permute-done.29.rest_8_
  121.1 4.0 %backward.1 = (bf16[1024,256]{1,0:T(8,128)(2,1)S(1)}, bf16[1024,256]{1,0:T(8,128)(2,1)S(1)}, bf16[1024,256]{1,0:T(8,128)(2,1)S(1)}, bf16[1024,256]{1,0:T(8,128)(...) custom-call(s32[4]{0:T(128)S(1)} %pad_add_fusion.where, ...), custom_call_target="tpu_custom_call", output_to_operand_aliasing={{0}: (17, {}), {1}: (18, {}), {2}: (19, {}), {3}: (20, {}),... | custom-call | tf_op jit(solution)/shard_map/backward/pallas_call | solution.py:481
  125.6 3.1 %collective-permute-start.34 = (bf16[1024,256]{1,0:T(8,128)(2,1)S(1)}, bf16[1024,256]{1,0:T(8,128)(2,1)S(1)}, u32[]{:S(2)}, u32[]{:S(2)}) collective-permute-start(bf16[1024,256]{1,0:T(8,128)(2,1)S(1)} %get-tuple-element.167), channel_id=1, source_target_pairs={{0,3},{1,0},{2,1},{3,2},{4,7},{5,4},{6,5},{7,6},{8,11},{9,8},{10,9... | collective-permute-start | bytes 1572872 | tf_op jit(solution)/shard_map/ppermute | solution.py:54
  128.7 2.2 %collective-permute-done.31.refs_0_ = bf16[6144,256]{1,0:T(8,128)(2,1)S(1)} collective-permute-done((bf16[6144,256]{1,0:T(8,128)(2,1)S(1)}, bf16[6144,256]{1,0:T(8,128)(2,1)S(1)}, u32[]{:S(2)}, u32[]{:S(2)}) %collective-permute-start.31) | collective-permute-done | bytes 3145760 | tf_op jit(solution)/shard_map/ppermute | solution.py:70
  131.0 3.5 %collective-permute-start.33 = (bf16[1024,256]{1,0:T(8,128)(2,1)S(1)}, bf16[1024,256]{1,0:T(8,128)(2,1)S(1)}, u32[]{:S(2)}, u32[]{:S(2)}) collective-permute-start(bf16[1024,256]{1,0:T(8,128)(2,1)S(1)} %get-tuple-element.198), channel_id=1, source_target_pairs={{0,3},{1,0},{2,1},{3,2},{4,7},{5,4},{6,5},{7,6},{8,11},{9,8},{10,9... | collective-permute-start | bytes 1572872 | tf_op jit(solution)/shard_map/ppermute | solution.py:54
  134.8 3.4 %collective-permute-done.35.refs_5_ = bf16[1024,256]{1,0:T(8,128)(2,1)S(1)} collective-permute-done((bf16[1024,256]{1,0:T(8,128)(2,1)S(1)}, bf16[1024,256]{1,0:T(8,128)(2,1)S(1)}, u32[]{:S(2)}, u32[]{:S(2)}) %collective-permute-start.35) | collective-permute-done | bytes 524320 | tf_op jit(solution)/shard_map/ppermute | solution.py:54
  138.6 1.5 collective-permute-start.40
  140.5 3.4 %collective-permute-done.32.refs_2_ = bf16[1024,256]{1,0:T(8,128)(2,1)S(1)} collective-permute-done((bf16[1024,256]{1,0:T(8,128)(2,1)S(1)}, bf16[1024,256]{1,0:T(8,128)(2,1)S(1)}, u32[]{:S(2)}, u32[]{:S(2)}) %collective-permute-start.32) | collective-permute-done | bytes 524320 | tf_op jit(solution)/shard_map/ppermute | solution.py:54
  144.3 1.2 collective-permute-start.37
  145.9 1.0 fusion
  146.9 5.6 %collective-permute-done.39.refs_2_ = bf16[2048,256]{1,0:T(8,128)(2,1)S(1)} collective-permute-done((bf16[2048,256]{1,0:T(8,128)(2,1)S(1)}, bf16[2048,256]{1,0:T(8,128)(2,1)S(1)}, u32[]{:S(2)}, u32[]{:S(2)}) %collective-permute-start.39) | collective-permute-done | bytes 1048608 | tf_op jit(solution)/shard_map/ppermute | solution.py:54
  152.5 2.7 %collective-permute-done.40.refs_3_ = bf16[2048,256]{1,0:T(8,128)(2,1)S(1)} collective-permute-done((bf16[2048,256]{1,0:T(8,128)(2,1)S(1)}, bf16[2048,256]{1,0:T(8,128)(2,1)S(1)}, u32[]{:S(2)}, u32[]{:S(2)}) %collective-permute-start.40) | collective-permute-done | bytes 1048608 | tf_op jit(solution)/shard_map/ppermute | solution.py:54
  155.7 2.6 %collective-permute-start.46 = (bf16[256,512]{1,0:T(8,128)(2,1)S(1)}, bf16[256,512]{1,0:T(8,128)(2,1)S(1)}, u32[]{:S(2)}, u32[]{:S(2)}) collective-permute-start(bf16[256,512]{1,0:T(8,128)(2,1)S(1)} %get-tuple-element.183), channel_id=1, source_target_pairs={{0,12},{1,13},{2,14},{3,15},{4,0},{5,1},{6,2},{7,3},{8,4},{9,5},{1... | collective-permute-start | bytes 786440 | tf_op jit(solution)/shard_map/ppermute | solution.py:54
  158.3 10.3 %collective-permute-done.37.refs_1_ = bf16[2048,256]{1,0:T(8,128)(2,1)S(1)} collective-permute-done((bf16[2048,256]{1,0:T(8,128)(2,1)S(1)}, bf16[2048,256]{1,0:T(8,128)(2,1)S(1)}, u32[]{:S(2)}, u32[]{:S(2)}) %collective-permute-start.37) | collective-permute-done | bytes 1048608 | tf_op jit(solution)/shard_map/ppermute | solution.py:54
  168.6 3.1 %collective-permute-done.38.refs_2_ = bf16[2048,256]{1,0:T(8,128)(2,1)S(1)} collective-permute-done((bf16[2048,256]{1,0:T(8,128)(2,1)S(1)}, bf16[2048,256]{1,0:T(8,128)(2,1)S(1)}, u32[]{:S(2)}, u32[]{:S(2)}) %collective-permute-start.38) | collective-permute-done | bytes 1048608 | tf_op jit(solution)/shard_map/ppermute | solution.py:54
  172.3 2.6 %collective-permute-start.43 = (bf16[256,512]{1,0:T(8,128)(2,1)S(1)}, bf16[256,512]{1,0:T(8,128)(2,1)S(1)}, u32[]{:S(2)}, u32[]{:S(2)}) collective-permute-start(bf16[256,512]{1,0:T(8,128)(2,1)S(1)} %get-tuple-element.189), channel_id=1, source_target_pairs={{0,12},{1,13},{2,14},{3,15},{4,0},{5,1},{6,2},{7,3},{8,4},{9,5},{1... | collective-permute-start | bytes 786440 | tf_op jit(solution)/shard_map/ppermute | solution.py:54
  174.9 1.8 place_mine.1.placed
  176.7 5.0 %collective-permute-done.41.up = bf16[256,512]{1,0:T(8,128)(2,1)S(1)} collective-permute-done((bf16[256,512]{1,0:T(8,128)(2,1)S(1)}, bf16[256,512]{1,0:T(8,128)(2,1)S(1)}, u32[]{:S(2)}, u32[]{:S(2)}) %collective-permute-start.41) | collective-permute-done | bytes 262176 | tf_op jit(solution)/shard_map/ppermute | solution.py:54
  183.2 1.5 collective-permute-done.47.value
  184.7 1.3 place_other.1
  (100 shorter events, 12.2 us)
Async XLA Ops:
  0.6 65.1 %copy-start = (bf16[512,512]{1,0:T(8,128)(2,1)S(1)}, bf16[512,512]{1,0:T(8,128)(2,1)}, u32[]{:S(2)}) copy-start(bf16[512,512]{1,0:T(8,128)(2,1)} %param.28) | copy-start | bytes 1572868
  0.7 1.1 copy-start.1
  1.8 1.0 copy-start.6
  2.9 23.1 %copy-start.14 = (bf16[256,512]{1,0:T(8,128)(2,1)S(1)}, bf16[256,512]{1,0:T(8,128)(2,1)}, u32[]{:S(2)}) copy-start(bf16[256,512]{1,0:T(8,128)(2,1)} %param.16) | copy-start | bytes 786436
  3.8 2.7 %collective-permute-start = (bf16[256,512]{1,0:T(8,128)(2,1)S(1)}, bf16[256,512]{1,0:T(8,128)(2,1)S(1)}, u32[]{:S(2)}, u32[]{:S(2)}) collective-permute-start(bf16[256,512]{1,0:T(8,128)(2,1)S(1)} %get-tuple-element.101), channel_id=1, source_target_pairs={{0,16},{16,0},{1,17},{17,1},{2,18},{18,2},{3,19},{19,3},{4,20},{20... | collective-permute-start | bytes 786440 | tf_op jit(solution)/shard_map/ppermute | solution.py:70
  6.5 15.6 %collective-permute-start.3 = (bf16[512,512]{1,0:T(8,128)(2,1)S(1)}, bf16[512,512]{1,0:T(8,128)(2,1)S(1)}, u32[]{:S(2)}, u32[]{:S(2)}) collective-permute-start(bf16[512,512]{1,0:T(8,128)(2,1)S(1)} %constant_dynamic-update-slice_fusion), channel_id=1, source_target_pairs={{0,4},{1,5},{2,6},{3,7},{4,8},{5,9},{6,10},{7,11},{8,12},{9,13},{1... | collective-permute-start | bytes 1572872 | tf_op jit(solution)/shard_map/ppermute | solution.py:54
  8.0 15.1 %collective-permute-start.2 = (bf16[512,512]{1,0:T(8,128)(2,1)S(1)}, bf16[512,512]{1,0:T(8,128)(2,1)S(1)}, u32[]{:S(2)}, u32[]{:S(2)}) collective-permute-start(bf16[512,512]{1,0:T(8,128)(2,1)S(1)} %constant_dynamic-update-slice_fusion), channel_id=1, source_target_pairs={{0,8},{1,9},{2,10},{3,11},{4,12},{5,13},{6,14},{7,15},{8,0},{9,1},... | collective-permute-start | bytes 1572872 | tf_op jit(solution)/shard_map/ppermute | solution.py:54
  10.6 12.5 %collective-permute-start.1 = (bf16[512,512]{1,0:T(8,128)(2,1)S(1)}, bf16[512,512]{1,0:T(8,128)(2,1)S(1)}, u32[]{:S(2)}, u32[]{:S(2)}) collective-permute-start(bf16[512,512]{1,0:T(8,128)(2,1)S(1)} %constant_dynamic-update-slice_fusion), channel_id=1, source_target_pairs={{0,12},{1,13},{2,14},{3,15},{4,0},{5,1},{6,2},{7,3},{8,4},{9,5},{1... | collective-permute-start | bytes 1572872 | tf_op jit(solution)/shard_map/ppermute | solution.py:54
  11.7 9.6 %collective-permute-start.5 = (bf16[256,512]{1,0:T(8,128)(2,1)}, bf16[256,512]{1,0:T(8,128)(2,1)S(1)}, u32[]{:S(2)}, u32[]{:S(2)}) collective-permute-start(bf16[256,512]{1,0:T(8,128)(2,1)} %param.16), channel_id=1, source_target_pairs={{0,96},{32,64},{64,32},{96,0},{1,97},{33,65},{65,33},{97,1},{2,98}... | collective-permute-start | bytes 786440 | tf_op jit(solution)/shard_map/ppermute | solution.py:66
  15.4 6.7 %collective-permute-start.4 = (bf16[256,512]{1,0:T(8,128)(2,1)}, bf16[256,512]{1,0:T(8,128)(2,1)S(1)}, u32[]{:S(2)}, u32[]{:S(2)}) collective-permute-start(bf16[256,512]{1,0:T(8,128)(2,1)} %param.16), channel_id=1, source_target_pairs={{0,32},{32,0},{64,96},{96,64},{1,33},{33,1},{65,97},{97,65},{2,34}... | collective-permute-start | bytes 786440 | tf_op jit(solution)/shard_map/ppermute | solution.py:66
  23.2 15.2 %collective-permute-start.7 = (bf16[2048,256]{1,0:T(8,128)(2,1)S(1)}, bf16[2048,256]{1,0:T(8,128)(2,1)S(1)}, u32[]{:S(2)}, u32[]{:S(2)}) collective-permute-start(bf16[2048,256]{1,0:T(8,128)(2,1)S(1)} %get-tuple-element.107.rest_0_), channel_id=1, source_target_pairs={{0,1},{1,2},{2,3},{3,0},{4,5},{5,6},{6,7},{7,4},{8,9},{9,10},{10,1... | collective-permute-start | bytes 3145736 | tf_op jit(solution)/shard_map/ppermute | solution.py:54
  24.5 13.9 %collective-permute-start.6 = (bf16[2048,256]{1,0:T(8,128)(2,1)S(1)}, bf16[2048,256]{1,0:T(8,128)(2,1)S(1)}, u32[]{:S(2)}, u32[]{:S(2)}) collective-permute-start(bf16[2048,256]{1,0:T(8,128)(2,1)S(1)} %get-tuple-element.107.rest_0_), channel_id=1, source_target_pairs={{0,3},{1,0},{2,1},{3,2},{4,7},{5,4},{6,5},{7,6},{8,11},{9,8},{10,9... | collective-permute-start | bytes 3145736 | tf_op jit(solution)/shard_map/ppermute | solution.py:54
  26.0 6.4 %collective-permute-start.8 = (bf16[256,512]{1,0:T(8,128)(2,1)S(1)}, bf16[256,512]{1,0:T(8,128)(2,1)S(1)}, u32[]{:S(2)}, u32[]{:S(2)}) collective-permute-start(bf16[256,512]{1,0:T(8,128)(2,1)S(1)} %collective-permute-done.5), channel_id=1, source_target_pairs={{0,32},{32,0},{64,96},{96,64},{1,33},{33,1},{65,97},{97,65},{2,34}... | collective-permute-start | bytes 786440 | tf_op jit(solution)/shard_map/ppermute | solution.py:66
  38.6 14.0 %copy-start.8 = (s32[16,128]{1,0:T(8,128)S(1)}, s32[16,128]{1,0:T(8,128)}, u32[]{:S(2)}) copy-start(s32[16,128]{1,0:T(8,128)} %recv.3) | copy-start | bytes 24580
  38.6 14.4 %copy-start.3 = (bf16[2048,512]{1,0:T(8,128)(2,1)S(1)}, bf16[2048,512]{1,0:T(8,128)(2,1)}, u32[]{:S(2)}) copy-start(bf16[2048,512]{1,0:T(8,128)(2,1)} %edge.1) | copy-start | bytes 6291460
  38.6 14.4 %copy-start.4 = (bf16[512,512]{1,0:T(8,128)(2,1)S(1)}, bf16[512,512]{1,0:T(8,128)(2,1)}, u32[]{:S(2)}) copy-start(bf16[512,512]{1,0:T(8,128)(2,1)} %w_mesh.1) | copy-start | bytes 1572868
  38.6 14.4 %copy-start.5 = (bf16[512,512]{1,0:T(8,128)(2,1)S(1)}, bf16[512,512]{1,0:T(8,128)(2,1)}, u32[]{:S(2)}) copy-start(bf16[512,512]{1,0:T(8,128)(2,1)} %w_edge.1) | copy-start | bytes 1572868
  38.6 14.4 %copy-start.10 = (s32[16]{0:T(128)S(1)}, s32[16]{0:T(128)}, u32[]{:S(2)}) copy-start(s32[16]{0:T(128)} %mesh_block.7) | copy-start | bytes 196
  38.6 14.4 %copy-start.12 = (f32[512]{0:T(512)S(1)}, f32[512]{0:T(512)}, u32[]{:S(2)}) copy-start(f32[512]{0:T(512)} %param.26) | copy-start | bytes 6148
  38.8 14.1 %collective-permute-start.11 = (bf16[5120,256]{1,0:T(8,128)(2,1)S(1)}, bf16[5120,256]{1,0:T(8,128)(2,1)S(1)}, u32[]{:S(2)}, u32[]{:S(2)}) collective-permute-start(bf16[5120,256]{1,0:T(8,128)(2,1)S(1)} %slice_dynamic-update-slice_fusion), channel_id=1, source_target_pairs={{0,16},{16,0},{1,17},{17,1},{2,18},{18,2},{3,19},{19,3},{4,20},{20... | collective-permute-start | bytes 7864328 | tf_op jit(solution)/shard_map/ppermute | solution.py:70
  41.1 9.5 %collective-permute-start.12 = (bf16[1024,256]{1,0:T(8,128)(2,1)S(1)}, bf16[1024,256]{1,0:T(8,128)(2,1)S(1)}, u32[]{:S(2)}, u32[]{:S(2)}) collective-permute-start(bf16[1024,256]{1,0:T(8,128)(2,1)S(1)} %get-tuple-element.204), channel_id=1, source_target_pairs={{0,1},{1,2},{2,3},{3,0},{4,5},{5,6},{6,7},{7,4},{8,9},{9,10},{10,1... | collective-permute-start | bytes 1572872 | tf_op jit(solution)/shard_map/ppermute | solution.py:54
  42.7 8.3 %collective-permute-start.13 = (bf16[1024,256]{1,0:T(8,128)(2,1)S(1)}, bf16[1024,256]{1,0:T(8,128)(2,1)S(1)}, u32[]{:S(2)}, u32[]{:S(2)}) collective-permute-start(bf16[1024,256]{1,0:T(8,128)(2,1)S(1)} %get-tuple-element.202), channel_id=1, source_target_pairs={{0,3},{1,0},{2,1},{3,2},{4,7},{5,4},{6,5},{7,6},{8,11},{9,8},{10,9... | collective-permute-start | bytes 1572872 | tf_op jit(solution)/shard_map/ppermute | solution.py:54
  43.8 18.1 %collective-permute-start.10 = (bf16[2048,256]{1,0:T(8,128)(2,1)S(1)}, bf16[2048,256]{1,0:T(8,128)(2,1)S(1)}, u32[]{:S(2)}, u32[]{:S(2)}) collective-permute-start(bf16[2048,256]{1,0:T(8,128)(2,1)S(1)} %get-tuple-element.110.rest_0_), channel_id=1, source_target_pairs={{0,1},{1,2},{2,3},{3,0},{4,5},{5,6},{6,7},{7,4},{8,9},{9,10},{10,1... | collective-permute-start | bytes 3145736 | tf_op jit(solution)/shard_map/ppermute | solution.py:54
  44.2 18.1 %collective-permute-start.9 = (bf16[2048,256]{1,0:T(8,128)(2,1)S(1)}, bf16[2048,256]{1,0:T(8,128)(2,1)S(1)}, u32[]{:S(2)}, u32[]{:S(2)}) collective-permute-start(bf16[2048,256]{1,0:T(8,128)(2,1)S(1)} %get-tuple-element.110.rest_0_), channel_id=1, source_target_pairs={{0,3},{1,0},{2,1},{3,2},{4,7},{5,4},{6,5},{7,6},{8,11},{9,8},{10,9... | collective-permute-start | bytes 3145736 | tf_op jit(solution)/shard_map/ppermute | solution.py:54
  51.0 11.2 %collective-permute-start.14 = (bf16[1024,256]{1,0:T(8,128)(2,1)S(1)}, bf16[1024,256]{1,0:T(8,128)(2,1)S(1)}, u32[]{:S(2)}, u32[]{:S(2)}) collective-permute-start(bf16[1024,256]{1,0:T(8,128)(2,1)S(1)} %collective-permute-done.13), channel_id=1, source_target_pairs={{0,16},{16,0},{1,17},{17,1},{2,18},{18,2},{3,19},{19,3},{4,20},{20... | collective-permute-start | bytes 1572872 | tf_op jit(solution)/shard_map/ppermute | solution.py:70
  62.3 3.5 %copy-start.13 = (bf16[256,512]{1,0:T(8,128)(2,1)S(1)}, bf16[256,512]{1,0:T(8,128)(2,1)}, u32[]{:S(2)}) copy-start(bf16[256,512]{1,0:T(8,128)(2,1)} %param.29) | copy-start | bytes 786436
  62.4 3.7 %copy-start.9 = (s32[16,128]{1,0:T(8,128)S(1)}, s32[16,128]{1,0:T(8,128)}, u32[]{:S(2)}) copy-start(s32[16,128]{1,0:T(8,128)} %send.1) | copy-start | bytes 24580
  62.4 4.1 %copy-start.11 = (s32[16]{0:T(128)S(1)}, s32[16]{0:T(128)}, u32[]{:S(2)}) copy-start(s32[16]{0:T(128)} %grid_block.5) | copy-start | bytes 196
  62.5 12.8 %collective-permute-start.17 = (bf16[3072,256]{1,0:T(8,128)(2,1)S(1)}, bf16[3072,256]{1,0:T(8,128)(2,1)S(1)}, u32[]{:S(2)}, u32[]{:S(2)}) collective-permute-start(bf16[3072,256]{1,0:T(8,128)(2,1)S(1)} %pad_maximum_fusion), channel_id=1, source_target_pairs={{0,16},{16,0},{1,17},{17,1},{2,18},{18,2},{3,19},{19,3},{4,20},{20... | collective-permute-start | bytes 4718600 | tf_op jit(solution)/shard_map/ppermute | solution.py:70
  63.5 8.5 %collective-permute-start.15 = (bf16[1024,256]{1,0:T(8,128)(2,1)S(1)}, bf16[1024,256]{1,0:T(8,128)(2,1)S(1)}, u32[]{:S(2)}, u32[]{:S(2)}) collective-permute-start(bf16[1024,256]{1,0:T(8,128)(2,1)S(1)} %slice.44), channel_id=1, source_target_pairs={{0,3},{1,0},{2,1},{3,2},{4,7},{5,4},{6,5},{7,6},{8,11},{9,8},{10,9... | collective-permute-start | bytes 1572872 | tf_op jit(solution)/shard_map/ppermute | solution.py:54
  65.8 9.5 %collective-permute-start.16 = (bf16[1024,256]{1,0:T(8,128)(2,1)S(1)}, bf16[1024,256]{1,0:T(8,128)(2,1)S(1)}, u32[]{:S(2)}, u32[]{:S(2)}) collective-permute-start(bf16[1024,256]{1,0:T(8,128)(2,1)S(1)} %get-tuple-element.201), channel_id=1, source_target_pairs={{0,1},{1,2},{2,3},{3,0},{4,5},{5,6},{6,7},{7,4},{8,9},{9,10},{10,1... | collective-permute-start | bytes 1572872 | tf_op jit(solution)/shard_map/ppermute | solution.py:54
  75.3 3.1 %collective-permute-start.18 = (bf16[1024,256]{1,0:T(8,128)(2,1)S(1)}, bf16[1024,256]{1,0:T(8,128)(2,1)S(1)}, u32[]{:S(2)}, u32[]{:S(2)}) collective-permute-start(bf16[1024,256]{1,0:T(8,128)(2,1)S(1)} %collective-permute-done.15), channel_id=1, source_target_pairs={{0,16},{16,0},{1,17},{17,1},{2,18},{18,2},{3,19},{19,3},{4,20},{20... | collective-permute-start | bytes 1572872 | tf_op jit(solution)/shard_map/ppermute | solution.py:70
  76.9 6.2 %collective-permute-start.19 = (bf16[1024,256]{1,0:T(8,128)(2,1)S(1)}, bf16[1024,256]{1,0:T(8,128)(2,1)S(1)}, u32[]{:S(2)}, u32[]{:S(2)}) collective-permute-start(bf16[1024,256]{1,0:T(8,128)(2,1)S(1)} %get-tuple-element.130), channel_id=1, source_target_pairs={{0,16},{16,0},{1,17},{17,1},{2,18},{18,2},{3,19},{19,3},{4,20},{20... | collective-permute-start | bytes 1572872 | tf_op jit(solution)/shard_map/ppermute | solution.py:70
  82.7 20.2 %copy-start.7 = (bf16[512,512]{1,0:T(8,128)(2,1)S(1)}, bf16[512,512]{1,0:T(8,128)(2,1)}, u32[]{:S(2)}) copy-start(bf16[512,512]{1,0:T(8,128)(2,1)} %w_out.1) | copy-start | bytes 1572868
  82.7 2.0 %collective-permute-start.20 = (bf16[1024,256]{1,0:T(8,128)(2,1)S(1)}, bf16[1024,256]{1,0:T(8,128)(2,1)S(1)}, u32[]{:S(2)}, u32[]{:S(2)}) collective-permute-start(bf16[1024,256]{1,0:T(8,128)(2,1)S(1)} %get-tuple-element.131), channel_id=1, source_target_pairs={{0,16},{16,0},{1,17},{17,1},{2,18},{18,2},{3,19},{19,3},{4,20},{20... | collective-permute-start | bytes 1572872 | tf_op jit(solution)/shard_map/ppermute | solution.py:70
  84.9 11.4 %collective-permute-start.21 = (bf16[256,512]{1,0:T(8,128)(2,1)S(1)}, bf16[256,512]{1,0:T(8,128)(2,1)S(1)}, u32[]{:S(2)}, u32[]{:S(2)}) collective-permute-start(bf16[256,512]{1,0:T(8,128)(2,1)S(1)} %get-tuple-element.133), channel_id=1, source_target_pairs={{0,32},{32,64},{64,96},{96,0},{1,33},{33,65},{65,97},{97,1},{2,34}... | collective-permute-start | bytes 786440 | tf_op jit(solution)/shard_map/ppermute | solution.py:58
  85.5 15.7 %collective-permute-start.22 = (bf16[256,512]{1,0:T(8,128)(2,1)S(1)}, bf16[256,512]{1,0:T(8,128)(2,1)S(1)}, u32[]{:S(2)}, u32[]{:S(2)}) collective-permute-start(bf16[256,512]{1,0:T(8,128)(2,1)S(1)} %get-tuple-element.134), channel_id=1, source_target_pairs={{0,96},{32,0},{64,32},{96,64},{1,97},{33,1},{65,33},{97,65},{2,98}... | collective-permute-start | bytes 786440 | tf_op jit(solution)/shard_map/ppermute | solution.py:58
  90.0 12.8 %collective-permute-start.23 = (bf16[256,512]{1,0:T(8,128)(2,1)S(1)}, bf16[256,512]{1,0:T(8,128)(2,1)S(1)}, u32[]{:S(2)}, u32[]{:S(2)}) collective-permute-start(bf16[256,512]{1,0:T(8,128)(2,1)S(1)} %get-tuple-element.135), channel_id=1, source_target_pairs={{0,64},{32,96},{64,0},{96,32},{1,65},{33,97},{65,1},{97,33},{2,66}... | collective-permute-start | bytes 786440 | tf_op jit(solution)/shard_map/ppermute | solution.py:58
  103.7 8.1 %collective-permute-start.26 = (bf16[256,512]{1,0:T(8,128)(2,1)S(1)}, bf16[256,512]{1,0:T(8,128)(2,1)S(1)}, u32[]{:S(2)}, u32[]{:S(2)}) collective-permute-start(bf16[256,512]{1,0:T(8,128)(2,1)S(1)} %get-tuple-element.139.rest_2_), channel_id=1, source_target_pairs={{0,32},{32,64},{64,96},{96,0},{1,33},{33,65},{65,97},{97,1},{2,34}... | collective-permute-start | bytes 786440 | tf_op jit(solution)/shard_map/ppermute | solution.py:58
  104.3 7.5 %collective-permute-start.24 = (bf16[256,512]{1,0:T(8,128)(2,1)S(1)}, bf16[256,512]{1,0:T(8,128)(2,1)S(1)}, u32[]{:S(2)}, u32[]{:S(2)}) collective-permute-start(bf16[256,512]{1,0:T(8,128)(2,1)S(1)} %get-tuple-element.139.rest_2_), channel_id=1, source_target_pairs={{0,96},{32,0},{64,32},{96,64},{1,97},{33,1},{65,33},{97,65},{2,98}... | collective-permute-start | bytes 786440 | tf_op jit(solution)/shard_map/ppermute | solution.py:58
  106.4 12.2 %collective-permute-start.25 = (bf16[256,512]{1,0:T(8,128)(2,1)S(1)}, bf16[256,512]{1,0:T(8,128)(2,1)S(1)}, u32[]{:S(2)}, u32[]{:S(2)}) collective-permute-start(bf16[256,512]{1,0:T(8,128)(2,1)S(1)} %get-tuple-element.139.rest_2_), channel_id=1, source_target_pairs={{0,64},{32,96},{64,0},{96,32},{1,65},{33,97},{65,1},{97,33},{2,66}... | collective-permute-start | bytes 786440 | tf_op jit(solution)/shard_map/ppermute | solution.py:58
  107.2 12.5 %collective-permute-start.27 = (bf16[256,512]{1,0:T(8,128)(2,1)S(1)}, bf16[256,512]{1,0:T(8,128)(2,1)S(1)}, u32[]{:S(2)}, u32[]{:S(2)}) collective-permute-start(bf16[256,512]{1,0:T(8,128)(2,1)S(1)} %get-tuple-element.139.rest_2_), channel_id=1, source_target_pairs={{0,16},{16,0},{1,17},{17,1},{2,18},{18,2},{3,19},{19,3},{4,20},{20... | collective-permute-start | bytes 786440 | tf_op jit(solution)/shard_map/ppermute | solution.py:70
  111.8 8.9 %collective-permute-start.28 = (bf16[256,512]{1,0:T(8,128)(2,1)S(1)}, bf16[256,512]{1,0:T(8,128)(2,1)S(1)}, u32[]{:S(2)}, u32[]{:S(2)}) collective-permute-start(bf16[256,512]{1,0:T(8,128)(2,1)S(1)} %collective-permute-done.24.rest_3_), channel_id=1, source_target_pairs={{0,16},{16,0},{1,17},{17,1},{2,18},{18,2},{3,19},{19,3},{4,20},{20... | collective-permute-start | bytes 786440 | tf_op jit(solution)/shard_map/ppermute | solution.py:70
  118.6 2.1 %collective-permute-start.29 = (bf16[256,512]{1,0:T(8,128)(2,1)S(1)}, bf16[256,512]{1,0:T(8,128)(2,1)S(1)}, u32[]{:S(2)}, u32[]{:S(2)}) collective-permute-start(bf16[256,512]{1,0:T(8,128)(2,1)S(1)} %collective-permute-done.25.rest_4_), channel_id=1, source_target_pairs={{0,16},{16,0},{1,17},{17,1},{2,18},{18,2},{3,19},{19,3},{4,20},{20... | collective-permute-start | bytes 786440 | tf_op jit(solution)/shard_map/ppermute | solution.py:70
  119.6 1.5 collective-permute-start.30
  125.1 5.7 %collective-permute-start.31 = (bf16[6144,256]{1,0:T(8,128)(2,1)S(1)}, bf16[6144,256]{1,0:T(8,128)(2,1)S(1)}, u32[]{:S(2)}, u32[]{:S(2)}) collective-permute-start(bf16[6144,256]{1,0:T(8,128)(2,1)S(1)} %get-tuple-element.162), channel_id=1, source_target_pairs={{0,16},{16,0},{1,17},{17,1},{2,18},{18,2},{3,19},{19,3},{4,20},{20... | collective-permute-start | bytes 9437192 | tf_op jit(solution)/shard_map/ppermute | solution.py:70
  125.6 9.2 %collective-permute-start.34 = (bf16[1024,256]{1,0:T(8,128)(2,1)S(1)}, bf16[1024,256]{1,0:T(8,128)(2,1)S(1)}, u32[]{:S(2)}, u32[]{:S(2)}) collective-permute-start(bf16[1024,256]{1,0:T(8,128)(2,1)S(1)} %get-tuple-element.167), channel_id=1, source_target_pairs={{0,3},{1,0},{2,1},{3,2},{4,7},{5,4},{6,5},{7,6},{8,11},{9,8},{10,9... | collective-permute-start | bytes 1572872 | tf_op jit(solution)/shard_map/ppermute | solution.py:54
  128.7 9.5 %collective-permute-start.35 = (bf16[1024,256]{1,0:T(8,128)(2,1)S(1)}, bf16[1024,256]{1,0:T(8,128)(2,1)S(1)}, u32[]{:S(2)}, u32[]{:S(2)}) collective-permute-start(bf16[1024,256]{1,0:T(8,128)(2,1)S(1)} %get-tuple-element.168), channel_id=1, source_target_pairs={{0,1},{1,2},{2,3},{3,0},{4,5},{5,6},{6,7},{7,4},{8,9},{9,10},{10,1... | collective-permute-start | bytes 1572872 | tf_op jit(solution)/shard_map/ppermute | solution.py:54
  131.0 9.6 %collective-permute-start.33 = (bf16[1024,256]{1,0:T(8,128)(2,1)S(1)}, bf16[1024,256]{1,0:T(8,128)(2,1)S(1)}, u32[]{:S(2)}, u32[]{:S(2)}) collective-permute-start(bf16[1024,256]{1,0:T(8,128)(2,1)S(1)} %get-tuple-element.198), channel_id=1, source_target_pairs={{0,3},{1,0},{2,1},{3,2},{4,7},{5,4},{6,5},{7,6},{8,11},{9,8},{10,9... | collective-permute-start | bytes 1572872 | tf_op jit(solution)/shard_map/ppermute | solution.py:54
  134.4 9.5 %collective-permute-start.32 = (bf16[1024,256]{1,0:T(8,128)(2,1)S(1)}, bf16[1024,256]{1,0:T(8,128)(2,1)S(1)}, u32[]{:S(2)}, u32[]{:S(2)}) collective-permute-start(bf16[1024,256]{1,0:T(8,128)(2,1)S(1)} %get-tuple-element.199), channel_id=1, source_target_pairs={{0,1},{1,2},{2,3},{3,0},{4,5},{5,6},{6,7},{7,4},{8,9},{9,10},{10,1... | collective-permute-start | bytes 1572872 | tf_op jit(solution)/shard_map/ppermute | solution.py:54
  138.5 14.0 %collective-permute-start.39 = (bf16[2048,256]{1,0:T(8,128)(2,1)S(1)}, bf16[2048,256]{1,0:T(8,128)(2,1)S(1)}, u32[]{:S(2)}, u32[]{:S(2)}) collective-permute-start(bf16[2048,256]{1,0:T(8,128)(2,1)S(1)} %get-tuple-element.177), channel_id=1, source_target_pairs={{0,3},{1,0},{2,1},{3,2},{4,7},{5,4},{6,5},{7,6},{8,11},{9,8},{10,9... | collective-permute-start | bytes 3145736 | tf_op jit(solution)/shard_map/ppermute | solution.py:54
  138.6 16.6 %collective-permute-start.40 = (bf16[2048,256]{1,0:T(8,128)(2,1)S(1)}, bf16[2048,256]{1,0:T(8,128)(2,1)S(1)}, u32[]{:S(2)}, u32[]{:S(2)}) collective-permute-start(bf16[2048,256]{1,0:T(8,128)(2,1)S(1)} %get-tuple-element.169), channel_id=1, source_target_pairs={{0,1},{1,2},{2,3},{3,0},{4,5},{5,6},{6,7},{7,4},{8,9},{9,10},{10,1... | collective-permute-start | bytes 3145736 | tf_op jit(solution)/shard_map/ppermute | solution.py:54
  144.2 10.9 %collective-permute-start.36 = (bf16[2048,256]{1,0:T(8,128)(2,1)S(1)}, bf16[2048,256]{1,0:T(8,128)(2,1)S(1)}, u32[]{:S(2)}, u32[]{:S(2)}) collective-permute-start(bf16[2048,256]{1,0:T(8,128)(2,1)S(1)} %get-tuple-element.173), channel_id=1, source_target_pairs={{0,16},{16,0},{1,17},{17,1},{2,18},{18,2},{3,19},{19,3},{4,20},{20... | collective-permute-start | bytes 3145736 | tf_op jit(solution)/shard_map/ppermute | solution.py:70
  144.3 24.3 %collective-permute-start.37 = (bf16[2048,256]{1,0:T(8,128)(2,1)S(1)}, bf16[2048,256]{1,0:T(8,128)(2,1)S(1)}, u32[]{:S(2)}, u32[]{:S(2)}) collective-permute-start(bf16[2048,256]{1,0:T(8,128)(2,1)S(1)} %get-tuple-element.174), channel_id=1, source_target_pairs={{0,3},{1,0},{2,1},{3,2},{4,7},{5,4},{6,5},{7,6},{8,11},{9,8},{10,9... | collective-permute-start | bytes 3145736 | tf_op jit(solution)/shard_map/ppermute | solution.py:54
  145.5 26.2 %collective-permute-start.38 = (bf16[2048,256]{1,0:T(8,128)(2,1)S(1)}, bf16[2048,256]{1,0:T(8,128)(2,1)S(1)}, u32[]{:S(2)}, u32[]{:S(2)}) collective-permute-start(bf16[2048,256]{1,0:T(8,128)(2,1)S(1)} %get-tuple-element.172), channel_id=1, source_target_pairs={{0,1},{1,2},{2,3},{3,0},{4,5},{5,6},{6,7},{7,4},{8,9},{9,10},{10,1... | collective-permute-start | bytes 3145736 | tf_op jit(solution)/shard_map/ppermute | solution.py:54
  155.2 19.7 %copy-start.2 = (bf16[512,512]{1,0:T(8,128)(2,1)S(1)}, bf16[512,512]{1,0:T(8,128)(2,1)}, u32[]{:S(2)}) copy-start(bf16[512,512]{1,0:T(8,128)(2,1)} %w_grid.5) | copy-start | bytes 1572868
  155.6 16.7 %collective-permute-start.44 = (bf16[256,512]{1,0:T(8,128)(2,1)S(1)}, bf16[256,512]{1,0:T(8,128)(2,1)S(1)}, u32[]{:S(2)}, u32[]{:S(2)}) collective-permute-start(bf16[256,512]{1,0:T(8,128)(2,1)S(1)} %get-tuple-element.181), channel_id=1, source_target_pairs={{0,4},{1,5},{2,6},{3,7},{4,8},{5,9},{6,10},{7,11},{8,12},{9,13},{1... | collective-permute-start | bytes 786440 | tf_op jit(solution)/shard_map/ppermute | solution.py:54
  155.6 19.2 %collective-permute-start.45 = (bf16[256,512]{1,0:T(8,128)(2,1)S(1)}, bf16[256,512]{1,0:T(8,128)(2,1)S(1)}, u32[]{:S(2)}, u32[]{:S(2)}) collective-permute-start(bf16[256,512]{1,0:T(8,128)(2,1)S(1)} %get-tuple-element.182), channel_id=1, source_target_pairs={{0,8},{1,9},{2,10},{3,11},{4,12},{5,13},{6,14},{7,15},{8,0},{9,1},... | collective-permute-start | bytes 786440 | tf_op jit(solution)/shard_map/ppermute | solution.py:54
  155.7 19.1 %collective-permute-start.46 = (bf16[256,512]{1,0:T(8,128)(2,1)S(1)}, bf16[256,512]{1,0:T(8,128)(2,1)S(1)}, u32[]{:S(2)}, u32[]{:S(2)}) collective-permute-start(bf16[256,512]{1,0:T(8,128)(2,1)S(1)} %get-tuple-element.183), channel_id=1, source_target_pairs={{0,12},{1,13},{2,14},{3,15},{4,0},{5,1},{6,2},{7,3},{8,4},{9,5},{1... | collective-permute-start | bytes 786440 | tf_op jit(solution)/shard_map/ppermute | solution.py:54
  172.1 9.6 %collective-permute-start.41 = (bf16[256,512]{1,0:T(8,128)(2,1)S(1)}, bf16[256,512]{1,0:T(8,128)(2,1)S(1)}, u32[]{:S(2)}, u32[]{:S(2)}) collective-permute-start(bf16[256,512]{1,0:T(8,128)(2,1)S(1)} %get-tuple-element.187), channel_id=1, source_target_pairs={{0,4},{1,5},{2,6},{3,7},{4,8},{5,9},{6,10},{7,11},{8,12},{9,13},{1... | collective-permute-start | bytes 786440 | tf_op jit(solution)/shard_map/ppermute | solution.py:54
  172.2 9.5 %collective-permute-start.42 = (bf16[256,512]{1,0:T(8,128)(2,1)S(1)}, bf16[256,512]{1,0:T(8,128)(2,1)S(1)}, u32[]{:S(2)}, u32[]{:S(2)}) collective-permute-start(bf16[256,512]{1,0:T(8,128)(2,1)S(1)} %get-tuple-element.188), channel_id=1, source_target_pairs={{0,8},{1,9},{2,10},{3,11},{4,12},{5,13},{6,14},{7,15},{8,0},{9,1},... | collective-permute-start | bytes 786440 | tf_op jit(solution)/shard_map/ppermute | solution.py:54
  172.3 9.9 %collective-permute-start.43 = (bf16[256,512]{1,0:T(8,128)(2,1)S(1)}, bf16[256,512]{1,0:T(8,128)(2,1)S(1)}, u32[]{:S(2)}, u32[]{:S(2)}) collective-permute-start(bf16[256,512]{1,0:T(8,128)(2,1)S(1)} %get-tuple-element.189), channel_id=1, source_target_pairs={{0,12},{1,13},{2,14},{3,15},{4,0},{5,1},{6,2},{7,3},{8,4},{9,5},{1... | collective-permute-start | bytes 786440 | tf_op jit(solution)/shard_map/ppermute | solution.py:54
  182.7 2.0 %collective-permute-start.47 = (f32[256,512]{1,0:T(8,128)S(1)}, f32[256,512]{1,0:T(8,128)S(1)}, u32[]{:S(2)}, u32[]{:S(2)}) collective-permute-start(f32[256,512]{1,0:T(8,128)S(1)} %row_sum_other.1), channel_id=1, source_target_pairs={{0,16},{16,0},{1,17},{17,1},{2,18},{18,2},{3,19},{19,3},{4,20},{20... | collective-permute-start | bytes 1572872 | tf_op jit(solution)/shard_map/ppermute | solution.py:70

commit v7 on v6

--- a/solution.py
+++ b/solution.py
@@ -464,7 +464,7 @@
     partial_shapes += [shape(CHUNKS * GATHERED, COLS, BF16), shape(3 * CHUNKS * GATHERED, COLS, BF16)]
     zeros = call(zeros_kernel, "zeros", partial_shapes)
     up, down, across = shift_z(grads, -1), shift_z(grads, 1), shift_z(grads, 2)
-    down, zeros = after((down, zeros), up)
+    down, zeros = after((down, zeros), (up, first_of))
     band = [grads, up, across, down]
     inputs = [
         where,

time: 186 us -> 186 us (level)
  Pallas kernels: 23.6 us -> 27.9 us
  starting transfers between devices: 63.1 us -> 59.3 us
    ppermute x25, starting transfers between devices: 30.6 us -> 27.2 us  [shift(): return lax.ppermute(value, CHIP_AXES, along(first, step))]
    pallas_call x13, Pallas kernels: 16.4 us -> 19.5 us  [call(): pl.pallas_call(kernel, in_specs=whole, out_specs=[VMEM] * len(outs), out_...]
    ppermute x25, waiting for transfers between devices: 56.9 us -> 54.4 us  [shift(): return lax.ppermute(value, CHIP_AXES, along(first, step))]
    ppermute x14, waiting for transfers between devices: 9.3 us -> 11.8 us  [swap(): return lax.ppermute(value, 'core', [(0, 1), (1, 0)])]
  transfers between devices with their start and end apart: 48 -> 48, of which waited for: 32 -> 32; matrix products, arithmetic and copies ran while one was open for 1% -> 1% of each run, Pallas kernels for 8% -> 10%
where the time goes in v7:
time: 186 us
  waiting for transfers between devices  92 us (49%)
  starting transfers between devices  59.3 us (32%)
  Pallas kernels  27.9 us (15%)
  local copies, waits for them, and re-layouts  2.78 us (1%)
  between operations  1.93 us (1%)
    ppermute x25, waiting for transfers between devices, shift(): return lax.ppermute(value, CHIP_AXES, along(first, step))  54.4 us
    ppermute x25, starting transfers between devices, shift(): return lax.ppermute(value, CHIP_AXES, along(first, step))  27.2 us
    pallas_call x13, Pallas kernels, call(): pl.pallas_call(kernel, in_specs=whole, out_specs=[VMEM] * len(outs), out_...  19.5 us
    ppermute x14, starting transfers between devices, swap(): return lax.ppermute(value, 'core', [(0, 1), (1, 0)])  18.5 us
    ppermute x6, waiting for transfers between devices, shift_z(): lax.ppermute(value, 'z', [(i, (i + step) % RING) for i in range(RING)])  14.6 us
    ppermute x14, waiting for transfers between devices, swap(): return lax.ppermute(value, 'core', [(0, 1), (1, 0)])  11.8 us
    ppermute x3, waiting for transfers between devices, pair_z(): return lax.ppermute(value, 'z', [(i, i ^ flip) for i in range(RING)])  11.3 us
    ppermute x6, starting transfers between devices, shift_z(): lax.ppermute(value, 'z', [(i, (i + step) % RING) for i in range(RING)])  8.1 us
  transfers between devices with their start and end apart: 48, of which 32 were waited for; matrix products, arithmetic and copies ran while one was open for 1% of the time, Pallas kernels for 10%

profile of v7, /device:TPU:1, one launch (start us, length us, event | category | flops | bytes accessed | tf_op | source)
XLA Modules:
  0.0 186.3 jit_solution(1861340830353652877)
XLA Ops:
  0.7 1.1 copy-done.1
  1.8 1.0 copy-done.6
  2.9 1.0 first_product.1
  3.8 1.5 collective-permute-start
  5.4 1.1 collective-permute-done.got
  6.5 1.4 collective-permute-start.3
  8.0 2.6 %collective-permute-start.2 = (bf16[512,512]{1,0:T(8,128)(2,1)S(1)}, bf16[512,512]{1,0:T(8,128)(2,1)S(1)}, u32[]{:S(2)}, u32[]{:S(2)}) collective-permute-start(bf16[512,512]{1,0:T(8,128)(2,1)S(1)} %constant_dynamic-update-slice_fusion), channel_id=1, source_target_pairs={{0,8},{1,9},{2,10},{3,11},{4,12},{5,13},{6,14},{7,15},{8,0},{9,1},... | collective-permute-start | bytes 1572872 | tf_op jit(solution)/shard_map/ppermute | solution.py:54
  10.6 1.1 collective-permute-start.1
  11.7 3.8 %collective-permute-start.5 = (bf16[256,512]{1,0:T(8,128)(2,1)}, bf16[256,512]{1,0:T(8,128)(2,1)S(1)}, u32[]{:S(2)}, u32[]{:S(2)}) collective-permute-start(bf16[256,512]{1,0:T(8,128)(2,1)} %param.16), channel_id=1, source_target_pairs={{0,96},{32,64},{64,32},{96,0},{1,97},{33,65},{65,33},{97,1},{2,98}... | collective-permute-start | bytes 786440 | tf_op jit(solution)/shard_map/ppermute | solution.py:66
  15.4 5.8 %collective-permute-done.5 = bf16[256,512]{1,0:T(8,128)(2,1)S(1)} collective-permute-done((bf16[256,512]{1,0:T(8,128)(2,1)}, bf16[256,512]{1,0:T(8,128)(2,1)S(1)}, u32[]{:S(2)}, u32[]{:S(2)}) %collective-permute-start.5) | collective-permute-done | bytes 262176 | tf_op jit(solution)/shard_map/ppermute | solution.py:66
  22.1 1.0 collective-permute-done.2.across
  23.2 1.3 collective-permute-start.7
  24.5 1.4 collective-permute-start.6
  26.0 1.7 collective-permute-start.8
  27.8 4.6 %collective-permute-done.8 = bf16[256,512]{1,0:T(8,128)(2,1)S(1)} collective-permute-done((bf16[256,512]{1,0:T(8,128)(2,1)S(1)}, bf16[256,512]{1,0:T(8,128)(2,1)S(1)}, u32[]{:S(2)}, u32[]{:S(2)}) %collective-permute-start.8) | collective-permute-done | bytes 262176 | tf_op jit(solution)/shard_map/ppermute | solution.py:66
  32.4 6.1 %collective-permute-done.7.rest_1_ = bf16[2048,256]{1,0:T(8,128)(2,1)S(1)} collective-permute-done((bf16[2048,256]{1,0:T(8,128)(2,1)S(1)}, bf16[2048,256]{1,0:T(8,128)(2,1)S(1)}, u32[]{:S(2)}, u32[]{:S(2)}) %collective-permute-start.7) | collective-permute-done | bytes 1048608 | tf_op jit(solution)/shard_map/ppermute | solution.py:54
  38.8 2.3 %collective-permute-start.11 = (bf16[5120,256]{1,0:T(8,128)(2,1)S(1)}, bf16[5120,256]{1,0:T(8,128)(2,1)S(1)}, u32[]{:S(2)}, u32[]{:S(2)}) collective-permute-start(bf16[5120,256]{1,0:T(8,128)(2,1)S(1)} %slice_dynamic-update-slice_fusion), channel_id=1, source_target_pairs={{0,16},{16,0},{1,17},{17,1},{2,18},{18,2},{3,19},{19,3},{4,20},{20... | collective-permute-start | bytes 7864328 | tf_op jit(solution)/shard_map/ppermute | solution.py:70
  41.1 1.6 collective-permute-start.12
  42.7 1.1 collective-permute-start.13
  44.2 2.3 %collective-permute-start.9 = (bf16[2048,256]{1,0:T(8,128)(2,1)S(1)}, bf16[2048,256]{1,0:T(8,128)(2,1)S(1)}, u32[]{:S(2)}, u32[]{:S(2)}) collective-permute-start(bf16[2048,256]{1,0:T(8,128)(2,1)S(1)} %get-tuple-element.110.rest_0_), channel_id=1, source_target_pairs={{0,3},{1,0},{2,1},{3,2},{4,7},{5,4},{6,5},{7,6},{8,11},{9,8},{10,9... | collective-permute-start | bytes 3145736 | tf_op jit(solution)/shard_map/ppermute | solution.py:54
  46.4 4.2 %collective-permute-done.12.rest_2_ = bf16[1024,256]{1,0:T(8,128)(2,1)S(1)} collective-permute-done((bf16[1024,256]{1,0:T(8,128)(2,1)S(1)}, bf16[1024,256]{1,0:T(8,128)(2,1)S(1)}, u32[]{:S(2)}, u32[]{:S(2)}) %collective-permute-start.12) | collective-permute-done | bytes 524320 | tf_op jit(solution)/shard_map/ppermute | solution.py:54
  53.0 4.4 %edge_terms.1 = (f32[2048,256]{1,0:T(8,128)S(1)}, f32[2048,256]{1,0:T(8,128)S(1)}) custom-call(s32[4]{0:T(128)S(1)} %pad_add_fusion.where, s32[1]{0:T(128)S(6)} %copy.47.live, s32[16]{0:T(128)S(1)} %copy-done.10, bf16[2048,128]{1,0:T(8,128)(2,1)S(1)} %fusion.1.pick, bf16[2048,512]{1,0:T(8,128)(2,1)S(1)} %copy-done.3, bf16[512,512]{1,0:T(8,128)(2,1)S(1)} %copy-done.4, ...), custom_call_target="tpu_custom_call" | custom-call | tf_op jit(solution)/shard_map/edge_terms/pallas_call | solution.py:354
  57.4 4.4 %collective-permute-done.10.rest_1_ = bf16[2048,256]{1,0:T(8,128)(2,1)S(1)} collective-permute-done((bf16[2048,256]{1,0:T(8,128)(2,1)S(1)}, bf16[2048,256]{1,0:T(8,128)(2,1)S(1)}, u32[]{:S(2)}, u32[]{:S(2)}) %collective-permute-start.10) | collective-permute-done | bytes 1048608 | tf_op jit(solution)/shard_map/ppermute | solution.py:54
  62.5 1.0 collective-permute-start.17
  63.5 2.3 %collective-permute-start.15 = (bf16[1024,256]{1,0:T(8,128)(2,1)S(1)}, bf16[1024,256]{1,0:T(8,128)(2,1)S(1)}, u32[]{:S(2)}, u32[]{:S(2)}) collective-permute-start(bf16[1024,256]{1,0:T(8,128)(2,1)S(1)} %slice.44), channel_id=1, source_target_pairs={{0,3},{1,0},{2,1},{3,2},{4,7},{5,4},{6,5},{7,6},{8,11},{9,8},{10,9... | collective-permute-start | bytes 1572872 | tf_op jit(solution)/shard_map/ppermute | solution.py:54
  66.5 5.3 %forward_0.1 = (f32[2048,256]{1,0:T(8,128)S(1)}, f32[1024,256]{1,0:T(8,128)S(1)}, bf16[1024,256]{1,0:T(8,128)(2,1)S(1)}) custom-call(s32[4]{0:T(128)S(1)} %pad_add_fusion.where, s32[1]{0:T(128)S(6)} %copy.47.live, s32[16]{0:T(128)S(1)} %copy-done.11, s32[16]{0:T(128)S(1)} %copy-done.10, bf16[2048,128]{1,0:T(8,128)(2,1)S(1)} %fusion.2.pick, ...), custom_call_target="tpu_custom_call" | custom-call | tf_op jit(solution)/shard_map/forward_0/pallas_call | solution.py:354
  72.0 3.3 %collective-permute-done.16.rest_2_ = bf16[1024,256]{1,0:T(8,128)(2,1)S(1)} collective-permute-done((bf16[1024,256]{1,0:T(8,128)(2,1)S(1)}, bf16[1024,256]{1,0:T(8,128)(2,1)S(1)}, u32[]{:S(2)}, u32[]{:S(2)}) %collective-permute-start.16) | collective-permute-done | bytes 524320 | tf_op jit(solution)/shard_map/ppermute | solution.py:54
  75.3 1.6 collective-permute-start.18
  76.9 1.5 collective-permute-done.18.rest_5_
  78.4 5.3 %forward_1.1 = (f32[2048,256]{1,0:T(8,128)S(1)}, f32[1024,256]{1,0:T(8,128)S(1)}, bf16[1024,256]{1,0:T(8,128)(2,1)S(1)}) custom-call(s32[4]{0:T(128)S(1)} %pad_add_fusion.where, s32[1]{0:T(128)S(6)} %copy.47.live, s32[16]{0:T(128)S(1)} %copy-done.11, s32[16]{0:T(128)S(1)} %copy-done.10, bf16[2048,128]{1,0:T(8,128)(2,1)S(1)} %fusion.2.pick, ...), custom_call_target="tpu_custom_call" | custom-call | tf_op jit(solution)/shard_map/forward_1/pallas_call | solution.py:354
  83.9 1.9 %collective-permute-done.20.refs_3_ = bf16[1024,256]{1,0:T(8,128)(2,1)S(1)} collective-permute-done((bf16[1024,256]{1,0:T(8,128)(2,1)S(1)}, bf16[1024,256]{1,0:T(8,128)(2,1)S(1)}, u32[]{:S(2)}, u32[]{:S(2)}) %collective-permute-start.20) | collective-permute-done | bytes 524320 | tf_op jit(solution)/shard_map/ppermute | solution.py:70
  86.0 1.7 collective-permute-start.21
  87.6 2.4 %collective-permute-start.22 = (bf16[256,512]{1,0:T(8,128)(2,1)S(1)}, bf16[256,512]{1,0:T(8,128)(2,1)S(1)}, u32[]{:S(2)}, u32[]{:S(2)}) collective-permute-start(bf16[256,512]{1,0:T(8,128)(2,1)S(1)} %get-tuple-element.134), channel_id=1, source_target_pairs={{0,96},{32,0},{64,32},{96,64},{1,97},{33,1},{65,33},{97,65},{2,98}... | collective-permute-start | bytes 786440 | tf_op jit(solution)/shard_map/ppermute | solution.py:58
  90.0 1.1 collective-permute-start.23
  91.1 5.2 %collective-permute-done.21.a = bf16[256,512]{1,0:T(8,128)(2,1)S(1)} collective-permute-done((bf16[256,512]{1,0:T(8,128)(2,1)S(1)}, bf16[256,512]{1,0:T(8,128)(2,1)S(1)}, u32[]{:S(2)}, u32[]{:S(2)}) %collective-permute-start.21) | collective-permute-done | bytes 262176 | tf_op jit(solution)/shard_map/ppermute | solution.py:58
  96.4 6.5 %collective-permute-done.23.c = bf16[256,512]{1,0:T(8,128)(2,1)S(1)} collective-permute-done((bf16[256,512]{1,0:T(8,128)(2,1)S(1)}, bf16[256,512]{1,0:T(8,128)(2,1)S(1)}, u32[]{:S(2)}, u32[]{:S(2)}) %collective-permute-start.23) | collective-permute-done | bytes 262176 | tf_op jit(solution)/shard_map/ppermute | solution.py:58
  104.3 2.1 %collective-permute-start.24 = (bf16[256,512]{1,0:T(8,128)(2,1)S(1)}, bf16[256,512]{1,0:T(8,128)(2,1)S(1)}, u32[]{:S(2)}, u32[]{:S(2)}) collective-permute-start(bf16[256,512]{1,0:T(8,128)(2,1)S(1)} %get-tuple-element.139.rest_2_), channel_id=1, source_target_pairs={{0,96},{32,0},{64,32},{96,64},{1,97},{33,1},{65,33},{97,65},{2,98}... | collective-permute-start | bytes 786440 | tf_op jit(solution)/shard_map/ppermute | solution.py:58
  107.4 1.6 collective-permute-start.27
  109.0 2.8 %collective-permute-done.26.rest_5_ = bf16[256,512]{1,0:T(8,128)(2,1)S(1)} collective-permute-done((bf16[256,512]{1,0:T(8,128)(2,1)S(1)}, bf16[256,512]{1,0:T(8,128)(2,1)S(1)}, u32[]{:S(2)}, u32[]{:S(2)}) %collective-permute-start.26) | collective-permute-done | bytes 262176 | tf_op jit(solution)/shard_map/ppermute | solution.py:58
  111.8 6.8 %collective-permute-start.28 = (bf16[256,512]{1,0:T(8,128)(2,1)S(1)}, bf16[256,512]{1,0:T(8,128)(2,1)S(1)}, u32[]{:S(2)}, u32[]{:S(2)}) collective-permute-start(bf16[256,512]{1,0:T(8,128)(2,1)S(1)} %collective-permute-done.24.rest_3_), channel_id=1, source_target_pairs={{0,16},{16,0},{1,17},{17,1},{2,18},{18,2},{3,19},{19,3},{4,20},{20... | collective-permute-start | bytes 786440 | tf_op jit(solution)/shard_map/ppermute | solution.py:70
  118.6 1.0 collective-permute-start.29
  119.6 1.2 collective-permute-done.29.rest_8_
  121.1 5.2 %backward.1 = (bf16[1024,256]{1,0:T(8,128)(2,1)S(1)}, bf16[1024,256]{1,0:T(8,128)(2,1)S(1)}, bf16[1024,256]{1,0:T(8,128)(2,1)S(1)}, bf16[1024,256]{1,0:T(8,128)(...) custom-call(s32[4]{0:T(128)S(1)} %pad_add_fusion.where, ...), custom_call_target="tpu_custom_call", output_to_operand_aliasing={{0}: (17, {}), {1}: (18, {}), {2}: (19, {}), {3}: (20, {}),... | custom-call | tf_op jit(solution)/shard_map/backward/pallas_call | solution.py:481
  126.4 1.2 collective-permute-start.34
  127.9 4.1 %collective-permute-done.31.refs_0_ = bf16[6144,256]{1,0:T(8,128)(2,1)S(1)} collective-permute-done((bf16[6144,256]{1,0:T(8,128)(2,1)S(1)}, bf16[6144,256]{1,0:T(8,128)(2,1)S(1)}, u32[]{:S(2)}, u32[]{:S(2)}) %collective-permute-start.31) | collective-permute-done | bytes 3145760 | tf_op jit(solution)/shard_map/ppermute | solution.py:70
  132.1 0.9 collective-permute-start.33
  133.6 1.1 collective-permute-done.34.refs_4_
  134.8 2.4 %collective-permute-done.35.refs_5_ = bf16[1024,256]{1,0:T(8,128)(2,1)S(1)} collective-permute-done((bf16[1024,256]{1,0:T(8,128)(2,1)S(1)}, bf16[1024,256]{1,0:T(8,128)(2,1)S(1)}, u32[]{:S(2)}, u32[]{:S(2)}) %collective-permute-start.35) | collective-permute-done | bytes 524320 | tf_op jit(solution)/shard_map/ppermute | solution.py:54
  137.5 1.5 collective-permute-start.40
  138.9 1.5 collective-permute-done.33.refs_1_
  140.5 2.3 %collective-permute-done.32.refs_2_ = bf16[1024,256]{1,0:T(8,128)(2,1)S(1)} collective-permute-done((bf16[1024,256]{1,0:T(8,128)(2,1)S(1)}, bf16[1024,256]{1,0:T(8,128)(2,1)S(1)}, u32[]{:S(2)}, u32[]{:S(2)}) %collective-permute-start.32) | collective-permute-done | bytes 524320 | tf_op jit(solution)/shard_map/ppermute | solution.py:54
  143.3 1.0 collective-permute-start.37
  144.9 1.1 fusion
  145.9 5.8 %collective-permute-done.39.refs_2_ = bf16[2048,256]{1,0:T(8,128)(2,1)S(1)} collective-permute-done((bf16[2048,256]{1,0:T(8,128)(2,1)S(1)}, bf16[2048,256]{1,0:T(8,128)(2,1)S(1)}, u32[]{:S(2)}, u32[]{:S(2)}) %collective-permute-start.39) | collective-permute-done | bytes 1048608 | tf_op jit(solution)/shard_map/ppermute | solution.py:54
  151.7 2.3 %collective-permute-done.40.refs_3_ = bf16[2048,256]{1,0:T(8,128)(2,1)S(1)} collective-permute-done((bf16[2048,256]{1,0:T(8,128)(2,1)S(1)}, bf16[2048,256]{1,0:T(8,128)(2,1)S(1)}, u32[]{:S(2)}, u32[]{:S(2)}) %collective-permute-start.40) | collective-permute-done | bytes 1048608 | tf_op jit(solution)/shard_map/ppermute | solution.py:54
  154.5 2.6 %collective-permute-start.46 = (bf16[256,512]{1,0:T(8,128)(2,1)S(1)}, bf16[256,512]{1,0:T(8,128)(2,1)S(1)}, u32[]{:S(2)}, u32[]{:S(2)}) collective-permute-start(bf16[256,512]{1,0:T(8,128)(2,1)S(1)} %get-tuple-element.183), channel_id=1, source_target_pairs={{0,12},{1,13},{2,14},{3,15},{4,0},{5,1},{6,2},{7,3},{8,4},{9,5},{1... | collective-permute-start | bytes 786440 | tf_op jit(solution)/shard_map/ppermute | solution.py:54
  157.1 9.9 %collective-permute-done.37.refs_1_ = bf16[2048,256]{1,0:T(8,128)(2,1)S(1)} collective-permute-done((bf16[2048,256]{1,0:T(8,128)(2,1)S(1)}, bf16[2048,256]{1,0:T(8,128)(2,1)S(1)}, u32[]{:S(2)}, u32[]{:S(2)}) %collective-permute-start.37) | collective-permute-done | bytes 1048608 | tf_op jit(solution)/shard_map/ppermute | solution.py:54
  167.0 3.6 %collective-permute-done.38.refs_2_ = bf16[2048,256]{1,0:T(8,128)(2,1)S(1)} collective-permute-done((bf16[2048,256]{1,0:T(8,128)(2,1)S(1)}, bf16[2048,256]{1,0:T(8,128)(2,1)S(1)}, u32[]{:S(2)}, u32[]{:S(2)}) %collective-permute-start.38) | collective-permute-done | bytes 1048608 | tf_op jit(solution)/shard_map/ppermute | solution.py:54
  171.2 2.5 %collective-permute-start.43 = (bf16[256,512]{1,0:T(8,128)(2,1)S(1)}, bf16[256,512]{1,0:T(8,128)(2,1)S(1)}, u32[]{:S(2)}, u32[]{:S(2)}) collective-permute-start(bf16[256,512]{1,0:T(8,128)(2,1)S(1)} %get-tuple-element.189), channel_id=1, source_target_pairs={{0,12},{1,13},{2,14},{3,15},{4,0},{5,1},{6,2},{7,3},{8,4},{9,5},{1... | collective-permute-start | bytes 786440 | tf_op jit(solution)/shard_map/ppermute | solution.py:54
  173.7 1.8 place_mine.1.placed
  175.6 5.0 %collective-permute-done.41.up = bf16[256,512]{1,0:T(8,128)(2,1)S(1)} collective-permute-done((bf16[256,512]{1,0:T(8,128)(2,1)S(1)}, bf16[256,512]{1,0:T(8,128)(2,1)S(1)}, u32[]{:S(2)}, u32[]{:S(2)}) %collective-permute-start.41) | collective-permute-done | bytes 262176 | tf_op jit(solution)/shard_map/ppermute | solution.py:54
  181.7 1.6 collective-permute-start.47
  183.3 1.5 collective-permute-done.47.value
  184.8 1.3 place_other.1
  (100 shorter events, 13.1 us)
Async XLA Ops:
  0.6 65.1 %copy-start = (bf16[512,512]{1,0:T(8,128)(2,1)S(1)}, bf16[512,512]{1,0:T(8,128)(2,1)}, u32[]{:S(2)}) copy-start(bf16[512,512]{1,0:T(8,128)(2,1)} %param.28) | copy-start | bytes 1572868
  0.7 1.1 copy-start.1
  1.8 1.0 copy-start.6
  2.9 23.1 %copy-start.14 = (bf16[256,512]{1,0:T(8,128)(2,1)S(1)}, bf16[256,512]{1,0:T(8,128)(2,1)}, u32[]{:S(2)}) copy-start(bf16[256,512]{1,0:T(8,128)(2,1)} %param.16) | copy-start | bytes 786436
  3.8 2.7 %collective-permute-start = (bf16[256,512]{1,0:T(8,128)(2,1)S(1)}, bf16[256,512]{1,0:T(8,128)(2,1)S(1)}, u32[]{:S(2)}, u32[]{:S(2)}) collective-permute-start(bf16[256,512]{1,0:T(8,128)(2,1)S(1)} %get-tuple-element.101), channel_id=1, source_target_pairs={{0,16},{16,0},{1,17},{17,1},{2,18},{18,2},{3,19},{19,3},{4,20},{20... | collective-permute-start | bytes 786440 | tf_op jit(solution)/shard_map/ppermute | solution.py:70
  6.5 15.6 %collective-permute-start.3 = (bf16[512,512]{1,0:T(8,128)(2,1)S(1)}, bf16[512,512]{1,0:T(8,128)(2,1)S(1)}, u32[]{:S(2)}, u32[]{:S(2)}) collective-permute-start(bf16[512,512]{1,0:T(8,128)(2,1)S(1)} %constant_dynamic-update-slice_fusion), channel_id=1, source_target_pairs={{0,4},{1,5},{2,6},{3,7},{4,8},{5,9},{6,10},{7,11},{8,12},{9,13},{1... | collective-permute-start | bytes 1572872 | tf_op jit(solution)/shard_map/ppermute | solution.py:54
  8.0 15.1 %collective-permute-start.2 = (bf16[512,512]{1,0:T(8,128)(2,1)S(1)}, bf16[512,512]{1,0:T(8,128)(2,1)S(1)}, u32[]{:S(2)}, u32[]{:S(2)}) collective-permute-start(bf16[512,512]{1,0:T(8,128)(2,1)S(1)} %constant_dynamic-update-slice_fusion), channel_id=1, source_target_pairs={{0,8},{1,9},{2,10},{3,11},{4,12},{5,13},{6,14},{7,15},{8,0},{9,1},... | collective-permute-start | bytes 1572872 | tf_op jit(solution)/shard_map/ppermute | solution.py:54
  10.6 12.5 %collective-permute-start.1 = (bf16[512,512]{1,0:T(8,128)(2,1)S(1)}, bf16[512,512]{1,0:T(8,128)(2,1)S(1)}, u32[]{:S(2)}, u32[]{:S(2)}) collective-permute-start(bf16[512,512]{1,0:T(8,128)(2,1)S(1)} %constant_dynamic-update-slice_fusion), channel_id=1, source_target_pairs={{0,12},{1,13},{2,14},{3,15},{4,0},{5,1},{6,2},{7,3},{8,4},{9,5},{1... | collective-permute-start | bytes 1572872 | tf_op jit(solution)/shard_map/ppermute | solution.py:54
  11.7 9.6 %collective-permute-start.5 = (bf16[256,512]{1,0:T(8,128)(2,1)}, bf16[256,512]{1,0:T(8,128)(2,1)S(1)}, u32[]{:S(2)}, u32[]{:S(2)}) collective-permute-start(bf16[256,512]{1,0:T(8,128)(2,1)} %param.16), channel_id=1, source_target_pairs={{0,96},{32,64},{64,32},{96,0},{1,97},{33,65},{65,33},{97,1},{2,98}... | collective-permute-start | bytes 786440 | tf_op jit(solution)/shard_map/ppermute | solution.py:66
  15.4 6.7 %collective-permute-start.4 = (bf16[256,512]{1,0:T(8,128)(2,1)}, bf16[256,512]{1,0:T(8,128)(2,1)S(1)}, u32[]{:S(2)}, u32[]{:S(2)}) collective-permute-start(bf16[256,512]{1,0:T(8,128)(2,1)} %param.16), channel_id=1, source_target_pairs={{0,32},{32,0},{64,96},{96,64},{1,33},{33,1},{65,97},{97,65},{2,34}... | collective-permute-start | bytes 786440 | tf_op jit(solution)/shard_map/ppermute | solution.py:66
  23.2 15.2 %collective-permute-start.7 = (bf16[2048,256]{1,0:T(8,128)(2,1)S(1)}, bf16[2048,256]{1,0:T(8,128)(2,1)S(1)}, u32[]{:S(2)}, u32[]{:S(2)}) collective-permute-start(bf16[2048,256]{1,0:T(8,128)(2,1)S(1)} %get-tuple-element.107.rest_0_), channel_id=1, source_target_pairs={{0,1},{1,2},{2,3},{3,0},{4,5},{5,6},{6,7},{7,4},{8,9},{9,10},{10,1... | collective-permute-start | bytes 3145736 | tf_op jit(solution)/shard_map/ppermute | solution.py:54
  24.5 13.9 %collective-permute-start.6 = (bf16[2048,256]{1,0:T(8,128)(2,1)S(1)}, bf16[2048,256]{1,0:T(8,128)(2,1)S(1)}, u32[]{:S(2)}, u32[]{:S(2)}) collective-permute-start(bf16[2048,256]{1,0:T(8,128)(2,1)S(1)} %get-tuple-element.107.rest_0_), channel_id=1, source_target_pairs={{0,3},{1,0},{2,1},{3,2},{4,7},{5,4},{6,5},{7,6},{8,11},{9,8},{10,9... | collective-permute-start | bytes 3145736 | tf_op jit(solution)/shard_map/ppermute | solution.py:54
  26.0 6.4 %collective-permute-start.8 = (bf16[256,512]{1,0:T(8,128)(2,1)S(1)}, bf16[256,512]{1,0:T(8,128)(2,1)S(1)}, u32[]{:S(2)}, u32[]{:S(2)}) collective-permute-start(bf16[256,512]{1,0:T(8,128)(2,1)S(1)} %collective-permute-done.5), channel_id=1, source_target_pairs={{0,32},{32,0},{64,96},{96,64},{1,33},{33,1},{65,97},{97,65},{2,34}... | collective-permute-start | bytes 786440 | tf_op jit(solution)/shard_map/ppermute | solution.py:66
  38.6 14.0 %copy-start.8 = (s32[16,128]{1,0:T(8,128)S(1)}, s32[16,128]{1,0:T(8,128)}, u32[]{:S(2)}) copy-start(s32[16,128]{1,0:T(8,128)} %recv.3) | copy-start | bytes 24580
  38.6 14.4 %copy-start.3 = (bf16[2048,512]{1,0:T(8,128)(2,1)S(1)}, bf16[2048,512]{1,0:T(8,128)(2,1)}, u32[]{:S(2)}) copy-start(bf16[2048,512]{1,0:T(8,128)(2,1)} %edge.1) | copy-start | bytes 6291460
  38.6 14.4 %copy-start.4 = (bf16[512,512]{1,0:T(8,128)(2,1)S(1)}, bf16[512,512]{1,0:T(8,128)(2,1)}, u32[]{:S(2)}) copy-start(bf16[512,512]{1,0:T(8,128)(2,1)} %w_mesh.1) | copy-start | bytes 1572868
  38.6 14.4 %copy-start.5 = (bf16[512,512]{1,0:T(8,128)(2,1)S(1)}, bf16[512,512]{1,0:T(8,128)(2,1)}, u32[]{:S(2)}) copy-start(bf16[512,512]{1,0:T(8,128)(2,1)} %w_edge.1) | copy-start | bytes 1572868
  38.6 14.4 %copy-start.10 = (s32[16]{0:T(128)S(1)}, s32[16]{0:T(128)}, u32[]{:S(2)}) copy-start(s32[16]{0:T(128)} %mesh_block.7) | copy-start | bytes 196
  38.6 14.4 %copy-start.12 = (f32[512]{0:T(512)S(1)}, f32[512]{0:T(512)}, u32[]{:S(2)}) copy-start(f32[512]{0:T(512)} %param.26) | copy-start | bytes 6148
  38.8 14.1 %collective-permute-start.11 = (bf16[5120,256]{1,0:T(8,128)(2,1)S(1)}, bf16[5120,256]{1,0:T(8,128)(2,1)S(1)}, u32[]{:S(2)}, u32[]{:S(2)}) collective-permute-start(bf16[5120,256]{1,0:T(8,128)(2,1)S(1)} %slice_dynamic-update-slice_fusion), channel_id=1, source_target_pairs={{0,16},{16,0},{1,17},{17,1},{2,18},{18,2},{3,19},{19,3},{4,20},{20... | collective-permute-start | bytes 7864328 | tf_op jit(solution)/shard_map/ppermute | solution.py:70
  41.1 9.5 %collective-permute-start.12 = (bf16[1024,256]{1,0:T(8,128)(2,1)S(1)}, bf16[1024,256]{1,0:T(8,128)(2,1)S(1)}, u32[]{:S(2)}, u32[]{:S(2)}) collective-permute-start(bf16[1024,256]{1,0:T(8,128)(2,1)S(1)} %get-tuple-element.204), channel_id=1, source_target_pairs={{0,1},{1,2},{2,3},{3,0},{4,5},{5,6},{6,7},{7,4},{8,9},{9,10},{10,1... | collective-permute-start | bytes 1572872 | tf_op jit(solution)/shard_map/ppermute | solution.py:54
  42.7 8.3 %collective-permute-start.13 = (bf16[1024,256]{1,0:T(8,128)(2,1)S(1)}, bf16[1024,256]{1,0:T(8,128)(2,1)S(1)}, u32[]{:S(2)}, u32[]{:S(2)}) collective-permute-start(bf16[1024,256]{1,0:T(8,128)(2,1)S(1)} %get-tuple-element.202), channel_id=1, source_target_pairs={{0,3},{1,0},{2,1},{3,2},{4,7},{5,4},{6,5},{7,6},{8,11},{9,8},{10,9... | collective-permute-start | bytes 1572872 | tf_op jit(solution)/shard_map/ppermute | solution.py:54
  43.8 18.1 %collective-permute-start.10 = (bf16[2048,256]{1,0:T(8,128)(2,1)S(1)}, bf16[2048,256]{1,0:T(8,128)(2,1)S(1)}, u32[]{:S(2)}, u32[]{:S(2)}) collective-permute-start(bf16[2048,256]{1,0:T(8,128)(2,1)S(1)} %get-tuple-element.110.rest_0_), channel_id=1, source_target_pairs={{0,1},{1,2},{2,3},{3,0},{4,5},{5,6},{6,7},{7,4},{8,9},{9,10},{10,1... | collective-permute-start | bytes 3145736 | tf_op jit(solution)/shard_map/ppermute | solution.py:54
  44.2 18.1 %collective-permute-start.9 = (bf16[2048,256]{1,0:T(8,128)(2,1)S(1)}, bf16[2048,256]{1,0:T(8,128)(2,1)S(1)}, u32[]{:S(2)}, u32[]{:S(2)}) collective-permute-start(bf16[2048,256]{1,0:T(8,128)(2,1)S(1)} %get-tuple-element.110.rest_0_), channel_id=1, source_target_pairs={{0,3},{1,0},{2,1},{3,2},{4,7},{5,4},{6,5},{7,6},{8,11},{9,8},{10,9... | collective-permute-start | bytes 3145736 | tf_op jit(solution)/shard_map/ppermute | solution.py:54
  51.0 11.2 %collective-permute-start.14 = (bf16[1024,256]{1,0:T(8,128)(2,1)S(1)}, bf16[1024,256]{1,0:T(8,128)(2,1)S(1)}, u32[]{:S(2)}, u32[]{:S(2)}) collective-permute-start(bf16[1024,256]{1,0:T(8,128)(2,1)S(1)} %collective-permute-done.13), channel_id=1, source_target_pairs={{0,16},{16,0},{1,17},{17,1},{2,18},{18,2},{3,19},{19,3},{4,20},{20... | collective-permute-start | bytes 1572872 | tf_op jit(solution)/shard_map/ppermute | solution.py:70
  62.3 3.5 %copy-start.13 = (bf16[256,512]{1,0:T(8,128)(2,1)S(1)}, bf16[256,512]{1,0:T(8,128)(2,1)}, u32[]{:S(2)}) copy-start(bf16[256,512]{1,0:T(8,128)(2,1)} %param.29) | copy-start | bytes 786436
  62.4 3.7 %copy-start.9 = (s32[16,128]{1,0:T(8,128)S(1)}, s32[16,128]{1,0:T(8,128)}, u32[]{:S(2)}) copy-start(s32[16,128]{1,0:T(8,128)} %send.1) | copy-start | bytes 24580
  62.4 4.1 %copy-start.11 = (s32[16]{0:T(128)S(1)}, s32[16]{0:T(128)}, u32[]{:S(2)}) copy-start(s32[16]{0:T(128)} %grid_block.5) | copy-start | bytes 196
  62.5 12.8 %collective-permute-start.17 = (bf16[3072,256]{1,0:T(8,128)(2,1)S(1)}, bf16[3072,256]{1,0:T(8,128)(2,1)S(1)}, u32[]{:S(2)}, u32[]{:S(2)}) collective-permute-start(bf16[3072,256]{1,0:T(8,128)(2,1)S(1)} %pad_maximum_fusion), channel_id=1, source_target_pairs={{0,16},{16,0},{1,17},{17,1},{2,18},{18,2},{3,19},{19,3},{4,20},{20... | collective-permute-start | bytes 4718600 | tf_op jit(solution)/shard_map/ppermute | solution.py:70
  63.5 8.5 %collective-permute-start.15 = (bf16[1024,256]{1,0:T(8,128)(2,1)S(1)}, bf16[1024,256]{1,0:T(8,128)(2,1)S(1)}, u32[]{:S(2)}, u32[]{:S(2)}) collective-permute-start(bf16[1024,256]{1,0:T(8,128)(2,1)S(1)} %slice.44), channel_id=1, source_target_pairs={{0,3},{1,0},{2,1},{3,2},{4,7},{5,4},{6,5},{7,6},{8,11},{9,8},{10,9... | collective-permute-start | bytes 1572872 | tf_op jit(solution)/shard_map/ppermute | solution.py:54
  65.8 9.5 %collective-permute-start.16 = (bf16[1024,256]{1,0:T(8,128)(2,1)S(1)}, bf16[1024,256]{1,0:T(8,128)(2,1)S(1)}, u32[]{:S(2)}, u32[]{:S(2)}) collective-permute-start(bf16[1024,256]{1,0:T(8,128)(2,1)S(1)} %get-tuple-element.201), channel_id=1, source_target_pairs={{0,1},{1,2},{2,3},{3,0},{4,5},{5,6},{6,7},{7,4},{8,9},{9,10},{10,1... | collective-permute-start | bytes 1572872 | tf_op jit(solution)/shard_map/ppermute | solution.py:54
  75.3 3.1 %collective-permute-start.18 = (bf16[1024,256]{1,0:T(8,128)(2,1)S(1)}, bf16[1024,256]{1,0:T(8,128)(2,1)S(1)}, u32[]{:S(2)}, u32[]{:S(2)}) collective-permute-start(bf16[1024,256]{1,0:T(8,128)(2,1)S(1)} %collective-permute-done.15), channel_id=1, source_target_pairs={{0,16},{16,0},{1,17},{17,1},{2,18},{18,2},{3,19},{19,3},{4,20},{20... | collective-permute-start | bytes 1572872 | tf_op jit(solution)/shard_map/ppermute | solution.py:70
  76.9 7.0 %collective-permute-start.19 = (bf16[1024,256]{1,0:T(8,128)(2,1)S(1)}, bf16[1024,256]{1,0:T(8,128)(2,1)S(1)}, u32[]{:S(2)}, u32[]{:S(2)}) collective-permute-start(bf16[1024,256]{1,0:T(8,128)(2,1)S(1)} %get-tuple-element.130), channel_id=1, source_target_pairs={{0,16},{16,0},{1,17},{17,1},{2,18},{18,2},{3,19},{19,3},{4,20},{20... | collective-permute-start | bytes 1572872 | tf_op jit(solution)/shard_map/ppermute | solution.py:70
  83.8 19.1 %copy-start.7 = (bf16[512,512]{1,0:T(8,128)(2,1)S(1)}, bf16[512,512]{1,0:T(8,128)(2,1)}, u32[]{:S(2)}) copy-start(bf16[512,512]{1,0:T(8,128)(2,1)} %w_out.1) | copy-start | bytes 1572868
  83.8 2.0 %collective-permute-start.20 = (bf16[1024,256]{1,0:T(8,128)(2,1)S(1)}, bf16[1024,256]{1,0:T(8,128)(2,1)S(1)}, u32[]{:S(2)}, u32[]{:S(2)}) collective-permute-start(bf16[1024,256]{1,0:T(8,128)(2,1)S(1)} %get-tuple-element.131), channel_id=1, source_target_pairs={{0,16},{16,0},{1,17},{17,1},{2,18},{18,2},{3,19},{19,3},{4,20},{20... | collective-permute-start | bytes 1572872 | tf_op jit(solution)/shard_map/ppermute | solution.py:70
  86.0 10.3 %collective-permute-start.21 = (bf16[256,512]{1,0:T(8,128)(2,1)S(1)}, bf16[256,512]{1,0:T(8,128)(2,1)S(1)}, u32[]{:S(2)}, u32[]{:S(2)}) collective-permute-start(bf16[256,512]{1,0:T(8,128)(2,1)S(1)} %get-tuple-element.133), channel_id=1, source_target_pairs={{0,32},{32,64},{64,96},{96,0},{1,33},{33,65},{65,97},{97,1},{2,34}... | collective-permute-start | bytes 786440 | tf_op jit(solution)/shard_map/ppermute | solution.py:58
  87.6 8.7 %collective-permute-start.22 = (bf16[256,512]{1,0:T(8,128)(2,1)S(1)}, bf16[256,512]{1,0:T(8,128)(2,1)S(1)}, u32[]{:S(2)}, u32[]{:S(2)}) collective-permute-start(bf16[256,512]{1,0:T(8,128)(2,1)S(1)} %get-tuple-element.134), channel_id=1, source_target_pairs={{0,96},{32,0},{64,32},{96,64},{1,97},{33,1},{65,33},{97,65},{2,98}... | collective-permute-start | bytes 786440 | tf_op jit(solution)/shard_map/ppermute | solution.py:58
  90.0 12.8 %collective-permute-start.23 = (bf16[256,512]{1,0:T(8,128)(2,1)S(1)}, bf16[256,512]{1,0:T(8,128)(2,1)S(1)}, u32[]{:S(2)}, u32[]{:S(2)}) collective-permute-start(bf16[256,512]{1,0:T(8,128)(2,1)S(1)} %get-tuple-element.135), channel_id=1, source_target_pairs={{0,64},{32,96},{64,0},{96,32},{1,65},{33,97},{65,1},{97,33},{2,66}... | collective-permute-start | bytes 786440 | tf_op jit(solution)/shard_map/ppermute | solution.py:58
  103.7 8.1 %collective-permute-start.26 = (bf16[256,512]{1,0:T(8,128)(2,1)S(1)}, bf16[256,512]{1,0:T(8,128)(2,1)S(1)}, u32[]{:S(2)}, u32[]{:S(2)}) collective-permute-start(bf16[256,512]{1,0:T(8,128)(2,1)S(1)} %get-tuple-element.139.rest_2_), channel_id=1, source_target_pairs={{0,32},{32,64},{64,96},{96,0},{1,33},{33,65},{65,97},{97,1},{2,34}... | collective-permute-start | bytes 786440 | tf_op jit(solution)/shard_map/ppermute | solution.py:58
  104.3 7.5 %collective-permute-start.24 = (bf16[256,512]{1,0:T(8,128)(2,1)S(1)}, bf16[256,512]{1,0:T(8,128)(2,1)S(1)}, u32[]{:S(2)}, u32[]{:S(2)}) collective-permute-start(bf16[256,512]{1,0:T(8,128)(2,1)S(1)} %get-tuple-element.139.rest_2_), channel_id=1, source_target_pairs={{0,96},{32,0},{64,32},{96,64},{1,97},{33,1},{65,33},{97,65},{2,98}... | collective-permute-start | bytes 786440 | tf_op jit(solution)/shard_map/ppermute | solution.py:58
  106.4 12.2 %collective-permute-start.25 = (bf16[256,512]{1,0:T(8,128)(2,1)S(1)}, bf16[256,512]{1,0:T(8,128)(2,1)S(1)}, u32[]{:S(2)}, u32[]{:S(2)}) collective-permute-start(bf16[256,512]{1,0:T(8,128)(2,1)S(1)} %get-tuple-element.139.rest_2_), channel_id=1, source_target_pairs={{0,64},{32,96},{64,0},{96,32},{1,65},{33,97},{65,1},{97,33},{2,66}... | collective-permute-start | bytes 786440 | tf_op jit(solution)/shard_map/ppermute | solution.py:58
  107.4 12.1 %collective-permute-start.27 = (bf16[256,512]{1,0:T(8,128)(2,1)S(1)}, bf16[256,512]{1,0:T(8,128)(2,1)S(1)}, u32[]{:S(2)}, u32[]{:S(2)}) collective-permute-start(bf16[256,512]{1,0:T(8,128)(2,1)S(1)} %get-tuple-element.139.rest_2_), channel_id=1, source_target_pairs={{0,16},{16,0},{1,17},{17,1},{2,18},{18,2},{3,19},{19,3},{4,20},{20... | collective-permute-start | bytes 786440 | tf_op jit(solution)/shard_map/ppermute | solution.py:70
  111.8 8.9 %collective-permute-start.28 = (bf16[256,512]{1,0:T(8,128)(2,1)S(1)}, bf16[256,512]{1,0:T(8,128)(2,1)S(1)}, u32[]{:S(2)}, u32[]{:S(2)}) collective-permute-start(bf16[256,512]{1,0:T(8,128)(2,1)S(1)} %collective-permute-done.24.rest_3_), channel_id=1, source_target_pairs={{0,16},{16,0},{1,17},{17,1},{2,18},{18,2},{3,19},{19,3},{4,20},{20... | collective-permute-start | bytes 786440 | tf_op jit(solution)/shard_map/ppermute | solution.py:70
  118.6 2.1 %collective-permute-start.29 = (bf16[256,512]{1,0:T(8,128)(2,1)S(1)}, bf16[256,512]{1,0:T(8,128)(2,1)S(1)}, u32[]{:S(2)}, u32[]{:S(2)}) collective-permute-start(bf16[256,512]{1,0:T(8,128)(2,1)S(1)} %collective-permute-done.25.rest_4_), channel_id=1, source_target_pairs={{0,16},{16,0},{1,17},{17,1},{2,18},{18,2},{3,19},{19,3},{4,20},{20... | collective-permute-start | bytes 786440 | tf_op jit(solution)/shard_map/ppermute | solution.py:70
  119.6 1.5 collective-permute-start.30
  126.3 5.7 %collective-permute-start.31 = (bf16[6144,256]{1,0:T(8,128)(2,1)S(1)}, bf16[6144,256]{1,0:T(8,128)(2,1)S(1)}, u32[]{:S(2)}, u32[]{:S(2)}) collective-permute-start(bf16[6144,256]{1,0:T(8,128)(2,1)S(1)} %get-tuple-element.162), channel_id=1, source_target_pairs={{0,16},{16,0},{1,17},{17,1},{2,18},{18,2},{3,19},{19,3},{4,20},{20... | collective-permute-start | bytes 9437192 | tf_op jit(solution)/shard_map/ppermute | solution.py:70
  126.4 8.4 %collective-permute-start.34 = (bf16[1024,256]{1,0:T(8,128)(2,1)S(1)}, bf16[1024,256]{1,0:T(8,128)(2,1)S(1)}, u32[]{:S(2)}, u32[]{:S(2)}) collective-permute-start(bf16[1024,256]{1,0:T(8,128)(2,1)S(1)} %get-tuple-element.167), channel_id=1, source_target_pairs={{0,3},{1,0},{2,1},{3,2},{4,7},{5,4},{6,5},{7,6},{8,11},{9,8},{10,9... | collective-permute-start | bytes 1572872 | tf_op jit(solution)/shard_map/ppermute | solution.py:54
  127.6 9.5 %collective-permute-start.35 = (bf16[1024,256]{1,0:T(8,128)(2,1)S(1)}, bf16[1024,256]{1,0:T(8,128)(2,1)S(1)}, u32[]{:S(2)}, u32[]{:S(2)}) collective-permute-start(bf16[1024,256]{1,0:T(8,128)(2,1)S(1)} %get-tuple-element.168), channel_id=1, source_target_pairs={{0,1},{1,2},{2,3},{3,0},{4,5},{5,6},{6,7},{7,4},{8,9},{9,10},{10,1... | collective-permute-start | bytes 1572872 | tf_op jit(solution)/shard_map/ppermute | solution.py:54
  132.1 8.4 %collective-permute-start.33 = (bf16[1024,256]{1,0:T(8,128)(2,1)S(1)}, bf16[1024,256]{1,0:T(8,128)(2,1)S(1)}, u32[]{:S(2)}, u32[]{:S(2)}) collective-permute-start(bf16[1024,256]{1,0:T(8,128)(2,1)S(1)} %get-tuple-element.198), channel_id=1, source_target_pairs={{0,3},{1,0},{2,1},{3,2},{4,7},{5,4},{6,5},{7,6},{8,11},{9,8},{10,9... | collective-permute-start | bytes 1572872 | tf_op jit(solution)/shard_map/ppermute | solution.py:54
  133.0 9.7 %collective-permute-start.32 = (bf16[1024,256]{1,0:T(8,128)(2,1)S(1)}, bf16[1024,256]{1,0:T(8,128)(2,1)S(1)}, u32[]{:S(2)}, u32[]{:S(2)}) collective-permute-start(bf16[1024,256]{1,0:T(8,128)(2,1)S(1)} %get-tuple-element.199), channel_id=1, source_target_pairs={{0,1},{1,2},{2,3},{3,0},{4,5},{5,6},{6,7},{7,4},{8,9},{9,10},{10,1... | collective-permute-start | bytes 1572872 | tf_op jit(solution)/shard_map/ppermute | solution.py:54
  137.4 14.3 %collective-permute-start.39 = (bf16[2048,256]{1,0:T(8,128)(2,1)S(1)}, bf16[2048,256]{1,0:T(8,128)(2,1)S(1)}, u32[]{:S(2)}, u32[]{:S(2)}) collective-permute-start(bf16[2048,256]{1,0:T(8,128)(2,1)S(1)} %get-tuple-element.177), channel_id=1, source_target_pairs={{0,3},{1,0},{2,1},{3,2},{4,7},{5,4},{6,5},{7,6},{8,11},{9,8},{10,9... | collective-permute-start | bytes 3145736 | tf_op jit(solution)/shard_map/ppermute | solution.py:54
  137.5 16.5 %collective-permute-start.40 = (bf16[2048,256]{1,0:T(8,128)(2,1)S(1)}, bf16[2048,256]{1,0:T(8,128)(2,1)S(1)}, u32[]{:S(2)}, u32[]{:S(2)}) collective-permute-start(bf16[2048,256]{1,0:T(8,128)(2,1)S(1)} %get-tuple-element.169), channel_id=1, source_target_pairs={{0,1},{1,2},{2,3},{3,0},{4,5},{5,6},{6,7},{7,4},{8,9},{9,10},{10,1... | collective-permute-start | bytes 3145736 | tf_op jit(solution)/shard_map/ppermute | solution.py:54
  143.0 10.9 %collective-permute-start.36 = (bf16[2048,256]{1,0:T(8,128)(2,1)S(1)}, bf16[2048,256]{1,0:T(8,128)(2,1)S(1)}, u32[]{:S(2)}, u32[]{:S(2)}) collective-permute-start(bf16[2048,256]{1,0:T(8,128)(2,1)S(1)} %get-tuple-element.173), channel_id=1, source_target_pairs={{0,16},{16,0},{1,17},{17,1},{2,18},{18,2},{3,19},{19,3},{4,20},{20... | collective-permute-start | bytes 3145736 | tf_op jit(solution)/shard_map/ppermute | solution.py:70
  143.3 23.7 %collective-permute-start.37 = (bf16[2048,256]{1,0:T(8,128)(2,1)S(1)}, bf16[2048,256]{1,0:T(8,128)(2,1)S(1)}, u32[]{:S(2)}, u32[]{:S(2)}) collective-permute-start(bf16[2048,256]{1,0:T(8,128)(2,1)S(1)} %get-tuple-element.174), channel_id=1, source_target_pairs={{0,3},{1,0},{2,1},{3,2},{4,7},{5,4},{6,5},{7,6},{8,11},{9,8},{10,9... | collective-permute-start | bytes 3145736 | tf_op jit(solution)/shard_map/ppermute | solution.py:54
  144.2 26.3 %collective-permute-start.38 = (bf16[2048,256]{1,0:T(8,128)(2,1)S(1)}, bf16[2048,256]{1,0:T(8,128)(2,1)S(1)}, u32[]{:S(2)}, u32[]{:S(2)}) collective-permute-start(bf16[2048,256]{1,0:T(8,128)(2,1)S(1)} %get-tuple-element.172), channel_id=1, source_target_pairs={{0,1},{1,2},{2,3},{3,0},{4,5},{5,6},{6,7},{7,4},{8,9},{9,10},{10,1... | collective-permute-start | bytes 3145736 | tf_op jit(solution)/shard_map/ppermute | solution.py:54
  154.0 19.7 %copy-start.2 = (bf16[512,512]{1,0:T(8,128)(2,1)S(1)}, bf16[512,512]{1,0:T(8,128)(2,1)}, u32[]{:S(2)}) copy-start(bf16[512,512]{1,0:T(8,128)(2,1)} %w_grid.5) | copy-start | bytes 1572868
  154.4 16.8 %collective-permute-start.44 = (bf16[256,512]{1,0:T(8,128)(2,1)S(1)}, bf16[256,512]{1,0:T(8,128)(2,1)S(1)}, u32[]{:S(2)}, u32[]{:S(2)}) collective-permute-start(bf16[256,512]{1,0:T(8,128)(2,1)S(1)} %get-tuple-element.181), channel_id=1, source_target_pairs={{0,4},{1,5},{2,6},{3,7},{4,8},{5,9},{6,10},{7,11},{8,12},{9,13},{1... | collective-permute-start | bytes 786440 | tf_op jit(solution)/shard_map/ppermute | solution.py:54
  154.4 19.3 %collective-permute-start.45 = (bf16[256,512]{1,0:T(8,128)(2,1)S(1)}, bf16[256,512]{1,0:T(8,128)(2,1)S(1)}, u32[]{:S(2)}, u32[]{:S(2)}) collective-permute-start(bf16[256,512]{1,0:T(8,128)(2,1)S(1)} %get-tuple-element.182), channel_id=1, source_target_pairs={{0,8},{1,9},{2,10},{3,11},{4,12},{5,13},{6,14},{7,15},{8,0},{9,1},... | collective-permute-start | bytes 786440 | tf_op jit(solution)/shard_map/ppermute | solution.py:54
  154.5 19.2 %collective-permute-start.46 = (bf16[256,512]{1,0:T(8,128)(2,1)S(1)}, bf16[256,512]{1,0:T(8,128)(2,1)S(1)}, u32[]{:S(2)}, u32[]{:S(2)}) collective-permute-start(bf16[256,512]{1,0:T(8,128)(2,1)S(1)} %get-tuple-element.183), channel_id=1, source_target_pairs={{0,12},{1,13},{2,14},{3,15},{4,0},{5,1},{6,2},{7,3},{8,4},{9,5},{1... | collective-permute-start | bytes 786440 | tf_op jit(solution)/shard_map/ppermute | solution.py:54
  171.0 9.6 %collective-permute-start.41 = (bf16[256,512]{1,0:T(8,128)(2,1)S(1)}, bf16[256,512]{1,0:T(8,128)(2,1)S(1)}, u32[]{:S(2)}, u32[]{:S(2)}) collective-permute-start(bf16[256,512]{1,0:T(8,128)(2,1)S(1)} %get-tuple-element.187), channel_id=1, source_target_pairs={{0,4},{1,5},{2,6},{3,7},{4,8},{5,9},{6,10},{7,11},{8,12},{9,13},{1... | collective-permute-start | bytes 786440 | tf_op jit(solution)/shard_map/ppermute | solution.py:54
  171.0 9.5 %collective-permute-start.42 = (bf16[256,512]{1,0:T(8,128)(2,1)S(1)}, bf16[256,512]{1,0:T(8,128)(2,1)S(1)}, u32[]{:S(2)}, u32[]{:S(2)}) collective-permute-start(bf16[256,512]{1,0:T(8,128)(2,1)S(1)} %get-tuple-element.188), channel_id=1, source_target_pairs={{0,8},{1,9},{2,10},{3,11},{4,12},{5,13},{6,14},{7,15},{8,0},{9,1},... | collective-permute-start | bytes 786440 | tf_op jit(solution)/shard_map/ppermute | solution.py:54
  171.2 10.0 %collective-permute-start.43 = (bf16[256,512]{1,0:T(8,128)(2,1)S(1)}, bf16[256,512]{1,0:T(8,128)(2,1)S(1)}, u32[]{:S(2)}, u32[]{:S(2)}) collective-permute-start(bf16[256,512]{1,0:T(8,128)(2,1)S(1)} %get-tuple-element.189), channel_id=1, source_target_pairs={{0,12},{1,13},{2,14},{3,15},{4,0},{5,1},{6,2},{7,3},{8,4},{9,5},{1... | collective-permute-start | bytes 786440 | tf_op jit(solution)/shard_map/ppermute | solution.py:54
  181.7 3.1 %collective-permute-start.47 = (f32[256,512]{1,0:T(8,128)S(1)}, f32[256,512]{1,0:T(8,128)S(1)}, u32[]{:S(2)}, u32[]{:S(2)}) collective-permute-start(f32[256,512]{1,0:T(8,128)S(1)} %row_sum_other.1), channel_id=1, source_target_pairs={{0,16},{16,0},{1,17},{17,1},{2,18},{18,2},{3,19},{19,3},{4,20},{20... | collective-permute-start | bytes 1572872 | tf_op jit(solution)/shard_map/ppermute | solution.py:70
